TPU v7x, 256 devices: a whole 4x4x8 slice. The times are simulated.
256 devices in a mesh: pair: 8 (over x, y_lo), grid: 32 (over z, y_hi, core).
Axes of the slice: x: 4, y: 4 (y_hi: 2, y_lo: 2; y = y_hi * 2 + y_lo), z: 8, core: 2. Of those that a mesh axis runs over, the one named last changes fastest.
Arguments:
- orbital_b: bfloat16 [16, 1408, 9600], P(None, 'pair', 'grid'), may hold values from -0.15625 to 0.15625
- pair_list: int32 [8, 2], replicated, may hold values from 0 to 15
- eps_occ: float32 [16], replicated, may hold values from -2 to -0.3
- eps_vir: float32 [1408], replicated, may hold values from 0.2 to 3
Outputs:
- density: float32 [1408, 1408], P('grid', 'pair')
All inputs are finite; a program needn't handle non-finite values.
Results may differ from a plain program's by a relative error of at most 0.0012.
Values may be sent and summed in bfloat16 or wider, within the bound.
No kernel may reach another device: no remote copies, remote signals or barrier semaphores. Data moves between devices by JAX's collectives and lax.ppermute only.
A program may use at most 64 MiB of HBM per device.

v0:
```python
import jax
import jax.numpy as jnp
from jax import lax
from jax.sharding import PartitionSpec as P


def local(orbital_b, pair_list, eps_occ, eps_vir):
    group = lax.axis_index("pair")
    block = lax.axis_index("grid")
    ngrid = lax.axis_size("grid")
    nvir = eps_vir.shape[0]
    width = nvir // ngrid
    outgoing = jnp.stack([orbital_b[pair_list[:, 0]], orbital_b[pair_list[:, 1]]], axis=1)
    incoming = lax.all_to_all(outgoing, "pair", split_axis=0, concat_axis=2, tiled=True)
    left_slab = incoming[0, 0]
    right_slab = incoming[0, 1]
    chosen = lax.dynamic_index_in_dim(pair_list, group, 0, keepdims=False)
    shift_occ = eps_occ[chosen[0]] + eps_occ[chosen[1]]
    row_start = block * width
    row_eps = lax.dynamic_slice_in_dim(eps_vir, row_start, width, 0)
    k_rows = lax.psum_scatter(
        jnp.dot(left_slab, right_slab.T, preferred_element_type=jnp.float32),
        "grid",
        scatter_dimension=0,
        tiled=True,
    )
    amp_rows = k_rows / (row_eps[:, None] + eps_vir[None, :] - shift_occ)
    amp_cols = lax.all_to_all(amp_rows, "grid", split_axis=1, concat_axis=0, tiled=True)
    tilde_rows = (2.0 * amp_rows - amp_cols.T).astype(jnp.bfloat16)
    tilde_cols = (2.0 * amp_cols - amp_rows.T).astype(jnp.bfloat16)
    rows16 = amp_rows.astype(jnp.bfloat16)
    piece = lax.all_gather(rows16, "grid", axis=0, tiled=True)
    carry = jnp.dot(tilde_cols.T, piece, preferred_element_type=jnp.float32)
    added = carry + jnp.dot(tilde_rows, piece.T, preferred_element_type=jnp.float32)
    return lax.psum_scatter(added, "pair", scatter_dimension=1, tiled=True)


def solution(mesh):
    in_specs = (P(None, "pair", "grid"), P(), P(), P())
    out_specs = P("grid", "pair")
    return jax.shard_map(local, mesh=mesh, in_specs=in_specs, out_specs=out_specs, check_vma=False)
```

profile of v0, /device:TPU:32, one launch (start us, length us, event | category | flops | bytes accessed | tf_op | source)
XLA Modules:
  0.0 340.3 jit_solution(3330779783447002022)
XLA Ops:
  6.5 0.8 fusion.9
  7.4 0.8 copy-done
  8.2 0.8 gather_fusion
  9.0 1.7 gather_fusion.1
  10.7 1.6 pad_maximum_fusion
  12.3 33.1 %all_to_all.37 = bf16[8,2,176,300]{3,2,1,0:T(8,128)(2,1)} all-to-all(bf16[8,2,176,300]{3,2,1,0:T(8,128)(2,1)S(1)} %pad_maximum_fusion), channel_id=1, replica_groups=mesh['pair'=8,'grid'=32] {'pair'}, dimensions={0} | all-to-all | bytes 3379200 | tf_op jit(solution)/shard_map/all_to_all | solution.py:14
  45.4 4.7 %copy.9 = bf16[1,2,8,176,300]{3,2,4,1,0:T(8,128)(2,1)} copy(bf16[1,2,8,176,300]{4,3,1,2,0:T(8,128)(2,1)} %bitcast.48) | data formatting | bytes 3379200 | tf_op jit(solution)/shard_map/all_to_all | solution.py:14
  50.1 5.3 %all_to_all.30 = bf16[1,2,1408,300]{2,3,1,0:T(8,128)(2,1)} reshape(bf16[1,2,8,176,300]{3,2,4,1,0:T(8,128)(2,1)} %copy.9) | data formatting | bytes 3379200 | tf_op jit(solution)/shard_map/all_to_all | solution.py:14
  55.4 6.8 %fusion.1 = f32[1408,1408]{1,0:T(8,128)} fusion(bf16[1,2,1408,300]{2,3,1,0:T(8,128)(2,1)} %all_to_all.30), kind=kOutput, calls=%fused_computation.5 | convolution fusion | flops 1189478400 | bytes 9619456 | tf_op jit(solution)/shard_map/dot_general | solution.py:22
  62.2 103.5 %fusion = f32[48,1408]{1,0:T(8,128)S(1)} fusion(f32[1408,1408]{1,0:T(8,128)} %fusion.1), kind=kCustom, calls=%all-reduce-scatter | all-reduce-scatter fusion | flops 2162689 | bytes 8201216
  165.7 2.2 collective-permute-start
  168.0 5.8 %collective-permute-start.1 = (f32[48,1408]{1,0:T(8,128)S(1)}, f32[48,1408]{1,0:T(8,128)}, u32[]{:S(2)}, u32[]{:S(2)}) collective-permute-start(f32[48,1408]{1,0:T(8,128)S(1)} %fusion), channel_id=1, source_target_pairs={{0,2},{1,3},{2,4},{3,5},{4,6},{5,7},{6,8},{7,9},{8,10},{9,11},{10,... | collective-permute-start | bytes 811016
  173.8 11.7 %collective-permute-start.2 = (f32[28,1408]{1,0:T(8,128)S(1)}, f32[28,1408]{1,0:T(8,128)S(1)}, u32[]{:S(2)}, u32[]{:S(2)}) collective-permute-start(f32[28,1408]{1,0:T(8,128)S(1)} %slice.32), channel_id=1, source_target_pairs={{0,3},{1,4},{2,5},{3,6},{4,7},{5,8},{6,9},{7,10},{8,11},{9,12},{10... | collective-permute-start | bytes 473096
  185.5 0.5 fusion.13
  189.9 0.6 fusion.14
  191.9 0.6 dynamic-slice.4
  193.1 0.6 copy-done.3
  193.8 0.7 copy-done.2
  194.5 3.3 concatenate
  197.8 0.8 convert_bitcast_fusion
  198.6 1.8 all_to_all.31
  200.5 1.6 copy.10
  202.1 1.0 reshape.31
  203.1 19.1 %all_to_all.38 = f32[32,1,1936]{2,1,0:T(1,128)S(1)} all-to-all(f32[32,1,1936]{2,1,0:T(1,128)S(1)} %reshape.31), channel_id=1, replica_groups=mesh['pair'=8,'grid'=32] {'grid'}, dimensions={0} | all-to-all | bytes 495616 | tf_op jit(solution)/shard_map/all_to_all | solution.py:28
  222.6 1.3 reduce
  225.1 56.8 %all-gather.3.cloned.1.call-done = bf16[32,44,1408]{2,1,0:T(8,128)(2,1)} async-done(((bf16[1,44,1408]{2,1,0:T(8,128)(2,1)}), bf16[32,44,1408]{2,1,0:T(8,128)(2,1)}) %all-gather.3.cloned.1.call-update) | async-done | bytes 3964944 | tf_op jit(solution)/shard_map/all_gather | solution.py:32
  281.9 6.0 %reshape.27 = bf16[1408,1408]{1,0:T(8,128)(2,1)} reshape(bf16[32,44,1408]{2,1,0:T(8,128)(2,1)} %all-gather.3.cloned.1.call-done) | data formatting | bytes 7929856
  288.0 3.0 fusion.4
  291.3 1.3 convolution_add_fusion
  292.6 1.1 copy.12
  293.7 38.1 %reduce-scatter.6.cloned.1.call-done = f32[176,44]{1,0:T(8,128)} async-done(((f32[1408,44]{1,0:T(8,128)}), f32[176,44]{1,0:T(8,128)}) %reduce-scatter.6.cloned.1.call-update) | async-done | bytes 30992
  331.8 1.6 copy.13
  (29 shorter events, 2.4 us)
Async XLA Ops:
  6.5 1.6 copy-start
  6.5 275.4 %all-gather.3.cloned.1.call-start = ((), (), s32[]{:S(2)}) async-start(), calls=%async_computation.3 | async-start | bytes 4460544 | tf_op jit(solution)/shard_map/all_gather | solution.py:32
  62.2 123.2 %copy-start.5 = (s32[8,2]{0,1:T(2,128)S(1)}, s32[8,2]{0,1:T(2,128)}, u32[]{:S(2)}) copy-start(s32[8,2]{0,1:T(2,128)} %param.5) | copy-start | bytes 196
  62.2 127.7 %copy-start.6 = (f32[16]{0:T(128)S(1)}, f32[16]{0:T(128)}, u32[]{:S(2)}) copy-start(f32[16]{0:T(128)} %param.6) | copy-start | bytes 196
  62.2 129.6 %copy-start.4 = (f32[1408]{0:T(1024)S(1)}, f32[1408]{0:T(1024)}, u32[]{:S(2)}) copy-start(f32[1408]{0:T(1024)} %param.7) | copy-start | bytes 16900
  62.2 129.7 %copy-start.7 = (u32[256]{0:T(256)S(1)}, u32[256]{0:T(256)}, u32[]{:S(2)}) copy-start(u32[256]{0:T(256)} %constant.30) | copy-start | bytes 3076
  165.7 27.4 %collective-permute-start = (f32[48,1408]{1,0:T(8,128)S(1)}, f32[48,1408]{1,0:T(8,128)S(1)}, u32[]{:S(2)}, u32[]{:S(2)}) collective-permute-start(f32[48,1408]{1,0:T(8,128)S(1)} %fusion), channel_id=1, source_target_pairs={{0,1},{1,2},{2,3},{3,4},{4,5},{5,6},{6,7},{7,8},{8,9},{9,10},{10,1... | collective-permute-start | bytes 811016
  168.0 26.5 %collective-permute-start.1 = (f32[48,1408]{1,0:T(8,128)S(1)}, f32[48,1408]{1,0:T(8,128)}, u32[]{:S(2)}, u32[]{:S(2)}) collective-permute-start(f32[48,1408]{1,0:T(8,128)S(1)} %fusion), channel_id=1, source_target_pairs={{0,2},{1,3},{2,4},{3,5},{4,6},{5,7},{6,8},{7,9},{8,10},{9,11},{10,... | collective-permute-start | bytes 811016
  173.8 19.3 %collective-permute-start.2 = (f32[28,1408]{1,0:T(8,128)S(1)}, f32[28,1408]{1,0:T(8,128)S(1)}, u32[]{:S(2)}, u32[]{:S(2)}) collective-permute-start(f32[28,1408]{1,0:T(8,128)S(1)} %slice.32), channel_id=1, source_target_pairs={{0,3},{1,4},{2,5},{3,6},{4,7},{5,8},{6,9},{7,10},{8,11},{9,12},{10... | collective-permute-start | bytes 473096
  193.1 0.7 copy-start.3
  193.8 0.7 copy-start.2
  198.6 133.2 %reduce-scatter.6.cloned.1.call-start = ((), (), s32[]{:S(2)}) async-start(), calls=%async_computation.4 | async-start | bytes 811008
  288.0 3.3 copy-start.1
Sparse Core Ops, SparseCore 0:
  198.7 83.1 all-gather.2
  293.9 37.9 reduce-scatter.5
where the time goes:
time: 341 us; the launch traced here: 340 us
  blocking collectives  156 us (46%)
  waiting for transfers between devices  94.9 us (28%)
  local copies, waits for them, and re-layouts  35.1 us (10%)
  starting transfers between devices  19.7 us (6%)
  between operations  19.2 us (6%)
  matrix products  11.1 us (3%)
  other arithmetic  4.5 us (1%)
    unnamed x1, blocking collectives  104 us
    all_gather x1, waiting for transfers between devices, local(): piece = lax.all_gather(rows16, 'grid', axis=0, tiled=True)  56.8 us
    unnamed x6, waiting for transfers between devices  38.1 us
    all_to_all x1, blocking collectives, local(): lax.all_to_all(outgoing, 'pair', split_axis=0, concat_axis=2, tiled=True)  33.1 us
    unnamed x4, starting transfers between devices  19.7 us
    all_to_all x1, blocking collectives, local(): lax.all_to_all(amp_rows, 'grid', split_axis=1, concat_axis=0, tiled=True)  19.1 us
    unnamed x24, local copies, waits for them, and re-layouts  16.7 us
    all_to_all x2, local copies, waits for them, and re-layouts, local(): lax.all_to_all(outgoing, 'pair', split_axis=0, concat_axis=2, tiled=True)  9.94 us
  transfers between devices with their start and end apart: 5, of which 2 were waited for; matrix products, arithmetic and copies ran while one was open for 2% of the time, Pallas kernels for 0%

commit v1 on v0

v1 whole, which is shorter than its diff:
```python
import functools

import jax
import jax.numpy as jnp
from jax import lax
from jax.experimental import pallas as pl
from jax.experimental.pallas import tpu as pltpu
from jax.sharding import Mesh
from jax.sharding import PartitionSpec as P

F32 = jnp.float32
BF16 = jnp.bfloat16
SLABS = ("x", "yl")
VMEM = pl.BlockSpec(memory_space=pltpu.VMEM)
SMEM = pl.BlockSpec(memory_space=pltpu.SMEM)
LIMIT = 48 * 1024 * 1024


def swap(value, axis):
    return lax.ppermute(value, axis, [(0, 1), (1, 0)])


def shift(value, axis, step):
    size = lax.axis_size(axis)
    return lax.ppermute(value, axis, [(i, (i + step) % size) for i in range(size)])


def dot_nt(a, b):
    return lax.dot_general(a, b, (((1,), (1,)), ((), ())), preferred_element_type=F32)


def integral_kernel(padded, where_ref, near_ref, far_ref, out_ref):
    sources, rows, naux = near_ref.shape
    half = sources // 2
    slab = rows - 2 * padded
    start = pl.multiple_of(where_ref[1] * padded, padded)
    total = None
    for ref in (near_ref, far_ref):
        for y in range(2):
            a = ref[half * y : half * (y + 1), pl.ds(start, padded), :].reshape(half * padded, naux)
            b = ref[half * y : half * (y + 1), 2 * padded :, :].reshape(half * slab, naux)
            term = dot_nt(a, b)
            total = term if total is None else total + term
    out_ref[...] = total


def density_kernel(nz, width, padded, where_ref, rows_ref, *refs):
    pieces = refs[: 2 * nz]
    out_ref, natural, blocks, highs = refs[2 * nz :]
    z, c, chunk = where_ref[0], where_ref[1], where_ref[2]
    nvir = rows_ref.shape[1]
    slab = nvir // nz

    def join(own, far):
        first, second = jnp.where(c == 0, own, far), jnp.where(c == 0, far, own)
        parts = []
        for y in range(2):
            for piece in (first, second):
                parts.append(piece[:, y * padded : y * padded + width])
        return jnp.concatenate(parts, axis=1)

    def pad(block):
        zeros = jnp.zeros((block.shape[0], padded - width), block.dtype)
        halves = []
        for h in range(2):
            parts = []
            for y in range(2):
                at = (2 * y + h) * width
                parts += [block[:, at : at + width], zeros]
            halves.append(jnp.concatenate(parts, axis=1))
        return jnp.where(c == 0, halves[0], halves[1]), jnp.where(c == 0, halves[1], halves[0])

    rows = rows_ref[...]
    column = lax.broadcasted_iota(jnp.int32, rows.shape, 1)
    row = lax.broadcasted_iota(jnp.int32, rows.shape, 0)
    pick = jnp.where((column == chunk * width + row) & (row < width), 1.0, 0.0).astype(BF16)
    flipped = []
    for i in range(2 * nz):
        value = pieces[i][...]
        high = value.astype(BF16)
        rest = value - high.astype(F32)
        middle = rest.astype(BF16)
        low = (rest - middle.astype(F32)).astype(BF16)
        highs[i] = high
        flipped.append(dot_nt(pick, high) + (dot_nt(pick, middle) + dot_nt(pick, low)))
    for k in range(nz):
        natural[k] = rows[:, k * slab : (k + 1) * slab]
    for r in range(nz):
        blocks[lax.rem(z + r, nz)] = join(flipped[2 * r], flipped[2 * r + 1])
    turned = jnp.concatenate([blocks[k] for k in range(nz)], axis=1)
    tilde = (2.0 * rows - turned).astype(BF16)
    total = None
    for r in range(nz):
        own, far = pad(natural[lax.rem(z + r, nz)])
        for i, mine in ((2 * r, own), (2 * r + 1, far)):
            tilde_t = (2.0 * flipped[i] - mine).astype(BF16)
            term = jnp.dot(tilde_t, highs[i], preferred_element_type=F32)
            total = term if total is None else total + term
    for k in range(nz):
        out_ref[k] = total[:, k * slab : (k + 1) * slab]
    for r in range(nz):
        at = lax.rem(z + r, nz)
        out_ref[at] += join(dot_nt(tilde, highs[2 * r]), dot_nt(tilde, highs[2 * r + 1]))


def local(orbital_b, pair_list, eps_occ, eps_vir):
    slab, naux = orbital_b.shape[1:]
    nvir = eps_vir.shape[0]
    z, yh, c = (lax.axis_index(a) for a in ("z", "yh", "c"))
    nz = lax.axis_size("z")
    width = slab // 4
    padded = (width + 8) // 8 * 8
    group = lax.axis_index(SLABS)
    chunk = z * 4 + yh * 2 + c
    where = jnp.stack([z, c, chunk])

    left = orbital_b[pair_list[:, 0]].reshape(8, 2, 2, width, naux)
    left = jnp.pad(left, ((0, 0), (0, 0), (0, 0), (0, padded - width), (0, 0)))
    left = left.reshape(8, 2, 2 * padded, naux).transpose(1, 0, 2, 3)
    right = jnp.broadcast_to(orbital_b[pair_list[:, 1]][None], (2, 8, slab, naux))
    outgoing = jnp.concatenate([left, right], axis=2).reshape(16, 2 * padded + slab, naux)
    near = lax.all_to_all(outgoing, ("yh", "x", "yl"), split_axis=0, concat_axis=0, tiled=True)
    far = swap(near, "c")

    part = pl.pallas_call(
        functools.partial(integral_kernel, padded),
        out_shape=jax.ShapeDtypeStruct((8 * padded, nvir), F32),
        in_specs=[SMEM, VMEM, VMEM],
        out_specs=VMEM,
        compiler_params=pltpu.CompilerParams(vmem_limit_bytes=LIMIT),
    )(where, near, far).reshape(8, padded, nvir)

    def own(offset):
        return lax.dynamic_index_in_dim(part, lax.rem(z + offset, nz), 0, keepdims=False)

    cut = padded // 2
    up = shift(own(nz // 2)[:cut], "z", 1)
    down = shift(own(nz // 2)[cut:], "z", -1)
    up = jnp.concatenate([up, jnp.zeros_like(down)])
    down = jnp.concatenate([jnp.zeros_like(down), down])
    for step in range(nz // 2 - 1, 0, -1):
        up = shift(own(step) + up, "z", 1)
        down = shift(own(nz - step) + down, "z", -1)
    k_rows = own(0) + (up + down)

    chosen = lax.dynamic_index_in_dim(pair_list, group, 0, keepdims=False)
    shift_occ = eps_occ[chosen[0]] + eps_occ[chosen[1]]
    row_eps = lax.dynamic_slice_in_dim(eps_vir, chunk * width, width, 0)
    row_eps = jnp.pad(row_eps, (0, padded - width), constant_values=1.0)
    amp_rows = k_rows / (row_eps[:, None] + eps_vir[None, :] - shift_occ)

    mine = amp_rows
    other = swap(mine, "yh")
    both = jnp.where(yh == 0, jnp.stack([mine, other]), jnp.stack([other, mine]))
    ring = {0: both}
    up = down = both
    for step in range(1, nz // 2):
        up = shift(up, "z", 1)
        down = shift(down, "z", -1)
        ring[nz - step] = up
        ring[step] = down
    ring[nz // 2] = jnp.stack([shift(up[0], "z", 1), shift(down[1], "z", -1)])
    pieces = []
    for r in range(nz):
        for piece in (ring[r], swap(ring[r], "c")):
            pieces.append(piece.reshape(2 * padded, nvir))

    added = pl.pallas_call(
        functools.partial(density_kernel, nz, width, padded),
        out_shape=jax.ShapeDtypeStruct((nz, padded, slab), F32),
        in_specs=[SMEM] + [VMEM] * (2 * nz + 1),
        out_specs=VMEM,
        scratch_shapes=[pltpu.VMEM((nz, padded, slab), F32)] * 2 + [pltpu.VMEM((2 * nz, 2 * padded, nvir), BF16)],
        compiler_params=pltpu.CompilerParams(vmem_limit_bytes=LIMIT),
    )(where, amp_rows, *pieces)
    added = lax.all_to_all(added, SLABS, split_axis=0, concat_axis=0, tiled=True)
    return jnp.sum(added, axis=0)[:width]


def solution(mesh):
    fine = Mesh(mesh.devices.reshape(4, 2, 8, 2, 2), ("x", "yl", "z", "yh", "c"))
    pair, grid = SLABS, ("z", "yh", "c")
    in_specs = (P(None, pair, grid), P(), P(), P())
    return jax.shard_map(local, mesh=fine, in_specs=in_specs, out_specs=P(grid, pair), check_vma=False)
```

time: 341 us -> 214 us (0.63)
  blocking collectives: 156 us -> 59.8 us
  local copies, waits for them, and re-layouts: 35.1 us -> 7.93 us
  Pallas kernels: 0 us -> 15.1 us
  between operations: 19.2 us -> 5.18 us
  matrix products: 11.1 us -> 0 us
  waiting for transfers between devices: 94.9 us -> 85.2 us
  starting transfers between devices: 19.7 us -> 28.8 us
  other arithmetic: 4.5 us -> 8.17 us
    unnamed x1 -> x0, blocking collectives: 104 us -> none
    ppermute x0 -> x26, waiting for transfers between devices: none -> 85.2 us  [the longest x16 69.1 us: shift(): lax.ppermute(value, axis, [(i, (i + step) % size) for i in range(size)])]
    all_gather x1 -> x0, waiting for transfers between devices: 56.8 us -> none  [local(): piece = lax.all_gather(rows16, 'grid', axis=0, tiled=True)]
    unnamed x6 -> x0, waiting for transfers between devices: 38.1 us -> none
    ppermute x0 -> x26, starting transfers between devices: none -> 28.8 us  [the longest x16 25.2 us: shift(): lax.ppermute(value, axis, [(i, (i + step) % size) for i in range(size)])]
    unnamed x4 -> x0, starting transfers between devices: 19.7 us -> none
    pallas_call x0 -> x2, Pallas kernels: none -> 15.1 us  [the longest x1 9.51 us: local(): pl.pallas_call(functools.partial(density_kernel, nz, width, padded), out_...]
    all_to_all x8 -> x0, local copies, waits for them, and re-layouts: 14.6 us -> none  [the longest x2 9.94 us: local(): lax.all_to_all(outgoing, 'pair', split_axis=0, concat_axis=2, tiled=True)]
  transfers between devices with their start and end apart: 5 -> 26, of which waited for: 2 -> 18; matrix products, arithmetic and copies ran while one was open for 2% -> 1% of each run, Pallas kernels for 0% -> 0%
where the time goes in v1:
time: 214 us; the launch traced here: 210 us
  waiting for transfers between devices  85.2 us (40%)
  blocking collectives  59.8 us (28%)
  starting transfers between devices  28.8 us (13%)
  Pallas kernels  15.1 us (7%)
  other arithmetic  8.17 us (4%)
  local copies, waits for them, and re-layouts  7.93 us (4%)
  between operations  5.18 us (2%)
    ppermute x16, waiting for transfers between devices, shift(): lax.ppermute(value, axis, [(i, (i + step) % size) for i in range(size)])  69.1 us
    all_to_all x1, blocking collectives, local(): lax.all_to_all(outgoing, ('yh', 'x', 'yl'), split_axis=0, concat_axis=0,...  48.4 us
    ppermute x16, starting transfers between devices, shift(): lax.ppermute(value, axis, [(i, (i + step) % size) for i in range(size)])  25.2 us
    ppermute x10, waiting for transfers between devices, swap(): return lax.ppermute(value, axis, [(0, 1), (1, 0)])  16.1 us
    all_to_all x1, blocking collectives, local(): lax.all_to_all(added, SLABS, split_axis=0, concat_axis=0, tiled=True)  11.5 us
    pallas_call x1, Pallas kernels, local(): pl.pallas_call(functools.partial(density_kernel, nz, width, padded), out_...  9.51 us
    pallas_call x1, Pallas kernels, local(): pl.pallas_call(functools.partial(integral_kernel, padded), out_shape=jax....  5.54 us
  transfers between devices with their start and end apart: 26, of which 18 were waited for; matrix products, arithmetic and copies ran while one was open for 1% of the time, Pallas kernels for 0%

profile of v1, /device:TPU:32, one launch (start us, length us, event | category | flops | bytes accessed | tf_op | source)
XLA Modules:
  0.0 210.1 jit_solution(4726785499292383371)
XLA Ops:
  2.4 1.7 gather_fusion
  4.1 1.5 copy.7
  6.5 48.4 %all_to_all.10.near_ref = bf16[16,272,300]{2,1,0:T(8,128)(2,1)} all-to-all(bf16[16,272,300]{2,1,0:T(8,128)(2,1)S(1)} %bitcast.80), channel_id=1, replica_groups=mesh['x'=4,'yl'=2,'z'=8,'yh'=2,'c'=2] {'yh','x','yl'}, dimensions={0} | all-to-all | bytes 5222400 | tf_op jit(solution)/shard_map/all_to_all | solution.py:122
  54.9 6.2 %collective-permute-done.far_ref = bf16[16,272,300]{2,1,0:T(8,128)(2,1)} collective-permute-done((bf16[16,272,300]{2,1,0:T(8,128)(2,1)}, bf16[16,272,300]{2,1,0:T(8,128)(2,1)}, u32[]{:S(2)}, u32[]{:S(2)}) %collective-permute-start) | collective-permute-done | bytes 2611232 | tf_op jit(solution)/shard_map/ppermute | solution.py:20
  61.1 5.5 %shard_map.46 = f32[384,1408]{1,0:T(8,128)S(1)} custom-call(s32[3]{0:T(128)S(1)} %pad_add_fusion.where_ref, bf16[16,272,300]{2,1,0:T(8,128)(2,1)} %all_to_all.10.near_ref, bf16[16,272,300]{2,1,0:T(8,128)(2,1)} %collective-permute-done.far_ref), custom_call_target="tpu_custom_call" | custom-call | tf_op jit(solution)/shard_map/pallas_call | solution.py:125
  66.7 1.4 copy-done.1
  68.2 5.7 %collective-permute-done.5 = f32[24,1408]{1,0:T(8,128)S(1)} collective-permute-done((f32[24,1408]{1,0:T(8,128)S(1)}, f32[24,1408]{1,0:T(8,128)S(1)}, u32[]{:S(2)}, u32[]{:S(2)}) %collective-permute-start.5) | collective-permute-done | bytes 135200 | tf_op jit(solution)/shard_map/ppermute | solution.py:25
  75.0 3.4 %collective-permute-start.6 = (f32[48,1408]{1,0:T(8,128)S(1)}, f32[48,1408]{1,0:T(8,128)S(1)}, u32[]{:S(2)}, u32[]{:S(2)}) collective-permute-start(f32[48,1408]{1,0:T(8,128)S(1)} %bitcast_add_fusion), channel_id=1, source_target_pairs={{0,28},{4,0},{8,4},{12,8},{16,12},{20,16},{24,20},{28,24},{1,29},{... | collective-permute-start | bytes 811016 | tf_op jit(solution)/shard_map/ppermute | solution.py:25
  78.3 5.2 %collective-permute-done.6 = f32[48,1408]{1,0:T(8,128)S(1)} collective-permute-done((f32[48,1408]{1,0:T(8,128)S(1)}, f32[48,1408]{1,0:T(8,128)S(1)}, u32[]{:S(2)}, u32[]{:S(2)}) %collective-permute-start.6) | collective-permute-done | bytes 270368 | tf_op jit(solution)/shard_map/ppermute | solution.py:25
  83.5 1.0 bitcast_add_fusion.1
  84.5 3.8 %collective-permute-start.7 = (f32[48,1408]{1,0:T(8,128)S(1)}, f32[48,1408]{1,0:T(8,128)S(1)}, u32[]{:S(2)}, u32[]{:S(2)}) collective-permute-start(f32[48,1408]{1,0:T(8,128)S(1)} %bitcast_add_fusion.1), channel_id=1, source_target_pairs={{0,28},{4,0},{8,4},{12,8},{16,12},{20,16},{24,20},{28,24},{1,29},{... | collective-permute-start | bytes 811016 | tf_op jit(solution)/shard_map/ppermute | solution.py:25
  88.3 6.7 %collective-permute-done.1 = f32[24,1408]{1,0:T(8,128)S(1)} collective-permute-done((f32[24,1408]{1,0:T(8,128)S(1)}, f32[24,1408]{1,0:T(8,128)S(1)}, u32[]{:S(2)}, u32[]{:S(2)}) %collective-permute-start.1) | collective-permute-done | bytes 135200 | tf_op jit(solution)/shard_map/ppermute | solution.py:25
  95.0 1.1 bitcast_add_fusion.2
  96.7 7.2 %collective-permute-done.2 = f32[48,1408]{1,0:T(8,128)S(1)} collective-permute-done((f32[48,1408]{1,0:T(8,128)S(1)}, f32[48,1408]{1,0:T(8,128)S(1)}, u32[]{:S(2)}, u32[]{:S(2)}) %collective-permute-start.2) | collective-permute-done | bytes 270368 | tf_op jit(solution)/shard_map/ppermute | solution.py:25
  103.8 1.0 bitcast_add_fusion.4
  104.9 3.3 %collective-permute-start.8 = (f32[48,1408]{1,0:T(8,128)S(1)}, f32[48,1408]{1,0:T(8,128)S(1)}, u32[]{:S(2)}, u32[]{:S(2)}) collective-permute-start(f32[48,1408]{1,0:T(8,128)S(1)} %get-tuple-element.5), channel_id=1, source_target_pairs={{0,28},{4,0},{8,4},{12,8},{16,12},{20,16},{24,20},{28,24},{1,29},{... | collective-permute-start | bytes 811016 | tf_op jit(solution)/shard_map/ppermute | solution.py:25
  108.2 4.5 %collective-permute-done.3 = f32[48,1408]{1,0:T(8,128)S(1)} collective-permute-done((f32[48,1408]{1,0:T(8,128)S(1)}, f32[48,1408]{1,0:T(8,128)S(1)}, u32[]{:S(2)}, u32[]{:S(2)}) %collective-permute-start.3) | collective-permute-done | bytes 270368 | tf_op jit(solution)/shard_map/ppermute | solution.py:25
  112.7 1.0 bitcast_add_fusion.5
  120.0 1.7 collective-permute-done.4
  121.7 1.1 fusion.rows_ref
  122.8 1.7 collective-permute-start.9
  124.5 6.4 %collective-permute-done.9 = f32[48,1408]{1,0:T(8,128)S(1)} collective-permute-done((f32[48,1408]{1,0:T(8,128)S(1)}, f32[48,1408]{1,0:T(8,128)S(1)}, u32[]{:S(2)}, u32[]{:S(2)}) %collective-permute-start.9) | collective-permute-done | bytes 270368 | tf_op jit(solution)/shard_map/ppermute | solution.py:20
  131.2 3.3 %collective-permute-start.11 = (f32[2,48,1408]{2,1,0:T(8,128)S(1)}, f32[2,48,1408]{2,1,0:T(8,128)S(1)}, u32[]{:S(2)}, u32[]{:S(2)}) collective-permute-start(f32[2,48,1408]{2,1,0:T(8,128)S(1)} %maximum_select_fusion), channel_id=1, source_target_pairs={{0,28},{4,0},{8,4},{12,8},{16,12},{20,16},{24,20},{28,24},{1,29},{... | collective-permute-start | bytes 1622024 | tf_op jit(solution)/shard_map/ppermute | solution.py:25
  134.5 11.9 %collective-permute-done.17 = f32[2,48,1408]{2,1,0:T(8,128)S(1)} collective-permute-done((f32[2,48,1408]{2,1,0:T(8,128)S(1)}, f32[2,48,1408]{2,1,0:T(8,128)S(1)}, u32[]{:S(2)}, u32[]{:S(2)}) %collective-permute-start.17) | collective-permute-done | bytes 540704 | tf_op jit(solution)/shard_map/ppermute | solution.py:25
  146.6 3.4 %collective-permute-start.13 = (f32[2,48,1408]{2,1,0:T(8,128)S(1)}, f32[2,48,1408]{2,1,0:T(8,128)S(1)}, u32[]{:S(2)}, u32[]{:S(2)}) collective-permute-start(f32[2,48,1408]{2,1,0:T(8,128)S(1)} %collective-permute-done.11), channel_id=1, source_target_pairs={{0,28},{4,0},{8,4},{12,8},{16,12},{20,16},{24,20},{28,24},{1,29},{... | collective-permute-start | bytes 1622024 | tf_op jit(solution)/shard_map/ppermute | solution.py:25
  150.0 13.0 %collective-permute-done.18 = f32[2,48,1408]{2,1,0:T(8,128)S(1)} collective-permute-done((f32[2,48,1408]{2,1,0:T(8,128)S(1)}, f32[2,48,1408]{2,1,0:T(8,128)S(1)}, u32[]{:S(2)}, u32[]{:S(2)}) %collective-permute-start.18) | collective-permute-done | bytes 540704 | tf_op jit(solution)/shard_map/ppermute | solution.py:25
  163.0 3.0 %collective-permute-start.15 = (f32[2,48,1408]{2,1,0:T(8,128)S(1)}, f32[2,48,1408]{2,1,0:T(8,128)S(1)}, u32[]{:S(2)}, u32[]{:S(2)}) collective-permute-start(f32[2,48,1408]{2,1,0:T(8,128)S(1)} %collective-permute-done.13), channel_id=1, source_target_pairs={{0,28},{4,0},{8,4},{12,8},{16,12},{20,16},{24,20},{28,24},{1,29},{... | collective-permute-start | bytes 1622024 | tf_op jit(solution)/shard_map/ppermute | solution.py:25
  166.6 8.8 %collective-permute-done.19 = f32[2,48,1408]{2,1,0:T(8,128)S(1)} collective-permute-done((f32[2,48,1408]{2,1,0:T(8,128)S(1)}, f32[2,48,1408]{2,1,0:T(8,128)S(1)}, u32[]{:S(2)}, u32[]{:S(2)}) %collective-permute-start.19) | collective-permute-done | bytes 540704 | tf_op jit(solution)/shard_map/ppermute | solution.py:25
  175.5 3.6 %collective-permute-start.21 = (f32[48,1408]{1,0:T(8,128)S(1)}, f32[48,1408]{1,0:T(8,128)S(1)}, u32[]{:S(2)}, u32[]{:S(2)}) collective-permute-start(f32[48,1408]{1,0:T(8,128)S(1)} %slice_bitcast_fusion), channel_id=1, source_target_pairs={{0,28},{4,0},{8,4},{12,8},{16,12},{20,16},{24,20},{28,24},{1,29},{... | collective-permute-start | bytes 811016 | tf_op jit(solution)/shard_map/ppermute | solution.py:25
  179.1 4.3 %collective-permute-done.20 = f32[48,1408]{1,0:T(8,128)S(1)} collective-permute-done((f32[48,1408]{1,0:T(8,128)S(1)}, f32[48,1408]{1,0:T(8,128)S(1)}, u32[]{:S(2)}, u32[]{:S(2)}) %collective-permute-start.20) | collective-permute-done | bytes 270368 | tf_op jit(solution)/shard_map/ppermute | solution.py:25
  188.5 9.5 %shard_map.47 = f32[8,48,176]{2,1,0:T(8,128)S(1)} custom-call(s32[3]{0:T(128)S(1)} %pad_add_fusion.where_ref, f32[48,1408]{1,0:T(8,128)S(1)} %fusion.rows_ref, f32[96,1408]{1,0:T(8,128)S(1)} %bitcast.70, f32[96,1408]{1,0:T(8,128)S(1)} %bitcast.75, f32[96,1408]{1,0:T(8,128)S(1)} %bitcast.73, f32[96,1408]{1,0:T(8,128)S(1)} %bitcast.76, ...), custom_call_target="tpu_custom_call" | custom-call | tf_op jit(solution)/shard_map/pallas_call | solution.py:168
  198.0 11.5 %all_to_all.11 = f32[8,48,176]{2,1,0:T(8,128)S(1)} all-to-all(f32[8,48,176]{2,1,0:T(8,128)S(1)} %shard_map.47), channel_id=1, replica_groups=mesh['x'=4,'yl'=2,'z'=8,'yh'=2,'c'=2] {'x','yl'}, dimensions={0} | all-to-all | bytes 540672 | tf_op jit(solution)/shard_map/all_to_all | solution.py:176
  (73 shorter events, 13.5 us)
Async XLA Ops:
  54.8 6.3 %collective-permute-start = (bf16[16,272,300]{2,1,0:T(8,128)(2,1)}, bf16[16,272,300]{2,1,0:T(8,128)(2,1)}, u32[]{:S(2)}, u32[]{:S(2)}) collective-permute-start(bf16[16,272,300]{2,1,0:T(8,128)(2,1)} %all_to_all.10.near_ref), channel_id=1, source_target_pairs={{0,1},{1,0},{2,3},{3,2},{4,5},{5,4},{6,7},{7,6},{8,9},{9,8},{10,11... | collective-permute-start | bytes 7833608 | tf_op jit(solution)/shard_map/ppermute | solution.py:20
  68.1 5.9 %collective-permute-start.5 = (f32[24,1408]{1,0:T(8,128)S(1)}, f32[24,1408]{1,0:T(8,128)S(1)}, u32[]{:S(2)}, u32[]{:S(2)}) collective-permute-start(f32[24,1408]{1,0:T(8,128)S(1)} %get-tuple-element.7), channel_id=1, source_target_pairs={{0,28},{4,0},{8,4},{12,8},{16,12},{20,16},{24,20},{28,24},{1,29},{... | collective-permute-start | bytes 405512 | tf_op jit(solution)/shard_map/ppermute | solution.py:25
  74.9 38.9 %copy-start.9 = (s32[8,2]{0,1:T(2,128)S(1)}, s32[8,2]{0,1:T(2,128)}, u32[]{:S(2)}) copy-start(s32[8,2]{0,1:T(2,128)} %param.5) | copy-start | bytes 196
  74.9 41.9 %copy-start.8 = (f32[1408]{0:T(1024)S(1)}, f32[1408]{0:T(1024)}, u32[]{:S(2)}) copy-start(f32[1408]{0:T(1024)} %param.7) | copy-start | bytes 16900
  74.9 43.2 %copy-start.10 = (f32[16]{0:T(128)S(1)}, f32[16]{0:T(128)}, u32[]{:S(2)}) copy-start(f32[16]{0:T(128)} %param.6) | copy-start | bytes 196
  75.0 8.6 %collective-permute-start.6 = (f32[48,1408]{1,0:T(8,128)S(1)}, f32[48,1408]{1,0:T(8,128)S(1)}, u32[]{:S(2)}, u32[]{:S(2)}) collective-permute-start(f32[48,1408]{1,0:T(8,128)S(1)} %bitcast_add_fusion), channel_id=1, source_target_pairs={{0,28},{4,0},{8,4},{12,8},{16,12},{20,16},{24,20},{28,24},{1,29},{... | collective-permute-start | bytes 811016 | tf_op jit(solution)/shard_map/ppermute | solution.py:25
  84.5 10.4 %collective-permute-start.7 = (f32[48,1408]{1,0:T(8,128)S(1)}, f32[48,1408]{1,0:T(8,128)S(1)}, u32[]{:S(2)}, u32[]{:S(2)}) collective-permute-start(f32[48,1408]{1,0:T(8,128)S(1)} %bitcast_add_fusion.1), channel_id=1, source_target_pairs={{0,28},{4,0},{8,4},{12,8},{16,12},{20,16},{24,20},{28,24},{1,29},{... | collective-permute-start | bytes 811016 | tf_op jit(solution)/shard_map/ppermute | solution.py:25
  88.3 6.7 %collective-permute-start.1 = (f32[24,1408]{1,0:T(8,128)S(1)}, f32[24,1408]{1,0:T(8,128)S(1)}, u32[]{:S(2)}, u32[]{:S(2)}) collective-permute-start(f32[24,1408]{1,0:T(8,128)S(1)} %get-tuple-element.8), channel_id=1, source_target_pairs={{0,4},{4,8},{8,12},{12,16},{16,20},{20,24},{24,28},{28,0},{1,5},{5... | collective-permute-start | bytes 405512 | tf_op jit(solution)/shard_map/ppermute | solution.py:25
  96.1 7.8 %collective-permute-start.2 = (f32[48,1408]{1,0:T(8,128)S(1)}, f32[48,1408]{1,0:T(8,128)S(1)}, u32[]{:S(2)}, u32[]{:S(2)}) collective-permute-start(f32[48,1408]{1,0:T(8,128)S(1)} %get-tuple-element.6), channel_id=1, source_target_pairs={{0,4},{4,8},{8,12},{12,16},{16,20},{20,24},{24,28},{28,0},{1,5},{5... | collective-permute-start | bytes 811016 | tf_op jit(solution)/shard_map/ppermute | solution.py:25
  104.8 7.9 %collective-permute-start.3 = (f32[48,1408]{1,0:T(8,128)S(1)}, f32[48,1408]{1,0:T(8,128)S(1)}, u32[]{:S(2)}, u32[]{:S(2)}) collective-permute-start(f32[48,1408]{1,0:T(8,128)S(1)} %bitcast_add_fusion.4), channel_id=1, source_target_pairs={{0,4},{4,8},{8,12},{12,16},{16,20},{20,24},{24,28},{28,0},{1,5},{5... | collective-permute-start | bytes 811016 | tf_op jit(solution)/shard_map/ppermute | solution.py:25
  104.9 15.1 %collective-permute-start.8 = (f32[48,1408]{1,0:T(8,128)S(1)}, f32[48,1408]{1,0:T(8,128)S(1)}, u32[]{:S(2)}, u32[]{:S(2)}) collective-permute-start(f32[48,1408]{1,0:T(8,128)S(1)} %get-tuple-element.5), channel_id=1, source_target_pairs={{0,28},{4,0},{8,4},{12,8},{16,12},{20,16},{24,20},{28,24},{1,29},{... | collective-permute-start | bytes 811016 | tf_op jit(solution)/shard_map/ppermute | solution.py:25
  113.7 8.0 %collective-permute-start.4 = (f32[48,1408]{1,0:T(8,128)S(1)}, f32[48,1408]{1,0:T(8,128)S(1)}, u32[]{:S(2)}, u32[]{:S(2)}) collective-permute-start(f32[48,1408]{1,0:T(8,128)S(1)} %bitcast_add_fusion.5), channel_id=1, source_target_pairs={{0,4},{4,8},{8,12},{12,16},{16,20},{20,24},{24,28},{28,0},{1,5},{5... | collective-permute-start | bytes 811016 | tf_op jit(solution)/shard_map/ppermute | solution.py:25
  122.8 8.1 %collective-permute-start.9 = (f32[48,1408]{1,0:T(8,128)S(1)}, f32[48,1408]{1,0:T(8,128)S(1)}, u32[]{:S(2)}, u32[]{:S(2)}) collective-permute-start(f32[48,1408]{1,0:T(8,128)S(1)} %fusion.rows_ref), channel_id=1, source_target_pairs={{0,2},{2,0},{1,3},{3,1},{4,6},{6,4},{5,7},{7,5},{8,10},{10,8},{9,1... | collective-permute-start | bytes 811016 | tf_op jit(solution)/shard_map/ppermute | solution.py:20
  130.9 15.5 %collective-permute-start.17 = (f32[2,48,1408]{2,1,0:T(8,128)S(1)}, f32[2,48,1408]{2,1,0:T(8,128)S(1)}, u32[]{:S(2)}, u32[]{:S(2)}) collective-permute-start(f32[2,48,1408]{2,1,0:T(8,128)S(1)} %maximum_select_fusion), channel_id=1, source_target_pairs={{0,4},{4,8},{8,12},{12,16},{16,20},{20,24},{24,28},{28,0},{1,5},{5... | collective-permute-start | bytes 1622024 | tf_op jit(solution)/shard_map/ppermute | solution.py:25
  131.2 15.4 %collective-permute-start.11 = (f32[2,48,1408]{2,1,0:T(8,128)S(1)}, f32[2,48,1408]{2,1,0:T(8,128)S(1)}, u32[]{:S(2)}, u32[]{:S(2)}) collective-permute-start(f32[2,48,1408]{2,1,0:T(8,128)S(1)} %maximum_select_fusion), channel_id=1, source_target_pairs={{0,28},{4,0},{8,4},{12,8},{16,12},{20,16},{24,20},{28,24},{1,29},{... | collective-permute-start | bytes 1622024 | tf_op jit(solution)/shard_map/ppermute | solution.py:25
  146.4 42.1 %copy-start.3 = (f32[2,48,1408]{2,1,0:T(8,128)}, f32[2,48,1408]{2,1,0:T(8,128)S(1)}, u32[]{:S(2)}) copy-start(f32[2,48,1408]{2,1,0:T(8,128)S(1)} %collective-permute-done.17) | copy-start | bytes 1622020
  146.4 16.6 %collective-permute-start.18 = (f32[2,48,1408]{2,1,0:T(8,128)S(1)}, f32[2,48,1408]{2,1,0:T(8,128)S(1)}, u32[]{:S(2)}, u32[]{:S(2)}) collective-permute-start(f32[2,48,1408]{2,1,0:T(8,128)S(1)} %collective-permute-done.17), channel_id=1, source_target_pairs={{0,4},{4,8},{8,12},{12,16},{16,20},{20,24},{24,28},{28,0},{1,5},{5... | collective-permute-start | bytes 1622024 | tf_op jit(solution)/shard_map/ppermute | solution.py:25
  146.6 16.4 %collective-permute-start.13 = (f32[2,48,1408]{2,1,0:T(8,128)S(1)}, f32[2,48,1408]{2,1,0:T(8,128)S(1)}, u32[]{:S(2)}, u32[]{:S(2)}) collective-permute-start(f32[2,48,1408]{2,1,0:T(8,128)S(1)} %collective-permute-done.11), channel_id=1, source_target_pairs={{0,28},{4,0},{8,4},{12,8},{16,12},{20,16},{24,20},{28,24},{1,29},{... | collective-permute-start | bytes 1622024 | tf_op jit(solution)/shard_map/ppermute | solution.py:25
  163.0 25.4 %copy-start.4 = (f32[2,48,1408]{2,1,0:T(8,128)}, f32[2,48,1408]{2,1,0:T(8,128)S(1)}, u32[]{:S(2)}) copy-start(f32[2,48,1408]{2,1,0:T(8,128)S(1)} %collective-permute-done.18) | copy-start | bytes 1622020
  163.0 12.3 %collective-permute-start.19 = (f32[2,48,1408]{2,1,0:T(8,128)S(1)}, f32[2,48,1408]{2,1,0:T(8,128)S(1)}, u32[]{:S(2)}, u32[]{:S(2)}) collective-permute-start(f32[2,48,1408]{2,1,0:T(8,128)S(1)} %collective-permute-done.18), channel_id=1, source_target_pairs={{0,4},{4,8},{8,12},{12,16},{16,20},{20,24},{24,28},{28,0},{1,5},{5... | collective-permute-start | bytes 1622024 | tf_op jit(solution)/shard_map/ppermute | solution.py:25
  163.0 12.4 %collective-permute-start.15 = (f32[2,48,1408]{2,1,0:T(8,128)S(1)}, f32[2,48,1408]{2,1,0:T(8,128)S(1)}, u32[]{:S(2)}, u32[]{:S(2)}) collective-permute-start(f32[2,48,1408]{2,1,0:T(8,128)S(1)} %collective-permute-done.13), channel_id=1, source_target_pairs={{0,28},{4,0},{8,4},{12,8},{16,12},{20,16},{24,20},{28,24},{1,29},{... | collective-permute-start | bytes 1622024 | tf_op jit(solution)/shard_map/ppermute | solution.py:25
  166.1 17.9 %collective-permute-start.10 = (f32[2,48,1408]{2,1,0:T(8,128)S(1)}, f32[2,48,1408]{2,1,0:T(8,128)S(1)}, u32[]{:S(2)}, u32[]{:S(2)}) collective-permute-start(f32[2,48,1408]{2,1,0:T(8,128)S(1)} %maximum_select_fusion), channel_id=1, source_target_pairs={{0,1},{1,0},{2,3},{3,2},{4,5},{5,4},{6,7},{7,6},{8,9},{9,8},{10,11... | collective-permute-start | bytes 1622024 | tf_op jit(solution)/shard_map/ppermute | solution.py:20
  166.1 18.0 %collective-permute-start.25 = (f32[2,48,1408]{2,1,0:T(8,128)S(1)}, f32[2,48,1408]{2,1,0:T(8,128)S(1)}, u32[]{:S(2)}, u32[]{:S(2)}) collective-permute-start(f32[2,48,1408]{2,1,0:T(8,128)S(1)} %collective-permute-done.17), channel_id=1, source_target_pairs={{0,1},{1,0},{2,3},{3,2},{4,5},{5,4},{6,7},{7,6},{8,9},{9,8},{10,11... | collective-permute-start | bytes 1622024 | tf_op jit(solution)/shard_map/ppermute | solution.py:20
  166.6 18.0 %collective-permute-start.12 = (f32[2,48,1408]{2,1,0:T(8,128)S(1)}, f32[2,48,1408]{2,1,0:T(8,128)S(1)}, u32[]{:S(2)}, u32[]{:S(2)}) collective-permute-start(f32[2,48,1408]{2,1,0:T(8,128)S(1)} %collective-permute-done.11), channel_id=1, source_target_pairs={{0,1},{1,0},{2,3},{3,2},{4,5},{5,4},{6,7},{7,6},{8,9},{9,8},{10,11... | collective-permute-start | bytes 1622024 | tf_op jit(solution)/shard_map/ppermute | solution.py:20
  175.3 13.1 %copy-start.2 = (f32[2,48,1408]{2,1,0:T(8,128)}, f32[2,48,1408]{2,1,0:T(8,128)S(1)}, u32[]{:S(2)}) copy-start(f32[2,48,1408]{2,1,0:T(8,128)S(1)} %collective-permute-done.19) | copy-start | bytes 1622020
  175.4 8.0 %collective-permute-start.20 = (f32[48,1408]{1,0:T(8,128)S(1)}, f32[48,1408]{1,0:T(8,128)S(1)}, u32[]{:S(2)}, u32[]{:S(2)}) collective-permute-start(f32[48,1408]{1,0:T(8,128)S(1)} %slice_bitcast_fusion.1), channel_id=1, source_target_pairs={{0,4},{4,8},{8,12},{12,16},{16,20},{20,24},{24,28},{28,0},{1,5},{5... | collective-permute-start | bytes 811016 | tf_op jit(solution)/shard_map/ppermute | solution.py:25
  175.5 7.9 %collective-permute-start.21 = (f32[48,1408]{1,0:T(8,128)S(1)}, f32[48,1408]{1,0:T(8,128)S(1)}, u32[]{:S(2)}, u32[]{:S(2)}) collective-permute-start(f32[48,1408]{1,0:T(8,128)S(1)} %slice_bitcast_fusion), channel_id=1, source_target_pairs={{0,28},{4,0},{8,4},{12,8},{16,12},{20,16},{24,20},{28,24},{1,29},{... | collective-permute-start | bytes 811016 | tf_op jit(solution)/shard_map/ppermute | solution.py:25
  183.4 1.9 collective-permute-start.24
  183.4 2.7 %collective-permute-start.14 = (f32[2,48,1408]{2,1,0:T(8,128)S(1)}, f32[2,48,1408]{2,1,0:T(8,128)S(1)}, u32[]{:S(2)}, u32[]{:S(2)}) collective-permute-start(f32[2,48,1408]{2,1,0:T(8,128)S(1)} %collective-permute-done.13), channel_id=1, source_target_pairs={{0,1},{1,0},{2,3},{3,2},{4,5},{5,4},{6,7},{7,6},{8,9},{9,8},{10,11... | collective-permute-start | bytes 1622024 | tf_op jit(solution)/shard_map/ppermute | solution.py:20
  184.0 2.9 %collective-permute-start.23 = (f32[2,48,1408]{2,1,0:T(8,128)S(1)}, f32[2,48,1408]{2,1,0:T(8,128)S(1)}, u32[]{:S(2)}, u32[]{:S(2)}) collective-permute-start(f32[2,48,1408]{2,1,0:T(8,128)S(1)} %collective-permute-done.19), channel_id=1, source_target_pairs={{0,1},{1,0},{2,3},{3,2},{4,5},{5,4},{6,7},{7,6},{8,9},{9,8},{10,11... | collective-permute-start | bytes 1622024 | tf_op jit(solution)/shard_map/ppermute | solution.py:20
  184.1 3.6 %collective-permute-start.16 = (f32[2,48,1408]{2,1,0:T(8,128)S(1)}, f32[2,48,1408]{2,1,0:T(8,128)S(1)}, u32[]{:S(2)}, u32[]{:S(2)}) collective-permute-start(f32[2,48,1408]{2,1,0:T(8,128)S(1)} %collective-permute-done.15), channel_id=1, source_target_pairs={{0,1},{1,0},{2,3},{3,2},{4,5},{5,4},{6,7},{7,6},{8,9},{9,8},{10,11... | collective-permute-start | bytes 1622024 | tf_op jit(solution)/shard_map/ppermute | solution.py:20
  184.6 3.9 %collective-permute-start.22 = (f32[2,48,1408]{2,1,0:T(8,128)S(1)}, f32[2,48,1408]{2,1,0:T(8,128)S(1)}, u32[]{:S(2)}, u32[]{:S(2)}) collective-permute-start(f32[2,48,1408]{2,1,0:T(8,128)S(1)} %pad_maximum_fusion.1), channel_id=1, source_target_pairs={{0,1},{1,0},{2,3},{3,2},{4,5},{5,4},{6,7},{7,6},{8,9},{9,8},{10,11... | collective-permute-start | bytes 1622024 | tf_op jit(solution)/shard_map/ppermute | solution.py:20
  (5 other events, 12.1 us)

commit v2 on v1

v2 whole, which is shorter than its diff:
```python
import functools

import jax
import jax.numpy as jnp
from jax import lax
from jax.experimental import pallas as pl
from jax.experimental.pallas import tpu as pltpu
from jax.sharding import Mesh
from jax.sharding import PartitionSpec as P

F32 = jnp.float32
BF16 = jnp.bfloat16
SLABS = ("x", "yl")
VMEM = pl.BlockSpec(memory_space=pltpu.VMEM)
SMEM = pl.BlockSpec(memory_space=pltpu.SMEM)
PARAMS = pltpu.CompilerParams(vmem_limit_bytes=48 * 1024 * 1024)


def swap(value, axis):
    return lax.ppermute(value, axis, [(0, 1), (1, 0)])


def shift(value, axis, step):
    size = lax.axis_size(axis)
    return lax.ppermute(value, axis, [(i, (i + step) % size) for i in range(size)])


def dot_nt(a, b):
    return lax.dot_general(a, b, (((1,), (1,)), ((), ())), preferred_element_type=F32)


def split3(value):
    high = value.astype(BF16)
    rest = value - high.astype(F32)
    middle = rest.astype(BF16)
    return high, middle, (rest - middle.astype(F32)).astype(BF16)


def cost(flops, moved):
    return pl.CostEstimate(flops=flops, bytes_accessed=moved, transcendentals=0)


def integral_kernel(padded, where_ref, pair_ref, occ_ref, vir_ref, near_ref, far_ref, out_ref, denom_ref):
    sources, rows, naux = near_ref.shape
    half = sources // 2
    slab = rows - 2 * padded
    c, chunk, group = where_ref[1], where_ref[2], where_ref[3]
    start = pl.multiple_of(c * padded, padded)
    total = None
    for ref in (near_ref, far_ref):
        for y in range(2):
            a = ref[half * y : half * (y + 1), pl.ds(start, padded), :].reshape(half * padded, naux)
            b = ref[half * y : half * (y + 1), 2 * padded :, :].reshape(half * slab, naux)
            term = dot_nt(a, b)
            total = term if total is None else total + term
    out_ref[...] = total
    columns = jnp.broadcast_to(vir_ref[...], denom_ref.shape)
    place = lax.broadcasted_iota(jnp.int32, denom_ref.shape, 1)
    row = lax.broadcasted_iota(jnp.int32, denom_ref.shape, 0)
    width = slab // 4
    own = jnp.sum(jnp.where(place == chunk * width + row, columns, 0.0), axis=1, keepdims=True)
    denom_ref[...] = (own + columns) - occ_ref[pair_ref[group, 0]] - occ_ref[pair_ref[group, 1]]


def turn_kernel(nz, width, padded, where_ref, near_ref, far_ref, out_ref):
    part = where_ref[4]
    nvir = near_ref.shape[1]
    slab = nvir // nz
    column = lax.broadcasted_iota(jnp.int32, (padded, slab), 1)
    row = lax.broadcasted_iota(jnp.int32, (padded, slab), 0)
    pick = jnp.where((column == part * width + row) & (row < width), 1.0, 0.0).astype(BF16)
    for slot, ref in enumerate((near_ref, far_ref)):
        for k in range(nz):
            high, middle, low = split3(ref[:, k * slab : (k + 1) * slab])
            out_ref[k, slot] = dot_nt(pick, high) + (dot_nt(pick, middle) + dot_nt(pick, low))


def density_pieces(steps, nz, width, padded, where_ref, tilde, tilde_t_ref, pieces, total, blocks_ref):
    z, c = where_ref[0], where_ref[1]
    for n, r in enumerate(steps):
        at = lax.rem(z + r, nz)
        sides = []
        for slot in range(2):
            piece = pieces[2 * n + slot][...]
            term = jnp.dot(tilde_t_ref[at, slot], piece, preferred_element_type=F32)
            total = term if total is None else total + term
            sides.append(dot_nt(tilde, piece))
        blocks_ref[at] = join(c, sides[0], sides[1], width, padded)
    return total


def join(c, near, far, width, padded):
    first, second = jnp.where(c == 0, near, far), jnp.where(c == 0, far, near)
    parts = []
    for y in range(2):
        for piece in (first, second):
            parts.append(piece[:, y * padded : y * padded + width])
    return jnp.concatenate(parts, axis=1)


def early_kernel(steps, nz, width, padded, where_ref, rows_ref, turned_ref, *refs):
    pieces = refs[: 2 * len(steps)]
    total_ref, blocks_ref, tilde_ref, tilde_t_ref = refs[2 * len(steps) :]
    c = where_ref[1]
    slab = rows_ref.shape[1] // nz
    rows = rows_ref[...]
    zeros = jnp.zeros((padded, padded - width), F32)
    turned = []
    for k in range(nz):
        mine = rows[:, k * slab : (k + 1) * slab]
        halves = []
        for h in range(2):
            parts = []
            for y in range(2):
                at = (2 * y + h) * width
                parts += [mine[:, at : at + width], zeros]
            halves.append(jnp.concatenate(parts, axis=1))
        near, far = turned_ref[k, 0], turned_ref[k, 1]
        tilde_t_ref[k, 0] = (2.0 * near - jnp.where(c == 0, halves[0], halves[1])).astype(BF16)
        tilde_t_ref[k, 1] = (2.0 * far - jnp.where(c == 0, halves[1], halves[0])).astype(BF16)
        turned.append(join(c, near, far, width, padded))
    tilde = (2.0 * rows - jnp.concatenate(turned, axis=1)).astype(BF16)
    tilde_ref[...] = tilde
    total_ref[...] = density_pieces(steps, nz, width, padded, where_ref, tilde, tilde_t_ref, pieces, None, blocks_ref)


def late_kernel(steps, nz, width, padded, where_ref, total_ref, blocks_ref, tilde_ref, tilde_t_ref, *refs):
    pieces, out_ref = refs[: 2 * len(steps)], refs[-1]
    slab = total_ref.shape[1] // nz
    for k in range(nz):
        out_ref[k] = blocks_ref[k]
    total = density_pieces(
        steps, nz, width, padded, where_ref, tilde_ref[...], tilde_t_ref, pieces, total_ref[...], out_ref
    )
    for k in range(nz):
        out_ref[k] += total[:, k * slab : (k + 1) * slab]


def local(orbital_b, pair_list, eps_occ, eps_vir):
    slab, naux = orbital_b.shape[1:]
    nvir = eps_vir.shape[0]
    z, yh, c = (lax.axis_index(a) for a in ("z", "yh", "c"))
    nz = lax.axis_size("z")
    width = slab // 4
    padded = (width + 8) // 8 * 8
    where = jnp.stack([z, c, z * 4 + yh * 2 + c, lax.axis_index(SLABS), yh * 2 + c])

    left = orbital_b[pair_list[:, 0]].reshape(8, 2, 2, width, naux)
    left = jnp.pad(left, ((0, 0), (0, 0), (0, 0), (0, padded - width), (0, 0)))
    left = left.reshape(8, 2, 2 * padded, naux).transpose(1, 0, 2, 3)
    right = jnp.broadcast_to(orbital_b[pair_list[:, 1]][None], (2, 8, slab, naux))
    outgoing = jnp.concatenate([left, right], axis=2).reshape(16, 2 * padded + slab, naux)
    near = lax.all_to_all(outgoing, ("yh", "x", "yl"), split_axis=0, concat_axis=0, tiled=True)
    far = swap(near, "c")

    part, denom = pl.pallas_call(
        functools.partial(integral_kernel, padded),
        out_shape=(jax.ShapeDtypeStruct((8 * padded, nvir), F32), jax.ShapeDtypeStruct((padded, nvir), F32)),
        in_specs=[SMEM, SMEM, SMEM, VMEM, VMEM, VMEM],
        out_specs=(VMEM, VMEM),
        compiler_params=PARAMS,
    )(where, pair_list, eps_occ, eps_vir[None], near, far)
    part = part.reshape(8, padded, nvir)

    def own(offset):
        return lax.dynamic_index_in_dim(part, lax.rem(z + offset, nz), 0, keepdims=False)

    cut = padded // 2
    up = shift(own(nz // 2)[:cut], "z", 1)
    down = shift(own(nz // 2)[cut:], "z", -1)
    up = jnp.concatenate([up, jnp.zeros_like(down)])
    down = jnp.concatenate([jnp.zeros_like(down), down])
    for step in range(nz // 2 - 1, 0, -1):
        up = shift(own(step) + up, "z", 1)
        down = shift(own(nz - step) + down, "z", -1)
    amp_rows = (own(0) + (up + down)) / denom

    other = swap(amp_rows, "yh")
    both = jnp.where(yh == 0, jnp.stack([amp_rows, other]), jnp.stack([other, amp_rows]))
    both16 = both.astype(BF16)
    ring = {0: both16}
    up = down = both16
    for step in range(1, nz // 2):
        up = shift(up, "z", 1)
        down = shift(down, "z", -1)
        ring[nz - step] = up
        ring[step] = down
    ring[nz // 2] = jnp.stack([shift(up[0], "z", 1), shift(down[1], "z", -1)])

    both = both.reshape(2 * padded, nvir)
    turned = pl.pallas_call(
        functools.partial(turn_kernel, nz, width, padded),
        out_shape=jax.ShapeDtypeStruct((nz, 2, padded, 2 * padded), F32),
        in_specs=[SMEM, VMEM, VMEM],
        out_specs=VMEM,
        compiler_params=PARAMS,
        cost_estimate=cost(6 * 4 * padded * padded * nvir, 4 * 4 * padded * nvir),
    )(where, both, swap(both, "c"))
    turned = lax.all_to_all(turned, "z", split_axis=0, concat_axis=0, tiled=True)

    def gathered(steps):
        pieces = []
        for r in steps:
            pieces += [ring[r].reshape(2 * padded, nvir), swap(ring[r], "c").reshape(2 * padded, nvir)]
        return pieces

    soon = (0, 1, nz - 1, 2, nz - 2)
    late = (3, nz - 3, nz // 2)
    state = pl.pallas_call(
        functools.partial(early_kernel, soon, nz, width, padded),
        out_shape=(
            jax.ShapeDtypeStruct((padded, nvir), F32),
            jax.ShapeDtypeStruct((nz, padded, slab), F32),
            jax.ShapeDtypeStruct((padded, nvir), BF16),
            jax.ShapeDtypeStruct((nz, 2, padded, 2 * padded), BF16),
        ),
        in_specs=[SMEM] + [VMEM] * (2 + 2 * len(soon)),
        out_specs=(VMEM,) * 4,
        compiler_params=PARAMS,
        cost_estimate=cost(len(soon) * 8 * padded * padded * nvir, len(soon) * 8 * padded * nvir),
    )(where, amp_rows, turned, *gathered(soon))
    added = pl.pallas_call(
        functools.partial(late_kernel, late, nz, width, padded),
        out_shape=jax.ShapeDtypeStruct((nz, padded, slab), F32),
        in_specs=[SMEM] + [VMEM] * (4 + 2 * len(late)),
        out_specs=VMEM,
        compiler_params=PARAMS,
        cost_estimate=cost(len(late) * 8 * padded * padded * nvir, len(late) * 8 * padded * nvir),
    )(where, *state, *gathered(late))
    added = lax.all_to_all(added, SLABS, split_axis=0, concat_axis=0, tiled=True)
    return jnp.sum(added, axis=0)[:width]


def solution(mesh):
    fine = Mesh(mesh.devices.reshape(4, 2, 8, 2, 2), ("x", "yl", "z", "yh", "c"))
    pair, grid = SLABS, ("z", "yh", "c")
    in_specs = (P(None, pair, grid), P(), P(), P())
    return jax.shard_map(local, mesh=fine, in_specs=in_specs, out_specs=P(grid, pair), check_vma=False)
```

time: 214 us -> 211 us (0.986)
  waiting for transfers between devices: 85.2 us -> 74 us
  local copies, waits for them, and re-layouts: 7.93 us -> 14.6 us
  starting transfers between devices: 28.8 us -> 34.9 us
  between operations: 5.18 us -> 0.25 us
  other arithmetic: 8.17 us -> 11.9 us
    ppermute x16, waiting for transfers between devices: 69.1 us -> 52.9 us  [shift(): lax.ppermute(value, axis, [(i, (i + step) % size) for i in range(size)])]
    all_to_all x0 -> x1, waiting for transfers between devices: none -> 8.64 us  [local(): lax.all_to_all(turned, 'z', split_axis=0, concat_axis=0, tiled=True)]
    all_to_all x0 -> x1, starting transfers between devices: none -> 7.47 us  [local(): lax.all_to_all(turned, 'z', split_axis=0, concat_axis=0, tiled=True)]
    unnamed x22 -> x33, local copies, waits for them, and re-layouts: 2.19 us -> 9.37 us
    ppermute x10 -> x11, waiting for transfers between devices: 16.1 us -> 12.5 us  [swap(): return lax.ppermute(value, axis, [(0, 1), (1, 0)])]
    pallas_call x2 -> x4, Pallas kernels: 15.1 us -> 13.2 us  [the longest x1 5.52 us: local(): pl.pallas_call(functools.partial(integral_kernel, padded), out_shape=(jax...]
  transfers between devices with their start and end apart: 26 -> 28, of which waited for: 18 -> 13; matrix products, arithmetic and copies ran while one was open for 1% -> 2% of each run, Pallas kernels for 0% -> 3%
where the time goes in v2:
time: 211 us; the launch traced here: 208 us
  waiting for transfers between devices  74 us (35%)
  blocking collectives  59.1 us (28%)
  starting transfers between devices  34.9 us (17%)
  local copies, waits for them, and re-layouts  14.6 us (7%)
  Pallas kernels  13.2 us (6%)
  other arithmetic  11.9 us (6%)
    ppermute x16, waiting for transfers between devices, shift(): lax.ppermute(value, axis, [(i, (i + step) % size) for i in range(size)])  52.9 us
    all_to_all x1, blocking collectives, local(): lax.all_to_all(outgoing, ('yh', 'x', 'yl'), split_axis=0, concat_axis=0,...  48.5 us
    ppermute x16, starting transfers between devices, shift(): lax.ppermute(value, axis, [(i, (i + step) % size) for i in range(size)])  23.8 us
    ppermute x11, waiting for transfers between devices, swap(): return lax.ppermute(value, axis, [(0, 1), (1, 0)])  12.5 us
    all_to_all x1, blocking collectives, local(): lax.all_to_all(added, SLABS, split_axis=0, concat_axis=0, tiled=True)  10.6 us
    unnamed x33, local copies, waits for them, and re-layouts  9.37 us
    all_to_all x1, waiting for transfers between devices, local(): lax.all_to_all(turned, 'z', split_axis=0, concat_axis=0, tiled=True)  8.64 us
    all_to_all x1, starting transfers between devices, local(): lax.all_to_all(turned, 'z', split_axis=0, concat_axis=0, tiled=True)  7.47 us
  transfers between devices with their start and end apart: 28, of which 13 were waited for; matrix products, arithmetic and copies ran while one was open for 2% of the time, Pallas kernels for 3%

profile of v2, /device:TPU:32, one launch (start us, length us, event | category | flops | bytes accessed | tf_op | source)
XLA Modules:
  0.0 207.9 jit_solution(3051300655518395095)
XLA Ops:
  2.4 1.7 gather_fusion
  4.1 1.5 copy.9
  6.5 48.5 %all_to_all.15.near_ref = bf16[16,272,300]{2,1,0:T(8,128)(2,1)} all-to-all(bf16[16,272,300]{2,1,0:T(8,128)(2,1)S(1)} %bitcast.77), channel_id=1, replica_groups=mesh['x'=4,'yl'=2,'z'=8,'yh'=2,'c'=2] {'yh','x','yl'}, dimensions={0} | all-to-all | bytes 5222400 | tf_op jit(solution)/shard_map/all_to_all | solution.py:153
  55.2 6.1 %collective-permute-done.far_ref = bf16[16,272,300]{2,1,0:T(8,128)(2,1)} collective-permute-done((bf16[16,272,300]{2,1,0:T(8,128)(2,1)}, bf16[16,272,300]{2,1,0:T(8,128)(2,1)}, u32[]{:S(2)}, u32[]{:S(2)}) %collective-permute-start) | collective-permute-done | bytes 2611232 | tf_op jit(solution)/shard_map/ppermute | solution.py:20
  61.3 5.5 %shard_map.46 = (f32[384,1408]{1,0:T(8,128)S(1)}, f32[48,1408]{1,0:T(8,128)S(1)}) custom-call(s32[5]{0:T(128)S(1)} %stack.46.where_ref, s32[8,2]{1,0:T(8,128)S(1)} %copy.11.pair_ref, f32[16]{0:T(128)S(1)} %copy-done.13, f32[1,1408]{1,0:T(1,128)S(1)} %broadcast_in_dim.4.vir_ref, bf16[16,272,300]{2,1,0:T(8,128)(2,1)} %all_to_all.15.near_ref, ...), custom_call_target="tpu_custom_call" | custom-call | tf_op jit(solution)/shard_map/pallas_call | solution.py:156
  68.4 5.7 %collective-permute-done.5 = f32[24,1408]{1,0:T(8,128)S(1)} collective-permute-done((f32[24,1408]{1,0:T(8,128)S(1)}, f32[24,1408]{1,0:T(8,128)S(1)}, u32[]{:S(2)}, u32[]{:S(2)}) %collective-permute-start.5) | collective-permute-done | bytes 135200 | tf_op jit(solution)/shard_map/ppermute | solution.py:25
  75.0 3.4 %collective-permute-start.6 = (f32[48,1408]{1,0:T(8,128)S(1)}, f32[48,1408]{1,0:T(8,128)S(1)}, u32[]{:S(2)}, u32[]{:S(2)}) collective-permute-start(f32[48,1408]{1,0:T(8,128)S(1)} %bitcast_add_fusion), channel_id=1, source_target_pairs={{0,28},{4,0},{8,4},{12,8},{16,12},{20,16},{24,20},{28,24},{1,29},{... | collective-permute-start | bytes 811016 | tf_op jit(solution)/shard_map/ppermute | solution.py:25
  78.4 5.2 %collective-permute-done.6 = f32[48,1408]{1,0:T(8,128)S(1)} collective-permute-done((f32[48,1408]{1,0:T(8,128)S(1)}, f32[48,1408]{1,0:T(8,128)S(1)}, u32[]{:S(2)}, u32[]{:S(2)}) %collective-permute-start.6) | collective-permute-done | bytes 270368 | tf_op jit(solution)/shard_map/ppermute | solution.py:25
  84.6 3.8 %collective-permute-start.7 = (f32[48,1408]{1,0:T(8,128)S(1)}, f32[48,1408]{1,0:T(8,128)S(1)}, u32[]{:S(2)}, u32[]{:S(2)}) collective-permute-start(f32[48,1408]{1,0:T(8,128)S(1)} %bitcast_add_fusion.1), channel_id=1, source_target_pairs={{0,28},{4,0},{8,4},{12,8},{16,12},{20,16},{24,20},{28,24},{1,29},{... | collective-permute-start | bytes 811016 | tf_op jit(solution)/shard_map/ppermute | solution.py:25
  88.4 6.7 %collective-permute-done.1 = f32[24,1408]{1,0:T(8,128)S(1)} collective-permute-done((f32[24,1408]{1,0:T(8,128)S(1)}, f32[24,1408]{1,0:T(8,128)S(1)}, u32[]{:S(2)}, u32[]{:S(2)}) %collective-permute-start.1) | collective-permute-done | bytes 135200 | tf_op jit(solution)/shard_map/ppermute | solution.py:25
  96.8 7.2 %collective-permute-done.2 = f32[48,1408]{1,0:T(8,128)S(1)} collective-permute-done((f32[48,1408]{1,0:T(8,128)S(1)}, f32[48,1408]{1,0:T(8,128)S(1)}, u32[]{:S(2)}, u32[]{:S(2)}) %collective-permute-start.2) | collective-permute-done | bytes 270368 | tf_op jit(solution)/shard_map/ppermute | solution.py:25
  105.0 3.3 %collective-permute-start.8 = (f32[48,1408]{1,0:T(8,128)S(1)}, f32[48,1408]{1,0:T(8,128)S(1)}, u32[]{:S(2)}, u32[]{:S(2)}) collective-permute-start(f32[48,1408]{1,0:T(8,128)S(1)} %get-tuple-element.19), channel_id=1, source_target_pairs={{0,28},{4,0},{8,4},{12,8},{16,12},{20,16},{24,20},{28,24},{1,29},{... | collective-permute-start | bytes 811016 | tf_op jit(solution)/shard_map/ppermute | solution.py:25
  108.4 4.4 %collective-permute-done.3 = f32[48,1408]{1,0:T(8,128)} collective-permute-done((f32[48,1408]{1,0:T(8,128)S(1)}, f32[48,1408]{1,0:T(8,128)}, u32[]{:S(2)}, u32[]{:S(2)}) %collective-permute-start.3) | collective-permute-done | bytes 270368 | tf_op jit(solution)/shard_map/ppermute | solution.py:25
  112.8 1.8 bitcast_add_fusion.5
  114.6 7.9 %collective-permute-done.4 = f32[48,1408]{1,0:T(8,128)S(1)} collective-permute-done((f32[48,1408]{1,0:T(8,128)}, f32[48,1408]{1,0:T(8,128)S(1)}, u32[]{:S(2)}, u32[]{:S(2)}) %collective-permute-start.4) | collective-permute-done | bytes 270368 | tf_op jit(solution)/shard_map/ppermute | solution.py:25
  123.5 1.7 collective-permute-start.9
  125.1 6.4 %collective-permute-done.9 = f32[48,1408]{1,0:T(8,128)S(1)} collective-permute-done((f32[48,1408]{1,0:T(8,128)S(1)}, f32[48,1408]{1,0:T(8,128)S(1)}, u32[]{:S(2)}, u32[]{:S(2)}) %collective-permute-start.9) | collective-permute-done | bytes 270368 | tf_op jit(solution)/shard_map/ppermute | solution.py:20
  132.3 3.2 %collective-permute-start.12 = (bf16[2,48,1408]{2,1,0:T(8,128)(2,1)}, bf16[2,48,1408]{2,1,0:T(8,128)(2,1)}, u32[]{:S(2)}, u32[]{:S(2)}) collective-permute-start(bf16[2,48,1408]{2,1,0:T(8,128)(2,1)} %get-tuple-element.17), channel_id=1, source_target_pairs={{0,28},{4,0},{8,4},{12,8},{16,12},{20,16},{24,20},{28,24},{1,29},{... | collective-permute-start | bytes 811016 | tf_op jit(solution)/shard_map/ppermute | solution.py:25
  135.5 4.5 %collective-permute-done.12 = bf16[2,48,1408]{2,1,0:T(8,128)(2,1)} collective-permute-done((bf16[2,48,1408]{2,1,0:T(8,128)(2,1)}, bf16[2,48,1408]{2,1,0:T(8,128)(2,1)}, u32[]{:S(2)}, u32[]{:S(2)}) %collective-permute-start.12) | collective-permute-done | bytes 270368 | tf_op jit(solution)/shard_map/ppermute | solution.py:25
  140.0 2.4 %collective-permute-start.16 = (bf16[2,48,1408]{2,1,0:T(8,128)(2,1)}, bf16[2,48,1408]{2,1,0:T(8,128)(2,1)}, u32[]{:S(2)}, u32[]{:S(2)}) collective-permute-start(bf16[2,48,1408]{2,1,0:T(8,128)(2,1)} %collective-permute-done.12), channel_id=1, source_target_pairs={{0,28},{4,0},{8,4},{12,8},{16,12},{20,16},{24,20},{28,24},{1,29},{... | collective-permute-start | bytes 811016 | tf_op jit(solution)/shard_map/ppermute | solution.py:25
  142.4 4.5 %collective-permute-done.16 = bf16[2,48,1408]{2,1,0:T(8,128)(2,1)} collective-permute-done((bf16[2,48,1408]{2,1,0:T(8,128)(2,1)}, bf16[2,48,1408]{2,1,0:T(8,128)(2,1)}, u32[]{:S(2)}, u32[]{:S(2)}) %collective-permute-start.16) | collective-permute-done | bytes 270368 | tf_op jit(solution)/shard_map/ppermute | solution.py:25
  146.9 2.8 %collective-permute-start.20 = (bf16[2,48,1408]{2,1,0:T(8,128)(2,1)}, bf16[2,48,1408]{2,1,0:T(8,128)(2,1)S(1)}, u32[]{:S(2)}, u32[]{:S(2)}) collective-permute-start(bf16[2,48,1408]{2,1,0:T(8,128)(2,1)} %collective-permute-done.16), channel_id=1, source_target_pairs={{0,28},{4,0},{8,4},{12,8},{16,12},{20,16},{24,20},{28,24},{1,29},{... | collective-permute-start | bytes 811016 | tf_op jit(solution)/shard_map/ppermute | solution.py:25
  149.8 4.4 %collective-permute-done.20 = bf16[2,48,1408]{2,1,0:T(8,128)(2,1)S(1)} collective-permute-done((bf16[2,48,1408]{2,1,0:T(8,128)(2,1)}, bf16[2,48,1408]{2,1,0:T(8,128)(2,1)S(1)}, u32[]{:S(2)}, u32[]{:S(2)}) %collective-permute-start.20) | collective-permute-done | bytes 270368 | tf_op jit(solution)/shard_map/ppermute | solution.py:25
  154.2 4.0 %collective-permute-start.25 = (bf16[48,1408]{1,0:T(8,128)(2,1)S(1)}, bf16[48,1408]{1,0:T(8,128)(2,1)}, u32[]{:S(2)}, u32[]{:S(2)}) collective-permute-start(bf16[48,1408]{1,0:T(8,128)(2,1)S(1)} %slice_bitcast_fusion), channel_id=1, source_target_pairs={{0,28},{4,0},{8,4},{12,8},{16,12},{20,16},{24,20},{28,24},{1,29},{... | collective-permute-start | bytes 405512 | tf_op jit(solution)/shard_map/ppermute | solution.py:25
  158.2 2.3 %collective-permute-done.22 = bf16[2,48,1408]{2,1,0:T(8,128)(2,1)S(1)} collective-permute-done((bf16[2,48,1408]{2,1,0:T(8,128)(2,1)S(1)}, bf16[2,48,1408]{2,1,0:T(8,128)(2,1)S(1)}, u32[]{:S(2)}, u32[]{:S(2)}) %collective-permute-start.22) | collective-permute-done | bytes 270368 | tf_op jit(solution)/shard_map/ppermute | solution.py:25
  161.9 2.3 %shard_map.47 = f32[8,2,48,96]{3,2,1,0:T(8,128)} custom-call(s32[5]{0:T(128)S(1)} %stack.46.where_ref, f32[96,1408]{1,0:T(8,128)S(1)} %bitcast.63, f32[96,1408]{1,0:T(8,128)S(1)} %collective-permute-done.10.far_ref), custom_call_target="tpu_custom_call" | custom-call | flops 77856768 | bytes 1081344 | tf_op jit(solution)/shard_map/pallas_call | solution.py:191
  164.2 7.5 %all-to-all-start.1 = ((f32[8,2,48,96]{3,2,1,0:T(8,128)}), f32[8,2,48,96]{3,2,1,0:T(8,128)S(1)}, u32[]{:S(2)}, u32[]{:S(2)}) async-start(f32[8,2,48,96]{3,2,1,0:T(8,128)} %shard_map.47), calls=%async_computation.1 | async-start | bytes 786432 | tf_op jit(solution)/shard_map/all_to_all | solution.py:199
  172.1 1.7 pad_maximum_fusion.1
  176.9 8.6 %all-to-all-done.1.turned_ref = f32[8,2,48,96]{3,2,1,0:T(8,128)S(1)} async-done(((f32[8,2,48,96]{3,2,1,0:T(8,128)}), f32[8,2,48,96]{3,2,1,0:T(8,128)S(1)}, u32[]{:S(2)}, u32[]{:S(2)}) %all-to-all-start.1) | async-done | bytes 294944 | tf_op jit(solution)/shard_map/all_to_all | solution.py:199
  189.3 3.2 %shard_map.48 = (f32[48,1408]{1,0:T(8,128)S(1)}, f32[8,48,176]{2,1,0:T(8,128)S(1)}, bf16[48,1408]{1,0:T(8,128)(2,1)S(1)}, bf16[8,2,48,96]{3,2,1,0:T(8,128)(2,1)S(1)}) custom-call(s32[5]{0:T(128)S(1)} %stack.46.where_ref, f32[48,1408]{1,0:T(8,128)S(1)} %fusion.rows_ref, f32[8,2,48,96]{3,2,1,0:T(8,128)S(1)} %all-to-all-done.1.turned_ref, ...), custom_call_target="tpu_custom_call" | custom-call | flops 129761280 | bytes 2703360 | tf_op jit(solution)/shard_map/pallas_call | solution.py:209
  194.5 2.2 %shard_map.49 = f32[8,48,176]{2,1,0:T(8,128)S(1)} custom-call(s32[5]{0:T(128)S(1)} %stack.46.where_ref, f32[48,1408]{1,0:T(8,128)S(1)} %get-tuple-element.13.total_ref, f32[8,48,176]{2,1,0:T(8,128)S(1)} %get-tuple-element.14.blocks_ref, bf16[48,1408]{1,0:T(8,128)(2,1)S(1)} %get-tuple-element.15.tilde_ref, ...), custom_call_target="tpu_custom_call" | custom-call | flops 77856768 | bytes 1622016 | tf_op jit(solution)/shard_map/pallas_call | solution.py:222
  196.7 10.6 %all_to_all.16 = f32[8,48,176]{2,1,0:T(8,128)S(1)} all-to-all(f32[8,48,176]{2,1,0:T(8,128)S(1)} %shard_map.49), channel_id=1, replica_groups=mesh['x'=4,'yl'=2,'z'=8,'yh'=2,'c'=2] {'x','yl'}, dimensions={0} | all-to-all | bytes 540672 | tf_op jit(solution)/shard_map/all_to_all | solution.py:230
  (87 shorter events, 22.8 us)
Async XLA Ops:
  6.4 48.5 %copy-start.15 = (s32[8,2]{0,1:T(2,128)S(1)}, s32[8,2]{0,1:T(2,128)}, u32[]{:S(2)}) copy-start(s32[8,2]{0,1:T(2,128)} %param.5) | copy-start | bytes 196
  6.5 48.6 %copy-start.14 = (f32[1408]{0:T(1024)S(1)}, f32[1408]{0:T(1024)}, u32[]{:S(2)}) copy-start(f32[1408]{0:T(1024)} %param.7) | copy-start | bytes 16900
  6.5 54.8 %copy-start.13 = (f32[16]{0:T(128)S(1)}, f32[16]{0:T(128)}, u32[]{:S(2)}) copy-start(f32[16]{0:T(128)} %occ_ref.1) | copy-start | bytes 196
  55.0 6.3 %collective-permute-start = (bf16[16,272,300]{2,1,0:T(8,128)(2,1)}, bf16[16,272,300]{2,1,0:T(8,128)(2,1)}, u32[]{:S(2)}, u32[]{:S(2)}) collective-permute-start(bf16[16,272,300]{2,1,0:T(8,128)(2,1)} %all_to_all.15.near_ref), channel_id=1, source_target_pairs={{0,1},{1,0},{2,3},{3,2},{4,5},{5,4},{6,7},{7,6},{8,9},{9,8},{10,11... | collective-permute-start | bytes 7833608 | tf_op jit(solution)/shard_map/ppermute | solution.py:20
  68.2 5.9 %collective-permute-start.5 = (f32[24,1408]{1,0:T(8,128)S(1)}, f32[24,1408]{1,0:T(8,128)S(1)}, u32[]{:S(2)}, u32[]{:S(2)}) collective-permute-start(f32[24,1408]{1,0:T(8,128)S(1)} %get-tuple-element.21), channel_id=1, source_target_pairs={{0,28},{4,0},{8,4},{12,8},{16,12},{20,16},{24,20},{28,24},{1,29},{... | collective-permute-start | bytes 405512 | tf_op jit(solution)/shard_map/ppermute | solution.py:25
  75.0 8.6 %collective-permute-start.6 = (f32[48,1408]{1,0:T(8,128)S(1)}, f32[48,1408]{1,0:T(8,128)S(1)}, u32[]{:S(2)}, u32[]{:S(2)}) collective-permute-start(f32[48,1408]{1,0:T(8,128)S(1)} %bitcast_add_fusion), channel_id=1, source_target_pairs={{0,28},{4,0},{8,4},{12,8},{16,12},{20,16},{24,20},{28,24},{1,29},{... | collective-permute-start | bytes 811016 | tf_op jit(solution)/shard_map/ppermute | solution.py:25
  84.6 10.4 %collective-permute-start.7 = (f32[48,1408]{1,0:T(8,128)S(1)}, f32[48,1408]{1,0:T(8,128)S(1)}, u32[]{:S(2)}, u32[]{:S(2)}) collective-permute-start(f32[48,1408]{1,0:T(8,128)S(1)} %bitcast_add_fusion.1), channel_id=1, source_target_pairs={{0,28},{4,0},{8,4},{12,8},{16,12},{20,16},{24,20},{28,24},{1,29},{... | collective-permute-start | bytes 811016 | tf_op jit(solution)/shard_map/ppermute | solution.py:25
  88.4 6.7 %collective-permute-start.1 = (f32[24,1408]{1,0:T(8,128)S(1)}, f32[24,1408]{1,0:T(8,128)S(1)}, u32[]{:S(2)}, u32[]{:S(2)}) collective-permute-start(f32[24,1408]{1,0:T(8,128)S(1)} %get-tuple-element.22), channel_id=1, source_target_pairs={{0,4},{4,8},{8,12},{12,16},{16,20},{20,24},{24,28},{28,0},{1,5},{5... | collective-permute-start | bytes 405512 | tf_op jit(solution)/shard_map/ppermute | solution.py:25
  96.2 7.8 %collective-permute-start.2 = (f32[48,1408]{1,0:T(8,128)S(1)}, f32[48,1408]{1,0:T(8,128)S(1)}, u32[]{:S(2)}, u32[]{:S(2)}) collective-permute-start(f32[48,1408]{1,0:T(8,128)S(1)} %get-tuple-element.20), channel_id=1, source_target_pairs={{0,4},{4,8},{8,12},{12,16},{16,20},{20,24},{24,28},{28,0},{1,5},{5... | collective-permute-start | bytes 811016 | tf_op jit(solution)/shard_map/ppermute | solution.py:25
  104.9 7.9 %collective-permute-start.3 = (f32[48,1408]{1,0:T(8,128)S(1)}, f32[48,1408]{1,0:T(8,128)}, u32[]{:S(2)}, u32[]{:S(2)}) collective-permute-start(f32[48,1408]{1,0:T(8,128)S(1)} %bitcast_add_fusion.4), channel_id=1, source_target_pairs={{0,4},{4,8},{8,12},{12,16},{16,20},{20,24},{24,28},{28,0},{1,5},{5... | collective-permute-start | bytes 811016 | tf_op jit(solution)/shard_map/ppermute | solution.py:25
  105.0 9.5 %collective-permute-start.8 = (f32[48,1408]{1,0:T(8,128)S(1)}, f32[48,1408]{1,0:T(8,128)S(1)}, u32[]{:S(2)}, u32[]{:S(2)}) collective-permute-start(f32[48,1408]{1,0:T(8,128)S(1)} %get-tuple-element.19), channel_id=1, source_target_pairs={{0,28},{4,0},{8,4},{12,8},{16,12},{20,16},{24,20},{28,24},{1,29},{... | collective-permute-start | bytes 811016 | tf_op jit(solution)/shard_map/ppermute | solution.py:25
  114.6 7.9 %collective-permute-start.4 = (f32[48,1408]{1,0:T(8,128)}, f32[48,1408]{1,0:T(8,128)S(1)}, u32[]{:S(2)}, u32[]{:S(2)}) collective-permute-start(f32[48,1408]{1,0:T(8,128)} %bitcast_add_fusion.5), channel_id=1, source_target_pairs={{0,4},{4,8},{8,12},{12,16},{16,20},{20,24},{24,28},{28,0},{1,5},{5... | collective-permute-start | bytes 811016 | tf_op jit(solution)/shard_map/ppermute | solution.py:25
  123.5 8.1 %collective-permute-start.9 = (f32[48,1408]{1,0:T(8,128)S(1)}, f32[48,1408]{1,0:T(8,128)S(1)}, u32[]{:S(2)}, u32[]{:S(2)}) collective-permute-start(f32[48,1408]{1,0:T(8,128)S(1)} %fusion.rows_ref), channel_id=1, source_target_pairs={{0,2},{2,0},{1,3},{3,1},{4,6},{6,4},{5,7},{7,5},{8,10},{10,8},{9,1... | collective-permute-start | bytes 811016 | tf_op jit(solution)/shard_map/ppermute | solution.py:20
  132.3 7.8 %collective-permute-start.12 = (bf16[2,48,1408]{2,1,0:T(8,128)(2,1)}, bf16[2,48,1408]{2,1,0:T(8,128)(2,1)}, u32[]{:S(2)}, u32[]{:S(2)}) collective-permute-start(bf16[2,48,1408]{2,1,0:T(8,128)(2,1)} %get-tuple-element.17), channel_id=1, source_target_pairs={{0,28},{4,0},{8,4},{12,8},{16,12},{20,16},{24,20},{28,24},{1,29},{... | collective-permute-start | bytes 811016 | tf_op jit(solution)/shard_map/ppermute | solution.py:25
  135.5 6.9 %collective-permute-start.14 = (bf16[2,48,1408]{2,1,0:T(8,128)(2,1)}, bf16[2,48,1408]{2,1,0:T(8,128)(2,1)}, u32[]{:S(2)}, u32[]{:S(2)}) collective-permute-start(bf16[2,48,1408]{2,1,0:T(8,128)(2,1)} %get-tuple-element.17), channel_id=1, source_target_pairs={{0,4},{4,8},{8,12},{12,16},{16,20},{20,24},{24,28},{28,0},{1,5},{5... | collective-permute-start | bytes 811016 | tf_op jit(solution)/shard_map/ppermute | solution.py:25
  140.0 6.9 %collective-permute-start.16 = (bf16[2,48,1408]{2,1,0:T(8,128)(2,1)}, bf16[2,48,1408]{2,1,0:T(8,128)(2,1)}, u32[]{:S(2)}, u32[]{:S(2)}) collective-permute-start(bf16[2,48,1408]{2,1,0:T(8,128)(2,1)} %collective-permute-done.12), channel_id=1, source_target_pairs={{0,28},{4,0},{8,4},{12,8},{16,12},{20,16},{24,20},{28,24},{1,29},{... | collective-permute-start | bytes 811016 | tf_op jit(solution)/shard_map/ppermute | solution.py:25
  142.4 7.3 %collective-permute-start.18 = (bf16[2,48,1408]{2,1,0:T(8,128)(2,1)}, bf16[2,48,1408]{2,1,0:T(8,128)(2,1)S(1)}, u32[]{:S(2)}, u32[]{:S(2)}) collective-permute-start(bf16[2,48,1408]{2,1,0:T(8,128)(2,1)} %collective-permute-done.14), channel_id=1, source_target_pairs={{0,4},{4,8},{8,12},{12,16},{16,20},{20,24},{24,28},{28,0},{1,5},{5... | collective-permute-start | bytes 811016 | tf_op jit(solution)/shard_map/ppermute | solution.py:25
  146.9 7.3 %collective-permute-start.20 = (bf16[2,48,1408]{2,1,0:T(8,128)(2,1)}, bf16[2,48,1408]{2,1,0:T(8,128)(2,1)S(1)}, u32[]{:S(2)}, u32[]{:S(2)}) collective-permute-start(bf16[2,48,1408]{2,1,0:T(8,128)(2,1)} %collective-permute-done.16), channel_id=1, source_target_pairs={{0,28},{4,0},{8,4},{12,8},{16,12},{20,16},{24,20},{28,24},{1,29},{... | collective-permute-start | bytes 811016 | tf_op jit(solution)/shard_map/ppermute | solution.py:25
  149.7 12.1 %collective-permute-start.10 = (f32[96,1408]{1,0:T(8,128)S(1)}, f32[96,1408]{1,0:T(8,128)S(1)}, u32[]{:S(2)}, u32[]{:S(2)}) collective-permute-start(f32[96,1408]{1,0:T(8,128)S(1)} %bitcast.62), channel_id=1, source_target_pairs={{0,1},{1,0},{2,3},{3,2},{4,5},{5,4},{6,7},{7,6},{8,9},{9,8},{10,11... | collective-permute-start | bytes 1622024 | tf_op jit(solution)/shard_map/ppermute | solution.py:20
  149.7 12.2 %copy-start.7 = (bf16[2,48,1408]{2,1,0:T(8,128)(2,1)}, bf16[2,48,1408]{2,1,0:T(8,128)(2,1)S(1)}, u32[]{:S(2)}) copy-start(bf16[2,48,1408]{2,1,0:T(8,128)(2,1)S(1)} %collective-permute-done.18) | copy-start | bytes 811012
  149.7 10.8 %collective-permute-start.22 = (bf16[2,48,1408]{2,1,0:T(8,128)(2,1)S(1)}, bf16[2,48,1408]{2,1,0:T(8,128)(2,1)S(1)}, u32[]{:S(2)}, u32[]{:S(2)}) collective-permute-start(bf16[2,48,1408]{2,1,0:T(8,128)(2,1)S(1)} %collective-permute-done.18), channel_id=1, source_target_pairs={{0,4},{4,8},{8,12},{12,16},{16,20},{20,24},{24,28},{28,0},{1,5},{5... | collective-permute-start | bytes 811016 | tf_op jit(solution)/shard_map/ppermute | solution.py:25
  154.2 17.4 %collective-permute-start.25 = (bf16[48,1408]{1,0:T(8,128)(2,1)S(1)}, bf16[48,1408]{1,0:T(8,128)(2,1)}, u32[]{:S(2)}, u32[]{:S(2)}) collective-permute-start(bf16[48,1408]{1,0:T(8,128)(2,1)S(1)} %slice_bitcast_fusion), channel_id=1, source_target_pairs={{0,28},{4,0},{8,4},{12,8},{16,12},{20,16},{24,20},{28,24},{1,29},{... | collective-permute-start | bytes 405512 | tf_op jit(solution)/shard_map/ppermute | solution.py:25
  161.3 10.4 %collective-permute-start.24 = (bf16[48,1408]{1,0:T(8,128)(2,1)}, bf16[48,1408]{1,0:T(8,128)(2,1)}, u32[]{:S(2)}, u32[]{:S(2)}) collective-permute-start(bf16[48,1408]{1,0:T(8,128)(2,1)} %slice_bitcast_fusion.1), channel_id=1, source_target_pairs={{0,4},{4,8},{8,12},{12,16},{16,20},{20,24},{24,28},{28,0},{1,5},{5... | collective-permute-start | bytes 405512 | tf_op jit(solution)/shard_map/ppermute | solution.py:25
  161.3 12.6 %collective-permute-start.11 = (bf16[2,48,1408]{2,1,0:T(8,128)(2,1)}, bf16[2,48,1408]{2,1,0:T(8,128)(2,1)}, u32[]{:S(2)}, u32[]{:S(2)}) collective-permute-start(bf16[2,48,1408]{2,1,0:T(8,128)(2,1)} %get-tuple-element.17), channel_id=1, source_target_pairs={{0,1},{1,0},{2,3},{3,2},{4,5},{5,4},{6,7},{7,6},{8,9},{9,8},{10,11... | collective-permute-start | bytes 811016 | tf_op jit(solution)/shard_map/ppermute | solution.py:20
  161.3 12.7 %collective-permute-start.13 = (bf16[2,48,1408]{2,1,0:T(8,128)(2,1)}, bf16[2,48,1408]{2,1,0:T(8,128)(2,1)}, u32[]{:S(2)}, u32[]{:S(2)}) collective-permute-start(bf16[2,48,1408]{2,1,0:T(8,128)(2,1)} %collective-permute-done.12), channel_id=1, source_target_pairs={{0,1},{1,0},{2,3},{3,2},{4,5},{5,4},{6,7},{7,6},{8,9},{9,8},{10,11... | collective-permute-start | bytes 811016 | tf_op jit(solution)/shard_map/ppermute | solution.py:20
  161.8 12.6 %collective-permute-start.15 = (bf16[2,48,1408]{2,1,0:T(8,128)(2,1)}, bf16[2,48,1408]{2,1,0:T(8,128)(2,1)}, u32[]{:S(2)}, u32[]{:S(2)}) collective-permute-start(bf16[2,48,1408]{2,1,0:T(8,128)(2,1)} %collective-permute-done.14), channel_id=1, source_target_pairs={{0,1},{1,0},{2,3},{3,2},{4,5},{5,4},{6,7},{7,6},{8,9},{9,8},{10,11... | collective-permute-start | bytes 811016 | tf_op jit(solution)/shard_map/ppermute | solution.py:20
  164.2 21.4 %all-to-all-start.1 = ((f32[8,2,48,96]{3,2,1,0:T(8,128)}), f32[8,2,48,96]{3,2,1,0:T(8,128)S(1)}, u32[]{:S(2)}, u32[]{:S(2)}) async-start(f32[8,2,48,96]{3,2,1,0:T(8,128)} %shard_map.47), calls=%async_computation.1 | async-start | bytes 786432 | tf_op jit(solution)/shard_map/all_to_all | solution.py:199
  171.6 3.8 %collective-permute-start.17 = (bf16[2,48,1408]{2,1,0:T(8,128)(2,1)}, bf16[2,48,1408]{2,1,0:T(8,128)(2,1)S(1)}, u32[]{:S(2)}, u32[]{:S(2)}) collective-permute-start(bf16[2,48,1408]{2,1,0:T(8,128)(2,1)} %collective-permute-done.16), channel_id=1, source_target_pairs={{0,1},{1,0},{2,3},{3,2},{4,5},{5,4},{6,7},{7,6},{8,9},{9,8},{10,11... | collective-permute-start | bytes 811016 | tf_op jit(solution)/shard_map/ppermute | solution.py:20
  171.7 4.5 %collective-permute-start.19 = (bf16[2,48,1408]{2,1,0:T(8,128)(2,1)}, bf16[2,48,1408]{2,1,0:T(8,128)(2,1)S(1)}, u32[]{:S(2)}, u32[]{:S(2)}) collective-permute-start(bf16[2,48,1408]{2,1,0:T(8,128)(2,1)} %copy-done.7), channel_id=1, source_target_pairs={{0,1},{1,0},{2,3},{3,2},{4,5},{5,4},{6,7},{7,6},{8,9},{9,8},{10,11... | collective-permute-start | bytes 811016 | tf_op jit(solution)/shard_map/ppermute | solution.py:20
  173.9 18.7 %collective-permute-start.21 = (bf16[2,48,1408]{2,1,0:T(8,128)(2,1)}, bf16[2,48,1408]{2,1,0:T(8,128)(2,1)}, u32[]{:S(2)}, u32[]{:S(2)}) collective-permute-start(bf16[2,48,1408]{2,1,0:T(8,128)(2,1)} %copy-done.3), channel_id=1, source_target_pairs={{0,1},{1,0},{2,3},{3,2},{4,5},{5,4},{6,7},{7,6},{8,9},{9,8},{10,11... | collective-permute-start | bytes 811016 | tf_op jit(solution)/shard_map/ppermute | solution.py:20
  174.0 18.6 %collective-permute-start.23 = (bf16[2,48,1408]{2,1,0:T(8,128)(2,1)}, bf16[2,48,1408]{2,1,0:T(8,128)(2,1)}, u32[]{:S(2)}, u32[]{:S(2)}) collective-permute-start(bf16[2,48,1408]{2,1,0:T(8,128)(2,1)} %copy-done.5), channel_id=1, source_target_pairs={{0,1},{1,0},{2,3},{3,2},{4,5},{5,4},{6,7},{7,6},{8,9},{9,8},{10,11... | collective-permute-start | bytes 811016 | tf_op jit(solution)/shard_map/ppermute | solution.py:20
  174.4 18.2 %collective-permute-start.26 = (bf16[2,48,1408]{2,1,0:T(8,128)(2,1)}, bf16[2,48,1408]{2,1,0:T(8,128)(2,1)}, u32[]{:S(2)}, u32[]{:S(2)}) collective-permute-start(bf16[2,48,1408]{2,1,0:T(8,128)(2,1)} %pad_maximum_fusion.1), channel_id=1, source_target_pairs={{0,1},{1,0},{2,3},{3,2},{4,5},{5,4},{6,7},{7,6},{8,9},{9,8},{10,11... | collective-permute-start | bytes 811016 | tf_op jit(solution)/shard_map/ppermute | solution.py:20
  (12 other events, 18.9 us)

commit v3 on v2

--- a/solution.py
+++ b/solution.py
@@ -13,7 +13,10 @@
 SLABS = ("x", "yl")
 VMEM = pl.BlockSpec(memory_space=pltpu.VMEM)
 SMEM = pl.BlockSpec(memory_space=pltpu.SMEM)
-PARAMS = pltpu.CompilerParams(vmem_limit_bytes=48 * 1024 * 1024)
+
+
+def params(mib):
+    return pltpu.CompilerParams(vmem_limit_bytes=mib * 1024 * 1024)
 
 
 def swap(value, axis):
@@ -40,26 +43,69 @@
     return pl.CostEstimate(flops=flops, bytes_accessed=moved, transcendentals=0)
 
 
-def integral_kernel(padded, where_ref, pair_ref, occ_ref, vir_ref, near_ref, far_ref, out_ref, denom_ref):
-    sources, rows, naux = near_ref.shape
+def factor_product(ref, left, padded):
+    sources, rows, naux = ref.shape
     half = sources // 2
     slab = rows - 2 * padded
-    c, chunk, group = where_ref[1], where_ref[2], where_ref[3]
-    start = pl.multiple_of(c * padded, padded)
     total = None
-    for ref in (near_ref, far_ref):
-        for y in range(2):
-            a = ref[half * y : half * (y + 1), pl.ds(start, padded), :].reshape(half * padded, naux)
-            b = ref[half * y : half * (y + 1), 2 * padded :, :].reshape(half * slab, naux)
-            term = dot_nt(a, b)
-            total = term if total is None else total + term
-    out_ref[...] = total
+    for y in range(2):
+        b = ref[half * y : half * (y + 1), 2 * padded :, :].reshape(half * slab, naux)
+        term = dot_nt(left(y), b)
+        total = term if total is None else total + term
+    return total
+
+
+def all_rows(ref, start, padded):
+    half = ref.shape[0] // 2
+
+    def left(y):
+        return ref[half * y : half * (y + 1), pl.ds(start, padded), :].reshape(half * padded, ref.shape[2])
+
+    return left
+
+
+def near_kernel(padded, where_ref, near_ref, out_ref):
+    start = pl.multiple_of(where_ref[1] * padded, padded)
+    out_ref[...] = factor_product(near_ref, all_rows(near_ref, start, padded), padded).reshape(out_ref.shape)
+
+
+def first_kernel(padded, where_ref, near_part_ref, far_ref, up_ref, down_ref):
+    nz = near_part_ref.shape[0]
+    half = far_ref.shape[0] // 2
+    start = pl.multiple_of(where_ref[1] * padded, padded)
+    at = lax.rem(where_ref[0] + nz // 2, nz)
+    total = factor_product(far_ref, lambda y: far_ref[half * y + at, pl.ds(start, padded), :], padded)
+    total = total + near_part_ref[at]
+    up_ref[...] = total[: padded // 2]
+    down_ref[...] = total[padded // 2 :]
+
+
+def rest_kernel(padded, where_ref, pair_ref, occ_ref, vir_ref, near_part_ref, far_ref, out_ref, denom_ref):
+    start = pl.multiple_of(where_ref[1] * padded, padded)
+    total = factor_product(far_ref, all_rows(far_ref, start, padded), padded)
+    out_ref[...] = near_part_ref[...] + total.reshape(out_ref.shape)
+    chunk, group, width = where_ref[2], where_ref[3], where_ref[5]
     columns = jnp.broadcast_to(vir_ref[...], denom_ref.shape)
     place = lax.broadcasted_iota(jnp.int32, denom_ref.shape, 1)
     row = lax.broadcasted_iota(jnp.int32, denom_ref.shape, 0)
-    width = slab // 4
     own = jnp.sum(jnp.where(place == chunk * width + row, columns, 0.0), axis=1, keepdims=True)
     denom_ref[...] = (own + columns) - occ_ref[pair_ref[group, 0]] - occ_ref[pair_ref[group, 1]]
+
+
+def hop_kernel(step, where_ref, part_ref, up_in, down_in, up_ref, down_ref):
+    nz, rows = part_ref.shape[:2]
+    above = lax.rem(where_ref[0] + step, nz)
+    below = lax.rem(where_ref[0] + nz - step, nz)
+    taken = up_in.shape[0]
+    up_ref[:taken] = part_ref[above, :taken] + up_in[...]
+    down_ref[rows - taken :] = part_ref[below, rows - taken :] + down_in[...]
+    if taken < rows:
+        up_ref[taken:] = part_ref[above, taken:]
+        down_ref[: rows - taken] = part_ref[below, : rows - taken]
+
+
+def amplitude_kernel(where_ref, part_ref, up_in, down_in, denom_ref, out_ref):
+    out_ref[...] = (part_ref[where_ref[0]] + (up_in[...] + down_in[...])) / denom_ref[...]
 
 
 def turn_kernel(nz, width, padded, where_ref, near_ref, far_ref, out_ref):
@@ -81,7 +127,8 @@
         at = lax.rem(z + r, nz)
         sides = []
         for slot in range(2):
-            piece = pieces[2 * n + slot][...]
+            piece = pieces[2 * n + slot]
+            piece = jnp.concatenate([ref[...] for ref in piece], axis=0) if isinstance(piece, tuple) else piece[...]
             term = jnp.dot(tilde_t_ref[at, slot], piece, preferred_element_type=F32)
             total = term if total is None else total + term
             sides.append(dot_nt(tilde, piece))
@@ -125,7 +172,8 @@
 
 
 def late_kernel(steps, nz, width, padded, where_ref, total_ref, blocks_ref, tilde_ref, tilde_t_ref, *refs):
-    pieces, out_ref = refs[: 2 * len(steps)], refs[-1]
+    pieces, out_ref = list(refs[: 2 * len(steps) - 2]), refs[-1]
+    pieces += [refs[-5:-3], refs[-3:-1]]
     slab = total_ref.shape[1] // nz
     for k in range(nz):
         out_ref[k] = blocks_ref[k]
@@ -143,7 +191,7 @@
     nz = lax.axis_size("z")
     width = slab // 4
     padded = (width + 8) // 8 * 8
-    where = jnp.stack([z, c, z * 4 + yh * 2 + c, lax.axis_index(SLABS), yh * 2 + c])
+    where = jnp.stack([z, c, z * 4 + yh * 2 + c, lax.axis_index(SLABS), yh * 2 + c, jnp.int32(width)])
 
     left = orbital_b[pair_list[:, 0]].reshape(8, 2, 2, width, naux)
     left = jnp.pad(left, ((0, 0), (0, 0), (0, 0), (0, padded - width), (0, 0)))
@@ -153,39 +201,57 @@
     near = lax.all_to_all(outgoing, ("yh", "x", "yl"), split_axis=0, concat_axis=0, tiled=True)
     far = swap(near, "c")
 
+    whole = jax.ShapeDtypeStruct((8, padded, nvir), F32)
+    rows = jax.ShapeDtypeStruct((padded, nvir), F32)
+    halves = jax.ShapeDtypeStruct((padded // 2, nvir), F32)
+    flops = 16 * padded * 8 * slab * 2 * naux
+    near_part = pl.pallas_call(
+        functools.partial(near_kernel, padded),
+        out_shape=whole,
+        in_specs=[SMEM, VMEM],
+        out_specs=VMEM,
+        compiler_params=params(16),
+        cost_estimate=cost(flops, 0),
+    )(where, near)
+    up, down = pl.pallas_call(
+        functools.partial(first_kernel, padded),
+        out_shape=(halves, halves),
+        in_specs=[SMEM, VMEM, VMEM],
+        out_specs=(VMEM, VMEM),
+        compiler_params=params(16),
+        cost_estimate=cost(flops // 8, 0),
+    )(where, near_part, far)
+    up, down = shift(up, "z", 1), shift(down, "z", -1)
     part, denom = pl.pallas_call(
-        functools.partial(integral_kernel, padded),
-        out_shape=(jax.ShapeDtypeStruct((8 * padded, nvir), F32), jax.ShapeDtypeStruct((padded, nvir), F32)),
+        functools.partial(rest_kernel, padded),
+        out_shape=(whole, rows),
         in_specs=[SMEM, SMEM, SMEM, VMEM, VMEM, VMEM],
         out_specs=(VMEM, VMEM),
-        compiler_params=PARAMS,
-    )(where, pair_list, eps_occ, eps_vir[None], near, far)
-    part = part.reshape(8, padded, nvir)
-
-    def own(offset):
-        return lax.dynamic_index_in_dim(part, lax.rem(z + offset, nz), 0, keepdims=False)
-
-    cut = padded // 2
-    up = shift(own(nz // 2)[:cut], "z", 1)
-    down = shift(own(nz // 2)[cut:], "z", -1)
-    up = jnp.concatenate([up, jnp.zeros_like(down)])
-    down = jnp.concatenate([jnp.zeros_like(down), down])
+        compiler_params=params(20),
+        cost_estimate=cost(flops, 0),
+    )(where, pair_list, eps_occ, eps_vir[None], near_part, far)
     for step in range(nz // 2 - 1, 0, -1):
-        up = shift(own(step) + up, "z", 1)
-        down = shift(own(nz - step) + down, "z", -1)
-    amp_rows = (own(0) + (up + down)) / denom
+        up, down = pl.pallas_call(
+            functools.partial(hop_kernel, step),
+            out_shape=(rows, rows),
+            in_specs=[SMEM, VMEM, VMEM, VMEM],
+            out_specs=(VMEM, VMEM),
+            compiler_params=params(8),
+        )(where, part, up, down)
+        up, down = shift(up, "z", 1), shift(down, "z", -1)
+    amp_rows = pl.pallas_call(
+        amplitude_kernel,
+        out_shape=rows,
+        in_specs=[SMEM, VMEM, VMEM, VMEM, VMEM],
+        out_specs=VMEM,
+        compiler_params=params(8),
+    )(where, part, up, down, denom)
 
     other = swap(amp_rows, "yh")
     both = jnp.where(yh == 0, jnp.stack([amp_rows, other]), jnp.stack([other, amp_rows]))
     both16 = both.astype(BF16)
     ring = {0: both16}
-    up = down = both16
-    for step in range(1, nz // 2):
-        up = shift(up, "z", 1)
-        down = shift(down, "z", -1)
-        ring[nz - step] = up
-        ring[step] = down
-    ring[nz // 2] = jnp.stack([shift(up[0], "z", 1), shift(down[1], "z", -1)])
+    up, down = shift(both16, "z", 1), shift(both16, "z", -1)
 
     both = both.reshape(2 * padded, nvir)
     turned = pl.pallas_call(
@@ -193,10 +259,19 @@
         out_shape=jax.ShapeDtypeStruct((nz, 2, padded, 2 * padded), F32),
         in_specs=[SMEM, VMEM, VMEM],
         out_specs=VMEM,
-        compiler_params=PARAMS,
+        compiler_params=params(8),
         cost_estimate=cost(6 * 4 * padded * padded * nvir, 4 * 4 * padded * nvir),
     )(where, both, swap(both, "c"))
+    up, down, turned = lax.optimization_barrier((up, down, turned))
     turned = lax.all_to_all(turned, "z", split_axis=0, concat_axis=0, tiled=True)
+    for step in range(1, nz // 2):
+        ring[nz - step] = up
+        ring[step] = down
+        if step == nz // 2 - 1:
+            up, down, turned = lax.optimization_barrier((up, down, turned))
+            up, down = shift(up[0], "z", 1), shift(down[1], "z", -1)
+        else:
+            up, down = shift(up, "z", 1), shift(down, "z", -1)
 
     def gathered(steps):
         pieces = []
@@ -205,7 +280,7 @@
         return pieces
 
     soon = (0, 1, nz - 1, 2, nz - 2)
-    late = (3, nz - 3, nz // 2)
+    late = (3, nz - 3)
     state = pl.pallas_call(
         functools.partial(early_kernel, soon, nz, width, padded),
         out_shape=(
@@ -216,17 +291,18 @@
         ),
         in_specs=[SMEM] + [VMEM] * (2 + 2 * len(soon)),
         out_specs=(VMEM,) * 4,
-        compiler_params=PARAMS,
+        compiler_params=params(16),
         cost_estimate=cost(len(soon) * 8 * padded * padded * nvir, len(soon) * 8 * padded * nvir),
     )(where, amp_rows, turned, *gathered(soon))
+    up, down, state = lax.optimization_barrier((up, down, state))
     added = pl.pallas_call(
-        functools.partial(late_kernel, late, nz, width, padded),
+        functools.partial(late_kernel, (*late, nz // 2), nz, width, padded),
         out_shape=jax.ShapeDtypeStruct((nz, padded, slab), F32),
-        in_specs=[SMEM] + [VMEM] * (4 + 2 * len(late)),
+        in_specs=[SMEM] + [VMEM] * (8 + 2 * len(late)),
         out_specs=VMEM,
-        compiler_params=PARAMS,
+        compiler_params=params(16),
         cost_estimate=cost(len(late) * 8 * padded * padded * nvir, len(late) * 8 * padded * nvir),
-    )(where, *state, *gathered(late))
+    )(where, *state, *gathered(late), up, down, swap(up, "c"), swap(down, "c"))
     added = lax.all_to_all(added, SLABS, split_axis=0, concat_axis=0, tiled=True)
     return jnp.sum(added, axis=0)[:width]
 

time: 211 us -> 175 us (0.83)
  waiting for transfers between devices: 74 us -> 52.6 us
  other arithmetic: 11.9 us -> 1.96 us
  Pallas kernels: 13.2 us -> 19.1 us
  starting transfers between devices: 34.9 us -> 29 us
  local copies, waits for them, and re-layouts: 14.6 us -> 9.54 us
    ppermute x16, waiting for transfers between devices: 52.9 us -> 42.3 us  [shift(): lax.ppermute(value, axis, [(i, (i + step) % size) for i in range(size)])]
    all_to_all x1, waiting for transfers between devices: 8.64 us -> 0.01 us  [local(): lax.all_to_all(turned, 'z', split_axis=0, concat_axis=0, tiled=True)]
    unnamed x33 -> x23, local copies, waits for them, and re-layouts: 9.37 us -> 3.2 us
    add x5 -> x0, other arithmetic: 5.81 us -> none  [the longest x3 3.06 us: local(): down = shift(own(nz - step) + down, 'z', -1)]
    pallas_call x2 -> x8, Pallas kernels: 7.74 us -> 13.4 us  [the longest x1 3.36 us: local(): pl.pallas_call(functools.partial(rest_kernel, padded), out_shape=(whole,...]
    ppermute x16, starting transfers between devices: 23.8 us -> 19.4 us  [shift(): lax.ppermute(value, axis, [(i, (i + step) % size) for i in range(size)])]
    ppermute x11 -> x12, waiting for transfers between devices: 12.5 us -> 10.2 us  [swap(): return lax.ppermute(value, axis, [(0, 1), (1, 0)])]
    gather x2, local copies, waits for them, and re-layouts: 3.16 us -> 1.01 us  [local(): left = orbital_b[pair_list[:, 0]].reshape(8, 2, 2, width, naux)]
  transfers between devices with their start and end apart: 28 -> 29, of which waited for: 13 -> 17; matrix products, arithmetic and copies ran while one was open for 2% -> 1% of each run, Pallas kernels for 3% -> 7%
where the time goes in v3:
time: 175 us; the launch traced here: 172 us
  blocking collectives  60 us (34%)
  waiting for transfers between devices  52.6 us (30%)
  starting transfers between devices  29 us (17%)
  Pallas kernels  19.1 us (11%)
  local copies, waits for them, and re-layouts  9.54 us (5%)
  other arithmetic  1.96 us (1%)
    all_to_all x1, blocking collectives, local(): lax.all_to_all(outgoing, ('yh', 'x', 'yl'), split_axis=0, concat_axis=0,...  48.4 us
    ppermute x16, waiting for transfers between devices, shift(): lax.ppermute(value, axis, [(i, (i + step) % size) for i in range(size)])  42.3 us
    ppermute x16, starting transfers between devices, shift(): lax.ppermute(value, axis, [(i, (i + step) % size) for i in range(size)])  19.4 us
    all_to_all x1, blocking collectives, local(): lax.all_to_all(added, SLABS, split_axis=0, concat_axis=0, tiled=True)  11.7 us
    ppermute x12, waiting for transfers between devices, swap(): return lax.ppermute(value, axis, [(0, 1), (1, 0)])  10.2 us
    all_to_all x1, starting transfers between devices, local(): lax.all_to_all(turned, 'z', split_axis=0, concat_axis=0, tiled=True)  6.1 us
    ppermute x12, starting transfers between devices, swap(): return lax.ppermute(value, axis, [(0, 1), (1, 0)])  3.52 us
  transfers between devices with their start and end apart: 29, of which 17 were waited for; matrix products, arithmetic and copies ran while one was open for 1% of the time, Pallas kernels for 7%

profile of v3, /device:TPU:32, one launch (start us, length us, event | category | flops | bytes accessed | tf_op | source)
XLA Modules:
  0.0 172.4 jit_solution(11344624376723760282)
XLA Ops:
  3.0 1.7 gather_fusion.1
  4.7 1.4 broadcast_in_dim.5
  6.5 48.4 %all_to_all.15.near_ref = bf16[16,272,300]{2,1,0:T(8,128)(2,1)} all-to-all(bf16[16,272,300]{2,1,0:T(8,128)(2,1)S(1)} %bitcast.44), channel_id=1, replica_groups=mesh['x'=4,'yl'=2,'z'=8,'yh'=2,'c'=2] {'yh','x','yl'}, dimensions={0} | all-to-all | bytes 5222400 | tf_op jit(solution)/shard_map/all_to_all | solution.py:201
  54.9 3.3 %shard_map.46.near_part_ref = f32[8,48,1408]{2,1,0:T(8,128)S(1)} custom-call(s32[6]{0:T(128)S(1)} %stack.37.where_ref, bf16[16,272,300]{2,1,0:T(8,128)(2,1)} %all_to_all.15.near_ref), custom_call_target="tpu_custom_call" | custom-call | flops 648806400 | tf_op jit(solution)/shard_map/pallas_call | solution.py:208
  58.3 2.8 %collective-permute-done.far_ref = bf16[16,272,300]{2,1,0:T(8,128)(2,1)} collective-permute-done((bf16[16,272,300]{2,1,0:T(8,128)(2,1)}, bf16[16,272,300]{2,1,0:T(8,128)(2,1)}, u32[]{:S(2)}, u32[]{:S(2)}) %collective-permute-start) | collective-permute-done | bytes 2611232 | tf_op jit(solution)/shard_map/ppermute | solution.py:23
  61.1 2.7 %shard_map.48 = (f32[24,1408]{1,0:T(8,128)S(1)}, f32[24,1408]{1,0:T(8,128)S(1)}) custom-call(s32[6]{0:T(128)S(1)} %stack.37.where_ref, f32[8,48,1408]{2,1,0:T(8,128)S(1)} %shard_map.46.near_part_ref, bf16[16,272,300]{2,1,0:T(8,128)(2,1)} %collective-permute-done.far_ref), custom_call_target="tpu_custom_call" | custom-call | flops 81100800 | tf_op jit(solution)/shard_map/pallas_call | solution.py:216
  63.8 2.0 %collective-permute-start.1 = (f32[24,1408]{1,0:T(8,128)S(1)}, f32[24,1408]{1,0:T(8,128)S(1)}, u32[]{:S(2)}, u32[]{:S(2)}) collective-permute-start(f32[24,1408]{1,0:T(8,128)S(1)} %get-tuple-element.32), channel_id=1, source_target_pairs={{0,4},{4,8},{8,12},{12,16},{16,20},{20,24},{24,28},{28,0},{1,5},{5... | collective-permute-start | bytes 405512 | tf_op jit(solution)/shard_map/ppermute | solution.py:28
  66.0 1.6 copy-done.2
  67.6 3.4 %shard_map.47 = (f32[8,48,1408]{2,1,0:T(8,128)S(1)}, f32[48,1408]{1,0:T(8,128)S(1)}) custom-call(s32[6]{0:T(128)S(1)} %stack.37.where_ref, s32[8,2]{1,0:T(8,128)S(1)} %copy.11.pair_ref, f32[16]{0:T(128)S(1)} %copy-done.7, f32[1,1408]{1,0:T(1,128)S(1)} %broadcast_in_dim.4.vir_ref, f32[8,48,1408]{2,1,0:T(8,128)S(1)} %copy-done.2, ...), custom_call_target="tpu_custom_call" | custom-call | flops 648806400 | tf_op jit(solution)/shard_map/pallas_call | solution.py:225
  71.9 3.2 %collective-permute-start.3 = (f32[48,1408]{1,0:T(8,128)S(1)}, f32[48,1408]{1,0:T(8,128)S(1)}, u32[]{:S(2)}, u32[]{:S(2)}) collective-permute-start(f32[48,1408]{1,0:T(8,128)S(1)} %get-tuple-element.34), channel_id=1, source_target_pairs={{0,4},{4,8},{8,12},{12,16},{16,20},{20,24},{24,28},{28,0},{1,5},{5... | collective-permute-start | bytes 811016 | tf_op jit(solution)/shard_map/ppermute | solution.py:28
  75.8 6.4 %collective-permute-done.3.up_in = f32[48,1408]{1,0:T(8,128)S(1)} collective-permute-done((f32[48,1408]{1,0:T(8,128)S(1)}, f32[48,1408]{1,0:T(8,128)S(1)}, u32[]{:S(2)}, u32[]{:S(2)}) %collective-permute-start.3) | collective-permute-done | bytes 270368 | tf_op jit(solution)/shard_map/ppermute | solution.py:28
  84.1 2.5 %collective-permute-start.5 = (f32[48,1408]{1,0:T(8,128)S(1)}, f32[48,1408]{1,0:T(8,128)S(1)}, u32[]{:S(2)}, u32[]{:S(2)}) collective-permute-start(f32[48,1408]{1,0:T(8,128)S(1)} %get-tuple-element.36), channel_id=1, source_target_pairs={{0,4},{4,8},{8,12},{12,16},{16,20},{20,24},{24,28},{28,0},{1,5},{5... | collective-permute-start | bytes 811016 | tf_op jit(solution)/shard_map/ppermute | solution.py:28
  86.5 5.0 %collective-permute-done.5.up_in = f32[48,1408]{1,0:T(8,128)S(1)} collective-permute-done((f32[48,1408]{1,0:T(8,128)S(1)}, f32[48,1408]{1,0:T(8,128)S(1)}, u32[]{:S(2)}, u32[]{:S(2)}) %collective-permute-start.5) | collective-permute-done | bytes 270368 | tf_op jit(solution)/shard_map/ppermute | solution.py:28
  91.5 2.7 %collective-permute-done.6.down_in = f32[48,1408]{1,0:T(8,128)S(1)} collective-permute-done((f32[48,1408]{1,0:T(8,128)S(1)}, f32[48,1408]{1,0:T(8,128)S(1)}, u32[]{:S(2)}, u32[]{:S(2)}) %collective-permute-start.6) | collective-permute-done | bytes 270368 | tf_op jit(solution)/shard_map/ppermute | solution.py:28
  94.8 1.8 %collective-permute-start.7 = (f32[48,1408]{1,0:T(8,128)S(1)}, f32[48,1408]{1,0:T(8,128)S(1)}, u32[]{:S(2)}, u32[]{:S(2)}) collective-permute-start(f32[48,1408]{1,0:T(8,128)S(1)} %get-tuple-element.38), channel_id=1, source_target_pairs={{0,4},{4,8},{8,12},{12,16},{16,20},{20,24},{24,28},{28,0},{1,5},{5... | collective-permute-start | bytes 811016 | tf_op jit(solution)/shard_map/ppermute | solution.py:28
  96.9 4.4 %collective-permute-done.7.up_in = f32[48,1408]{1,0:T(8,128)S(1)} collective-permute-done((f32[48,1408]{1,0:T(8,128)S(1)}, f32[48,1408]{1,0:T(8,128)S(1)}, u32[]{:S(2)}, u32[]{:S(2)}) %collective-permute-start.7) | collective-permute-done | bytes 270368 | tf_op jit(solution)/shard_map/ppermute | solution.py:28
  101.4 1.7 %collective-permute-done.8.down_in = f32[48,1408]{1,0:T(8,128)S(1)} collective-permute-done((f32[48,1408]{1,0:T(8,128)S(1)}, f32[48,1408]{1,0:T(8,128)S(1)}, u32[]{:S(2)}, u32[]{:S(2)}) %collective-permute-start.8) | collective-permute-done | bytes 270368 | tf_op jit(solution)/shard_map/ppermute | solution.py:28
  103.7 1.7 collective-permute-start.9
  105.4 6.4 %collective-permute-done.9 = f32[48,1408]{1,0:T(8,128)S(1)} collective-permute-done((f32[48,1408]{1,0:T(8,128)S(1)}, f32[48,1408]{1,0:T(8,128)S(1)}, u32[]{:S(2)}, u32[]{:S(2)}) %collective-permute-start.9) | collective-permute-done | bytes 270368 | tf_op jit(solution)/shard_map/ppermute | solution.py:23
  112.2 1.8 %collective-permute-start.10 = (bf16[2,48,1408]{2,1,0:T(8,128)(2,1)S(1)}, bf16[2,48,1408]{2,1,0:T(8,128)(2,1)}, u32[]{:S(2)}, u32[]{:S(2)}) collective-permute-start(bf16[2,48,1408]{2,1,0:T(8,128)(2,1)S(1)} %get-tuple-element.57), channel_id=1, source_target_pairs={{0,4},{4,8},{8,12},{12,16},{16,20},{20,24},{24,28},{28,0},{1,5},{5... | collective-permute-start | bytes 811016 | tf_op jit(solution)/shard_map/ppermute | solution.py:28
  114.3 2.3 %shard_map.53 = f32[8,2,48,96]{3,2,1,0:T(8,128)} custom-call(s32[6]{0:T(128)S(1)} %stack.37.where_ref, f32[96,1408]{1,0:T(8,128)S(1)} %bitcast.38, f32[96,1408]{1,0:T(8,128)S(1)} %collective-permute-done.12.far_ref), custom_call_target="tpu_custom_call" | custom-call | flops 77856768 | bytes 1081344 | tf_op jit(solution)/shard_map/pallas_call | solution.py:257
  116.5 4.6 %collective-permute-done.10 = bf16[2,48,1408]{2,1,0:T(8,128)(2,1)} collective-permute-done((bf16[2,48,1408]{2,1,0:T(8,128)(2,1)S(1)}, bf16[2,48,1408]{2,1,0:T(8,128)(2,1)}, u32[]{:S(2)}, u32[]{:S(2)}) %collective-permute-start.10) | collective-permute-done | bytes 270368 | tf_op jit(solution)/shard_map/ppermute | solution.py:28
  121.2 1.5 collective-permute-done.11
  122.6 1.5 collective-permute-start.13
  124.7 6.1 %all-to-all-start.1 = ((f32[8,2,48,96]{3,2,1,0:T(8,128)}), f32[8,2,48,96]{3,2,1,0:T(8,128)S(1)}, u32[]{:S(2)}, u32[]{:S(2)}) async-start(f32[8,2,48,96]{3,2,1,0:T(8,128)} %shard_map.53), calls=%async_computation.1 | async-start | bytes 786432 | tf_op jit(solution)/shard_map/all_to_all | solution.py:266
  130.8 1.5 collective-permute-start.14
  133.3 11.8 %collective-permute-done.14 = bf16[2,48,1408]{2,1,0:T(8,128)(2,1)S(1)} collective-permute-done((bf16[2,48,1408]{2,1,0:T(8,128)(2,1)}, bf16[2,48,1408]{2,1,0:T(8,128)(2,1)S(1)}, u32[]{:S(2)}, u32[]{:S(2)}) %collective-permute-start.14) | collective-permute-done | bytes 270368 | tf_op jit(solution)/shard_map/ppermute | solution.py:28
  148.8 1.6 collective-permute-start.17
  152.1 3.5 %shard_map.54 = (f32[48,1408]{1,0:T(8,128)S(1)}, f32[8,48,176]{2,1,0:T(8,128)S(1)}, bf16[48,1408]{1,0:T(8,128)(2,1)S(1)}, bf16[8,2,48,96]{3,2,1,0:T(8,128)(2,1)S(1)}) custom-call(s32[6]{0:T(128)S(1)} %stack.37.where_ref, f32[48,1408]{1,0:T(8,128)S(1)} %shard_map.52.rows_ref, f32[8,2,48,96]{3,2,1,0:T(8,128)S(1)} %all-to-all-done.1.turned_ref, ...), custom_call_target="tpu_custom_call" | custom-call | flops 129761280 | bytes 2703360 | tf_op jit(solution)/shard_map/pallas_call | solution.py:284
  155.6 1.4 collective-permute-done.18.refs_5_
  158.6 1.6 shard_map.55
  160.1 11.7 %all_to_all.16 = f32[8,48,176]{2,1,0:T(8,128)S(1)} all-to-all(f32[8,48,176]{2,1,0:T(8,128)S(1)} %shard_map.55), channel_id=1, replica_groups=mesh['x'=4,'yl'=2,'z'=8,'yh'=2,'c'=2] {'x','yl'}, dimensions={0} | all-to-all | bytes 540672 | tf_op jit(solution)/shard_map/all_to_all | solution.py:306
  (77 shorter events, 18.3 us)
Async XLA Ops:
  54.8 6.3 %collective-permute-start = (bf16[16,272,300]{2,1,0:T(8,128)(2,1)}, bf16[16,272,300]{2,1,0:T(8,128)(2,1)}, u32[]{:S(2)}, u32[]{:S(2)}) collective-permute-start(bf16[16,272,300]{2,1,0:T(8,128)(2,1)} %all_to_all.15.near_ref), channel_id=1, source_target_pairs={{0,1},{1,0},{2,3},{3,2},{4,5},{5,4},{6,7},{7,6},{8,9},{9,8},{10,11... | collective-permute-start | bytes 7833608 | tf_op jit(solution)/shard_map/ppermute | solution.py:23
  58.3 7.7 %copy-start.9 = (f32[1408]{0:T(1024)S(1)}, f32[1408]{0:T(1024)}, u32[]{:S(2)}) copy-start(f32[1408]{0:T(1024)} %param.7) | copy-start | bytes 16900
  63.8 7.2 %collective-permute-start.1 = (f32[24,1408]{1,0:T(8,128)S(1)}, f32[24,1408]{1,0:T(8,128)S(1)}, u32[]{:S(2)}, u32[]{:S(2)}) collective-permute-start(f32[24,1408]{1,0:T(8,128)S(1)} %get-tuple-element.32), channel_id=1, source_target_pairs={{0,4},{4,8},{8,12},{12,16},{16,20},{20,24},{24,28},{28,0},{1,5},{5... | collective-permute-start | bytes 405512 | tf_op jit(solution)/shard_map/ppermute | solution.py:28
  65.8 5.5 %collective-permute-start.2 = (f32[24,1408]{1,0:T(8,128)S(1)}, f32[24,1408]{1,0:T(8,128)S(1)}, u32[]{:S(2)}, u32[]{:S(2)}) collective-permute-start(f32[24,1408]{1,0:T(8,128)S(1)} %get-tuple-element.33), channel_id=1, source_target_pairs={{0,28},{4,0},{8,4},{12,8},{16,12},{20,16},{24,20},{28,24},{1,29},{... | collective-permute-start | bytes 405512 | tf_op jit(solution)/shard_map/ppermute | solution.py:28
  71.9 10.3 %collective-permute-start.3 = (f32[48,1408]{1,0:T(8,128)S(1)}, f32[48,1408]{1,0:T(8,128)S(1)}, u32[]{:S(2)}, u32[]{:S(2)}) collective-permute-start(f32[48,1408]{1,0:T(8,128)S(1)} %get-tuple-element.34), channel_id=1, source_target_pairs={{0,4},{4,8},{8,12},{12,16},{16,20},{20,24},{24,28},{28,0},{1,5},{5... | collective-permute-start | bytes 811016 | tf_op jit(solution)/shard_map/ppermute | solution.py:28
  75.2 8.3 %collective-permute-start.4 = (f32[48,1408]{1,0:T(8,128)S(1)}, f32[48,1408]{1,0:T(8,128)S(1)}, u32[]{:S(2)}, u32[]{:S(2)}) collective-permute-start(f32[48,1408]{1,0:T(8,128)S(1)} %get-tuple-element.35), channel_id=1, source_target_pairs={{0,28},{4,0},{8,4},{12,8},{16,12},{20,16},{24,20},{28,24},{1,29},{... | collective-permute-start | bytes 811016 | tf_op jit(solution)/shard_map/ppermute | solution.py:28
  84.1 7.5 %collective-permute-start.5 = (f32[48,1408]{1,0:T(8,128)S(1)}, f32[48,1408]{1,0:T(8,128)S(1)}, u32[]{:S(2)}, u32[]{:S(2)}) collective-permute-start(f32[48,1408]{1,0:T(8,128)S(1)} %get-tuple-element.36), channel_id=1, source_target_pairs={{0,4},{4,8},{8,12},{12,16},{16,20},{20,24},{24,28},{28,0},{1,5},{5... | collective-permute-start | bytes 811016 | tf_op jit(solution)/shard_map/ppermute | solution.py:28
  86.5 7.7 %collective-permute-start.6 = (f32[48,1408]{1,0:T(8,128)S(1)}, f32[48,1408]{1,0:T(8,128)S(1)}, u32[]{:S(2)}, u32[]{:S(2)}) collective-permute-start(f32[48,1408]{1,0:T(8,128)S(1)} %get-tuple-element.37), channel_id=1, source_target_pairs={{0,28},{4,0},{8,4},{12,8},{16,12},{20,16},{24,20},{28,24},{1,29},{... | collective-permute-start | bytes 811016 | tf_op jit(solution)/shard_map/ppermute | solution.py:28
  94.8 6.5 %collective-permute-start.7 = (f32[48,1408]{1,0:T(8,128)S(1)}, f32[48,1408]{1,0:T(8,128)S(1)}, u32[]{:S(2)}, u32[]{:S(2)}) collective-permute-start(f32[48,1408]{1,0:T(8,128)S(1)} %get-tuple-element.38), channel_id=1, source_target_pairs={{0,4},{4,8},{8,12},{12,16},{16,20},{20,24},{24,28},{28,0},{1,5},{5... | collective-permute-start | bytes 811016 | tf_op jit(solution)/shard_map/ppermute | solution.py:28
  96.7 6.5 %collective-permute-start.8 = (f32[48,1408]{1,0:T(8,128)S(1)}, f32[48,1408]{1,0:T(8,128)S(1)}, u32[]{:S(2)}, u32[]{:S(2)}) collective-permute-start(f32[48,1408]{1,0:T(8,128)S(1)} %get-tuple-element.39), channel_id=1, source_target_pairs={{0,28},{4,0},{8,4},{12,8},{16,12},{20,16},{24,20},{28,24},{1,29},{... | collective-permute-start | bytes 811016 | tf_op jit(solution)/shard_map/ppermute | solution.py:28
  103.7 8.1 %collective-permute-start.9 = (f32[48,1408]{1,0:T(8,128)S(1)}, f32[48,1408]{1,0:T(8,128)S(1)}, u32[]{:S(2)}, u32[]{:S(2)}) collective-permute-start(f32[48,1408]{1,0:T(8,128)S(1)} %shard_map.52.rows_ref), channel_id=1, source_target_pairs={{0,2},{2,0},{1,3},{3,1},{4,6},{6,4},{5,7},{7,5},{8,10},{10,8},{9,1... | collective-permute-start | bytes 811016 | tf_op jit(solution)/shard_map/ppermute | solution.py:23
  111.9 2.4 %collective-permute-start.12 = (f32[96,1408]{1,0:T(8,128)S(1)}, f32[96,1408]{1,0:T(8,128)S(1)}, u32[]{:S(2)}, u32[]{:S(2)}) collective-permute-start(f32[96,1408]{1,0:T(8,128)S(1)} %bitcast.37), channel_id=1, source_target_pairs={{0,1},{1,0},{2,3},{3,2},{4,5},{5,4},{6,7},{7,6},{8,9},{9,8},{10,11... | collective-permute-start | bytes 1622024 | tf_op jit(solution)/shard_map/ppermute | solution.py:23
  112.2 9.0 %collective-permute-start.10 = (bf16[2,48,1408]{2,1,0:T(8,128)(2,1)S(1)}, bf16[2,48,1408]{2,1,0:T(8,128)(2,1)}, u32[]{:S(2)}, u32[]{:S(2)}) collective-permute-start(bf16[2,48,1408]{2,1,0:T(8,128)(2,1)S(1)} %get-tuple-element.57), channel_id=1, source_target_pairs={{0,4},{4,8},{8,12},{12,16},{16,20},{20,24},{24,28},{28,0},{1,5},{5... | collective-permute-start | bytes 811016 | tf_op jit(solution)/shard_map/ppermute | solution.py:28
  114.0 8.6 %collective-permute-start.11 = (bf16[2,48,1408]{2,1,0:T(8,128)(2,1)S(1)}, bf16[2,48,1408]{2,1,0:T(8,128)(2,1)}, u32[]{:S(2)}, u32[]{:S(2)}) collective-permute-start(bf16[2,48,1408]{2,1,0:T(8,128)(2,1)S(1)} %get-tuple-element.57), channel_id=1, source_target_pairs={{0,28},{4,0},{8,4},{12,8},{16,12},{20,16},{24,20},{28,24},{1,29},{... | collective-permute-start | bytes 811016 | tf_op jit(solution)/shard_map/ppermute | solution.py:28
  122.6 8.1 %collective-permute-start.13 = (bf16[2,48,1408]{2,1,0:T(8,128)(2,1)}, bf16[2,48,1408]{2,1,0:T(8,128)(2,1)}, u32[]{:S(2)}, u32[]{:S(2)}) collective-permute-start(bf16[2,48,1408]{2,1,0:T(8,128)(2,1)} %collective-permute-done.10), channel_id=1, source_target_pairs={{0,4},{4,8},{8,12},{12,16},{16,20},{20,24},{24,28},{28,0},{1,5},{5... | collective-permute-start | bytes 811016 | tf_op jit(solution)/shard_map/ppermute | solution.py:28
  124.2 8.1 %collective-permute-start.15 = (bf16[2,48,1408]{2,1,0:T(8,128)(2,1)}, bf16[2,48,1408]{2,1,0:T(8,128)(2,1)}, u32[]{:S(2)}, u32[]{:S(2)}) collective-permute-start(bf16[2,48,1408]{2,1,0:T(8,128)(2,1)} %collective-permute-done.11), channel_id=1, source_target_pairs={{0,28},{4,0},{8,4},{12,8},{16,12},{20,16},{24,20},{28,24},{1,29},{... | collective-permute-start | bytes 811016 | tf_op jit(solution)/shard_map/ppermute | solution.py:28
  124.7 22.3 %all-to-all-start.1 = ((f32[8,2,48,96]{3,2,1,0:T(8,128)}), f32[8,2,48,96]{3,2,1,0:T(8,128)S(1)}, u32[]{:S(2)}, u32[]{:S(2)}) async-start(f32[8,2,48,96]{3,2,1,0:T(8,128)} %shard_map.53), calls=%async_computation.1 | async-start | bytes 786432 | tf_op jit(solution)/shard_map/all_to_all | solution.py:266
  130.8 14.3 %collective-permute-start.14 = (bf16[2,48,1408]{2,1,0:T(8,128)(2,1)}, bf16[2,48,1408]{2,1,0:T(8,128)(2,1)S(1)}, u32[]{:S(2)}, u32[]{:S(2)}) collective-permute-start(bf16[2,48,1408]{2,1,0:T(8,128)(2,1)} %collective-permute-done.13), channel_id=1, source_target_pairs={{0,4},{4,8},{8,12},{12,16},{16,20},{20,24},{24,28},{28,0},{1,5},{5... | collective-permute-start | bytes 811016 | tf_op jit(solution)/shard_map/ppermute | solution.py:28
  132.2 14.0 %collective-permute-start.16 = (bf16[2,48,1408]{2,1,0:T(8,128)(2,1)}, bf16[2,48,1408]{2,1,0:T(8,128)(2,1)S(1)}, u32[]{:S(2)}, u32[]{:S(2)}) collective-permute-start(bf16[2,48,1408]{2,1,0:T(8,128)(2,1)} %collective-permute-done.15), channel_id=1, source_target_pairs={{0,28},{4,0},{8,4},{12,8},{16,12},{20,16},{24,20},{28,24},{1,29},{... | collective-permute-start | bytes 811016 | tf_op jit(solution)/shard_map/ppermute | solution.py:28
  132.8 16.0 %collective-permute-start.19 = (bf16[2,48,1408]{2,1,0:T(8,128)(2,1)}, bf16[2,48,1408]{2,1,0:T(8,128)(2,1)}, u32[]{:S(2)}, u32[]{:S(2)}) collective-permute-start(bf16[2,48,1408]{2,1,0:T(8,128)(2,1)} %copy-done.8), channel_id=1, source_target_pairs={{0,1},{1,0},{2,3},{3,2},{4,5},{5,4},{6,7},{7,6},{8,9},{9,8},{10,11... | collective-permute-start | bytes 811016 | tf_op jit(solution)/shard_map/ppermute | solution.py:23
  132.8 17.6 %collective-permute-start.20 = (bf16[2,48,1408]{2,1,0:T(8,128)(2,1)}, bf16[2,48,1408]{2,1,0:T(8,128)(2,1)}, u32[]{:S(2)}, u32[]{:S(2)}) collective-permute-start(bf16[2,48,1408]{2,1,0:T(8,128)(2,1)} %collective-permute-done.11), channel_id=1, source_target_pairs={{0,1},{1,0},{2,3},{3,2},{4,5},{5,4},{6,7},{7,6},{8,9},{9,8},{10,11... | collective-permute-start | bytes 811016 | tf_op jit(solution)/shard_map/ppermute | solution.py:23
  133.3 18.1 %collective-permute-start.21 = (bf16[2,48,1408]{2,1,0:T(8,128)(2,1)}, bf16[2,48,1408]{2,1,0:T(8,128)(2,1)}, u32[]{:S(2)}, u32[]{:S(2)}) collective-permute-start(bf16[2,48,1408]{2,1,0:T(8,128)(2,1)} %collective-permute-done.10), channel_id=1, source_target_pairs={{0,1},{1,0},{2,3},{3,2},{4,5},{5,4},{6,7},{7,6},{8,9},{9,8},{10,11... | collective-permute-start | bytes 811016 | tf_op jit(solution)/shard_map/ppermute | solution.py:23
  145.1 6.6 %collective-permute-start.22 = (bf16[2,48,1408]{2,1,0:T(8,128)(2,1)}, bf16[2,48,1408]{2,1,0:T(8,128)(2,1)}, u32[]{:S(2)}, u32[]{:S(2)}) collective-permute-start(bf16[2,48,1408]{2,1,0:T(8,128)(2,1)} %collective-permute-done.15), channel_id=1, source_target_pairs={{0,1},{1,0},{2,3},{3,2},{4,5},{5,4},{6,7},{7,6},{8,9},{9,8},{10,11... | collective-permute-start | bytes 811016 | tf_op jit(solution)/shard_map/ppermute | solution.py:23
  146.9 5.1 %collective-permute-start.23 = (bf16[2,48,1408]{2,1,0:T(8,128)(2,1)}, bf16[2,48,1408]{2,1,0:T(8,128)(2,1)}, u32[]{:S(2)}, u32[]{:S(2)}) collective-permute-start(bf16[2,48,1408]{2,1,0:T(8,128)(2,1)} %collective-permute-done.13), channel_id=1, source_target_pairs={{0,1},{1,0},{2,3},{3,2},{4,5},{5,4},{6,7},{7,6},{8,9},{9,8},{10,11... | collective-permute-start | bytes 811016 | tf_op jit(solution)/shard_map/ppermute | solution.py:23
  148.8 9.8 %copy-start.4 = (bf16[2,48,1408]{2,1,0:T(8,128)(2,1)S(1)}, bf16[2,48,1408]{2,1,0:T(8,128)(2,1)}, u32[]{:S(2)}) copy-start(bf16[2,48,1408]{2,1,0:T(8,128)(2,1)} %copy-done.3) | copy-start | bytes 811012
  148.8 9.8 %copy-start.6 = (bf16[2,48,1408]{2,1,0:T(8,128)(2,1)S(1)}, bf16[2,48,1408]{2,1,0:T(8,128)(2,1)}, u32[]{:S(2)}) copy-start(bf16[2,48,1408]{2,1,0:T(8,128)(2,1)} %copy-done.5) | copy-start | bytes 811012
  148.8 6.8 %collective-permute-start.17 = (bf16[48,1408]{1,0:T(8,128)(2,1)S(1)}, bf16[48,1408]{1,0:T(8,128)(2,1)S(1)}, u32[]{:S(2)}, u32[]{:S(2)}) collective-permute-start(bf16[48,1408]{1,0:T(8,128)(2,1)S(1)} %slice_bitcast_fusion.1), channel_id=1, source_target_pairs={{0,4},{4,8},{8,12},{12,16},{16,20},{20,24},{24,28},{28,0},{1,5},{5... | collective-permute-start | bytes 405512 | tf_op jit(solution)/shard_map/ppermute | solution.py:28
  150.4 6.6 %collective-permute-start.18 = (bf16[48,1408]{1,0:T(8,128)(2,1)S(1)}, bf16[48,1408]{1,0:T(8,128)(2,1)S(1)}, u32[]{:S(2)}, u32[]{:S(2)}) collective-permute-start(bf16[48,1408]{1,0:T(8,128)(2,1)S(1)} %slice_bitcast_fusion), channel_id=1, source_target_pairs={{0,28},{4,0},{8,4},{12,8},{16,12},{20,16},{24,20},{28,24},{1,29},{... | collective-permute-start | bytes 405512 | tf_op jit(solution)/shard_map/ppermute | solution.py:28
  151.5 7.1 %collective-permute-start.24 = (bf16[2,48,1408]{2,1,0:T(8,128)(2,1)}, bf16[2,48,1408]{2,1,0:T(8,128)(2,1)S(1)}, u32[]{:S(2)}, u32[]{:S(2)}) collective-permute-start(bf16[2,48,1408]{2,1,0:T(8,128)(2,1)} %copy-done.5), channel_id=1, source_target_pairs={{0,1},{1,0},{2,3},{3,2},{4,5},{5,4},{6,7},{7,6},{8,9},{9,8},{10,11... | collective-permute-start | bytes 811016 | tf_op jit(solution)/shard_map/ppermute | solution.py:23
  151.7 6.9 %collective-permute-start.25 = (bf16[2,48,1408]{2,1,0:T(8,128)(2,1)}, bf16[2,48,1408]{2,1,0:T(8,128)(2,1)S(1)}, u32[]{:S(2)}, u32[]{:S(2)}) collective-permute-start(bf16[2,48,1408]{2,1,0:T(8,128)(2,1)} %copy-done.3), channel_id=1, source_target_pairs={{0,1},{1,0},{2,3},{3,2},{4,5},{5,4},{6,7},{7,6},{8,9},{9,8},{10,11... | collective-permute-start | bytes 811016 | tf_op jit(solution)/shard_map/ppermute | solution.py:23
  157.0 1.4 collective-permute-start.26
  157.0 1.5 collective-permute-start.27
  (8 other events, 30.7 us)

commit v4 on v3

--- a/solution.py
+++ b/solution.py
@@ -30,13 +30,6 @@
 
 def dot_nt(a, b):
     return lax.dot_general(a, b, (((1,), (1,)), ((), ())), preferred_element_type=F32)
-
-
-def split3(value):
-    high = value.astype(BF16)
-    rest = value - high.astype(F32)
-    middle = rest.astype(BF16)
-    return high, middle, (rest - middle.astype(F32)).astype(BF16)
 
 
 def cost(flops, moved):
@@ -104,76 +97,98 @@
         down_ref[: rows - taken] = part_ref[below, : rows - taken]
 
 
-def amplitude_kernel(where_ref, part_ref, up_in, down_in, denom_ref, out_ref):
-    out_ref[...] = (part_ref[where_ref[0]] + (up_in[...] + down_in[...])) / denom_ref[...]
-
-
-def turn_kernel(nz, width, padded, where_ref, near_ref, far_ref, out_ref):
-    part = where_ref[4]
-    nvir = near_ref.shape[1]
-    slab = nvir // nz
-    column = lax.broadcasted_iota(jnp.int32, (padded, slab), 1)
-    row = lax.broadcasted_iota(jnp.int32, (padded, slab), 0)
-    pick = jnp.where((column == part * width + row) & (row < width), 1.0, 0.0).astype(BF16)
-    for slot, ref in enumerate((near_ref, far_ref)):
-        for k in range(nz):
-            high, middle, low = split3(ref[:, k * slab : (k + 1) * slab])
-            out_ref[k, slot] = dot_nt(pick, high) + (dot_nt(pick, middle) + dot_nt(pick, low))
+def amplitude_kernel(where_ref, part_ref, up_in, down_in, denom_ref, out_ref, rounded_ref, blocks_ref):
+    amps = (part_ref[where_ref[0]] + (up_in[...] + down_in[...])) / denom_ref[...]
+    out_ref[...] = amps
+    rounded_ref[...] = amps.astype(BF16)
+    slab = blocks_ref.shape[2]
+    for k in range(blocks_ref.shape[0]):
+        blocks_ref[k] = amps[:, k * slab : (k + 1) * slab]
+
+
+def outward_kernel(where_ref, columns_ref, out_ref):
+    half = columns_ref.shape[2] // 2
+    for k in range(columns_ref.shape[0]):
+        columns = columns_ref[k]
+        out_ref[k] = jnp.where(where_ref[6] == 0, columns[:, half:], columns[:, :half])
+
+
+def inward_kernel(where_ref, columns_ref, other_ref, keep_ref, send_ref):
+    c, yh = where_ref[1], where_ref[6]
+    half = columns_ref.shape[2] // 2
+    width = half // 2
+    gap = jnp.zeros((columns_ref.shape[1], keep_ref.shape[2] // 2 - width), F32)
+    for k in range(columns_ref.shape[0]):
+        columns = columns_ref[k]
+        own = jnp.where(yh == 0, columns[:, :half], columns[:, half:])
+        other = other_ref[k]
+        sides = []
+        for h in range(2):
+            at = h * width
+            sides.append(jnp.concatenate([own[:, at : at + width], gap, other[:, at : at + width], gap], axis=1))
+        keep_ref[k] = jnp.where(c == 0, sides[0], sides[1])
+        send_ref[k] = jnp.where(c == 0, sides[1], sides[0])
+
+
+def natural(c, yh, near, far, width, padded):
+    parts = []
+    for y in range(2):
+        for h in range(2):
+            side = jnp.where(c == h, near, far)
+            parts.append(jnp.where(yh == y, side[:, :width], side[:, padded : padded + width]))
+    return jnp.concatenate(parts, axis=1)
+
+
+def relative(c, yh, block, width, padded):
+    gap = jnp.zeros((block.shape[0], padded - width), block.dtype)
+    sides = []
+    for h in range(2):
+        first, second = block[:, h * width : (h + 1) * width], block[:, (2 + h) * width : (3 + h) * width]
+        own, other = jnp.where(yh == 0, first, second), jnp.where(yh == 0, second, first)
+        sides.append(jnp.concatenate([own, gap, other, gap], axis=1))
+    return jnp.where(c == 0, sides[0], sides[1]), jnp.where(c == 0, sides[1], sides[0])
 
 
 def density_pieces(steps, nz, width, padded, where_ref, tilde, tilde_t_ref, pieces, total, blocks_ref):
-    z, c = where_ref[0], where_ref[1]
+    z, c, yh = where_ref[0], where_ref[1], where_ref[6]
     for n, r in enumerate(steps):
         at = lax.rem(z + r, nz)
         sides = []
         for slot in range(2):
-            piece = pieces[2 * n + slot]
-            piece = jnp.concatenate([ref[...] for ref in piece], axis=0) if isinstance(piece, tuple) else piece[...]
+            first, second = pieces[4 * n + 2 * slot], pieces[4 * n + 2 * slot + 1]
+            piece = jnp.concatenate([first[...], second[...]], axis=0)
             term = jnp.dot(tilde_t_ref[at, slot], piece, preferred_element_type=F32)
             total = term if total is None else total + term
             sides.append(dot_nt(tilde, piece))
-        blocks_ref[at] = join(c, sides[0], sides[1], width, padded)
+        blocks_ref[at] = natural(c, yh, sides[0], sides[1], width, padded)
     return total
 
 
-def join(c, near, far, width, padded):
-    first, second = jnp.where(c == 0, near, far), jnp.where(c == 0, far, near)
-    parts = []
-    for y in range(2):
-        for piece in (first, second):
-            parts.append(piece[:, y * padded : y * padded + width])
-    return jnp.concatenate(parts, axis=1)
-
-
-def early_kernel(steps, nz, width, padded, where_ref, rows_ref, turned_ref, *refs):
-    pieces = refs[: 2 * len(steps)]
-    total_ref, blocks_ref, tilde_ref, tilde_t_ref = refs[2 * len(steps) :]
-    c = where_ref[1]
+def turn(block, padded):
+    flipped = block.T
+    return jnp.concatenate([flipped[:padded], flipped[padded:]], axis=1)
+
+
+def early_kernel(steps, nz, width, padded, where_ref, rows_ref, near_ref, far_ref, *refs):
+    pieces = refs[: 4 * len(steps)]
+    total_ref, blocks_ref, tilde_ref, tilde_t_ref = refs[4 * len(steps) :]
+    c, yh = where_ref[1], where_ref[6]
     slab = rows_ref.shape[1] // nz
     rows = rows_ref[...]
-    zeros = jnp.zeros((padded, padded - width), F32)
     turned = []
     for k in range(nz):
-        mine = rows[:, k * slab : (k + 1) * slab]
-        halves = []
-        for h in range(2):
-            parts = []
-            for y in range(2):
-                at = (2 * y + h) * width
-                parts += [mine[:, at : at + width], zeros]
-            halves.append(jnp.concatenate(parts, axis=1))
-        near, far = turned_ref[k, 0], turned_ref[k, 1]
-        tilde_t_ref[k, 0] = (2.0 * near - jnp.where(c == 0, halves[0], halves[1])).astype(BF16)
-        tilde_t_ref[k, 1] = (2.0 * far - jnp.where(c == 0, halves[1], halves[0])).astype(BF16)
-        turned.append(join(c, near, far, width, padded))
+        near, far = turn(near_ref[k], padded), turn(far_ref[k], padded)
+        mine = relative(c, yh, rows[:, k * slab : (k + 1) * slab], width, padded)
+        tilde_t_ref[k, 0] = (2.0 * near - mine[0]).astype(BF16)
+        tilde_t_ref[k, 1] = (2.0 * far - mine[1]).astype(BF16)
+        turned.append(natural(c, yh, near, far, width, padded))
     tilde = (2.0 * rows - jnp.concatenate(turned, axis=1)).astype(BF16)
     tilde_ref[...] = tilde
     total_ref[...] = density_pieces(steps, nz, width, padded, where_ref, tilde, tilde_t_ref, pieces, None, blocks_ref)
 
 
 def late_kernel(steps, nz, width, padded, where_ref, total_ref, blocks_ref, tilde_ref, tilde_t_ref, *refs):
-    pieces, out_ref = list(refs[: 2 * len(steps) - 2]), refs[-1]
-    pieces += [refs[-5:-3], refs[-3:-1]]
+    pieces, out_ref = refs[:-1], refs[-1]
     slab = total_ref.shape[1] // nz
     for k in range(nz):
         out_ref[k] = blocks_ref[k]
@@ -191,7 +206,7 @@
     nz = lax.axis_size("z")
     width = slab // 4
     padded = (width + 8) // 8 * 8
-    where = jnp.stack([z, c, z * 4 + yh * 2 + c, lax.axis_index(SLABS), yh * 2 + c, jnp.int32(width)])
+    where = jnp.stack([z, c, z * 4 + yh * 2 + c, lax.axis_index(SLABS), yh * 2 + c, jnp.int32(width), yh])
 
     left = orbital_b[pair_list[:, 0]].reshape(8, 2, 2, width, naux)
     left = jnp.pad(left, ((0, 0), (0, 0), (0, 0), (0, padded - width), (0, 0)))
@@ -239,70 +254,69 @@
             compiler_params=params(8),
         )(where, part, up, down)
         up, down = shift(up, "z", 1), shift(down, "z", -1)
-    amp_rows = pl.pallas_call(
+    rows16 = jax.ShapeDtypeStruct((padded, nvir), BF16)
+    amp_rows, mine, columns = pl.pallas_call(
         amplitude_kernel,
-        out_shape=rows,
+        out_shape=(rows, rows16, jax.ShapeDtypeStruct((nz, padded, slab), F32)),
         in_specs=[SMEM, VMEM, VMEM, VMEM, VMEM],
+        out_specs=(VMEM,) * 3,
+        compiler_params=params(8),
+    )(where, part, up, down, denom)
+
+    mine = (mine, swap(mine, "yh"))
+    columns = lax.all_to_all(columns, "z", split_axis=0, concat_axis=0, tiled=True)
+    outward = pl.pallas_call(
+        outward_kernel,
+        out_shape=jax.ShapeDtypeStruct((nz, padded, slab // 2), F32),
+        in_specs=[SMEM, VMEM],
         out_specs=VMEM,
         compiler_params=params(8),
-    )(where, part, up, down, denom)
-
-    other = swap(amp_rows, "yh")
-    both = jnp.where(yh == 0, jnp.stack([amp_rows, other]), jnp.stack([other, amp_rows]))
-    both16 = both.astype(BF16)
-    ring = {0: both16}
-    up, down = shift(both16, "z", 1), shift(both16, "z", -1)
-
-    both = both.reshape(2 * padded, nvir)
-    turned = pl.pallas_call(
-        functools.partial(turn_kernel, nz, width, padded),
-        out_shape=jax.ShapeDtypeStruct((nz, 2, padded, 2 * padded), F32),
+    )(where, columns)
+    ring = {0: mine}
+    up = down = mine
+    for step in range(1, nz // 2 - 1):
+        up, down = tuple(shift(v, "z", 1) for v in up), tuple(shift(v, "z", -1) for v in down)
+        ring[nz - step], ring[step] = up, down
+    up, down, outward = lax.optimization_barrier((up, down, outward))
+    other = swap(outward, "yh")
+    kept, sent = pl.pallas_call(
+        inward_kernel,
+        out_shape=(jax.ShapeDtypeStruct((nz, padded, 2 * padded), F32),) * 2,
         in_specs=[SMEM, VMEM, VMEM],
-        out_specs=VMEM,
+        out_specs=(VMEM, VMEM),
         compiler_params=params(8),
-        cost_estimate=cost(6 * 4 * padded * padded * nvir, 4 * 4 * padded * nvir),
-    )(where, both, swap(both, "c"))
-    up, down, turned = lax.optimization_barrier((up, down, turned))
-    turned = lax.all_to_all(turned, "z", split_axis=0, concat_axis=0, tiled=True)
-    for step in range(1, nz // 2):
-        ring[nz - step] = up
-        ring[step] = down
-        if step == nz // 2 - 1:
-            up, down, turned = lax.optimization_barrier((up, down, turned))
-            up, down = shift(up[0], "z", 1), shift(down[1], "z", -1)
-        else:
-            up, down = shift(up, "z", 1), shift(down, "z", -1)
-
-    def gathered(steps):
-        pieces = []
-        for r in steps:
-            pieces += [ring[r].reshape(2 * padded, nvir), swap(ring[r], "c").reshape(2 * padded, nvir)]
-        return pieces
+    )(where, columns, other)
+    taken = swap(sent, "c")
+    last = (tuple(shift(v, "z", -1) for v in down), tuple(shift(v, "z", 1) for v in up))
+    last += ((shift(up[0], "z", 2), shift(down[1], "z", -2)),)
+
+    def crossed(pieces):
+        return [v for piece in pieces for v in (*piece, *(swap(v, "c") for v in piece))]
 
     soon = (0, 1, nz - 1, 2, nz - 2)
-    late = (3, nz - 3)
+    late = (3, nz - 3, nz // 2)
     state = pl.pallas_call(
         functools.partial(early_kernel, soon, nz, width, padded),
         out_shape=(
-            jax.ShapeDtypeStruct((padded, nvir), F32),
+            rows,
             jax.ShapeDtypeStruct((nz, padded, slab), F32),
-            jax.ShapeDtypeStruct((padded, nvir), BF16),
+            rows16,
             jax.ShapeDtypeStruct((nz, 2, padded, 2 * padded), BF16),
         ),
-        in_specs=[SMEM] + [VMEM] * (2 + 2 * len(soon)),
+        in_specs=[SMEM] + [VMEM] * (3 + 4 * len(soon)),
         out_specs=(VMEM,) * 4,
         compiler_params=params(16),
         cost_estimate=cost(len(soon) * 8 * padded * padded * nvir, len(soon) * 8 * padded * nvir),
-    )(where, amp_rows, turned, *gathered(soon))
-    up, down, state = lax.optimization_barrier((up, down, state))
+    )(where, amp_rows, kept, taken, *crossed(ring[r] for r in soon))
+    last, state = lax.optimization_barrier((last, state))
     added = pl.pallas_call(
-        functools.partial(late_kernel, (*late, nz // 2), nz, width, padded),
+        functools.partial(late_kernel, late, nz, width, padded),
         out_shape=jax.ShapeDtypeStruct((nz, padded, slab), F32),
-        in_specs=[SMEM] + [VMEM] * (8 + 2 * len(late)),
+        in_specs=[SMEM] + [VMEM] * (4 + 4 * len(late)),
         out_specs=VMEM,
         compiler_params=params(16),
         cost_estimate=cost(len(late) * 8 * padded * padded * nvir, len(late) * 8 * padded * nvir),
-    )(where, *state, *gathered(late), up, down, swap(up, "c"), swap(down, "c"))
+    )(where, *state, *crossed(last))
     added = lax.all_to_all(added, SLABS, split_axis=0, concat_axis=0, tiled=True)
     return jnp.sum(added, axis=0)[:width]
 

time: 175 us -> 179 us (1.023)
  starting transfers between devices: 29 us -> 47.7 us
  waiting for transfers between devices: 52.6 us -> 39.7 us
  local copies, waits for them, and re-layouts: 9.54 us -> 7.01 us
    ppermute x16 -> x22, starting transfers between devices: 19.4 us -> 34.7 us  [shift(): lax.ppermute(value, axis, [(i, (i + step) % size) for i in range(size)])]
    ppermute x16 -> x22, waiting for transfers between devices: 42.3 us -> 28 us  [shift(): lax.ppermute(value, axis, [(i, (i + step) % size) for i in range(size)])]
    ppermute x12 -> x20, starting transfers between devices: 3.52 us -> 7.47 us  [swap(): return lax.ppermute(value, axis, [(0, 1), (1, 0)])]
    squeeze x2 -> x0, local copies, waits for them, and re-layouts: 1.84 us -> none  [local(): up, down = (shift(up[0], 'z', 1), shift(down[1], 'z', -1))]
    ppermute x12 -> x20, waiting for transfers between devices: 10.2 us -> 11.7 us  [swap(): return lax.ppermute(value, axis, [(0, 1), (1, 0)])]
    pallas_call x3 -> x4, Pallas kernels: 4.44 us -> 5.13 us  [the longest x1 1.63 us: local(): pl.pallas_call(functools.partial(late_kernel, late, nz, width, padded), o...]
  transfers between devices with their start and end apart: 29 -> 43, of which waited for: 17 -> 20; matrix products, arithmetic and copies ran while one was open for 1% -> 0% of each run, Pallas kernels for 7% -> 7%
where the time goes in v4:
time: 179 us; the launch traced here: 177 us
  blocking collectives  59.9 us (33%)
  starting transfers between devices  47.7 us (27%)
  waiting for transfers between devices  39.7 us (22%)
  Pallas kernels  20.2 us (11%)
  local copies, waits for them, and re-layouts  7.01 us (4%)
  other arithmetic  1.87 us (1%)
    all_to_all x1, blocking collectives, local(): lax.all_to_all(outgoing, ('yh', 'x', 'yl'), split_axis=0, concat_axis=0,...  48.4 us
    ppermute x22, starting transfers between devices, shift(): lax.ppermute(value, axis, [(i, (i + step) % size) for i in range(size)])  34.7 us
    ppermute x22, waiting for transfers between devices, shift(): lax.ppermute(value, axis, [(i, (i + step) % size) for i in range(size)])  28 us
    ppermute x20, waiting for transfers between devices, swap(): return lax.ppermute(value, axis, [(0, 1), (1, 0)])  11.7 us
    all_to_all x1, blocking collectives, local(): lax.all_to_all(added, SLABS, split_axis=0, concat_axis=0, tiled=True)  11.5 us
    ppermute x20, starting transfers between devices, swap(): return lax.ppermute(value, axis, [(0, 1), (1, 0)])  7.47 us
    all_to_all x1, starting transfers between devices, local(): lax.all_to_all(columns, 'z', split_axis=0, concat_axis=0, tiled=True)  5.45 us
    pallas_call x1, Pallas kernels, local(): pl.pallas_call(functools.partial(early_kernel, soon, nz, width, padded),...  3.87 us
  transfers between devices with their start and end apart: 43, of which 20 were waited for; matrix products, arithmetic and copies ran while one was open for 0% of the time, Pallas kernels for 7%

profile of v4, /device:TPU:32, one launch (start us, length us, event | category | flops | bytes accessed | tf_op | source)
XLA Modules:
  0.0 176.6 jit_solution(7139046373887757853)
XLA Ops:
  3.0 1.7 gather_fusion.1
  6.5 48.4 %all_to_all.15.near_ref = bf16[16,272,300]{2,1,0:T(8,128)(2,1)} all-to-all(bf16[16,272,300]{2,1,0:T(8,128)(2,1)S(1)} %bitcast.17), channel_id=1, replica_groups=mesh['x'=4,'yl'=2,'z'=8,'yh'=2,'c'=2] {'yh','x','yl'}, dimensions={0} | all-to-all | bytes 5222400 | tf_op jit(solution)/shard_map/all_to_all | solution.py:216
  54.9 3.3 %shard_map.46.near_part_ref = f32[8,48,1408]{2,1,0:T(8,128)S(1)} custom-call(s32[7]{0:T(128)S(1)} %stack.27.where_ref, bf16[16,272,300]{2,1,0:T(8,128)(2,1)} %all_to_all.15.near_ref), custom_call_target="tpu_custom_call" | custom-call | flops 648806400 | tf_op jit(solution)/shard_map/pallas_call | solution.py:223
  58.3 2.8 %collective-permute-done.far_ref = bf16[16,272,300]{2,1,0:T(8,128)(2,1)} collective-permute-done((bf16[16,272,300]{2,1,0:T(8,128)(2,1)}, bf16[16,272,300]{2,1,0:T(8,128)(2,1)}, u32[]{:S(2)}, u32[]{:S(2)}) %collective-permute-start) | collective-permute-done | bytes 2611232 | tf_op jit(solution)/shard_map/ppermute | solution.py:23
  61.1 2.7 %shard_map.48 = (f32[24,1408]{1,0:T(8,128)S(1)}, f32[24,1408]{1,0:T(8,128)S(1)}) custom-call(s32[7]{0:T(128)S(1)} %stack.27.where_ref, f32[8,48,1408]{2,1,0:T(8,128)S(1)} %shard_map.46.near_part_ref, bf16[16,272,300]{2,1,0:T(8,128)(2,1)} %collective-permute-done.far_ref), custom_call_target="tpu_custom_call" | custom-call | flops 81100800 | tf_op jit(solution)/shard_map/pallas_call | solution.py:231
  63.8 2.0 %collective-permute-start.1 = (f32[24,1408]{1,0:T(8,128)S(1)}, f32[24,1408]{1,0:T(8,128)S(1)}, u32[]{:S(2)}, u32[]{:S(2)}) collective-permute-start(f32[24,1408]{1,0:T(8,128)S(1)} %get-tuple-element.40), channel_id=1, source_target_pairs={{0,4},{4,8},{8,12},{12,16},{16,20},{20,24},{24,28},{28,0},{1,5},{5... | collective-permute-start | bytes 405512 | tf_op jit(solution)/shard_map/ppermute | solution.py:28
  66.1 1.6 copy-done.2
  67.7 3.4 %shard_map.47 = (f32[8,48,1408]{2,1,0:T(8,128)S(1)}, f32[48,1408]{1,0:T(8,128)S(1)}) custom-call(s32[7]{0:T(128)S(1)} %stack.27.where_ref, s32[8,2]{1,0:T(8,128)S(1)} %copy.11.pair_ref, f32[16]{0:T(128)S(1)} %copy-done.3, f32[1,1408]{1,0:T(1,128)S(1)} %broadcast_in_dim.4.vir_ref, f32[8,48,1408]{2,1,0:T(8,128)S(1)} %copy-done.2, ...), custom_call_target="tpu_custom_call" | custom-call | flops 648806400 | tf_op jit(solution)/shard_map/pallas_call | solution.py:240
  72.0 3.2 %collective-permute-start.3 = (f32[48,1408]{1,0:T(8,128)S(1)}, f32[48,1408]{1,0:T(8,128)S(1)}, u32[]{:S(2)}, u32[]{:S(2)}) collective-permute-start(f32[48,1408]{1,0:T(8,128)S(1)} %get-tuple-element.42), channel_id=1, source_target_pairs={{0,4},{4,8},{8,12},{12,16},{16,20},{20,24},{24,28},{28,0},{1,5},{5... | collective-permute-start | bytes 811016 | tf_op jit(solution)/shard_map/ppermute | solution.py:28
  75.8 6.4 %collective-permute-done.3.up_in = f32[48,1408]{1,0:T(8,128)S(1)} collective-permute-done((f32[48,1408]{1,0:T(8,128)S(1)}, f32[48,1408]{1,0:T(8,128)S(1)}, u32[]{:S(2)}, u32[]{:S(2)}) %collective-permute-start.3) | collective-permute-done | bytes 270368 | tf_op jit(solution)/shard_map/ppermute | solution.py:28
  84.1 2.5 %collective-permute-start.5 = (f32[48,1408]{1,0:T(8,128)S(1)}, f32[48,1408]{1,0:T(8,128)S(1)}, u32[]{:S(2)}, u32[]{:S(2)}) collective-permute-start(f32[48,1408]{1,0:T(8,128)S(1)} %get-tuple-element.44), channel_id=1, source_target_pairs={{0,4},{4,8},{8,12},{12,16},{16,20},{20,24},{24,28},{28,0},{1,5},{5... | collective-permute-start | bytes 811016 | tf_op jit(solution)/shard_map/ppermute | solution.py:28
  86.5 5.0 %collective-permute-done.5.up_in = f32[48,1408]{1,0:T(8,128)S(1)} collective-permute-done((f32[48,1408]{1,0:T(8,128)S(1)}, f32[48,1408]{1,0:T(8,128)S(1)}, u32[]{:S(2)}, u32[]{:S(2)}) %collective-permute-start.5) | collective-permute-done | bytes 270368 | tf_op jit(solution)/shard_map/ppermute | solution.py:28
  91.6 2.7 %collective-permute-done.6.down_in = f32[48,1408]{1,0:T(8,128)S(1)} collective-permute-done((f32[48,1408]{1,0:T(8,128)S(1)}, f32[48,1408]{1,0:T(8,128)S(1)}, u32[]{:S(2)}, u32[]{:S(2)}) %collective-permute-start.6) | collective-permute-done | bytes 270368 | tf_op jit(solution)/shard_map/ppermute | solution.py:28
  94.8 1.8 %collective-permute-start.7 = (f32[48,1408]{1,0:T(8,128)S(1)}, f32[48,1408]{1,0:T(8,128)S(1)}, u32[]{:S(2)}, u32[]{:S(2)}) collective-permute-start(f32[48,1408]{1,0:T(8,128)S(1)} %get-tuple-element.46), channel_id=1, source_target_pairs={{0,4},{4,8},{8,12},{12,16},{16,20},{20,24},{24,28},{28,0},{1,5},{5... | collective-permute-start | bytes 811016 | tf_op jit(solution)/shard_map/ppermute | solution.py:28
  97.0 4.4 %collective-permute-done.7.up_in = f32[48,1408]{1,0:T(8,128)S(1)} collective-permute-done((f32[48,1408]{1,0:T(8,128)S(1)}, f32[48,1408]{1,0:T(8,128)S(1)}, u32[]{:S(2)}, u32[]{:S(2)}) %collective-permute-start.7) | collective-permute-done | bytes 270368 | tf_op jit(solution)/shard_map/ppermute | solution.py:28
  101.4 1.7 collective-permute-done.8.down_in
  104.6 5.5 %all-to-all-start.1 = ((f32[8,48,176]{2,1,0:T(8,128)}), f32[8,48,176]{2,1,0:T(8,128)S(1)}, u32[]{:S(2)}, u32[]{:S(2)}) async-start(f32[8,48,176]{2,1,0:T(8,128)} %get-tuple-element.50), calls=%async_computation.1 | async-start | bytes 786432 | tf_op jit(solution)/shard_map/all_to_all | solution.py:267
  110.1 1.6 collective-permute-start.11
  113.7 2.9 %collective-permute-done.11.refs_1_ = bf16[48,1408]{1,0:T(8,128)(2,1)S(1)} collective-permute-done((bf16[48,1408]{1,0:T(8,128)(2,1)S(1)}, bf16[48,1408]{1,0:T(8,128)(2,1)S(1)}, u32[]{:S(2)}, u32[]{:S(2)}) %collective-permute-start.11) | collective-permute-done | bytes 135200 | tf_op jit(solution)/shard_map/ppermute | solution.py:23
  118.6 2.0 %collective-permute-done.9.refs_8_ = bf16[48,1408]{1,0:T(8,128)(2,1)S(1)} collective-permute-done((bf16[48,1408]{1,0:T(8,128)(2,1)S(1)}, bf16[48,1408]{1,0:T(8,128)(2,1)S(1)}, u32[]{:S(2)}, u32[]{:S(2)}) %collective-permute-start.9) | collective-permute-done | bytes 135200 | tf_op jit(solution)/shard_map/ppermute | solution.py:28
  122.0 2.3 %collective-permute-start.15 = (bf16[48,1408]{1,0:T(8,128)(2,1)S(1)}, bf16[48,1408]{1,0:T(8,128)(2,1)}, u32[]{:S(2)}, u32[]{:S(2)}) collective-permute-start(bf16[48,1408]{1,0:T(8,128)(2,1)S(1)} %collective-permute-done.14.refs_4_), channel_id=1, source_target_pairs={{0,28},{4,0},{8,4},{12,8},{16,12},{20,16},{24,20},{28,24},{1,29},{... | collective-permute-start | bytes 405512 | tf_op jit(solution)/shard_map/ppermute | solution.py:28
  125.6 2.1 %collective-permute-start.17 = (bf16[48,1408]{1,0:T(8,128)(2,1)}, bf16[48,1408]{1,0:T(8,128)(2,1)}, u32[]{:S(2)}, u32[]{:S(2)}) collective-permute-start(bf16[48,1408]{1,0:T(8,128)(2,1)} %collective-permute-done.16.refs_5_), channel_id=1, source_target_pairs={{0,28},{4,0},{8,4},{12,8},{16,12},{20,16},{24,20},{28,24},{1,29},{... | collective-permute-start | bytes 405512 | tf_op jit(solution)/shard_map/ppermute | solution.py:28
  129.1 1.8 collective-permute-done.13.refs_17_
  130.9 1.6 collective-permute-start.24
  133.6 4.5 %collective-permute-done.24.other_ref = f32[8,48,88]{2,1,0:T(8,128)S(1)} collective-permute-done((f32[8,48,88]{2,1,0:T(8,128)S(1)}, f32[8,48,88]{2,1,0:T(8,128)S(1)}, u32[]{:S(2)}, u32[]{:S(2)}) %collective-permute-start.24) | collective-permute-done | bytes 135200 | tf_op jit(solution)/shard_map/ppermute | solution.py:23
  140.7 3.2 %collective-permute-start.18 = (bf16[48,1408]{1,0:T(8,128)(2,1)}, bf16[48,1408]{1,0:T(8,128)(2,1)S(1)}, u32[]{:S(2)}, u32[]{:S(2)}) collective-permute-start(bf16[48,1408]{1,0:T(8,128)(2,1)} %collective-permute-done.15.refs_12_), channel_id=1, source_target_pairs={{0,28},{4,0},{8,4},{12,8},{16,12},{20,16},{24,20},{28,24},{1,29},{... | collective-permute-start | bytes 405512 | tf_op jit(solution)/shard_map/ppermute | solution.py:28
  143.9 5.1 %collective-permute-start.22 = (bf16[48,1408]{1,0:T(8,128)(2,1)S(1)}, bf16[48,1408]{1,0:T(8,128)(2,1)S(1)}, u32[]{:S(2)}, u32[]{:S(2)}) collective-permute-start(bf16[48,1408]{1,0:T(8,128)(2,1)S(1)} %collective-permute-done.10.refs_16_), channel_id=1, source_target_pairs={{0,8},{4,12},{8,16},{12,20},{16,24},{20,28},{24,0},{28,4},{1,9},{5... | collective-permute-start | bytes 405512 | tf_op jit(solution)/shard_map/ppermute | solution.py:28
  149.0 2.0 %collective-permute-start.21 = (bf16[48,1408]{1,0:T(8,128)(2,1)}, bf16[48,1408]{1,0:T(8,128)(2,1)S(1)}, u32[]{:S(2)}, u32[]{:S(2)}) collective-permute-start(bf16[48,1408]{1,0:T(8,128)(2,1)} %collective-permute-done.13.refs_17_), channel_id=1, source_target_pairs={{0,4},{4,8},{8,12},{12,16},{16,20},{20,24},{24,28},{28,0},{1,5},{5... | collective-permute-start | bytes 405512 | tf_op jit(solution)/shard_map/ppermute | solution.py:28
  151.0 2.7 %collective-permute-start.23 = (bf16[48,1408]{1,0:T(8,128)(2,1)}, bf16[48,1408]{1,0:T(8,128)(2,1)S(1)}, u32[]{:S(2)}, u32[]{:S(2)}) collective-permute-start(bf16[48,1408]{1,0:T(8,128)(2,1)} %collective-permute-done.17.refs_13_), channel_id=1, source_target_pairs={{0,24},{4,28},{8,0},{12,4},{16,8},{20,12},{24,16},{28,20},{1,25},{... | collective-permute-start | bytes 405512 | tf_op jit(solution)/shard_map/ppermute | solution.py:28
  153.8 3.9 %shard_map.55 = (f32[48,1408]{1,0:T(8,128)S(1)}, f32[8,48,176]{2,1,0:T(8,128)S(1)}, bf16[48,1408]{1,0:T(8,128)(2,1)S(1)}, bf16[8,2,48,96]{3,2,1,0:T(8,128)(2,1)S(1)}) custom-call(s32[7]{0:T(128)S(1)} %stack.27.where_ref, f32[48,1408]{1,0:T(8,128)S(1)} %get-tuple-element.55.rows_ref, f32[8,48,96]{2,1,0:T(8,128)S(1)} %get-tuple-element.57.near_ref, ...), custom_call_target="tpu_custom_call" | custom-call | flops 129761280 | bytes 2703360 | tf_op jit(solution)/shard_map/pallas_call | solution.py:298
  162.8 1.6 shard_map.56
  164.4 11.5 %all_to_all.16 = f32[8,48,176]{2,1,0:T(8,128)S(1)} all-to-all(f32[8,48,176]{2,1,0:T(8,128)S(1)} %shard_map.56), channel_id=1, replica_groups=mesh['x'=4,'yl'=2,'z'=8,'yh'=2,'c'=2] {'x','yl'}, dimensions={0} | all-to-all | bytes 540672 | tf_op jit(solution)/shard_map/all_to_all | solution.py:320
  (92 shorter events, 28.3 us)
Async XLA Ops:
  54.8 6.3 %collective-permute-start = (bf16[16,272,300]{2,1,0:T(8,128)(2,1)}, bf16[16,272,300]{2,1,0:T(8,128)(2,1)}, u32[]{:S(2)}, u32[]{:S(2)}) collective-permute-start(bf16[16,272,300]{2,1,0:T(8,128)(2,1)} %all_to_all.15.near_ref), channel_id=1, source_target_pairs={{0,1},{1,0},{2,3},{3,2},{4,5},{5,4},{6,7},{7,6},{8,9},{9,8},{10,11... | collective-permute-start | bytes 7833608 | tf_op jit(solution)/shard_map/ppermute | solution.py:23
  63.8 7.2 %collective-permute-start.1 = (f32[24,1408]{1,0:T(8,128)S(1)}, f32[24,1408]{1,0:T(8,128)S(1)}, u32[]{:S(2)}, u32[]{:S(2)}) collective-permute-start(f32[24,1408]{1,0:T(8,128)S(1)} %get-tuple-element.40), channel_id=1, source_target_pairs={{0,4},{4,8},{8,12},{12,16},{16,20},{20,24},{24,28},{28,0},{1,5},{5... | collective-permute-start | bytes 405512 | tf_op jit(solution)/shard_map/ppermute | solution.py:28
  65.8 5.5 %collective-permute-start.2 = (f32[24,1408]{1,0:T(8,128)S(1)}, f32[24,1408]{1,0:T(8,128)S(1)}, u32[]{:S(2)}, u32[]{:S(2)}) collective-permute-start(f32[24,1408]{1,0:T(8,128)S(1)} %get-tuple-element.41), channel_id=1, source_target_pairs={{0,28},{4,0},{8,4},{12,8},{16,12},{20,16},{24,20},{28,24},{1,29},{... | collective-permute-start | bytes 405512 | tf_op jit(solution)/shard_map/ppermute | solution.py:28
  72.0 10.3 %collective-permute-start.3 = (f32[48,1408]{1,0:T(8,128)S(1)}, f32[48,1408]{1,0:T(8,128)S(1)}, u32[]{:S(2)}, u32[]{:S(2)}) collective-permute-start(f32[48,1408]{1,0:T(8,128)S(1)} %get-tuple-element.42), channel_id=1, source_target_pairs={{0,4},{4,8},{8,12},{12,16},{16,20},{20,24},{24,28},{28,0},{1,5},{5... | collective-permute-start | bytes 811016 | tf_op jit(solution)/shard_map/ppermute | solution.py:28
  75.2 8.3 %collective-permute-start.4 = (f32[48,1408]{1,0:T(8,128)S(1)}, f32[48,1408]{1,0:T(8,128)S(1)}, u32[]{:S(2)}, u32[]{:S(2)}) collective-permute-start(f32[48,1408]{1,0:T(8,128)S(1)} %get-tuple-element.43), channel_id=1, source_target_pairs={{0,28},{4,0},{8,4},{12,8},{16,12},{20,16},{24,20},{28,24},{1,29},{... | collective-permute-start | bytes 811016 | tf_op jit(solution)/shard_map/ppermute | solution.py:28
  84.1 7.5 %collective-permute-start.5 = (f32[48,1408]{1,0:T(8,128)S(1)}, f32[48,1408]{1,0:T(8,128)S(1)}, u32[]{:S(2)}, u32[]{:S(2)}) collective-permute-start(f32[48,1408]{1,0:T(8,128)S(1)} %get-tuple-element.44), channel_id=1, source_target_pairs={{0,4},{4,8},{8,12},{12,16},{16,20},{20,24},{24,28},{28,0},{1,5},{5... | collective-permute-start | bytes 811016 | tf_op jit(solution)/shard_map/ppermute | solution.py:28
  86.5 7.7 %collective-permute-start.6 = (f32[48,1408]{1,0:T(8,128)S(1)}, f32[48,1408]{1,0:T(8,128)S(1)}, u32[]{:S(2)}, u32[]{:S(2)}) collective-permute-start(f32[48,1408]{1,0:T(8,128)S(1)} %get-tuple-element.45), channel_id=1, source_target_pairs={{0,28},{4,0},{8,4},{12,8},{16,12},{20,16},{24,20},{28,24},{1,29},{... | collective-permute-start | bytes 811016 | tf_op jit(solution)/shard_map/ppermute | solution.py:28
  94.8 6.5 %collective-permute-start.7 = (f32[48,1408]{1,0:T(8,128)S(1)}, f32[48,1408]{1,0:T(8,128)S(1)}, u32[]{:S(2)}, u32[]{:S(2)}) collective-permute-start(f32[48,1408]{1,0:T(8,128)S(1)} %get-tuple-element.46), channel_id=1, source_target_pairs={{0,4},{4,8},{8,12},{12,16},{16,20},{20,24},{24,28},{28,0},{1,5},{5... | collective-permute-start | bytes 811016 | tf_op jit(solution)/shard_map/ppermute | solution.py:28
  96.7 6.5 %collective-permute-start.8 = (f32[48,1408]{1,0:T(8,128)S(1)}, f32[48,1408]{1,0:T(8,128)S(1)}, u32[]{:S(2)}, u32[]{:S(2)}) collective-permute-start(f32[48,1408]{1,0:T(8,128)S(1)} %get-tuple-element.47), channel_id=1, source_target_pairs={{0,28},{4,0},{8,4},{12,8},{16,12},{20,16},{24,20},{28,24},{1,29},{... | collective-permute-start | bytes 811016 | tf_op jit(solution)/shard_map/ppermute | solution.py:28
  104.6 23.1 %all-to-all-start.1 = ((f32[8,48,176]{2,1,0:T(8,128)}), f32[8,48,176]{2,1,0:T(8,128)S(1)}, u32[]{:S(2)}, u32[]{:S(2)}) async-start(f32[8,48,176]{2,1,0:T(8,128)} %get-tuple-element.50), calls=%async_computation.1 | async-start | bytes 786432 | tf_op jit(solution)/shard_map/all_to_all | solution.py:267
  110.1 6.5 %collective-permute-start.11 = (bf16[48,1408]{1,0:T(8,128)(2,1)S(1)}, bf16[48,1408]{1,0:T(8,128)(2,1)S(1)}, u32[]{:S(2)}, u32[]{:S(2)}) collective-permute-start(bf16[48,1408]{1,0:T(8,128)(2,1)S(1)} %get-tuple-element.49.refs_0_), channel_id=1, source_target_pairs={{0,2},{2,0},{1,3},{3,1},{4,6},{6,4},{5,7},{7,5},{8,10},{10,8},{9,1... | collective-permute-start | bytes 405512 | tf_op jit(solution)/shard_map/ppermute | solution.py:23
  111.7 8.9 %collective-permute-start.9 = (bf16[48,1408]{1,0:T(8,128)(2,1)S(1)}, bf16[48,1408]{1,0:T(8,128)(2,1)S(1)}, u32[]{:S(2)}, u32[]{:S(2)}) collective-permute-start(bf16[48,1408]{1,0:T(8,128)(2,1)S(1)} %get-tuple-element.49.refs_0_), channel_id=1, source_target_pairs={{0,4},{4,8},{8,12},{12,16},{16,20},{20,24},{24,28},{28,0},{1,5},{5... | collective-permute-start | bytes 405512 | tf_op jit(solution)/shard_map/ppermute | solution.py:28
  113.2 8.9 %collective-permute-start.14 = (bf16[48,1408]{1,0:T(8,128)(2,1)S(1)}, bf16[48,1408]{1,0:T(8,128)(2,1)S(1)}, u32[]{:S(2)}, u32[]{:S(2)}) collective-permute-start(bf16[48,1408]{1,0:T(8,128)(2,1)S(1)} %get-tuple-element.49.refs_0_), channel_id=1, source_target_pairs={{0,28},{4,0},{8,4},{12,8},{16,12},{20,16},{24,20},{28,24},{1,29},{... | collective-permute-start | bytes 405512 | tf_op jit(solution)/shard_map/ppermute | solution.py:28
  116.6 7.8 %collective-permute-start.12 = (bf16[48,1408]{1,0:T(8,128)(2,1)S(1)}, bf16[48,1408]{1,0:T(8,128)(2,1)}, u32[]{:S(2)}, u32[]{:S(2)}) collective-permute-start(bf16[48,1408]{1,0:T(8,128)(2,1)S(1)} %collective-permute-done.11.refs_1_), channel_id=1, source_target_pairs={{0,4},{4,8},{8,12},{12,16},{16,20},{20,24},{24,28},{28,0},{1,5},{5... | collective-permute-start | bytes 405512 | tf_op jit(solution)/shard_map/ppermute | solution.py:28
  118.1 7.5 %collective-permute-start.16 = (bf16[48,1408]{1,0:T(8,128)(2,1)S(1)}, bf16[48,1408]{1,0:T(8,128)(2,1)}, u32[]{:S(2)}, u32[]{:S(2)}) collective-permute-start(bf16[48,1408]{1,0:T(8,128)(2,1)S(1)} %collective-permute-done.11.refs_1_), channel_id=1, source_target_pairs={{0,28},{4,0},{8,4},{12,8},{16,12},{20,16},{24,20},{28,24},{1,29},{... | collective-permute-start | bytes 405512 | tf_op jit(solution)/shard_map/ppermute | solution.py:28
  120.6 7.9 %collective-permute-start.10 = (bf16[48,1408]{1,0:T(8,128)(2,1)S(1)}, bf16[48,1408]{1,0:T(8,128)(2,1)S(1)}, u32[]{:S(2)}, u32[]{:S(2)}) collective-permute-start(bf16[48,1408]{1,0:T(8,128)(2,1)S(1)} %collective-permute-done.9.refs_8_), channel_id=1, source_target_pairs={{0,4},{4,8},{8,12},{12,16},{16,20},{20,24},{24,28},{28,0},{1,5},{5... | collective-permute-start | bytes 405512 | tf_op jit(solution)/shard_map/ppermute | solution.py:28
  122.0 7.1 %collective-permute-start.15 = (bf16[48,1408]{1,0:T(8,128)(2,1)S(1)}, bf16[48,1408]{1,0:T(8,128)(2,1)}, u32[]{:S(2)}, u32[]{:S(2)}) collective-permute-start(bf16[48,1408]{1,0:T(8,128)(2,1)S(1)} %collective-permute-done.14.refs_4_), channel_id=1, source_target_pairs={{0,28},{4,0},{8,4},{12,8},{16,12},{20,16},{24,20},{28,24},{1,29},{... | collective-permute-start | bytes 405512 | tf_op jit(solution)/shard_map/ppermute | solution.py:28
  124.4 6.5 %collective-permute-start.13 = (bf16[48,1408]{1,0:T(8,128)(2,1)}, bf16[48,1408]{1,0:T(8,128)(2,1)}, u32[]{:S(2)}, u32[]{:S(2)}) collective-permute-start(bf16[48,1408]{1,0:T(8,128)(2,1)} %collective-permute-done.12.refs_9_), channel_id=1, source_target_pairs={{0,4},{4,8},{8,12},{12,16},{16,20},{20,24},{24,28},{28,0},{1,5},{5... | collective-permute-start | bytes 405512 | tf_op jit(solution)/shard_map/ppermute | solution.py:28
  127.7 5.3 %collective-permute-start.26 = (bf16[48,1408]{1,0:T(8,128)(2,1)S(1)}, bf16[48,1408]{1,0:T(8,128)(2,1)}, u32[]{:S(2)}, u32[]{:S(2)}) collective-permute-start(bf16[48,1408]{1,0:T(8,128)(2,1)S(1)} %get-tuple-element.49.refs_0_), channel_id=1, source_target_pairs={{0,1},{1,0},{2,3},{3,2},{4,5},{5,4},{6,7},{7,6},{8,9},{9,8},{10,11... | collective-permute-start | bytes 405512 | tf_op jit(solution)/shard_map/ppermute | solution.py:23
  130.9 7.2 %collective-permute-start.24 = (f32[8,48,88]{2,1,0:T(8,128)S(1)}, f32[8,48,88]{2,1,0:T(8,128)S(1)}, u32[]{:S(2)}, u32[]{:S(2)}) collective-permute-start(f32[8,48,88]{2,1,0:T(8,128)S(1)} %shard_map.53), channel_id=1, source_target_pairs={{0,2},{2,0},{1,3},{3,1},{4,6},{6,4},{5,7},{7,5},{8,10},{10,8},{9,1... | collective-permute-start | bytes 405512 | tf_op jit(solution)/shard_map/ppermute | solution.py:23
  132.5 6.7 %collective-permute-start.28 = (bf16[48,1408]{1,0:T(8,128)(2,1)S(1)}, bf16[48,1408]{1,0:T(8,128)(2,1)S(1)}, u32[]{:S(2)}, u32[]{:S(2)}) collective-permute-start(bf16[48,1408]{1,0:T(8,128)(2,1)S(1)} %collective-permute-done.14.refs_4_), channel_id=1, source_target_pairs={{0,1},{1,0},{2,3},{3,2},{4,5},{5,4},{6,7},{7,6},{8,9},{9,8},{10,11... | collective-permute-start | bytes 405512 | tf_op jit(solution)/shard_map/ppermute | solution.py:23
  132.5 7.3 %collective-permute-start.30 = (bf16[48,1408]{1,0:T(8,128)(2,1)S(1)}, bf16[48,1408]{1,0:T(8,128)(2,1)S(1)}, u32[]{:S(2)}, u32[]{:S(2)}) collective-permute-start(bf16[48,1408]{1,0:T(8,128)(2,1)S(1)} %collective-permute-done.9.refs_8_), channel_id=1, source_target_pairs={{0,1},{1,0},{2,3},{3,2},{4,5},{5,4},{6,7},{7,6},{8,9},{9,8},{10,11... | collective-permute-start | bytes 405512 | tf_op jit(solution)/shard_map/ppermute | solution.py:23
  133.0 6.9 %collective-permute-start.29 = (bf16[48,1408]{1,0:T(8,128)(2,1)}, bf16[48,1408]{1,0:T(8,128)(2,1)S(1)}, u32[]{:S(2)}, u32[]{:S(2)}) collective-permute-start(bf16[48,1408]{1,0:T(8,128)(2,1)} %collective-permute-done.16.refs_5_), channel_id=1, source_target_pairs={{0,1},{1,0},{2,3},{3,2},{4,5},{5,4},{6,7},{7,6},{8,9},{9,8},{10,11... | collective-permute-start | bytes 405512 | tf_op jit(solution)/shard_map/ppermute | solution.py:23
  133.0 7.3 %collective-permute-start.31 = (bf16[48,1408]{1,0:T(8,128)(2,1)}, bf16[48,1408]{1,0:T(8,128)(2,1)S(1)}, u32[]{:S(2)}, u32[]{:S(2)}) collective-permute-start(bf16[48,1408]{1,0:T(8,128)(2,1)} %collective-permute-done.12.refs_9_), channel_id=1, source_target_pairs={{0,1},{1,0},{2,3},{3,2},{4,5},{5,4},{6,7},{7,6},{8,9},{9,8},{10,11... | collective-permute-start | bytes 405512 | tf_op jit(solution)/shard_map/ppermute | solution.py:23
  139.3 11.8 %collective-permute-start.25 = (f32[8,48,96]{2,1,0:T(8,128)S(1)}, f32[8,48,96]{2,1,0:T(8,128)S(1)}, u32[]{:S(2)}, u32[]{:S(2)}) collective-permute-start(f32[8,48,96]{2,1,0:T(8,128)S(1)} %get-tuple-element.58), channel_id=1, source_target_pairs={{0,1},{1,0},{2,3},{3,2},{4,5},{5,4},{6,7},{7,6},{8,9},{9,8},{10,11... | collective-permute-start | bytes 442376 | tf_op jit(solution)/shard_map/ppermute | solution.py:23
  140.4 8.6 %collective-permute-start.35 = (bf16[48,1408]{1,0:T(8,128)(2,1)}, bf16[48,1408]{1,0:T(8,128)(2,1)S(1)}, u32[]{:S(2)}, u32[]{:S(2)}) collective-permute-start(bf16[48,1408]{1,0:T(8,128)(2,1)} %collective-permute-done.13.refs_17_), channel_id=1, source_target_pairs={{0,1},{1,0},{2,3},{3,2},{4,5},{5,4},{6,7},{7,6},{8,9},{9,8},{10,11... | collective-permute-start | bytes 405512 | tf_op jit(solution)/shard_map/ppermute | solution.py:23
  140.7 8.3 %collective-permute-start.18 = (bf16[48,1408]{1,0:T(8,128)(2,1)}, bf16[48,1408]{1,0:T(8,128)(2,1)S(1)}, u32[]{:S(2)}, u32[]{:S(2)}) collective-permute-start(bf16[48,1408]{1,0:T(8,128)(2,1)} %collective-permute-done.15.refs_12_), channel_id=1, source_target_pairs={{0,28},{4,0},{8,4},{12,8},{16,12},{20,16},{24,20},{28,24},{1,29},{... | collective-permute-start | bytes 405512 | tf_op jit(solution)/shard_map/ppermute | solution.py:28
  143.9 13.9 %collective-permute-start.20 = (bf16[48,1408]{1,0:T(8,128)(2,1)S(1)}, bf16[48,1408]{1,0:T(8,128)(2,1)S(1)}, u32[]{:S(2)}, u32[]{:S(2)}) collective-permute-start(bf16[48,1408]{1,0:T(8,128)(2,1)S(1)} %collective-permute-done.10.refs_16_), channel_id=1, source_target_pairs={{0,4},{4,8},{8,12},{12,16},{16,20},{20,24},{24,28},{28,0},{1,5},{5... | collective-permute-start | bytes 405512 | tf_op jit(solution)/shard_map/ppermute | solution.py:28
  143.9 16.1 %collective-permute-start.22 = (bf16[48,1408]{1,0:T(8,128)(2,1)S(1)}, bf16[48,1408]{1,0:T(8,128)(2,1)S(1)}, u32[]{:S(2)}, u32[]{:S(2)}) collective-permute-start(bf16[48,1408]{1,0:T(8,128)(2,1)S(1)} %collective-permute-done.10.refs_16_), channel_id=1, source_target_pairs={{0,8},{4,12},{8,16},{12,20},{16,24},{20,28},{24,0},{28,4},{1,9},{5... | collective-permute-start | bytes 405512 | tf_op jit(solution)/shard_map/ppermute | solution.py:28
  149.0 8.8 %collective-permute-start.19 = (bf16[48,1408]{1,0:T(8,128)(2,1)}, bf16[48,1408]{1,0:T(8,128)(2,1)S(1)}, u32[]{:S(2)}, u32[]{:S(2)}) collective-permute-start(bf16[48,1408]{1,0:T(8,128)(2,1)} %collective-permute-done.17.refs_13_), channel_id=1, source_target_pairs={{0,28},{4,0},{8,4},{12,8},{16,12},{20,16},{24,20},{28,24},{1,29},{... | collective-permute-start | bytes 405512 | tf_op jit(solution)/shard_map/ppermute | solution.py:28
  149.0 10.0 %collective-permute-start.21 = (bf16[48,1408]{1,0:T(8,128)(2,1)}, bf16[48,1408]{1,0:T(8,128)(2,1)S(1)}, u32[]{:S(2)}, u32[]{:S(2)}) collective-permute-start(bf16[48,1408]{1,0:T(8,128)(2,1)} %collective-permute-done.13.refs_17_), channel_id=1, source_target_pairs={{0,4},{4,8},{8,12},{12,16},{16,20},{20,24},{24,28},{28,0},{1,5},{5... | collective-permute-start | bytes 405512 | tf_op jit(solution)/shard_map/ppermute | solution.py:28
  151.0 9.0 %collective-permute-start.23 = (bf16[48,1408]{1,0:T(8,128)(2,1)}, bf16[48,1408]{1,0:T(8,128)(2,1)S(1)}, u32[]{:S(2)}, u32[]{:S(2)}) collective-permute-start(bf16[48,1408]{1,0:T(8,128)(2,1)} %collective-permute-done.17.refs_13_), channel_id=1, source_target_pairs={{0,24},{4,28},{8,0},{12,4},{16,8},{20,12},{24,16},{28,20},{1,25},{... | collective-permute-start | bytes 405512 | tf_op jit(solution)/shard_map/ppermute | solution.py:28
  (17 other events, 60.9 us)

commit v5 on v4

--- a/solution.py
+++ b/solution.py
@@ -97,13 +97,21 @@
         down_ref[: rows - taken] = part_ref[below, : rows - taken]
 
 
-def amplitude_kernel(where_ref, part_ref, up_in, down_in, denom_ref, out_ref, rounded_ref, blocks_ref):
+def amplitude_kernel(where_ref, part_ref, up_in, down_in, denom_ref, out_ref, rounded_ref):
     amps = (part_ref[where_ref[0]] + (up_in[...] + down_in[...])) / denom_ref[...]
     out_ref[...] = amps
     rounded_ref[...] = amps.astype(BF16)
+
+
+def blocks_kernel(rows_ref, after_ref, blocks_ref):
     slab = blocks_ref.shape[2]
     for k in range(blocks_ref.shape[0]):
-        blocks_ref[k] = amps[:, k * slab : (k + 1) * slab]
+        blocks_ref[k] = rows_ref[:, k * slab : (k + 1) * slab]
+
+
+def halves_kernel(up_ref, down_ref, first_ref, second_ref):
+    first_ref[...] = up_ref[: first_ref.shape[0]]
+    second_ref[...] = down_ref[first_ref.shape[0] :]
 
 
 def outward_kernel(where_ref, columns_ref, out_ref):
@@ -151,12 +159,14 @@
 
 def density_pieces(steps, nz, width, padded, where_ref, tilde, tilde_t_ref, pieces, total, blocks_ref):
     z, c, yh = where_ref[0], where_ref[1], where_ref[6]
-    for n, r in enumerate(steps):
+    pieces = list(pieces)
+    for r in steps:
         at = lax.rem(z + r, nz)
         sides = []
         for slot in range(2):
-            first, second = pieces[4 * n + 2 * slot], pieces[4 * n + 2 * slot + 1]
-            piece = jnp.concatenate([first[...], second[...]], axis=0)
+            piece = pieces.pop(0)[...]
+            if piece.shape[0] == padded:
+                piece = jnp.concatenate([piece, pieces.pop(0)[...]], axis=0)
             term = jnp.dot(tilde_t_ref[at, slot], piece, preferred_element_type=F32)
             total = term if total is None else total + term
             sides.append(dot_nt(tilde, piece))
@@ -170,8 +180,8 @@
 
 
 def early_kernel(steps, nz, width, padded, where_ref, rows_ref, near_ref, far_ref, *refs):
-    pieces = refs[: 4 * len(steps)]
-    total_ref, blocks_ref, tilde_ref, tilde_t_ref = refs[4 * len(steps) :]
+    pieces = refs[:-4]
+    total_ref, blocks_ref, tilde_ref, tilde_t_ref = refs[-4:]
     c, yh = where_ref[1], where_ref[6]
     slab = rows_ref.shape[1] // nz
     rows = rows_ref[...]
@@ -255,16 +265,25 @@
         )(where, part, up, down)
         up, down = shift(up, "z", 1), shift(down, "z", -1)
     rows16 = jax.ShapeDtypeStruct((padded, nvir), BF16)
-    amp_rows, mine, columns = pl.pallas_call(
+    amp_rows, mine = pl.pallas_call(
         amplitude_kernel,
-        out_shape=(rows, rows16, jax.ShapeDtypeStruct((nz, padded, slab), F32)),
+        out_shape=(rows, rows16),
         in_specs=[SMEM, VMEM, VMEM, VMEM, VMEM],
-        out_specs=(VMEM,) * 3,
+        out_specs=(VMEM, VMEM),
         compiler_params=params(8),
     )(where, part, up, down, denom)
 
-    mine = (mine, swap(mine, "yh"))
+    other = swap(mine, "yh")
+    mine_far = swap(mine, "c")
+    columns = pl.pallas_call(
+        blocks_kernel,
+        out_shape=jax.ShapeDtypeStruct((nz, padded, slab), F32),
+        in_specs=[VMEM, VMEM],
+        out_specs=VMEM,
+        compiler_params=params(8),
+    )(amp_rows, mine_far)
     columns = lax.all_to_all(columns, "z", split_axis=0, concat_axis=0, tiled=True)
+    both = jnp.concatenate([mine, other])
     outward = pl.pallas_call(
         outward_kernel,
         out_shape=jax.ShapeDtypeStruct((nz, padded, slab // 2), F32),
@@ -272,29 +291,36 @@
         out_specs=VMEM,
         compiler_params=params(8),
     )(where, columns)
-    ring = {0: mine}
-    up = down = mine
+    ring = {}
+    up = down = both
     for step in range(1, nz // 2 - 1):
-        up, down = tuple(shift(v, "z", 1) for v in up), tuple(shift(v, "z", -1) for v in down)
+        up, down = shift(up, "z", 1), shift(down, "z", -1)
         ring[nz - step], ring[step] = up, down
-    up, down, outward = lax.optimization_barrier((up, down, outward))
-    other = swap(outward, "yh")
+    far = {r: swap(ring[r], "c") for r in (1, nz - 1)}
+    outward, other_far = swap(outward, "yh"), swap(other, "c")
+    up, down, outward, far, other_far = lax.optimization_barrier((up, down, outward, far, other_far))
     kept, sent = pl.pallas_call(
         inward_kernel,
         out_shape=(jax.ShapeDtypeStruct((nz, padded, 2 * padded), F32),) * 2,
         in_specs=[SMEM, VMEM, VMEM],
         out_specs=(VMEM, VMEM),
         compiler_params=params(8),
-    )(where, columns, other)
+    )(where, columns, outward)
     taken = swap(sent, "c")
-    last = (tuple(shift(v, "z", -1) for v in down), tuple(shift(v, "z", 1) for v in up))
-    last += ((shift(up[0], "z", 2), shift(down[1], "z", -2)),)
-
-    def crossed(pieces):
-        return [v for piece in pieces for v in (*piece, *(swap(v, "c") for v in piece))]
+    half = jax.ShapeDtypeStruct((padded, nvir), BF16)
+    half_up, half_down = pl.pallas_call(
+        halves_kernel,
+        out_shape=(half, half),
+        in_specs=[VMEM, VMEM],
+        out_specs=(VMEM, VMEM),
+        compiler_params=params(8),
+    )(up, down)
+    last = (shift(down, "z", -1), shift(up, "z", 1), shift(half_up, "z", 2), shift(half_down, "z", -2))
 
     soon = (0, 1, nz - 1, 2, nz - 2)
     late = (3, nz - 3, nz // 2)
+    far.update({r: swap(ring[r], "c") for r in (2, nz - 2)})
+    pieces = [v for r in soon[1:] for v in (ring[r], far[r])]
     state = pl.pallas_call(
         functools.partial(early_kernel, soon, nz, width, padded),
         out_shape=(
@@ -303,20 +329,31 @@
             rows16,
             jax.ShapeDtypeStruct((nz, 2, padded, 2 * padded), BF16),
         ),
-        in_specs=[SMEM] + [VMEM] * (3 + 4 * len(soon)),
+        in_specs=[SMEM] + [VMEM] * (4 + 2 * len(soon)),
         out_specs=(VMEM,) * 4,
         compiler_params=params(16),
         cost_estimate=cost(len(soon) * 8 * padded * padded * nvir, len(soon) * 8 * padded * nvir),
-    )(where, amp_rows, kept, taken, *crossed(ring[r] for r in soon))
+    )(where, amp_rows, kept, taken, both, mine_far, other_far, *pieces)
     last, state = lax.optimization_barrier((last, state))
     added = pl.pallas_call(
         functools.partial(late_kernel, late, nz, width, padded),
         out_shape=jax.ShapeDtypeStruct((nz, padded, slab), F32),
-        in_specs=[SMEM] + [VMEM] * (4 + 4 * len(late)),
+        in_specs=[SMEM] + [VMEM] * (6 + 2 * len(late)),
         out_specs=VMEM,
         compiler_params=params(16),
         cost_estimate=cost(len(late) * 8 * padded * padded * nvir, len(late) * 8 * padded * nvir),
-    )(where, *state, *crossed(last))
+    )(
+        where,
+        *state,
+        last[0],
+        swap(last[0], "c"),
+        last[1],
+        swap(last[1], "c"),
+        last[2],
+        last[3],
+        swap(last[2], "c"),
+        swap(last[3], "c"),
+    )
     added = lax.all_to_all(added, SLABS, split_axis=0, concat_axis=0, tiled=True)
     return jnp.sum(added, axis=0)[:width]
 

time: 179 us -> 184 us (1.028)
  waiting for transfers between devices: 39.7 us -> 57.2 us
  starting transfers between devices: 47.7 us -> 35.9 us
    ppermute x22 -> x16, waiting for transfers between devices: 28 us -> 45.1 us  [shift(): lax.ppermute(value, axis, [(i, (i + step) % size) for i in range(size)])]
    ppermute x22 -> x16, starting transfers between devices: 34.7 us -> 22.2 us  [shift(): lax.ppermute(value, axis, [(i, (i + step) % size) for i in range(size)])]
    all_to_all x1, starting transfers between devices: 5.45 us -> 7.87 us  [local(): lax.all_to_all(columns, 'z', split_axis=0, concat_axis=0, tiled=True)]
    ppermute x20 -> x14, starting transfers between devices: 7.47 us -> 5.84 us  [swap(): return lax.ppermute(value, axis, [(0, 1), (1, 0)])]
    ppermute x20 -> x14, waiting for transfers between devices: 11.7 us -> 12.1 us  [swap(): return lax.ppermute(value, axis, [(0, 1), (1, 0)])]
  transfers between devices with their start and end apart: 43 -> 31, of which waited for: 20 -> 15; matrix products, arithmetic and copies ran while one was open for 0% -> 0% of each run, Pallas kernels for 7% -> 7%
where the time goes in v5:
time: 184 us; the launch traced here: 183 us
  blocking collectives  59.8 us (32%)
  waiting for transfers between devices  57.2 us (31%)
  starting transfers between devices  35.9 us (20%)
  Pallas kernels  20.2 us (11%)
  local copies, waits for them, and re-layouts  7.97 us (4%)
  other arithmetic  1.87 us (1%)
    all_to_all x1, blocking collectives, local(): lax.all_to_all(outgoing, ('yh', 'x', 'yl'), split_axis=0, concat_axis=0,...  48.4 us
    ppermute x16, waiting for transfers between devices, shift(): lax.ppermute(value, axis, [(i, (i + step) % size) for i in range(size)])  45.1 us
    ppermute x16, starting transfers between devices, shift(): lax.ppermute(value, axis, [(i, (i + step) % size) for i in range(size)])  22.2 us
    ppermute x14, waiting for transfers between devices, swap(): return lax.ppermute(value, axis, [(0, 1), (1, 0)])  12.1 us
    all_to_all x1, blocking collectives, local(): lax.all_to_all(added, SLABS, split_axis=0, concat_axis=0, tiled=True)  11.5 us
    all_to_all x1, starting transfers between devices, local(): lax.all_to_all(columns, 'z', split_axis=0, concat_axis=0, tiled=True)  7.87 us
    ppermute x14, starting transfers between devices, swap(): return lax.ppermute(value, axis, [(0, 1), (1, 0)])  5.84 us
    pallas_call x1, Pallas kernels, local(): pl.pallas_call(functools.partial(early_kernel, soon, nz, width, padded),...  3.89 us
  transfers between devices with their start and end apart: 31, of which 15 were waited for; matrix products, arithmetic and copies ran while one was open for 0% of the time, Pallas kernels for 7%

profile of v5, /device:TPU:32, one launch (start us, length us, event | category | flops | bytes accessed | tf_op | source)
XLA Modules:
  0.0 183.3 jit_solution(16245981121362268923)
XLA Ops:
  3.0 1.7 gather_fusion.1
  4.7 1.4 broadcast_in_dim.5
  6.5 48.4 %all_to_all.15.near_ref = bf16[16,272,300]{2,1,0:T(8,128)(2,1)} all-to-all(bf16[16,272,300]{2,1,0:T(8,128)(2,1)S(1)} %bitcast.17), channel_id=1, replica_groups=mesh['x'=4,'yl'=2,'z'=8,'yh'=2,'c'=2] {'yh','x','yl'}, dimensions={0} | all-to-all | bytes 5222400 | tf_op jit(solution)/shard_map/all_to_all | solution.py:226
  54.9 3.3 %shard_map.46.near_part_ref = f32[8,48,1408]{2,1,0:T(8,128)S(1)} custom-call(s32[7]{0:T(128)S(1)} %stack.27.where_ref, bf16[16,272,300]{2,1,0:T(8,128)(2,1)} %all_to_all.15.near_ref), custom_call_target="tpu_custom_call" | custom-call | flops 648806400 | tf_op jit(solution)/shard_map/pallas_call | solution.py:233
  58.3 2.8 %collective-permute-done.far_ref = bf16[16,272,300]{2,1,0:T(8,128)(2,1)} collective-permute-done((bf16[16,272,300]{2,1,0:T(8,128)(2,1)}, bf16[16,272,300]{2,1,0:T(8,128)(2,1)}, u32[]{:S(2)}, u32[]{:S(2)}) %collective-permute-start) | collective-permute-done | bytes 2611232 | tf_op jit(solution)/shard_map/ppermute | solution.py:23
  61.1 2.7 %shard_map.48 = (f32[24,1408]{1,0:T(8,128)S(1)}, f32[24,1408]{1,0:T(8,128)S(1)}) custom-call(s32[7]{0:T(128)S(1)} %stack.27.where_ref, f32[8,48,1408]{2,1,0:T(8,128)S(1)} %shard_map.46.near_part_ref, bf16[16,272,300]{2,1,0:T(8,128)(2,1)} %collective-permute-done.far_ref), custom_call_target="tpu_custom_call" | custom-call | flops 81100800 | tf_op jit(solution)/shard_map/pallas_call | solution.py:241
  63.8 2.0 %collective-permute-start.1 = (f32[24,1408]{1,0:T(8,128)S(1)}, f32[24,1408]{1,0:T(8,128)S(1)}, u32[]{:S(2)}, u32[]{:S(2)}) collective-permute-start(f32[24,1408]{1,0:T(8,128)S(1)} %get-tuple-element.40), channel_id=1, source_target_pairs={{0,4},{4,8},{8,12},{12,16},{16,20},{20,24},{24,28},{28,0},{1,5},{5... | collective-permute-start | bytes 405512 | tf_op jit(solution)/shard_map/ppermute | solution.py:28
  66.0 1.6 copy-done.2
  67.6 3.4 %shard_map.47 = (f32[8,48,1408]{2,1,0:T(8,128)S(1)}, f32[48,1408]{1,0:T(8,128)S(1)}) custom-call(s32[7]{0:T(128)S(1)} %stack.27.where_ref, s32[8,2]{1,0:T(8,128)S(1)} %copy.11.pair_ref, f32[16]{0:T(128)S(1)} %copy-done.5, f32[1,1408]{1,0:T(1,128)S(1)} %broadcast_in_dim.4.vir_ref, f32[8,48,1408]{2,1,0:T(8,128)S(1)} %copy-done.2, ...), custom_call_target="tpu_custom_call" | custom-call | flops 648806400 | tf_op jit(solution)/shard_map/pallas_call | solution.py:250
  71.9 3.2 %collective-permute-start.3 = (f32[48,1408]{1,0:T(8,128)S(1)}, f32[48,1408]{1,0:T(8,128)S(1)}, u32[]{:S(2)}, u32[]{:S(2)}) collective-permute-start(f32[48,1408]{1,0:T(8,128)S(1)} %get-tuple-element.42), channel_id=1, source_target_pairs={{0,4},{4,8},{8,12},{12,16},{16,20},{20,24},{24,28},{28,0},{1,5},{5... | collective-permute-start | bytes 811016 | tf_op jit(solution)/shard_map/ppermute | solution.py:28
  75.8 6.4 %collective-permute-done.3.up_in = f32[48,1408]{1,0:T(8,128)S(1)} collective-permute-done((f32[48,1408]{1,0:T(8,128)S(1)}, f32[48,1408]{1,0:T(8,128)S(1)}, u32[]{:S(2)}, u32[]{:S(2)}) %collective-permute-start.3) | collective-permute-done | bytes 270368 | tf_op jit(solution)/shard_map/ppermute | solution.py:28
  84.0 2.5 %collective-permute-start.5 = (f32[48,1408]{1,0:T(8,128)S(1)}, f32[48,1408]{1,0:T(8,128)S(1)}, u32[]{:S(2)}, u32[]{:S(2)}) collective-permute-start(f32[48,1408]{1,0:T(8,128)S(1)} %get-tuple-element.44), channel_id=1, source_target_pairs={{0,4},{4,8},{8,12},{12,16},{16,20},{20,24},{24,28},{28,0},{1,5},{5... | collective-permute-start | bytes 811016 | tf_op jit(solution)/shard_map/ppermute | solution.py:28
  86.5 5.0 %collective-permute-done.5.up_in = f32[48,1408]{1,0:T(8,128)S(1)} collective-permute-done((f32[48,1408]{1,0:T(8,128)S(1)}, f32[48,1408]{1,0:T(8,128)S(1)}, u32[]{:S(2)}, u32[]{:S(2)}) %collective-permute-start.5) | collective-permute-done | bytes 270368 | tf_op jit(solution)/shard_map/ppermute | solution.py:28
  91.5 2.7 %collective-permute-done.6.down_in = f32[48,1408]{1,0:T(8,128)S(1)} collective-permute-done((f32[48,1408]{1,0:T(8,128)S(1)}, f32[48,1408]{1,0:T(8,128)S(1)}, u32[]{:S(2)}, u32[]{:S(2)}) %collective-permute-start.6) | collective-permute-done | bytes 270368 | tf_op jit(solution)/shard_map/ppermute | solution.py:28
  94.8 1.8 collective-permute-start.7
  96.9 4.4 %collective-permute-done.7.up_in = f32[48,1408]{1,0:T(8,128)S(1)} collective-permute-done((f32[48,1408]{1,0:T(8,128)S(1)}, f32[48,1408]{1,0:T(8,128)S(1)}, u32[]{:S(2)}, u32[]{:S(2)}) %collective-permute-start.7) | collective-permute-done | bytes 270368 | tf_op jit(solution)/shard_map/ppermute | solution.py:28
  101.3 1.7 collective-permute-done.8.down_in
  103.8 1.9 %collective-permute-start.9 = (bf16[48,1408]{1,0:T(8,128)(2,1)S(1)}, bf16[48,1408]{1,0:T(8,128)(2,1)S(1)}, u32[]{:S(2)}, u32[]{:S(2)}) collective-permute-start(bf16[48,1408]{1,0:T(8,128)(2,1)S(1)} %get-tuple-element.49), channel_id=1, source_target_pairs={{0,2},{2,0},{1,3},{3,1},{4,6},{6,4},{5,7},{7,5},{8,10},{10,8},{9,1... | collective-permute-start | bytes 405512 | tf_op jit(solution)/shard_map/ppermute | solution.py:23
  105.7 5.6 %collective-permute-done.9 = bf16[48,1408]{1,0:T(8,128)(2,1)S(1)} collective-permute-done((bf16[48,1408]{1,0:T(8,128)(2,1)S(1)}, bf16[48,1408]{1,0:T(8,128)(2,1)S(1)}, u32[]{:S(2)}, u32[]{:S(2)}) %collective-permute-start.9) | collective-permute-done | bytes 135200 | tf_op jit(solution)/shard_map/ppermute | solution.py:23
  112.6 7.9 %all-to-all-start.1 = ((f32[8,48,176]{2,1,0:T(8,128)}), f32[8,48,176]{2,1,0:T(8,128)S(1)}, u32[]{:S(2)}, u32[]{:S(2)}) async-start(f32[8,48,176]{2,1,0:T(8,128)} %shard_map.53), calls=%async_computation.1 | async-start | bytes 786432 | tf_op jit(solution)/shard_map/all_to_all | solution.py:285
  120.5 1.5 collective-permute-start.10
  122.5 12.2 %collective-permute-done.10.refs_5_ = bf16[96,1408]{1,0:T(8,128)(2,1)} collective-permute-done((bf16[96,1408]{1,0:T(8,128)(2,1)S(1)}, bf16[96,1408]{1,0:T(8,128)(2,1)}, u32[]{:S(2)}, u32[]{:S(2)}) %collective-permute-start.10) | collective-permute-done | bytes 270368 | tf_op jit(solution)/shard_map/ppermute | solution.py:28
  134.7 1.5 collective-permute-start.11
  137.5 1.7 collective-permute-start.15
  139.2 4.3 %collective-permute-done.11.up_ref.refs_9_ = bf16[96,1408]{1,0:T(8,128)(2,1)S(1)} collective-permute-done((bf16[96,1408]{1,0:T(8,128)(2,1)}, bf16[96,1408]{1,0:T(8,128)(2,1)S(1)}, u32[]{:S(2)}, u32[]{:S(2)}) %collective-permute-start.11) | collective-permute-done | bytes 270368 | tf_op jit(solution)/shard_map/ppermute | solution.py:28
  143.6 2.4 %collective-permute-done.15.other_ref = f32[8,48,88]{2,1,0:T(8,128)S(1)} collective-permute-done((f32[8,48,88]{2,1,0:T(8,128)S(1)}, f32[8,48,88]{2,1,0:T(8,128)S(1)}, u32[]{:S(2)}, u32[]{:S(2)}) %collective-permute-start.15) | collective-permute-done | bytes 135200 | tf_op jit(solution)/shard_map/ppermute | solution.py:23
  147.7 1.5 collective-permute-start.19
  149.8 5.1 %collective-permute-start.21 = (bf16[48,1408]{1,0:T(8,128)(2,1)S(1)}, bf16[48,1408]{1,0:T(8,128)(2,1)S(1)}, u32[]{:S(2)}, u32[]{:S(2)}) collective-permute-start(bf16[48,1408]{1,0:T(8,128)(2,1)S(1)} %get-tuple-element.53), channel_id=1, source_target_pairs={{0,8},{4,12},{8,16},{12,20},{16,24},{20,28},{24,0},{28,4},{1,9},{5... | collective-permute-start | bytes 405512 | tf_op jit(solution)/shard_map/ppermute | solution.py:28
  156.5 3.9 %shard_map.57 = (f32[48,1408]{1,0:T(8,128)S(1)}, f32[8,48,176]{2,1,0:T(8,128)S(1)}, bf16[48,1408]{1,0:T(8,128)(2,1)S(1)}, bf16[8,2,48,96]{3,2,1,0:T(8,128)(2,1)S(1)}) custom-call(s32[7]{0:T(128)S(1)} %stack.27.where_ref, f32[48,1408]{1,0:T(8,128)S(1)} %get-tuple-element.50.rows_ref, f32[8,48,96]{2,1,0:T(8,128)S(1)} %get-tuple-element.56.near_ref, ...), custom_call_target="tpu_custom_call" | custom-call | flops 129761280 | bytes 2703360 | tf_op jit(solution)/shard_map/pallas_call | solution.py:324
  160.4 6.7 %collective-permute-done.21.refs_4_ = bf16[48,1408]{1,0:T(8,128)(2,1)S(1)} collective-permute-done((bf16[48,1408]{1,0:T(8,128)(2,1)S(1)}, bf16[48,1408]{1,0:T(8,128)(2,1)S(1)}, u32[]{:S(2)}, u32[]{:S(2)}) %collective-permute-start.21) | collective-permute-done | bytes 135200 | tf_op jit(solution)/shard_map/ppermute | solution.py:28
  169.5 1.6 shard_map.58
  171.1 11.5 %all_to_all.16 = f32[8,48,176]{2,1,0:T(8,128)S(1)} all-to-all(f32[8,48,176]{2,1,0:T(8,128)S(1)} %shard_map.58), channel_id=1, replica_groups=mesh['x'=4,'yl'=2,'z'=8,'yh'=2,'c'=2] {'x','yl'}, dimensions={0} | all-to-all | bytes 540672 | tf_op jit(solution)/shard_map/all_to_all | solution.py:357
  (78 shorter events, 18.7 us)
Async XLA Ops:
  54.8 6.3 %collective-permute-start = (bf16[16,272,300]{2,1,0:T(8,128)(2,1)}, bf16[16,272,300]{2,1,0:T(8,128)(2,1)}, u32[]{:S(2)}, u32[]{:S(2)}) collective-permute-start(bf16[16,272,300]{2,1,0:T(8,128)(2,1)} %all_to_all.15.near_ref), channel_id=1, source_target_pairs={{0,1},{1,0},{2,3},{3,2},{4,5},{5,4},{6,7},{7,6},{8,9},{9,8},{10,11... | collective-permute-start | bytes 7833608 | tf_op jit(solution)/shard_map/ppermute | solution.py:23
  63.8 7.2 %collective-permute-start.1 = (f32[24,1408]{1,0:T(8,128)S(1)}, f32[24,1408]{1,0:T(8,128)S(1)}, u32[]{:S(2)}, u32[]{:S(2)}) collective-permute-start(f32[24,1408]{1,0:T(8,128)S(1)} %get-tuple-element.40), channel_id=1, source_target_pairs={{0,4},{4,8},{8,12},{12,16},{16,20},{20,24},{24,28},{28,0},{1,5},{5... | collective-permute-start | bytes 405512 | tf_op jit(solution)/shard_map/ppermute | solution.py:28
  65.8 5.5 %collective-permute-start.2 = (f32[24,1408]{1,0:T(8,128)S(1)}, f32[24,1408]{1,0:T(8,128)S(1)}, u32[]{:S(2)}, u32[]{:S(2)}) collective-permute-start(f32[24,1408]{1,0:T(8,128)S(1)} %get-tuple-element.41), channel_id=1, source_target_pairs={{0,28},{4,0},{8,4},{12,8},{16,12},{20,16},{24,20},{28,24},{1,29},{... | collective-permute-start | bytes 405512 | tf_op jit(solution)/shard_map/ppermute | solution.py:28
  71.9 10.3 %collective-permute-start.3 = (f32[48,1408]{1,0:T(8,128)S(1)}, f32[48,1408]{1,0:T(8,128)S(1)}, u32[]{:S(2)}, u32[]{:S(2)}) collective-permute-start(f32[48,1408]{1,0:T(8,128)S(1)} %get-tuple-element.42), channel_id=1, source_target_pairs={{0,4},{4,8},{8,12},{12,16},{16,20},{20,24},{24,28},{28,0},{1,5},{5... | collective-permute-start | bytes 811016 | tf_op jit(solution)/shard_map/ppermute | solution.py:28
  75.1 8.3 %collective-permute-start.4 = (f32[48,1408]{1,0:T(8,128)S(1)}, f32[48,1408]{1,0:T(8,128)S(1)}, u32[]{:S(2)}, u32[]{:S(2)}) collective-permute-start(f32[48,1408]{1,0:T(8,128)S(1)} %get-tuple-element.43), channel_id=1, source_target_pairs={{0,28},{4,0},{8,4},{12,8},{16,12},{20,16},{24,20},{28,24},{1,29},{... | collective-permute-start | bytes 811016 | tf_op jit(solution)/shard_map/ppermute | solution.py:28
  84.0 7.5 %collective-permute-start.5 = (f32[48,1408]{1,0:T(8,128)S(1)}, f32[48,1408]{1,0:T(8,128)S(1)}, u32[]{:S(2)}, u32[]{:S(2)}) collective-permute-start(f32[48,1408]{1,0:T(8,128)S(1)} %get-tuple-element.44), channel_id=1, source_target_pairs={{0,4},{4,8},{8,12},{12,16},{16,20},{20,24},{24,28},{28,0},{1,5},{5... | collective-permute-start | bytes 811016 | tf_op jit(solution)/shard_map/ppermute | solution.py:28
  86.5 7.7 %collective-permute-start.6 = (f32[48,1408]{1,0:T(8,128)S(1)}, f32[48,1408]{1,0:T(8,128)S(1)}, u32[]{:S(2)}, u32[]{:S(2)}) collective-permute-start(f32[48,1408]{1,0:T(8,128)S(1)} %get-tuple-element.45), channel_id=1, source_target_pairs={{0,28},{4,0},{8,4},{12,8},{16,12},{20,16},{24,20},{28,24},{1,29},{... | collective-permute-start | bytes 811016 | tf_op jit(solution)/shard_map/ppermute | solution.py:28
  94.8 6.5 %collective-permute-start.7 = (f32[48,1408]{1,0:T(8,128)S(1)}, f32[48,1408]{1,0:T(8,128)S(1)}, u32[]{:S(2)}, u32[]{:S(2)}) collective-permute-start(f32[48,1408]{1,0:T(8,128)S(1)} %get-tuple-element.46), channel_id=1, source_target_pairs={{0,4},{4,8},{8,12},{12,16},{16,20},{20,24},{24,28},{28,0},{1,5},{5... | collective-permute-start | bytes 811016 | tf_op jit(solution)/shard_map/ppermute | solution.py:28
  96.6 6.5 %collective-permute-start.8 = (f32[48,1408]{1,0:T(8,128)S(1)}, f32[48,1408]{1,0:T(8,128)S(1)}, u32[]{:S(2)}, u32[]{:S(2)}) collective-permute-start(f32[48,1408]{1,0:T(8,128)S(1)} %get-tuple-element.47), channel_id=1, source_target_pairs={{0,28},{4,0},{8,4},{12,8},{16,12},{20,16},{24,20},{28,24},{1,29},{... | collective-permute-start | bytes 811016 | tf_op jit(solution)/shard_map/ppermute | solution.py:28
  103.7 8.0 %collective-permute-start.14 = (bf16[48,1408]{1,0:T(8,128)(2,1)S(1)}, bf16[48,1408]{1,0:T(8,128)(2,1)S(1)}, u32[]{:S(2)}, u32[]{:S(2)}) collective-permute-start(bf16[48,1408]{1,0:T(8,128)(2,1)S(1)} %get-tuple-element.49), channel_id=1, source_target_pairs={{0,1},{1,0},{2,3},{3,2},{4,5},{5,4},{6,7},{7,6},{8,9},{9,8},{10,11... | collective-permute-start | bytes 405512 | tf_op jit(solution)/shard_map/ppermute | solution.py:23
  103.8 7.5 %collective-permute-start.9 = (bf16[48,1408]{1,0:T(8,128)(2,1)S(1)}, bf16[48,1408]{1,0:T(8,128)(2,1)S(1)}, u32[]{:S(2)}, u32[]{:S(2)}) collective-permute-start(bf16[48,1408]{1,0:T(8,128)(2,1)S(1)} %get-tuple-element.49), channel_id=1, source_target_pairs={{0,2},{2,0},{1,3},{3,1},{4,6},{6,4},{5,7},{7,5},{8,10},{10,8},{9,1... | collective-permute-start | bytes 405512 | tf_op jit(solution)/shard_map/ppermute | solution.py:23
  111.3 11.2 %copy-start.3 = (bf16[96,1408]{1,0:T(8,128)(2,1)}, bf16[96,1408]{1,0:T(8,128)(2,1)S(1)}, u32[]{:S(2)}) copy-start(bf16[96,1408]{1,0:T(8,128)(2,1)S(1)} %constant_dynamic-update-slice_fusion.refs_0_) | copy-start | bytes 811012
  111.3 10.6 %collective-permute-start.12 = (bf16[96,1408]{1,0:T(8,128)(2,1)S(1)}, bf16[96,1408]{1,0:T(8,128)(2,1)}, u32[]{:S(2)}, u32[]{:S(2)}) collective-permute-start(bf16[96,1408]{1,0:T(8,128)(2,1)S(1)} %constant_dynamic-update-slice_fusion.refs_0_), channel_id=1, source_target_pairs={{0,28},{4,0},{8,4},{12,8},{16,12},{20,16},{24,20},{28,24},{1,29},{... | collective-permute-start | bytes 811016 | tf_op jit(solution)/shard_map/ppermute | solution.py:28
  112.6 24.1 %all-to-all-start.1 = ((f32[8,48,176]{2,1,0:T(8,128)}), f32[8,48,176]{2,1,0:T(8,128)S(1)}, u32[]{:S(2)}, u32[]{:S(2)}) async-start(f32[8,48,176]{2,1,0:T(8,128)} %shard_map.53), calls=%async_computation.1 | async-start | bytes 786432 | tf_op jit(solution)/shard_map/all_to_all | solution.py:285
  120.5 14.2 %collective-permute-start.10 = (bf16[96,1408]{1,0:T(8,128)(2,1)S(1)}, bf16[96,1408]{1,0:T(8,128)(2,1)}, u32[]{:S(2)}, u32[]{:S(2)}) collective-permute-start(bf16[96,1408]{1,0:T(8,128)(2,1)S(1)} %constant_dynamic-update-slice_fusion.refs_0_), channel_id=1, source_target_pairs={{0,4},{4,8},{8,12},{12,16},{16,20},{20,24},{24,28},{28,0},{1,5},{5... | collective-permute-start | bytes 811016 | tf_op jit(solution)/shard_map/ppermute | solution.py:28
  121.9 17.3 %collective-permute-start.13 = (bf16[96,1408]{1,0:T(8,128)(2,1)}, bf16[96,1408]{1,0:T(8,128)(2,1)S(1)}, u32[]{:S(2)}, u32[]{:S(2)}) collective-permute-start(bf16[96,1408]{1,0:T(8,128)(2,1)} %collective-permute-done.12.refs_3_), channel_id=1, source_target_pairs={{0,28},{4,0},{8,4},{12,8},{16,12},{20,16},{24,20},{28,24},{1,29},{... | collective-permute-start | bytes 811016 | tf_op jit(solution)/shard_map/ppermute | solution.py:28
  122.5 15.0 %collective-permute-start.18 = (bf16[48,1408]{1,0:T(8,128)(2,1)}, bf16[48,1408]{1,0:T(8,128)(2,1)}, u32[]{:S(2)}, u32[]{:S(2)}) collective-permute-start(bf16[48,1408]{1,0:T(8,128)(2,1)} %copy-done.6), channel_id=1, source_target_pairs={{0,1},{1,0},{2,3},{3,2},{4,5},{5,4},{6,7},{7,6},{8,9},{9,8},{10,11... | collective-permute-start | bytes 405512 | tf_op jit(solution)/shard_map/ppermute | solution.py:23
  134.7 8.9 %collective-permute-start.11 = (bf16[96,1408]{1,0:T(8,128)(2,1)}, bf16[96,1408]{1,0:T(8,128)(2,1)S(1)}, u32[]{:S(2)}, u32[]{:S(2)}) collective-permute-start(bf16[96,1408]{1,0:T(8,128)(2,1)} %collective-permute-done.10.refs_5_), channel_id=1, source_target_pairs={{0,4},{4,8},{8,12},{12,16},{16,20},{20,24},{24,28},{28,0},{1,5},{5... | collective-permute-start | bytes 811016 | tf_op jit(solution)/shard_map/ppermute | solution.py:28
  136.2 7.4 %collective-permute-start.16 = (bf16[96,1408]{1,0:T(8,128)(2,1)}, bf16[96,1408]{1,0:T(8,128)(2,1)}, u32[]{:S(2)}, u32[]{:S(2)}) collective-permute-start(bf16[96,1408]{1,0:T(8,128)(2,1)} %collective-permute-done.12.refs_3_), channel_id=1, source_target_pairs={{0,1},{1,0},{2,3},{3,2},{4,5},{5,4},{6,7},{7,6},{8,9},{9,8},{10,11... | collective-permute-start | bytes 811016 | tf_op jit(solution)/shard_map/ppermute | solution.py:23
  136.2 7.4 %collective-permute-start.17 = (bf16[96,1408]{1,0:T(8,128)(2,1)}, bf16[96,1408]{1,0:T(8,128)(2,1)}, u32[]{:S(2)}, u32[]{:S(2)}) collective-permute-start(bf16[96,1408]{1,0:T(8,128)(2,1)} %collective-permute-done.10.refs_5_), channel_id=1, source_target_pairs={{0,1},{1,0},{2,3},{3,2},{4,5},{5,4},{6,7},{7,6},{8,9},{9,8},{10,11... | collective-permute-start | bytes 811016 | tf_op jit(solution)/shard_map/ppermute | solution.py:23
  137.5 8.4 %collective-permute-start.15 = (f32[8,48,88]{2,1,0:T(8,128)S(1)}, f32[8,48,88]{2,1,0:T(8,128)S(1)}, u32[]{:S(2)}, u32[]{:S(2)}) collective-permute-start(f32[8,48,88]{2,1,0:T(8,128)S(1)} %shard_map.54), channel_id=1, source_target_pairs={{0,2},{2,0},{1,3},{3,1},{4,6},{6,4},{5,7},{7,5},{8,10},{10,8},{9,1... | collective-permute-start | bytes 405512 | tf_op jit(solution)/shard_map/ppermute | solution.py:23
  139.2 15.7 %collective-permute-start.24 = (bf16[96,1408]{1,0:T(8,128)(2,1)S(1)}, bf16[96,1408]{1,0:T(8,128)(2,1)S(1)}, u32[]{:S(2)}, u32[]{:S(2)}) collective-permute-start(bf16[96,1408]{1,0:T(8,128)(2,1)S(1)} %collective-permute-done.13.down_ref.refs_7_), channel_id=1, source_target_pairs={{0,1},{1,0},{2,3},{3,2},{4,5},{5,4},{6,7},{7,6},{8,9},{9,8},{10,11... | collective-permute-start | bytes 811016 | tf_op jit(solution)/shard_map/ppermute | solution.py:23
  147.1 2.7 %collective-permute-start.23 = (f32[8,48,96]{2,1,0:T(8,128)S(1)}, f32[8,48,96]{2,1,0:T(8,128)S(1)}, u32[]{:S(2)}, u32[]{:S(2)}) collective-permute-start(f32[8,48,96]{2,1,0:T(8,128)S(1)} %get-tuple-element.57), channel_id=1, source_target_pairs={{0,1},{1,0},{2,3},{3,2},{4,5},{5,4},{6,7},{7,6},{8,9},{9,8},{10,11... | collective-permute-start | bytes 442376 | tf_op jit(solution)/shard_map/ppermute | solution.py:23
  147.2 8.3 %collective-permute-start.25 = (bf16[96,1408]{1,0:T(8,128)(2,1)S(1)}, bf16[96,1408]{1,0:T(8,128)(2,1)S(1)}, u32[]{:S(2)}, u32[]{:S(2)}) collective-permute-start(bf16[96,1408]{1,0:T(8,128)(2,1)S(1)} %collective-permute-done.11.up_ref.refs_9_), channel_id=1, source_target_pairs={{0,1},{1,0},{2,3},{3,2},{4,5},{5,4},{6,7},{7,6},{8,9},{9,8},{10,11... | collective-permute-start | bytes 811016 | tf_op jit(solution)/shard_map/ppermute | solution.py:23
  147.7 19.4 %collective-permute-start.19 = (bf16[96,1408]{1,0:T(8,128)(2,1)S(1)}, bf16[96,1408]{1,0:T(8,128)(2,1)S(1)}, u32[]{:S(2)}, u32[]{:S(2)}) collective-permute-start(bf16[96,1408]{1,0:T(8,128)(2,1)S(1)} %collective-permute-done.13.down_ref.refs_7_), channel_id=1, source_target_pairs={{0,28},{4,0},{8,4},{12,8},{16,12},{20,16},{24,20},{28,24},{1,29},{... | collective-permute-start | bytes 811016 | tf_op jit(solution)/shard_map/ppermute | solution.py:28
  149.2 17.9 %collective-permute-start.20 = (bf16[96,1408]{1,0:T(8,128)(2,1)S(1)}, bf16[96,1408]{1,0:T(8,128)(2,1)S(1)}, u32[]{:S(2)}, u32[]{:S(2)}) collective-permute-start(bf16[96,1408]{1,0:T(8,128)(2,1)S(1)} %collective-permute-done.11.up_ref.refs_9_), channel_id=1, source_target_pairs={{0,4},{4,8},{8,12},{12,16},{16,20},{20,24},{24,28},{28,0},{1,5},{5... | collective-permute-start | bytes 811016 | tf_op jit(solution)/shard_map/ppermute | solution.py:28
  149.8 17.3 %collective-permute-start.21 = (bf16[48,1408]{1,0:T(8,128)(2,1)S(1)}, bf16[48,1408]{1,0:T(8,128)(2,1)S(1)}, u32[]{:S(2)}, u32[]{:S(2)}) collective-permute-start(bf16[48,1408]{1,0:T(8,128)(2,1)S(1)} %get-tuple-element.53), channel_id=1, source_target_pairs={{0,8},{4,12},{8,16},{12,20},{16,24},{20,28},{24,0},{28,4},{1,9},{5... | collective-permute-start | bytes 405512 | tf_op jit(solution)/shard_map/ppermute | solution.py:28
  154.9 12.2 %collective-permute-start.22 = (bf16[48,1408]{1,0:T(8,128)(2,1)S(1)}, bf16[48,1408]{1,0:T(8,128)(2,1)S(1)}, u32[]{:S(2)}, u32[]{:S(2)}) collective-permute-start(bf16[48,1408]{1,0:T(8,128)(2,1)S(1)} %get-tuple-element.54), channel_id=1, source_target_pairs={{0,24},{4,28},{8,0},{12,4},{16,8},{20,12},{24,16},{28,20},{1,25},{... | collective-permute-start | bytes 405512 | tf_op jit(solution)/shard_map/ppermute | solution.py:28
  167.1 2.4 %collective-permute-start.26 = (bf16[96,1408]{1,0:T(8,128)(2,1)S(1)}, bf16[96,1408]{1,0:T(8,128)(2,1)S(1)}, u32[]{:S(2)}, u32[]{:S(2)}) collective-permute-start(bf16[96,1408]{1,0:T(8,128)(2,1)S(1)} %collective-permute-done.19.refs_0_), channel_id=1, source_target_pairs={{0,1},{1,0},{2,3},{3,2},{4,5},{5,4},{6,7},{7,6},{8,9},{9,8},{10,11... | collective-permute-start | bytes 811016 | tf_op jit(solution)/shard_map/ppermute | solution.py:23
  167.2 2.3 %collective-permute-start.27 = (bf16[96,1408]{1,0:T(8,128)(2,1)S(1)}, bf16[96,1408]{1,0:T(8,128)(2,1)S(1)}, u32[]{:S(2)}, u32[]{:S(2)}) collective-permute-start(bf16[96,1408]{1,0:T(8,128)(2,1)S(1)} %collective-permute-done.20.refs_2_), channel_id=1, source_target_pairs={{0,1},{1,0},{2,3},{3,2},{4,5},{5,4},{6,7},{7,6},{8,9},{9,8},{10,11... | collective-permute-start | bytes 811016 | tf_op jit(solution)/shard_map/ppermute | solution.py:23
  167.7 1.6 collective-permute-start.28
  167.8 1.7 collective-permute-start.29
  (8 other events, 43.5 us)

commit v6 on v5

--- a/solution.py
+++ b/solution.py
@@ -103,7 +103,7 @@
     rounded_ref[...] = amps.astype(BF16)
 
 
-def blocks_kernel(rows_ref, after_ref, blocks_ref):
+def blocks_kernel(rows_ref, blocks_ref):
     slab = blocks_ref.shape[2]
     for k in range(blocks_ref.shape[0]):
         blocks_ref[k] = rows_ref[:, k * slab : (k + 1) * slab]
@@ -274,14 +274,14 @@
     )(where, part, up, down, denom)
 
     other = swap(mine, "yh")
-    mine_far = swap(mine, "c")
     columns = pl.pallas_call(
         blocks_kernel,
         out_shape=jax.ShapeDtypeStruct((nz, padded, slab), F32),
-        in_specs=[VMEM, VMEM],
+        in_specs=[VMEM],
         out_specs=VMEM,
         compiler_params=params(8),
-    )(amp_rows, mine_far)
+    )(amp_rows)
+    other, _ = lax.optimization_barrier((other, columns))
     columns = lax.all_to_all(columns, "z", split_axis=0, concat_axis=0, tiled=True)
     both = jnp.concatenate([mine, other])
     outward = pl.pallas_call(
@@ -296,9 +296,12 @@
     for step in range(1, nz // 2 - 1):
         up, down = shift(up, "z", 1), shift(down, "z", -1)
         ring[nz - step], ring[step] = up, down
+        if step == 1:
+            up, down, outward = lax.optimization_barrier((up, down, outward))
     far = {r: swap(ring[r], "c") for r in (1, nz - 1)}
-    outward, other_far = swap(outward, "yh"), swap(other, "c")
-    up, down, outward, far, other_far = lax.optimization_barrier((up, down, outward, far, other_far))
+    far[0] = swap(both, "c")
+    outward = swap(outward, "yh")
+    up, down, outward, far = lax.optimization_barrier((up, down, outward, far))
     kept, sent = pl.pallas_call(
         inward_kernel,
         out_shape=(jax.ShapeDtypeStruct((nz, padded, 2 * padded), F32),) * 2,
@@ -320,7 +323,8 @@
     soon = (0, 1, nz - 1, 2, nz - 2)
     late = (3, nz - 3, nz // 2)
     far.update({r: swap(ring[r], "c") for r in (2, nz - 2)})
-    pieces = [v for r in soon[1:] for v in (ring[r], far[r])]
+    ring[0] = both
+    pieces = [v for r in soon for v in (ring[r], far[r])]
     state = pl.pallas_call(
         functools.partial(early_kernel, soon, nz, width, padded),
         out_shape=(
@@ -329,11 +333,11 @@
             rows16,
             jax.ShapeDtypeStruct((nz, 2, padded, 2 * padded), BF16),
         ),
-        in_specs=[SMEM] + [VMEM] * (4 + 2 * len(soon)),
+        in_specs=[SMEM] + [VMEM] * (3 + 2 * len(soon)),
         out_specs=(VMEM,) * 4,
         compiler_params=params(16),
         cost_estimate=cost(len(soon) * 8 * padded * padded * nvir, len(soon) * 8 * padded * nvir),
-    )(where, amp_rows, kept, taken, both, mine_far, other_far, *pieces)
+    )(where, amp_rows, kept, taken, *pieces)
     last, state = lax.optimization_barrier((last, state))
     added = pl.pallas_call(
         functools.partial(late_kernel, late, nz, width, padded),

time: 184 us -> 172 us (0.935)
  waiting for transfers between devices: 57.2 us -> 50 us
  starting transfers between devices: 35.9 us -> 32.6 us
    ppermute x16, waiting for transfers between devices: 45.1 us -> 31.7 us  [shift(): lax.ppermute(value, axis, [(i, (i + step) % size) for i in range(size)])]
    all_to_all x1, waiting for transfers between devices: 0.01 us -> 10.3 us  [local(): lax.all_to_all(columns, 'z', split_axis=0, concat_axis=0, tiled=True)]
    ppermute x14 -> x13, waiting for transfers between devices: 12.1 us -> 8.03 us  [swap(): return lax.ppermute(value, axis, [(0, 1), (1, 0)])]
    all_to_all x1, starting transfers between devices: 7.87 us -> 5.46 us  [local(): lax.all_to_all(columns, 'z', split_axis=0, concat_axis=0, tiled=True)]
    ppermute x14 -> x13, starting transfers between devices: 5.84 us -> 5.74 us  [swap(): return lax.ppermute(value, axis, [(0, 1), (1, 0)])]
  transfers between devices with their start and end apart: 31 -> 30, of which waited for: 15 -> 15; matrix products, arithmetic and copies ran while one was open for 0% -> 0% of each run, Pallas kernels for 7% -> 7%
where the time goes in v6:
time: 172 us
  blocking collectives  59.8 us (35%)
  waiting for transfers between devices  50 us (29%)
  starting transfers between devices  32.6 us (19%)
  Pallas kernels  20 us (12%)
  local copies, waits for them, and re-layouts  7.03 us (4%)
  other arithmetic  1.87 us (1%)
    all_to_all x1, blocking collectives, local(): lax.all_to_all(outgoing, ('yh', 'x', 'yl'), split_axis=0, concat_axis=0,...  48.4 us
    ppermute x16, waiting for transfers between devices, shift(): lax.ppermute(value, axis, [(i, (i + step) % size) for i in range(size)])  31.7 us
    ppermute x16, starting transfers between devices, shift(): lax.ppermute(value, axis, [(i, (i + step) % size) for i in range(size)])  21.4 us
    all_to_all x1, blocking collectives, local(): lax.all_to_all(added, SLABS, split_axis=0, concat_axis=0, tiled=True)  11.5 us
    all_to_all x1, waiting for transfers between devices, local(): lax.all_to_all(columns, 'z', split_axis=0, concat_axis=0, tiled=True)  10.3 us
    ppermute x13, waiting for transfers between devices, swap(): return lax.ppermute(value, axis, [(0, 1), (1, 0)])  8.03 us
    ppermute x13, starting transfers between devices, swap(): return lax.ppermute(value, axis, [(0, 1), (1, 0)])  5.74 us
    all_to_all x1, starting transfers between devices, local(): lax.all_to_all(columns, 'z', split_axis=0, concat_axis=0, tiled=True)  5.46 us
  transfers between devices with their start and end apart: 30, of which 15 were waited for; matrix products, arithmetic and copies ran while one was open for 0% of the time, Pallas kernels for 7%

profile of v6, /device:TPU:32, one launch (start us, length us, event | category | flops | bytes accessed | tf_op | source)
XLA Modules:
  0.0 171.6 jit_solution(15513792975830558842)
XLA Ops:
  3.0 1.7 gather_fusion.1
  4.7 1.4 broadcast_in_dim.5
  6.5 48.4 %all_to_all.15.near_ref = bf16[16,272,300]{2,1,0:T(8,128)(2,1)} all-to-all(bf16[16,272,300]{2,1,0:T(8,128)(2,1)S(1)} %bitcast.17), channel_id=1, replica_groups=mesh['x'=4,'yl'=2,'z'=8,'yh'=2,'c'=2] {'yh','x','yl'}, dimensions={0} | all-to-all | bytes 5222400 | tf_op jit(solution)/shard_map/all_to_all | solution.py:226
  54.9 3.3 %shard_map.46.near_part_ref = f32[8,48,1408]{2,1,0:T(8,128)S(1)} custom-call(s32[7]{0:T(128)S(1)} %stack.27.where_ref, bf16[16,272,300]{2,1,0:T(8,128)(2,1)} %all_to_all.15.near_ref), custom_call_target="tpu_custom_call" | custom-call | flops 648806400 | tf_op jit(solution)/shard_map/pallas_call | solution.py:233
  58.3 2.8 %collective-permute-done.far_ref = bf16[16,272,300]{2,1,0:T(8,128)(2,1)} collective-permute-done((bf16[16,272,300]{2,1,0:T(8,128)(2,1)}, bf16[16,272,300]{2,1,0:T(8,128)(2,1)}, u32[]{:S(2)}, u32[]{:S(2)}) %collective-permute-start) | collective-permute-done | bytes 2611232 | tf_op jit(solution)/shard_map/ppermute | solution.py:23
  61.1 2.7 %shard_map.48 = (f32[24,1408]{1,0:T(8,128)S(1)}, f32[24,1408]{1,0:T(8,128)S(1)}) custom-call(s32[7]{0:T(128)S(1)} %stack.27.where_ref, f32[8,48,1408]{2,1,0:T(8,128)S(1)} %shard_map.46.near_part_ref, bf16[16,272,300]{2,1,0:T(8,128)(2,1)} %collective-permute-done.far_ref), custom_call_target="tpu_custom_call" | custom-call | flops 81100800 | tf_op jit(solution)/shard_map/pallas_call | solution.py:241
  63.8 2.0 %collective-permute-start.1 = (f32[24,1408]{1,0:T(8,128)S(1)}, f32[24,1408]{1,0:T(8,128)S(1)}, u32[]{:S(2)}, u32[]{:S(2)}) collective-permute-start(f32[24,1408]{1,0:T(8,128)S(1)} %get-tuple-element.44), channel_id=1, source_target_pairs={{0,4},{4,8},{8,12},{12,16},{16,20},{20,24},{24,28},{28,0},{1,5},{5... | collective-permute-start | bytes 405512 | tf_op jit(solution)/shard_map/ppermute | solution.py:28
  66.0 1.6 copy-done.2
  67.7 3.4 %shard_map.47 = (f32[8,48,1408]{2,1,0:T(8,128)S(1)}, f32[48,1408]{1,0:T(8,128)S(1)}) custom-call(s32[7]{0:T(128)S(1)} %stack.27.where_ref, s32[8,2]{1,0:T(8,128)S(1)} %copy.11.pair_ref, f32[16]{0:T(128)S(1)} %copy-done.3, f32[1,1408]{1,0:T(1,128)S(1)} %broadcast_in_dim.4.vir_ref, f32[8,48,1408]{2,1,0:T(8,128)S(1)} %copy-done.2, ...), custom_call_target="tpu_custom_call" | custom-call | flops 648806400 | tf_op jit(solution)/shard_map/pallas_call | solution.py:250
  71.9 3.2 %collective-permute-start.3 = (f32[48,1408]{1,0:T(8,128)S(1)}, f32[48,1408]{1,0:T(8,128)S(1)}, u32[]{:S(2)}, u32[]{:S(2)}) collective-permute-start(f32[48,1408]{1,0:T(8,128)S(1)} %get-tuple-element.46), channel_id=1, source_target_pairs={{0,4},{4,8},{8,12},{12,16},{16,20},{20,24},{24,28},{28,0},{1,5},{5... | collective-permute-start | bytes 811016 | tf_op jit(solution)/shard_map/ppermute | solution.py:28
  75.8 6.4 %collective-permute-done.3.up_in = f32[48,1408]{1,0:T(8,128)S(1)} collective-permute-done((f32[48,1408]{1,0:T(8,128)S(1)}, f32[48,1408]{1,0:T(8,128)S(1)}, u32[]{:S(2)}, u32[]{:S(2)}) %collective-permute-start.3) | collective-permute-done | bytes 270368 | tf_op jit(solution)/shard_map/ppermute | solution.py:28
  82.3 1.2 collective-permute-done.4.down_in
  84.1 2.5 %collective-permute-start.5 = (f32[48,1408]{1,0:T(8,128)S(1)}, f32[48,1408]{1,0:T(8,128)S(1)}, u32[]{:S(2)}, u32[]{:S(2)}) collective-permute-start(f32[48,1408]{1,0:T(8,128)S(1)} %get-tuple-element.48), channel_id=1, source_target_pairs={{0,4},{4,8},{8,12},{12,16},{16,20},{20,24},{24,28},{28,0},{1,5},{5... | collective-permute-start | bytes 811016 | tf_op jit(solution)/shard_map/ppermute | solution.py:28
  86.5 5.0 %collective-permute-done.5.up_in = f32[48,1408]{1,0:T(8,128)S(1)} collective-permute-done((f32[48,1408]{1,0:T(8,128)S(1)}, f32[48,1408]{1,0:T(8,128)S(1)}, u32[]{:S(2)}, u32[]{:S(2)}) %collective-permute-start.5) | collective-permute-done | bytes 270368 | tf_op jit(solution)/shard_map/ppermute | solution.py:28
  91.6 2.7 %collective-permute-done.6.down_in = f32[48,1408]{1,0:T(8,128)S(1)} collective-permute-done((f32[48,1408]{1,0:T(8,128)S(1)}, f32[48,1408]{1,0:T(8,128)S(1)}, u32[]{:S(2)}, u32[]{:S(2)}) %collective-permute-start.6) | collective-permute-done | bytes 270368 | tf_op jit(solution)/shard_map/ppermute | solution.py:28
  94.9 1.8 %collective-permute-start.7 = (f32[48,1408]{1,0:T(8,128)S(1)}, f32[48,1408]{1,0:T(8,128)S(1)}, u32[]{:S(2)}, u32[]{:S(2)}) collective-permute-start(f32[48,1408]{1,0:T(8,128)S(1)} %get-tuple-element.50), channel_id=1, source_target_pairs={{0,4},{4,8},{8,12},{12,16},{16,20},{20,24},{24,28},{28,0},{1,5},{5... | collective-permute-start | bytes 811016 | tf_op jit(solution)/shard_map/ppermute | solution.py:28
  97.0 4.4 %collective-permute-done.7.up_in = f32[48,1408]{1,0:T(8,128)S(1)} collective-permute-done((f32[48,1408]{1,0:T(8,128)S(1)}, f32[48,1408]{1,0:T(8,128)S(1)}, u32[]{:S(2)}, u32[]{:S(2)}) %collective-permute-start.7) | collective-permute-done | bytes 270368 | tf_op jit(solution)/shard_map/ppermute | solution.py:28
  101.4 1.7 %collective-permute-done.8.down_in = f32[48,1408]{1,0:T(8,128)S(1)} collective-permute-done((f32[48,1408]{1,0:T(8,128)S(1)}, f32[48,1408]{1,0:T(8,128)S(1)}, u32[]{:S(2)}, u32[]{:S(2)}) %collective-permute-start.8) | collective-permute-done | bytes 270368 | tf_op jit(solution)/shard_map/ppermute | solution.py:28
  104.7 1.6 collective-permute-start.9
  106.2 5.5 %all-to-all-start.1 = ((f32[8,48,176]{2,1,0:T(8,128)}), f32[8,48,176]{2,1,0:T(8,128)S(1)}, u32[]{:S(2)}, u32[]{:S(2)}) async-start(f32[8,48,176]{2,1,0:T(8,128)} %shard_map.53), calls=%async_computation.1 | async-start | bytes 786432 | tf_op jit(solution)/shard_map/all_to_all | solution.py:285
  111.8 1.5 collective-permute-start.10
  113.9 10.3 %all-to-all-done.1.columns_ref = f32[8,48,176]{2,1,0:T(8,128)S(1)} async-done(((f32[8,48,176]{2,1,0:T(8,128)}), f32[8,48,176]{2,1,0:T(8,128)S(1)}, u32[]{:S(2)}, u32[]{:S(2)}) %all-to-all-start.1) | async-done | bytes 270368 | tf_op jit(solution)/shard_map/all_to_all | solution.py:285
  128.0 1.9 %collective-permute-start.14 = (f32[8,48,88]{2,1,0:T(8,128)S(1)}, f32[8,48,88]{2,1,0:T(8,128)S(1)}, u32[]{:S(2)}, u32[]{:S(2)}) collective-permute-start(f32[8,48,88]{2,1,0:T(8,128)S(1)} %shard_map.54), channel_id=1, source_target_pairs={{0,2},{2,0},{1,3},{3,1},{4,6},{6,4},{5,7},{7,5},{8,10},{10,8},{9,1... | collective-permute-start | bytes 405512 | tf_op jit(solution)/shard_map/ppermute | solution.py:23
  129.9 2.2 %collective-permute-done.13.down_ref.refs_6_ = bf16[96,1408]{1,0:T(8,128)(2,1)S(1)} collective-permute-done((bf16[96,1408]{1,0:T(8,128)(2,1)}, bf16[96,1408]{1,0:T(8,128)(2,1)S(1)}, u32[]{:S(2)}, u32[]{:S(2)}) %collective-permute-start.13) | collective-permute-done | bytes 270368 | tf_op jit(solution)/shard_map/ppermute | solution.py:28
  132.1 3.9 %collective-permute-done.14.other_ref = f32[8,48,88]{2,1,0:T(8,128)S(1)} collective-permute-done((f32[8,48,88]{2,1,0:T(8,128)S(1)}, f32[8,48,88]{2,1,0:T(8,128)S(1)}, u32[]{:S(2)}, u32[]{:S(2)}) %collective-permute-start.14) | collective-permute-done | bytes 135200 | tf_op jit(solution)/shard_map/ppermute | solution.py:23
  136.0 1.2 shard_map.56
  137.8 1.3 collective-permute-start.18
  139.9 4.7 %collective-permute-start.20 = (bf16[48,1408]{1,0:T(8,128)(2,1)S(1)}, bf16[48,1408]{1,0:T(8,128)(2,1)S(1)}, u32[]{:S(2)}, u32[]{:S(2)}) collective-permute-start(bf16[48,1408]{1,0:T(8,128)(2,1)S(1)} %get-tuple-element.61), channel_id=1, source_target_pairs={{0,8},{4,12},{8,16},{12,20},{16,24},{20,28},{24,0},{28,4},{1,9},{5... | collective-permute-start | bytes 405512 | tf_op jit(solution)/shard_map/ppermute | solution.py:28
  144.5 3.7 %shard_map.57 = (f32[48,1408]{1,0:T(8,128)S(1)}, f32[8,48,176]{2,1,0:T(8,128)S(1)}, bf16[48,1408]{1,0:T(8,128)(2,1)S(1)}, bf16[8,2,48,96]{3,2,1,0:T(8,128)(2,1)S(1)}) custom-call(s32[7]{0:T(128)S(1)} %stack.27.where_ref, f32[48,1408]{1,0:T(8,128)S(1)} %get-tuple-element.54.rows_ref, f32[8,48,96]{2,1,0:T(8,128)S(1)} %get-tuple-element.64.near_ref, ...), custom_call_target="tpu_custom_call" | custom-call | flops 129761280 | bytes 2703360 | tf_op jit(solution)/shard_map/pallas_call | solution.py:328
  148.2 7.2 %collective-permute-done.20.refs_4_ = bf16[48,1408]{1,0:T(8,128)(2,1)S(1)} collective-permute-done((bf16[48,1408]{1,0:T(8,128)(2,1)S(1)}, bf16[48,1408]{1,0:T(8,128)(2,1)S(1)}, u32[]{:S(2)}, u32[]{:S(2)}) %collective-permute-start.20) | collective-permute-done | bytes 135200 | tf_op jit(solution)/shard_map/ppermute | solution.py:28
  157.9 1.6 shard_map.58
  159.5 11.5 %all_to_all.16 = f32[8,48,176]{2,1,0:T(8,128)S(1)} all-to-all(f32[8,48,176]{2,1,0:T(8,128)S(1)} %shard_map.58), channel_id=1, replica_groups=mesh['x'=4,'yl'=2,'z'=8,'yh'=2,'c'=2] {'x','yl'}, dimensions={0} | all-to-all | bytes 540672 | tf_op jit(solution)/shard_map/all_to_all | solution.py:361
  (70 shorter events, 17.0 us)
Async XLA Ops:
  54.8 6.3 %collective-permute-start = (bf16[16,272,300]{2,1,0:T(8,128)(2,1)}, bf16[16,272,300]{2,1,0:T(8,128)(2,1)}, u32[]{:S(2)}, u32[]{:S(2)}) collective-permute-start(bf16[16,272,300]{2,1,0:T(8,128)(2,1)} %all_to_all.15.near_ref), channel_id=1, source_target_pairs={{0,1},{1,0},{2,3},{3,2},{4,5},{5,4},{6,7},{7,6},{8,9},{9,8},{10,11... | collective-permute-start | bytes 7833608 | tf_op jit(solution)/shard_map/ppermute | solution.py:23
  58.3 7.7 %copy-start.4 = (f32[1408]{0:T(1024)S(1)}, f32[1408]{0:T(1024)}, u32[]{:S(2)}) copy-start(f32[1408]{0:T(1024)} %param.7) | copy-start | bytes 16900
  58.3 7.7 %copy-start.3 = (f32[16]{0:T(128)S(1)}, f32[16]{0:T(128)}, u32[]{:S(2)}) copy-start(f32[16]{0:T(128)} %occ_ref.1) | copy-start | bytes 196
  63.8 7.2 %collective-permute-start.1 = (f32[24,1408]{1,0:T(8,128)S(1)}, f32[24,1408]{1,0:T(8,128)S(1)}, u32[]{:S(2)}, u32[]{:S(2)}) collective-permute-start(f32[24,1408]{1,0:T(8,128)S(1)} %get-tuple-element.44), channel_id=1, source_target_pairs={{0,4},{4,8},{8,12},{12,16},{16,20},{20,24},{24,28},{28,0},{1,5},{5... | collective-permute-start | bytes 405512 | tf_op jit(solution)/shard_map/ppermute | solution.py:28
  65.8 5.5 %collective-permute-start.2 = (f32[24,1408]{1,0:T(8,128)S(1)}, f32[24,1408]{1,0:T(8,128)S(1)}, u32[]{:S(2)}, u32[]{:S(2)}) collective-permute-start(f32[24,1408]{1,0:T(8,128)S(1)} %get-tuple-element.45), channel_id=1, source_target_pairs={{0,28},{4,0},{8,4},{12,8},{16,12},{20,16},{24,20},{28,24},{1,29},{... | collective-permute-start | bytes 405512 | tf_op jit(solution)/shard_map/ppermute | solution.py:28
  71.9 10.3 %collective-permute-start.3 = (f32[48,1408]{1,0:T(8,128)S(1)}, f32[48,1408]{1,0:T(8,128)S(1)}, u32[]{:S(2)}, u32[]{:S(2)}) collective-permute-start(f32[48,1408]{1,0:T(8,128)S(1)} %get-tuple-element.46), channel_id=1, source_target_pairs={{0,4},{4,8},{8,12},{12,16},{16,20},{20,24},{24,28},{28,0},{1,5},{5... | collective-permute-start | bytes 811016 | tf_op jit(solution)/shard_map/ppermute | solution.py:28
  75.2 8.3 %collective-permute-start.4 = (f32[48,1408]{1,0:T(8,128)S(1)}, f32[48,1408]{1,0:T(8,128)S(1)}, u32[]{:S(2)}, u32[]{:S(2)}) collective-permute-start(f32[48,1408]{1,0:T(8,128)S(1)} %get-tuple-element.47), channel_id=1, source_target_pairs={{0,28},{4,0},{8,4},{12,8},{16,12},{20,16},{24,20},{28,24},{1,29},{... | collective-permute-start | bytes 811016 | tf_op jit(solution)/shard_map/ppermute | solution.py:28
  84.1 7.5 %collective-permute-start.5 = (f32[48,1408]{1,0:T(8,128)S(1)}, f32[48,1408]{1,0:T(8,128)S(1)}, u32[]{:S(2)}, u32[]{:S(2)}) collective-permute-start(f32[48,1408]{1,0:T(8,128)S(1)} %get-tuple-element.48), channel_id=1, source_target_pairs={{0,4},{4,8},{8,12},{12,16},{16,20},{20,24},{24,28},{28,0},{1,5},{5... | collective-permute-start | bytes 811016 | tf_op jit(solution)/shard_map/ppermute | solution.py:28
  86.5 7.7 %collective-permute-start.6 = (f32[48,1408]{1,0:T(8,128)S(1)}, f32[48,1408]{1,0:T(8,128)S(1)}, u32[]{:S(2)}, u32[]{:S(2)}) collective-permute-start(f32[48,1408]{1,0:T(8,128)S(1)} %get-tuple-element.49), channel_id=1, source_target_pairs={{0,28},{4,0},{8,4},{12,8},{16,12},{20,16},{24,20},{28,24},{1,29},{... | collective-permute-start | bytes 811016 | tf_op jit(solution)/shard_map/ppermute | solution.py:28
  94.9 6.5 %collective-permute-start.7 = (f32[48,1408]{1,0:T(8,128)S(1)}, f32[48,1408]{1,0:T(8,128)S(1)}, u32[]{:S(2)}, u32[]{:S(2)}) collective-permute-start(f32[48,1408]{1,0:T(8,128)S(1)} %get-tuple-element.50), channel_id=1, source_target_pairs={{0,4},{4,8},{8,12},{12,16},{16,20},{20,24},{24,28},{28,0},{1,5},{5... | collective-permute-start | bytes 811016 | tf_op jit(solution)/shard_map/ppermute | solution.py:28
  96.7 6.5 %collective-permute-start.8 = (f32[48,1408]{1,0:T(8,128)S(1)}, f32[48,1408]{1,0:T(8,128)S(1)}, u32[]{:S(2)}, u32[]{:S(2)}) collective-permute-start(f32[48,1408]{1,0:T(8,128)S(1)} %get-tuple-element.51), channel_id=1, source_target_pairs={{0,28},{4,0},{8,4},{12,8},{16,12},{20,16},{24,20},{28,24},{1,29},{... | collective-permute-start | bytes 811016 | tf_op jit(solution)/shard_map/ppermute | solution.py:28
  104.7 7.1 %collective-permute-start.9 = (bf16[48,1408]{1,0:T(8,128)(2,1)S(1)}, bf16[48,1408]{1,0:T(8,128)(2,1)S(1)}, u32[]{:S(2)}, u32[]{:S(2)}) collective-permute-start(bf16[48,1408]{1,0:T(8,128)(2,1)S(1)} %get-tuple-element.53), channel_id=1, source_target_pairs={{0,2},{2,0},{1,3},{3,1},{4,6},{6,4},{5,7},{7,5},{8,10},{10,8},{9,1... | collective-permute-start | bytes 405512 | tf_op jit(solution)/shard_map/ppermute | solution.py:23
  106.2 17.9 %all-to-all-start.1 = ((f32[8,48,176]{2,1,0:T(8,128)}), f32[8,48,176]{2,1,0:T(8,128)S(1)}, u32[]{:S(2)}, u32[]{:S(2)}) async-start(f32[8,48,176]{2,1,0:T(8,128)} %shard_map.53), calls=%async_computation.1 | async-start | bytes 786432 | tf_op jit(solution)/shard_map/all_to_all | solution.py:285
  111.8 13.2 %collective-permute-start.10 = (bf16[96,1408]{1,0:T(8,128)(2,1)S(1)}, bf16[96,1408]{1,0:T(8,128)(2,1)S(1)}, u32[]{:S(2)}, u32[]{:S(2)}) collective-permute-start(bf16[96,1408]{1,0:T(8,128)(2,1)S(1)} %constant_dynamic-update-slice_fusion.refs_0_), channel_id=1, source_target_pairs={{0,4},{4,8},{8,12},{12,16},{16,20},{20,24},{24,28},{28,0},{1,5},{5... | collective-permute-start | bytes 811016 | tf_op jit(solution)/shard_map/ppermute | solution.py:28
  113.3 12.1 %collective-permute-start.11 = (bf16[96,1408]{1,0:T(8,128)(2,1)S(1)}, bf16[96,1408]{1,0:T(8,128)(2,1)}, u32[]{:S(2)}, u32[]{:S(2)}) collective-permute-start(bf16[96,1408]{1,0:T(8,128)(2,1)S(1)} %constant_dynamic-update-slice_fusion.refs_0_), channel_id=1, source_target_pairs={{0,28},{4,0},{8,4},{12,8},{16,12},{20,16},{24,20},{28,24},{1,29},{... | collective-permute-start | bytes 811016 | tf_op jit(solution)/shard_map/ppermute | solution.py:28
  113.9 14.1 %collective-permute-start.15 = (bf16[96,1408]{1,0:T(8,128)(2,1)S(1)}, bf16[96,1408]{1,0:T(8,128)(2,1)}, u32[]{:S(2)}, u32[]{:S(2)}) collective-permute-start(bf16[96,1408]{1,0:T(8,128)(2,1)S(1)} %constant_dynamic-update-slice_fusion.refs_0_), channel_id=1, source_target_pairs={{0,1},{1,0},{2,3},{3,2},{4,5},{5,4},{6,7},{7,6},{8,9},{9,8},{10,11... | collective-permute-start | bytes 811016 | tf_op jit(solution)/shard_map/ppermute | solution.py:23
  125.4 6.7 %collective-permute-start.13 = (bf16[96,1408]{1,0:T(8,128)(2,1)}, bf16[96,1408]{1,0:T(8,128)(2,1)S(1)}, u32[]{:S(2)}, u32[]{:S(2)}) collective-permute-start(bf16[96,1408]{1,0:T(8,128)(2,1)} %collective-permute-done.11.refs_2_), channel_id=1, source_target_pairs={{0,28},{4,0},{8,4},{12,8},{16,12},{20,16},{24,20},{28,24},{1,29},{... | collective-permute-start | bytes 811016 | tf_op jit(solution)/shard_map/ppermute | solution.py:28
  126.5 9.5 %collective-permute-start.16 = (bf16[96,1408]{1,0:T(8,128)(2,1)}, bf16[96,1408]{1,0:T(8,128)(2,1)S(1)}, u32[]{:S(2)}, u32[]{:S(2)}) collective-permute-start(bf16[96,1408]{1,0:T(8,128)(2,1)} %collective-permute-done.11.refs_2_), channel_id=1, source_target_pairs={{0,1},{1,0},{2,3},{3,2},{4,5},{5,4},{6,7},{7,6},{8,9},{9,8},{10,11... | collective-permute-start | bytes 811016 | tf_op jit(solution)/shard_map/ppermute | solution.py:23
  126.5 9.5 %collective-permute-start.17 = (bf16[96,1408]{1,0:T(8,128)(2,1)S(1)}, bf16[96,1408]{1,0:T(8,128)(2,1)S(1)}, u32[]{:S(2)}, u32[]{:S(2)}) collective-permute-start(bf16[96,1408]{1,0:T(8,128)(2,1)S(1)} %collective-permute-done.10.refs_4_), channel_id=1, source_target_pairs={{0,1},{1,0},{2,3},{3,2},{4,5},{5,4},{6,7},{7,6},{8,9},{9,8},{10,11... | collective-permute-start | bytes 811016 | tf_op jit(solution)/shard_map/ppermute | solution.py:23
  127.0 9.0 %collective-permute-start.12 = (bf16[96,1408]{1,0:T(8,128)(2,1)S(1)}, bf16[96,1408]{1,0:T(8,128)(2,1)S(1)}, u32[]{:S(2)}, u32[]{:S(2)}) collective-permute-start(bf16[96,1408]{1,0:T(8,128)(2,1)S(1)} %collective-permute-done.10.refs_4_), channel_id=1, source_target_pairs={{0,4},{4,8},{8,12},{12,16},{16,20},{20,24},{24,28},{28,0},{1,5},{5... | collective-permute-start | bytes 811016 | tf_op jit(solution)/shard_map/ppermute | solution.py:28
  128.0 8.0 %collective-permute-start.14 = (f32[8,48,88]{2,1,0:T(8,128)S(1)}, f32[8,48,88]{2,1,0:T(8,128)S(1)}, u32[]{:S(2)}, u32[]{:S(2)}) collective-permute-start(f32[8,48,88]{2,1,0:T(8,128)S(1)} %shard_map.54), channel_id=1, source_target_pairs={{0,2},{2,0},{1,3},{3,1},{4,6},{6,4},{5,7},{7,5},{8,10},{10,8},{9,1... | collective-permute-start | bytes 405512 | tf_op jit(solution)/shard_map/ppermute | solution.py:23
  132.1 12.4 %collective-permute-start.23 = (bf16[96,1408]{1,0:T(8,128)(2,1)S(1)}, bf16[96,1408]{1,0:T(8,128)(2,1)S(1)}, u32[]{:S(2)}, u32[]{:S(2)}) collective-permute-start(bf16[96,1408]{1,0:T(8,128)(2,1)S(1)} %collective-permute-done.13.down_ref.refs_6_), channel_id=1, source_target_pairs={{0,1},{1,0},{2,3},{3,2},{4,5},{5,4},{6,7},{7,6},{8,9},{9,8},{10,11... | collective-permute-start | bytes 811016 | tf_op jit(solution)/shard_map/ppermute | solution.py:23
  137.2 2.7 %collective-permute-start.22 = (f32[8,48,96]{2,1,0:T(8,128)S(1)}, f32[8,48,96]{2,1,0:T(8,128)S(1)}, u32[]{:S(2)}, u32[]{:S(2)}) collective-permute-start(f32[8,48,96]{2,1,0:T(8,128)S(1)} %get-tuple-element.65), channel_id=1, source_target_pairs={{0,1},{1,0},{2,3},{3,2},{4,5},{5,4},{6,7},{7,6},{8,9},{9,8},{10,11... | collective-permute-start | bytes 442376 | tf_op jit(solution)/shard_map/ppermute | solution.py:23
  137.3 7.3 %collective-permute-start.24 = (bf16[96,1408]{1,0:T(8,128)(2,1)S(1)}, bf16[96,1408]{1,0:T(8,128)(2,1)S(1)}, u32[]{:S(2)}, u32[]{:S(2)}) collective-permute-start(bf16[96,1408]{1,0:T(8,128)(2,1)S(1)} %collective-permute-done.12.up_ref.refs_8_), channel_id=1, source_target_pairs={{0,1},{1,0},{2,3},{3,2},{4,5},{5,4},{6,7},{7,6},{8,9},{9,8},{10,11... | collective-permute-start | bytes 811016 | tf_op jit(solution)/shard_map/ppermute | solution.py:23
  137.8 17.7 %collective-permute-start.18 = (bf16[96,1408]{1,0:T(8,128)(2,1)S(1)}, bf16[96,1408]{1,0:T(8,128)(2,1)S(1)}, u32[]{:S(2)}, u32[]{:S(2)}) collective-permute-start(bf16[96,1408]{1,0:T(8,128)(2,1)S(1)} %collective-permute-done.13.down_ref.refs_6_), channel_id=1, source_target_pairs={{0,28},{4,0},{8,4},{12,8},{16,12},{20,16},{24,20},{28,24},{1,29},{... | collective-permute-start | bytes 811016 | tf_op jit(solution)/shard_map/ppermute | solution.py:28
  139.1 16.3 %collective-permute-start.19 = (bf16[96,1408]{1,0:T(8,128)(2,1)S(1)}, bf16[96,1408]{1,0:T(8,128)(2,1)S(1)}, u32[]{:S(2)}, u32[]{:S(2)}) collective-permute-start(bf16[96,1408]{1,0:T(8,128)(2,1)S(1)} %collective-permute-done.12.up_ref.refs_8_), channel_id=1, source_target_pairs={{0,4},{4,8},{8,12},{12,16},{16,20},{20,24},{24,28},{28,0},{1,5},{5... | collective-permute-start | bytes 811016 | tf_op jit(solution)/shard_map/ppermute | solution.py:28
  139.9 15.6 %collective-permute-start.20 = (bf16[48,1408]{1,0:T(8,128)(2,1)S(1)}, bf16[48,1408]{1,0:T(8,128)(2,1)S(1)}, u32[]{:S(2)}, u32[]{:S(2)}) collective-permute-start(bf16[48,1408]{1,0:T(8,128)(2,1)S(1)} %get-tuple-element.61), channel_id=1, source_target_pairs={{0,8},{4,12},{8,16},{12,20},{16,24},{20,28},{24,0},{28,4},{1,9},{5... | collective-permute-start | bytes 405512 | tf_op jit(solution)/shard_map/ppermute | solution.py:28
  144.5 10.9 %collective-permute-start.21 = (bf16[48,1408]{1,0:T(8,128)(2,1)S(1)}, bf16[48,1408]{1,0:T(8,128)(2,1)S(1)}, u32[]{:S(2)}, u32[]{:S(2)}) collective-permute-start(bf16[48,1408]{1,0:T(8,128)(2,1)S(1)} %get-tuple-element.62), channel_id=1, source_target_pairs={{0,24},{4,28},{8,0},{12,4},{16,8},{20,12},{24,16},{28,20},{1,25},{... | collective-permute-start | bytes 405512 | tf_op jit(solution)/shard_map/ppermute | solution.py:28
  155.5 2.4 %collective-permute-start.25 = (bf16[96,1408]{1,0:T(8,128)(2,1)S(1)}, bf16[96,1408]{1,0:T(8,128)(2,1)S(1)}, u32[]{:S(2)}, u32[]{:S(2)}) collective-permute-start(bf16[96,1408]{1,0:T(8,128)(2,1)S(1)} %collective-permute-done.18.refs_0_), channel_id=1, source_target_pairs={{0,1},{1,0},{2,3},{3,2},{4,5},{5,4},{6,7},{7,6},{8,9},{9,8},{10,11... | collective-permute-start | bytes 811016 | tf_op jit(solution)/shard_map/ppermute | solution.py:23
  155.6 2.3 %collective-permute-start.26 = (bf16[96,1408]{1,0:T(8,128)(2,1)S(1)}, bf16[96,1408]{1,0:T(8,128)(2,1)S(1)}, u32[]{:S(2)}, u32[]{:S(2)}) collective-permute-start(bf16[96,1408]{1,0:T(8,128)(2,1)S(1)} %collective-permute-done.19.refs_2_), channel_id=1, source_target_pairs={{0,1},{1,0},{2,3},{3,2},{4,5},{5,4},{6,7},{7,6},{8,9},{9,8},{10,11... | collective-permute-start | bytes 811016 | tf_op jit(solution)/shard_map/ppermute | solution.py:23
  156.1 1.6 collective-permute-start.27
  156.2 1.7 collective-permute-start.28
  (4 other events, 16.5 us)

commit v7 on v6

--- a/solution.py
+++ b/solution.py
@@ -36,47 +36,98 @@
     return pl.CostEstimate(flops=flops, bytes_accessed=moved, transcendentals=0)
 
 
-def factor_product(ref, left, padded):
-    sources, rows, naux = ref.shape
+def fill(side, width, padded, pair_ref, orbital_ref, put):
+    half = orbital_ref.shape[1] // 2
+    gap = jnp.zeros((padded - width, orbital_ref.shape[2]), BF16)
+    for p in range(pair_ref.shape[0]):
+        left = orbital_ref[pair_ref[p, 0]]
+        right = orbital_ref[pair_ref[p, 1]]
+        for y in range(2):
+            at = (2 * y + side) * width
+            put(p, y, jnp.concatenate([left[at : at + width], gap], axis=0))
+        put(p, 2, right[side * half : (side + 1) * half])
+
+
+def select_kernel(width, padded, where_ref, pair_ref, orbital_ref, out_ref):
+    def put(p, block, value):
+        out_ref[p, block * padded : block * padded + value.shape[0]] = value
+
+    for c in range(2):
+
+        @pl.when(where_ref[1] == c)
+        def _():
+            fill(1 - c, width, padded, pair_ref, orbital_ref, put)
+
+
+def own_kernel(width, padded, where_ref, pair_ref, orbital_ref, out_ref):
+    groups, naux = pair_ref.shape[0], orbital_ref.shape[2]
+    for c in range(2):
+        lanes = slice(c * naux, (c + 1) * naux)
+
+        def put(p, block, value, lanes=lanes):
+            if block < 2:
+                out_ref[block * groups + p, :padded, lanes] = value
+            else:
+                for y in range(2):
+                    out_ref[y * groups + p, padded:, lanes] = value
+
+        @pl.when(where_ref[1] == c)
+        def _(c=c, put=put):
+            fill(c, width, padded, pair_ref, orbital_ref, put)
+
+
+def other_kernel(padded, where_ref, taken_ref, own_ref, out_ref):
+    groups, naux = taken_ref.shape[0], taken_ref.shape[2]
+    for c in range(2):
+        lanes = slice((1 - c) * naux, (2 - c) * naux)
+
+        @pl.when(where_ref[1] == c)
+        def _(lanes=lanes):
+            for p in range(groups):
+                for y in range(2):
+                    out_ref[y * groups + p, :padded, lanes] = taken_ref[p, y * padded : (y + 1) * padded]
+                    out_ref[y * groups + p, padded:, lanes] = taken_ref[p, 2 * padded :]
+
+
+def half_product(left, right_ref, padded):
+    sources = right_ref.shape[0]
     half = sources // 2
-    slab = rows - 2 * padded
     total = None
     for y in range(2):
-        b = ref[half * y : half * (y + 1), 2 * padded :, :].reshape(half * slab, naux)
-        term = dot_nt(left(y), b)
+        right = jnp.concatenate([right_ref[half * y + k, padded:, :] for k in range(half)], axis=0)
+        term = dot_nt(left(y), right)
         total = term if total is None else total + term
     return total
 
 
-def all_rows(ref, start, padded):
-    half = ref.shape[0] // 2
+def all_rows(near_ref, padded):
+    half = near_ref.shape[0] // 2
 
     def left(y):
-        return ref[half * y : half * (y + 1), pl.ds(start, padded), :].reshape(half * padded, ref.shape[2])
+        return near_ref[half * y : half * (y + 1), :padded, :].reshape(half * padded, near_ref.shape[2])
 
     return left
 
 
-def near_kernel(padded, where_ref, near_ref, out_ref):
-    start = pl.multiple_of(where_ref[1] * padded, padded)
-    out_ref[...] = factor_product(near_ref, all_rows(near_ref, start, padded), padded).reshape(out_ref.shape)
-
-
-def first_kernel(padded, where_ref, near_part_ref, far_ref, up_ref, down_ref):
-    nz = near_part_ref.shape[0]
-    half = far_ref.shape[0] // 2
-    start = pl.multiple_of(where_ref[1] * padded, padded)
+def near_kernel(padded, near_ref, out_ref):
+    out_ref[...] = half_product(all_rows(near_ref, padded), near_ref, padded).reshape(out_ref.shape)
+
+
+def first_kernel(padded, where_ref, near_part_ref, near_ref, far_ref, up_ref, down_ref):
+    nz, width = near_part_ref.shape[0], near_part_ref.shape[2]
+    half = near_ref.shape[0] // 2
+    cut = padded // 2
     at = lax.rem(where_ref[0] + nz // 2, nz)
-    total = factor_product(far_ref, lambda y: far_ref[half * y + at, pl.ds(start, padded), :], padded)
-    total = total + near_part_ref[at]
-    up_ref[...] = total[: padded // 2]
-    down_ref[...] = total[padded // 2 :]
-
-
-def rest_kernel(padded, where_ref, pair_ref, occ_ref, vir_ref, near_part_ref, far_ref, out_ref, denom_ref):
-    start = pl.multiple_of(where_ref[1] * padded, padded)
-    total = factor_product(far_ref, all_rows(far_ref, start, padded), padded)
-    out_ref[...] = near_part_ref[...] + total.reshape(out_ref.shape)
+    total = half_product(lambda y: near_ref[half * y + at, :padded, :], far_ref, padded)
+    near = near_part_ref[at]
+    up_ref[...] = jnp.concatenate([near[:cut], total[:cut]], axis=1)
+    down_ref[...] = jnp.concatenate([near[cut:], total[cut:]], axis=1)
+
+
+def rest_kernel(padded, where_ref, pair_ref, occ_ref, vir_ref, near_part_ref, near_ref, far_ref, out_ref, denom_ref):
+    total = half_product(all_rows(near_ref, padded), far_ref, padded).reshape(near_part_ref.shape)
+    for k in range(near_part_ref.shape[0]):
+        out_ref[k] = jnp.concatenate([near_part_ref[k], total[k]], axis=1)
     chunk, group, width = where_ref[2], where_ref[3], where_ref[5]
     columns = jnp.broadcast_to(vir_ref[...], denom_ref.shape)
     place = lax.broadcasted_iota(jnp.int32, denom_ref.shape, 1)
@@ -98,7 +149,13 @@
 
 
 def amplitude_kernel(where_ref, part_ref, up_in, down_in, denom_ref, out_ref, rounded_ref):
-    amps = (part_ref[where_ref[0]] + (up_in[...] + down_in[...])) / denom_ref[...]
+    sums = part_ref[where_ref[0]] + (up_in[...] + down_in[...])
+    half = sums.shape[1] // 2
+    near, far = sums[:, :half], sums[:, half:]
+    halves = (jnp.where(where_ref[1] == 0, near, far), jnp.where(where_ref[1] == 0, far, near))
+    step = half // part_ref.shape[0]
+    parts = [h[:, k * step : (k + 1) * step] for k in range(part_ref.shape[0]) for h in halves]
+    amps = jnp.concatenate(parts, axis=1) / denom_ref[...]
     out_ref[...] = amps
     rounded_ref[...] = amps.astype(BF16)
 
@@ -218,12 +275,32 @@
     padded = (width + 8) // 8 * 8
     where = jnp.stack([z, c, z * 4 + yh * 2 + c, lax.axis_index(SLABS), yh * 2 + c, jnp.int32(width), yh])
 
-    left = orbital_b[pair_list[:, 0]].reshape(8, 2, 2, width, naux)
-    left = jnp.pad(left, ((0, 0), (0, 0), (0, 0), (0, padded - width), (0, 0)))
-    left = left.reshape(8, 2, 2 * padded, naux).transpose(1, 0, 2, 3)
-    right = jnp.broadcast_to(orbital_b[pair_list[:, 1]][None], (2, 8, slab, naux))
-    outgoing = jnp.concatenate([left, right], axis=2).reshape(16, 2 * padded + slab, naux)
-    near = lax.all_to_all(outgoing, ("yh", "x", "yl"), split_axis=0, concat_axis=0, tiled=True)
+    sent = 2 * padded + slab // 2
+    theirs = pl.pallas_call(
+        functools.partial(select_kernel, width, padded),
+        out_shape=jax.ShapeDtypeStruct((8, sent, naux), BF16),
+        in_specs=[SMEM, SMEM, VMEM],
+        out_specs=VMEM,
+        compiler_params=params(8),
+    )(where, pair_list, orbital_b)
+    taken = swap(theirs, "c")
+    outgoing = jax.ShapeDtypeStruct((16, sent - padded, 2 * naux), BF16)
+    ours = pl.pallas_call(
+        functools.partial(own_kernel, width, padded),
+        out_shape=outgoing,
+        in_specs=[SMEM, SMEM, VMEM],
+        out_specs=VMEM,
+        compiler_params=params(8),
+    )(where, pair_list, orbital_b)
+    ours = pl.pallas_call(
+        functools.partial(other_kernel, padded),
+        out_shape=outgoing,
+        in_specs=[SMEM, VMEM, VMEM],
+        out_specs=VMEM,
+        input_output_aliases={2: 0},
+        compiler_params=params(8),
+    )(where, taken, ours)
+    near = lax.all_to_all(ours, ("yh", "x", "yl"), split_axis=0, concat_axis=0, tiled=True)
     far = swap(near, "c")
 
     whole = jax.ShapeDtypeStruct((8, padded, nvir), F32)
@@ -232,29 +309,29 @@
     flops = 16 * padded * 8 * slab * 2 * naux
     near_part = pl.pallas_call(
         functools.partial(near_kernel, padded),
-        out_shape=whole,
-        in_specs=[SMEM, VMEM],
+        out_shape=jax.ShapeDtypeStruct((8, padded, nvir // 2), F32),
+        in_specs=[VMEM],
         out_specs=VMEM,
         compiler_params=params(16),
         cost_estimate=cost(flops, 0),
-    )(where, near)
+    )(near)
     up, down = pl.pallas_call(
         functools.partial(first_kernel, padded),
         out_shape=(halves, halves),
-        in_specs=[SMEM, VMEM, VMEM],
+        in_specs=[SMEM, VMEM, VMEM, VMEM],
         out_specs=(VMEM, VMEM),
         compiler_params=params(16),
         cost_estimate=cost(flops // 8, 0),
-    )(where, near_part, far)
+    )(where, near_part, near, far)
     up, down = shift(up, "z", 1), shift(down, "z", -1)
     part, denom = pl.pallas_call(
         functools.partial(rest_kernel, padded),
         out_shape=(whole, rows),
-        in_specs=[SMEM, SMEM, SMEM, VMEM, VMEM, VMEM],
+        in_specs=[SMEM, SMEM, SMEM, VMEM, VMEM, VMEM, VMEM],
         out_specs=(VMEM, VMEM),
-        compiler_params=params(20),
+        compiler_params=params(16),
         cost_estimate=cost(flops, 0),
-    )(where, pair_list, eps_occ, eps_vir[None], near_part, far)
+    )(where, pair_list, eps_occ, eps_vir[None], near_part, near, far)
     for step in range(nz // 2 - 1, 0, -1):
         up, down = pl.pallas_call(
             functools.partial(hop_kernel, step),
@@ -300,8 +377,8 @@
             up, down, outward = lax.optimization_barrier((up, down, outward))
     far = {r: swap(ring[r], "c") for r in (1, nz - 1)}
     far[0] = swap(both, "c")
+    up, down, far = lax.optimization_barrier((up, down, far))
     outward = swap(outward, "yh")
-    up, down, outward, far = lax.optimization_barrier((up, down, outward, far))
     kept, sent = pl.pallas_call(
         inward_kernel,
         out_shape=(jax.ShapeDtypeStruct((nz, padded, 2 * padded), F32),) * 2,

time: 172 us -> 161 us (0.936)
  blocking collectives: 59.8 us -> 53.6 us
  waiting for transfers between devices: 50 us -> 55.7 us
  local copies, waits for them, and re-layouts: 7.03 us -> 2.49 us
  Pallas kernels: 20 us -> 17.3 us
    all_to_all x1, blocking collectives: 48.4 us -> 42.1 us  [local(): lax.all_to_all(ours, ('yh', 'x', 'yl'), split_axis=0, concat_axis=0, tile...]
    ppermute x16, waiting for transfers between devices: 31.7 us -> 35.5 us  [shift(): lax.ppermute(value, axis, [(i, (i + step) % size) for i in range(size)])]
    gather x3 -> x0, local copies, waits for them, and re-layouts: 2.73 us -> none  [the longest x1 1.72 us: local(): orbital_b[pair_list[:, 1]][None]]
    ppermute x13 -> x14, waiting for transfers between devices: 8.03 us -> 10.3 us  [swap(): return lax.ppermute(value, axis, [(0, 1), (1, 0)])]
    pallas_call x1 -> x4, Pallas kernels: 3.33 us -> 3.77 us  [the longest x1 1.18 us: local(): pl.pallas_call(functools.partial(other_kernel, padded), out_shape=outgoin...]
    ppermute x13 -> x14, starting transfers between devices: 5.74 us -> 5.89 us  [swap(): return lax.ppermute(value, axis, [(0, 1), (1, 0)])]
  transfers between devices with their start and end apart: 30 -> 31, of which waited for: 15 -> 17; matrix products, arithmetic and copies ran while one was open for 0% -> 0% of each run, Pallas kernels for 7% -> 6%
where the time goes in v7:
time: 161 us
  waiting for transfers between devices  55.7 us (35%)
  blocking collectives  53.6 us (33%)
  starting transfers between devices  31 us (19%)
  Pallas kernels  17.3 us (11%)
  local copies, waits for them, and re-layouts  2.49 us (2%)
    all_to_all x1, blocking collectives, local(): lax.all_to_all(ours, ('yh', 'x', 'yl'), split_axis=0, concat_axis=0, tile...  42.1 us
    ppermute x16, waiting for transfers between devices, shift(): lax.ppermute(value, axis, [(i, (i + step) % size) for i in range(size)])  35.5 us
    ppermute x16, starting transfers between devices, shift(): lax.ppermute(value, axis, [(i, (i + step) % size) for i in range(size)])  20 us
    all_to_all x1, blocking collectives, local(): lax.all_to_all(added, SLABS, split_axis=0, concat_axis=0, tiled=True)  11.5 us
    ppermute x14, waiting for transfers between devices, swap(): return lax.ppermute(value, axis, [(0, 1), (1, 0)])  10.3 us
    all_to_all x1, waiting for transfers between devices, local(): lax.all_to_all(columns, 'z', split_axis=0, concat_axis=0, tiled=True)  9.96 us
    ppermute x14, starting transfers between devices, swap(): return lax.ppermute(value, axis, [(0, 1), (1, 0)])  5.89 us
    all_to_all x1, starting transfers between devices, local(): lax.all_to_all(columns, 'z', split_axis=0, concat_axis=0, tiled=True)  5.19 us
  transfers between devices with their start and end apart: 31, of which 17 were waited for; matrix products, arithmetic and copies ran while one was open for 0% of the time, Pallas kernels for 6%

profile of v7, /device:TPU:32, one launch (start us, length us, event | category | flops | bytes accessed | tf_op | source)
XLA Modules:
  0.0 161.0 jit_solution(7088968265062791689)
XLA Ops:
  0.8 1.6 copy-done
  4.1 2.0 %collective-permute-done.taken_ref = bf16[8,184,300]{2,1,0:T(8,128)(2,1)S(1)} collective-permute-done((bf16[8,184,300]{2,1,0:T(8,128)(2,1)S(1)}, bf16[8,184,300]{2,1,0:T(8,128)(2,1)S(1)}, u32[]{:S(2)}, u32[]{:S(2)}) %collective-permute-start) | collective-permute-done | bytes 883232 | tf_op jit(solution)/shard_map/ppermute | solution.py:23
  7.2 42.1 %all_to_all.15.near_ref = bf16[16,136,600]{2,1,0:T(8,128)(2,1)S(1)} all-to-all(bf16[16,136,600]{2,1,0:T(8,128)(2,1)S(1)} %shard_map.48), channel_id=1, replica_groups=mesh['x'=4,'yl'=2,'z'=8,'yh'=2,'c'=2] {'yh','x','yl'}, dimensions={0} | all-to-all | bytes 5222400 | tf_op jit(solution)/shard_map/all_to_all | solution.py:303
  50.5 4.0 %collective-permute-done.1.far_ref = bf16[16,136,600]{2,1,0:T(8,128)(2,1)S(1)} collective-permute-done((bf16[16,136,600]{2,1,0:T(8,128)(2,1)S(1)}, bf16[16,136,600]{2,1,0:T(8,128)(2,1)S(1)}, u32[]{:S(2)}, u32[]{:S(2)}) %collective-permute-start.1) | collective-permute-done | bytes 2611232 | tf_op jit(solution)/shard_map/ppermute | solution.py:23
  54.5 1.2 shard_map.51
  55.8 2.0 %collective-permute-start.2 = (f32[24,1408]{1,0:T(8,128)S(1)}, f32[24,1408]{1,0:T(8,128)S(1)}, u32[]{:S(2)}, u32[]{:S(2)}) collective-permute-start(f32[24,1408]{1,0:T(8,128)S(1)} %get-tuple-element.43), channel_id=1, source_target_pairs={{0,4},{4,8},{8,12},{12,16},{16,20},{20,24},{24,28},{28,0},{1,5},{5... | collective-permute-start | bytes 405512 | tf_op jit(solution)/shard_map/ppermute | solution.py:28
  57.9 1.8 %shard_map.50 = (f32[8,48,1408]{2,1,0:T(8,128)S(1)}, f32[48,1408]{1,0:T(8,128)S(1)}) custom-call(s32[7]{0:T(128)S(1)} %stack.27.where_ref, s32[8,2]{1,0:T(8,128)S(1)} %copy.8.pair_ref, f32[16]{0:T(128)S(1)} %copy-done.1, f32[1,1408]{1,0:T(1,128)S(1)} %broadcast_in_dim.3.vir_ref, f32[8,48,704]{2,1,0:T(8,128)S(1)} %shard_map.49.near_part_ref, ...), custom_call_target="tpu_custom_call" | custom-call | flops 648806400 | tf_op jit(solution)/shard_map/pallas_call | solution.py:327
  59.7 1.8 %collective-permute-done.2.up_in = f32[24,1408]{1,0:T(8,128)S(1)} collective-permute-done((f32[24,1408]{1,0:T(8,128)S(1)}, f32[24,1408]{1,0:T(8,128)S(1)}, u32[]{:S(2)}, u32[]{:S(2)}) %collective-permute-start.2) | collective-permute-done | bytes 135200 | tf_op jit(solution)/shard_map/ppermute | solution.py:28
  61.5 1.8 %collective-permute-done.3.down_in = f32[24,1408]{1,0:T(8,128)S(1)} collective-permute-done((f32[24,1408]{1,0:T(8,128)S(1)}, f32[24,1408]{1,0:T(8,128)S(1)}, u32[]{:S(2)}, u32[]{:S(2)}) %collective-permute-start.3) | collective-permute-done | bytes 135200 | tf_op jit(solution)/shard_map/ppermute | solution.py:28
  63.9 3.2 %collective-permute-start.4 = (f32[48,1408]{1,0:T(8,128)S(1)}, f32[48,1408]{1,0:T(8,128)S(1)}, u32[]{:S(2)}, u32[]{:S(2)}) collective-permute-start(f32[48,1408]{1,0:T(8,128)S(1)} %get-tuple-element.45), channel_id=1, source_target_pairs={{0,4},{4,8},{8,12},{12,16},{16,20},{20,24},{24,28},{28,0},{1,5},{5... | collective-permute-start | bytes 811016 | tf_op jit(solution)/shard_map/ppermute | solution.py:28
  67.1 5.6 %collective-permute-done.4.up_in = f32[48,1408]{1,0:T(8,128)S(1)} collective-permute-done((f32[48,1408]{1,0:T(8,128)S(1)}, f32[48,1408]{1,0:T(8,128)S(1)}, u32[]{:S(2)}, u32[]{:S(2)}) %collective-permute-start.4) | collective-permute-done | bytes 270368 | tf_op jit(solution)/shard_map/ppermute | solution.py:28
  72.7 2.7 %collective-permute-done.5.down_in = f32[48,1408]{1,0:T(8,128)S(1)} collective-permute-done((f32[48,1408]{1,0:T(8,128)S(1)}, f32[48,1408]{1,0:T(8,128)S(1)}, u32[]{:S(2)}, u32[]{:S(2)}) %collective-permute-start.5) | collective-permute-done | bytes 270368 | tf_op jit(solution)/shard_map/ppermute | solution.py:28
  76.0 1.8 %collective-permute-start.6 = (f32[48,1408]{1,0:T(8,128)S(1)}, f32[48,1408]{1,0:T(8,128)S(1)}, u32[]{:S(2)}, u32[]{:S(2)}) collective-permute-start(f32[48,1408]{1,0:T(8,128)S(1)} %get-tuple-element.47), channel_id=1, source_target_pairs={{0,4},{4,8},{8,12},{12,16},{16,20},{20,24},{24,28},{28,0},{1,5},{5... | collective-permute-start | bytes 811016 | tf_op jit(solution)/shard_map/ppermute | solution.py:28
  78.1 4.4 %collective-permute-done.6.up_in = f32[48,1408]{1,0:T(8,128)S(1)} collective-permute-done((f32[48,1408]{1,0:T(8,128)S(1)}, f32[48,1408]{1,0:T(8,128)S(1)}, u32[]{:S(2)}, u32[]{:S(2)}) %collective-permute-start.6) | collective-permute-done | bytes 270368 | tf_op jit(solution)/shard_map/ppermute | solution.py:28
  82.6 1.7 %collective-permute-done.7.down_in = f32[48,1408]{1,0:T(8,128)S(1)} collective-permute-done((f32[48,1408]{1,0:T(8,128)S(1)}, f32[48,1408]{1,0:T(8,128)S(1)}, u32[]{:S(2)}, u32[]{:S(2)}) %collective-permute-start.7) | collective-permute-done | bytes 270368 | tf_op jit(solution)/shard_map/ppermute | solution.py:28
  84.9 1.9 %collective-permute-start.8 = (f32[48,1408]{1,0:T(8,128)S(1)}, f32[48,1408]{1,0:T(8,128)S(1)}, u32[]{:S(2)}, u32[]{:S(2)}) collective-permute-start(f32[48,1408]{1,0:T(8,128)S(1)} %get-tuple-element.49), channel_id=1, source_target_pairs={{0,4},{4,8},{8,12},{12,16},{16,20},{20,24},{24,28},{28,0},{1,5},{5... | collective-permute-start | bytes 811016 | tf_op jit(solution)/shard_map/ppermute | solution.py:28
  87.0 4.4 %collective-permute-done.8.up_in = f32[48,1408]{1,0:T(8,128)S(1)} collective-permute-done((f32[48,1408]{1,0:T(8,128)S(1)}, f32[48,1408]{1,0:T(8,128)S(1)}, u32[]{:S(2)}, u32[]{:S(2)}) %collective-permute-start.8) | collective-permute-done | bytes 270368 | tf_op jit(solution)/shard_map/ppermute | solution.py:28
  91.5 1.8 %collective-permute-done.9.down_in = f32[48,1408]{1,0:T(8,128)S(1)} collective-permute-done((f32[48,1408]{1,0:T(8,128)S(1)}, f32[48,1408]{1,0:T(8,128)S(1)}, u32[]{:S(2)}, u32[]{:S(2)}) %collective-permute-start.9) | collective-permute-done | bytes 270368 | tf_op jit(solution)/shard_map/ppermute | solution.py:28
  94.2 1.8 %collective-permute-start.10 = (bf16[48,1408]{1,0:T(8,128)(2,1)S(1)}, bf16[48,1408]{1,0:T(8,128)(2,1)S(1)}, u32[]{:S(2)}, u32[]{:S(2)}) collective-permute-start(bf16[48,1408]{1,0:T(8,128)(2,1)S(1)} %get-tuple-element.52), channel_id=1, source_target_pairs={{0,2},{2,0},{1,3},{3,1},{4,6},{6,4},{5,7},{7,5},{8,10},{10,8},{9,1... | collective-permute-start | bytes 405512 | tf_op jit(solution)/shard_map/ppermute | solution.py:23
  96.9 5.2 %all-to-all-start.1 = ((f32[8,48,176]{2,1,0:T(8,128)}), f32[8,48,176]{2,1,0:T(8,128)S(1)}, u32[]{:S(2)}, u32[]{:S(2)}) async-start(f32[8,48,176]{2,1,0:T(8,128)} %shard_map.56), calls=%async_computation.1 | async-start | bytes 786432 | tf_op jit(solution)/shard_map/all_to_all | solution.py:362
  102.2 1.5 collective-permute-start.11
  104.3 10.0 %all-to-all-done.1.columns_ref = f32[8,48,176]{2,1,0:T(8,128)S(1)} async-done(((f32[8,48,176]{2,1,0:T(8,128)}), f32[8,48,176]{2,1,0:T(8,128)S(1)}, u32[]{:S(2)}, u32[]{:S(2)}) %all-to-all-start.1) | async-done | bytes 270368 | tf_op jit(solution)/shard_map/all_to_all | solution.py:362
  115.1 2.0 %collective-permute-start.22 = (f32[8,48,88]{2,1,0:T(8,128)S(1)}, f32[8,48,88]{2,1,0:T(8,128)S(1)}, u32[]{:S(2)}, u32[]{:S(2)}) collective-permute-start(f32[8,48,88]{2,1,0:T(8,128)S(1)} %shard_map.57), channel_id=1, source_target_pairs={{0,2},{2,0},{1,3},{3,1},{4,6},{6,4},{5,7},{7,5},{8,10},{10,8},{9,1... | collective-permute-start | bytes 405512 | tf_op jit(solution)/shard_map/ppermute | solution.py:23
  117.1 1.6 collective-permute-start.14
  119.4 3.0 %collective-permute-done.22.other_ref = f32[8,48,88]{2,1,0:T(8,128)S(1)} collective-permute-done((f32[8,48,88]{2,1,0:T(8,128)S(1)}, f32[8,48,88]{2,1,0:T(8,128)S(1)}, u32[]{:S(2)}, u32[]{:S(2)}) %collective-permute-start.22) | collective-permute-done | bytes 135200 | tf_op jit(solution)/shard_map/ppermute | solution.py:23
  125.4 2.3 %collective-permute-done.13.up_ref.refs_8_ = bf16[96,1408]{1,0:T(8,128)(2,1)S(1)} collective-permute-done((bf16[96,1408]{1,0:T(8,128)(2,1)S(1)}, bf16[96,1408]{1,0:T(8,128)(2,1)S(1)}, u32[]{:S(2)}, u32[]{:S(2)}) %collective-permute-start.13) | collective-permute-done | bytes 270368 | tf_op jit(solution)/shard_map/ppermute | solution.py:28
  127.6 1.8 %collective-permute-start.18 = (bf16[96,1408]{1,0:T(8,128)(2,1)S(1)}, bf16[96,1408]{1,0:T(8,128)(2,1)S(1)}, u32[]{:S(2)}, u32[]{:S(2)}) collective-permute-start(bf16[96,1408]{1,0:T(8,128)(2,1)S(1)} %collective-permute-done.14.down_ref.refs_6_), channel_id=1, source_target_pairs={{0,28},{4,0},{8,4},{12,8},{16,12},{20,16},{24,20},{28,24},{1,29},{... | collective-permute-start | bytes 811016 | tf_op jit(solution)/shard_map/ppermute | solution.py:28
  129.8 3.4 %collective-permute-start.20 = (bf16[48,1408]{1,0:T(8,128)(2,1)S(1)}, bf16[48,1408]{1,0:T(8,128)(2,1)S(1)}, u32[]{:S(2)}, u32[]{:S(2)}) collective-permute-start(bf16[48,1408]{1,0:T(8,128)(2,1)S(1)} %get-tuple-element.59), channel_id=1, source_target_pairs={{0,8},{4,12},{8,16},{12,20},{16,24},{20,28},{24,0},{28,4},{1,9},{5... | collective-permute-start | bytes 405512 | tf_op jit(solution)/shard_map/ppermute | solution.py:28
  134.0 3.2 %shard_map.60 = (f32[48,1408]{1,0:T(8,128)S(1)}, f32[8,48,176]{2,1,0:T(8,128)S(1)}, bf16[48,1408]{1,0:T(8,128)(2,1)S(1)}, bf16[8,2,48,96]{3,2,1,0:T(8,128)(2,1)S(1)}) custom-call(s32[7]{0:T(128)S(1)} %stack.27.where_ref, f32[48,1408]{1,0:T(8,128)S(1)} %get-tuple-element.53.rows_ref, f32[8,48,96]{2,1,0:T(8,128)S(1)} %get-tuple-element.62.near_ref, ...), custom_call_target="tpu_custom_call" | custom-call | flops 129761280 | bytes 2703360 | tf_op jit(solution)/shard_map/pallas_call | solution.py:405
  137.2 7.6 %collective-permute-done.20.refs_4_ = bf16[48,1408]{1,0:T(8,128)(2,1)S(1)} collective-permute-done((bf16[48,1408]{1,0:T(8,128)(2,1)S(1)}, bf16[48,1408]{1,0:T(8,128)(2,1)S(1)}, u32[]{:S(2)}, u32[]{:S(2)}) %collective-permute-start.20) | collective-permute-done | bytes 135200 | tf_op jit(solution)/shard_map/ppermute | solution.py:28
  147.3 1.6 %shard_map.61 = f32[8,48,176]{2,1,0:T(8,128)S(1)} custom-call(s32[7]{0:T(128)S(1)} %stack.27.where_ref, f32[48,1408]{1,0:T(8,128)S(1)} %get-tuple-element.71.total_ref, f32[8,48,176]{2,1,0:T(8,128)S(1)} %get-tuple-element.72.blocks_ref, bf16[48,1408]{1,0:T(8,128)(2,1)S(1)} %get-tuple-element.73.tilde_ref, ...), custom_call_target="tpu_custom_call" | custom-call | flops 77856768 | bytes 1622016 | tf_op jit(solution)/shard_map/pallas_call | solution.py:419
  148.9 11.5 %all_to_all.16 = f32[8,48,176]{2,1,0:T(8,128)S(1)} all-to-all(f32[8,48,176]{2,1,0:T(8,128)S(1)} %shard_map.61), channel_id=1, replica_groups=mesh['x'=4,'yl'=2,'z'=8,'yh'=2,'c'=2] {'x','yl'}, dimensions={0} | all-to-all | bytes 540672 | tf_op jit(solution)/shard_map/all_to_all | solution.py:438
  (60 shorter events, 18.2 us)
Async XLA Ops:
  3.2 2.9 %collective-permute-start = (bf16[8,184,300]{2,1,0:T(8,128)(2,1)S(1)}, bf16[8,184,300]{2,1,0:T(8,128)(2,1)S(1)}, u32[]{:S(2)}, u32[]{:S(2)}) collective-permute-start(bf16[8,184,300]{2,1,0:T(8,128)(2,1)S(1)} %shard_map.46), channel_id=1, source_target_pairs={{0,1},{1,0},{2,3},{3,2},{4,5},{5,4},{6,7},{7,6},{8,9},{9,8},{10,11... | collective-permute-start | bytes 2649608 | tf_op jit(solution)/shard_map/ppermute | solution.py:23
  49.4 5.1 %collective-permute-start.1 = (bf16[16,136,600]{2,1,0:T(8,128)(2,1)S(1)}, bf16[16,136,600]{2,1,0:T(8,128)(2,1)S(1)}, u32[]{:S(2)}, u32[]{:S(2)}) collective-permute-start(bf16[16,136,600]{2,1,0:T(8,128)(2,1)S(1)} %all_to_all.15.near_ref), channel_id=1, source_target_pairs={{0,1},{1,0},{2,3},{3,2},{4,5},{5,4},{6,7},{7,6},{8,9},{9,8},{10,11... | collective-permute-start | bytes 7833608 | tf_op jit(solution)/shard_map/ppermute | solution.py:23
  50.5 7.4 %copy-start.2 = (f32[1408]{0:T(1024)S(1)}, f32[1408]{0:T(1024)}, u32[]{:S(2)}) copy-start(f32[1408]{0:T(1024)} %param.7) | copy-start | bytes 16900
  55.8 5.7 %collective-permute-start.2 = (f32[24,1408]{1,0:T(8,128)S(1)}, f32[24,1408]{1,0:T(8,128)S(1)}, u32[]{:S(2)}, u32[]{:S(2)}) collective-permute-start(f32[24,1408]{1,0:T(8,128)S(1)} %get-tuple-element.43), channel_id=1, source_target_pairs={{0,4},{4,8},{8,12},{12,16},{16,20},{20,24},{24,28},{28,0},{1,5},{5... | collective-permute-start | bytes 405512 | tf_op jit(solution)/shard_map/ppermute | solution.py:28
  57.8 5.5 %collective-permute-start.3 = (f32[24,1408]{1,0:T(8,128)S(1)}, f32[24,1408]{1,0:T(8,128)S(1)}, u32[]{:S(2)}, u32[]{:S(2)}) collective-permute-start(f32[24,1408]{1,0:T(8,128)S(1)} %get-tuple-element.44), channel_id=1, source_target_pairs={{0,28},{4,0},{8,4},{12,8},{16,12},{20,16},{24,20},{28,24},{1,29},{... | collective-permute-start | bytes 405512 | tf_op jit(solution)/shard_map/ppermute | solution.py:28
  63.9 8.8 %collective-permute-start.4 = (f32[48,1408]{1,0:T(8,128)S(1)}, f32[48,1408]{1,0:T(8,128)S(1)}, u32[]{:S(2)}, u32[]{:S(2)}) collective-permute-start(f32[48,1408]{1,0:T(8,128)S(1)} %get-tuple-element.45), channel_id=1, source_target_pairs={{0,4},{4,8},{8,12},{12,16},{16,20},{20,24},{24,28},{28,0},{1,5},{5... | collective-permute-start | bytes 811016 | tf_op jit(solution)/shard_map/ppermute | solution.py:28
  67.1 8.3 %collective-permute-start.5 = (f32[48,1408]{1,0:T(8,128)S(1)}, f32[48,1408]{1,0:T(8,128)S(1)}, u32[]{:S(2)}, u32[]{:S(2)}) collective-permute-start(f32[48,1408]{1,0:T(8,128)S(1)} %get-tuple-element.46), channel_id=1, source_target_pairs={{0,28},{4,0},{8,4},{12,8},{16,12},{20,16},{24,20},{28,24},{1,29},{... | collective-permute-start | bytes 811016 | tf_op jit(solution)/shard_map/ppermute | solution.py:28
  76.0 6.5 %collective-permute-start.6 = (f32[48,1408]{1,0:T(8,128)S(1)}, f32[48,1408]{1,0:T(8,128)S(1)}, u32[]{:S(2)}, u32[]{:S(2)}) collective-permute-start(f32[48,1408]{1,0:T(8,128)S(1)} %get-tuple-element.47), channel_id=1, source_target_pairs={{0,4},{4,8},{8,12},{12,16},{16,20},{20,24},{24,28},{28,0},{1,5},{5... | collective-permute-start | bytes 811016 | tf_op jit(solution)/shard_map/ppermute | solution.py:28
  77.9 6.5 %collective-permute-start.7 = (f32[48,1408]{1,0:T(8,128)S(1)}, f32[48,1408]{1,0:T(8,128)S(1)}, u32[]{:S(2)}, u32[]{:S(2)}) collective-permute-start(f32[48,1408]{1,0:T(8,128)S(1)} %get-tuple-element.48), channel_id=1, source_target_pairs={{0,28},{4,0},{8,4},{12,8},{16,12},{20,16},{24,20},{28,24},{1,29},{... | collective-permute-start | bytes 811016 | tf_op jit(solution)/shard_map/ppermute | solution.py:28
  84.9 6.5 %collective-permute-start.8 = (f32[48,1408]{1,0:T(8,128)S(1)}, f32[48,1408]{1,0:T(8,128)S(1)}, u32[]{:S(2)}, u32[]{:S(2)}) collective-permute-start(f32[48,1408]{1,0:T(8,128)S(1)} %get-tuple-element.49), channel_id=1, source_target_pairs={{0,4},{4,8},{8,12},{12,16},{16,20},{20,24},{24,28},{28,0},{1,5},{5... | collective-permute-start | bytes 811016 | tf_op jit(solution)/shard_map/ppermute | solution.py:28
  86.8 6.5 %collective-permute-start.9 = (f32[48,1408]{1,0:T(8,128)S(1)}, f32[48,1408]{1,0:T(8,128)S(1)}, u32[]{:S(2)}, u32[]{:S(2)}) collective-permute-start(f32[48,1408]{1,0:T(8,128)S(1)} %get-tuple-element.50), channel_id=1, source_target_pairs={{0,28},{4,0},{8,4},{12,8},{16,12},{20,16},{24,20},{28,24},{1,29},{... | collective-permute-start | bytes 811016 | tf_op jit(solution)/shard_map/ppermute | solution.py:28
  94.2 8.0 %collective-permute-start.10 = (bf16[48,1408]{1,0:T(8,128)(2,1)S(1)}, bf16[48,1408]{1,0:T(8,128)(2,1)S(1)}, u32[]{:S(2)}, u32[]{:S(2)}) collective-permute-start(bf16[48,1408]{1,0:T(8,128)(2,1)S(1)} %get-tuple-element.52), channel_id=1, source_target_pairs={{0,2},{2,0},{1,3},{3,1},{4,6},{6,4},{5,7},{7,5},{8,10},{10,8},{9,1... | collective-permute-start | bytes 405512 | tf_op jit(solution)/shard_map/ppermute | solution.py:23
  96.9 17.3 %all-to-all-start.1 = ((f32[8,48,176]{2,1,0:T(8,128)}), f32[8,48,176]{2,1,0:T(8,128)S(1)}, u32[]{:S(2)}, u32[]{:S(2)}) async-start(f32[8,48,176]{2,1,0:T(8,128)} %shard_map.56), calls=%async_computation.1 | async-start | bytes 786432 | tf_op jit(solution)/shard_map/all_to_all | solution.py:362
  102.2 12.9 %collective-permute-start.11 = (bf16[96,1408]{1,0:T(8,128)(2,1)S(1)}, bf16[96,1408]{1,0:T(8,128)(2,1)S(1)}, u32[]{:S(2)}, u32[]{:S(2)}) collective-permute-start(bf16[96,1408]{1,0:T(8,128)(2,1)S(1)} %constant_dynamic-update-slice_fusion.refs_0_), channel_id=1, source_target_pairs={{0,4},{4,8},{8,12},{12,16},{16,20},{20,24},{24,28},{28,0},{1,5},{5... | collective-permute-start | bytes 811016 | tf_op jit(solution)/shard_map/ppermute | solution.py:28
  103.7 11.4 %collective-permute-start.12 = (bf16[96,1408]{1,0:T(8,128)(2,1)S(1)}, bf16[96,1408]{1,0:T(8,128)(2,1)S(1)}, u32[]{:S(2)}, u32[]{:S(2)}) collective-permute-start(bf16[96,1408]{1,0:T(8,128)(2,1)S(1)} %constant_dynamic-update-slice_fusion.refs_0_), channel_id=1, source_target_pairs={{0,28},{4,0},{8,4},{12,8},{16,12},{20,16},{24,20},{28,24},{1,29},{... | collective-permute-start | bytes 811016 | tf_op jit(solution)/shard_map/ppermute | solution.py:28
  115.1 7.3 %collective-permute-start.22 = (f32[8,48,88]{2,1,0:T(8,128)S(1)}, f32[8,48,88]{2,1,0:T(8,128)S(1)}, u32[]{:S(2)}, u32[]{:S(2)}) collective-permute-start(f32[8,48,88]{2,1,0:T(8,128)S(1)} %shard_map.57), channel_id=1, source_target_pairs={{0,2},{2,0},{1,3},{3,1},{4,6},{6,4},{5,7},{7,5},{8,10},{10,8},{9,1... | collective-permute-start | bytes 405512 | tf_op jit(solution)/shard_map/ppermute | solution.py:23
  117.1 6.5 %collective-permute-start.14 = (bf16[96,1408]{1,0:T(8,128)(2,1)S(1)}, bf16[96,1408]{1,0:T(8,128)(2,1)S(1)}, u32[]{:S(2)}, u32[]{:S(2)}) collective-permute-start(bf16[96,1408]{1,0:T(8,128)(2,1)S(1)} %collective-permute-done.12.refs_2_), channel_id=1, source_target_pairs={{0,28},{4,0},{8,4},{12,8},{16,12},{20,16},{24,20},{28,24},{1,29},{... | collective-permute-start | bytes 811016 | tf_op jit(solution)/shard_map/ppermute | solution.py:28
  118.7 6.0 %collective-permute-start.15 = (bf16[96,1408]{1,0:T(8,128)(2,1)S(1)}, bf16[96,1408]{1,0:T(8,128)(2,1)S(1)}, u32[]{:S(2)}, u32[]{:S(2)}) collective-permute-start(bf16[96,1408]{1,0:T(8,128)(2,1)S(1)} %constant_dynamic-update-slice_fusion.refs_0_), channel_id=1, source_target_pairs={{0,1},{1,0},{2,3},{3,2},{4,5},{5,4},{6,7},{7,6},{8,9},{9,8},{10,11... | collective-permute-start | bytes 811016 | tf_op jit(solution)/shard_map/ppermute | solution.py:23
  118.7 8.9 %collective-permute-start.13 = (bf16[96,1408]{1,0:T(8,128)(2,1)S(1)}, bf16[96,1408]{1,0:T(8,128)(2,1)S(1)}, u32[]{:S(2)}, u32[]{:S(2)}) collective-permute-start(bf16[96,1408]{1,0:T(8,128)(2,1)S(1)} %collective-permute-done.11.refs_4_), channel_id=1, source_target_pairs={{0,4},{4,8},{8,12},{12,16},{16,20},{20,24},{24,28},{28,0},{1,5},{5... | collective-permute-start | bytes 811016 | tf_op jit(solution)/shard_map/ppermute | solution.py:28
  119.2 8.5 %collective-permute-start.16 = (bf16[96,1408]{1,0:T(8,128)(2,1)S(1)}, bf16[96,1408]{1,0:T(8,128)(2,1)S(1)}, u32[]{:S(2)}, u32[]{:S(2)}) collective-permute-start(bf16[96,1408]{1,0:T(8,128)(2,1)S(1)} %collective-permute-done.12.refs_2_), channel_id=1, source_target_pairs={{0,1},{1,0},{2,3},{3,2},{4,5},{5,4},{6,7},{7,6},{8,9},{9,8},{10,11... | collective-permute-start | bytes 811016 | tf_op jit(solution)/shard_map/ppermute | solution.py:23
  122.4 5.3 %collective-permute-start.17 = (bf16[96,1408]{1,0:T(8,128)(2,1)S(1)}, bf16[96,1408]{1,0:T(8,128)(2,1)S(1)}, u32[]{:S(2)}, u32[]{:S(2)}) collective-permute-start(bf16[96,1408]{1,0:T(8,128)(2,1)S(1)} %collective-permute-done.11.refs_4_), channel_id=1, source_target_pairs={{0,1},{1,0},{2,3},{3,2},{4,5},{5,4},{6,7},{7,6},{8,9},{9,8},{10,11... | collective-permute-start | bytes 811016 | tf_op jit(solution)/shard_map/ppermute | solution.py:23
  123.6 9.6 %collective-permute-start.24 = (bf16[96,1408]{1,0:T(8,128)(2,1)S(1)}, bf16[96,1408]{1,0:T(8,128)(2,1)S(1)}, u32[]{:S(2)}, u32[]{:S(2)}) collective-permute-start(bf16[96,1408]{1,0:T(8,128)(2,1)S(1)} %collective-permute-done.14.down_ref.refs_6_), channel_id=1, source_target_pairs={{0,1},{1,0},{2,3},{3,2},{4,5},{5,4},{6,7},{7,6},{8,9},{9,8},{10,11... | collective-permute-start | bytes 811016 | tf_op jit(solution)/shard_map/ppermute | solution.py:23
  124.8 5.0 %collective-permute-start.23 = (f32[8,48,96]{2,1,0:T(8,128)S(1)}, f32[8,48,96]{2,1,0:T(8,128)S(1)}, u32[]{:S(2)}, u32[]{:S(2)}) collective-permute-start(f32[8,48,96]{2,1,0:T(8,128)S(1)} %get-tuple-element.63), channel_id=1, source_target_pairs={{0,1},{1,0},{2,3},{3,2},{4,5},{5,4},{6,7},{7,6},{8,9},{9,8},{10,11... | collective-permute-start | bytes 442376 | tf_op jit(solution)/shard_map/ppermute | solution.py:23
  127.6 6.4 %collective-permute-start.25 = (bf16[96,1408]{1,0:T(8,128)(2,1)S(1)}, bf16[96,1408]{1,0:T(8,128)(2,1)S(1)}, u32[]{:S(2)}, u32[]{:S(2)}) collective-permute-start(bf16[96,1408]{1,0:T(8,128)(2,1)S(1)} %collective-permute-done.13.up_ref.refs_8_), channel_id=1, source_target_pairs={{0,1},{1,0},{2,3},{3,2},{4,5},{5,4},{6,7},{7,6},{8,9},{9,8},{10,11... | collective-permute-start | bytes 811016 | tf_op jit(solution)/shard_map/ppermute | solution.py:23
  127.6 17.2 %collective-permute-start.18 = (bf16[96,1408]{1,0:T(8,128)(2,1)S(1)}, bf16[96,1408]{1,0:T(8,128)(2,1)S(1)}, u32[]{:S(2)}, u32[]{:S(2)}) collective-permute-start(bf16[96,1408]{1,0:T(8,128)(2,1)S(1)} %collective-permute-done.14.down_ref.refs_6_), channel_id=1, source_target_pairs={{0,28},{4,0},{8,4},{12,8},{16,12},{20,16},{24,20},{28,24},{1,29},{... | collective-permute-start | bytes 811016 | tf_op jit(solution)/shard_map/ppermute | solution.py:28
  129.5 15.3 %collective-permute-start.19 = (bf16[96,1408]{1,0:T(8,128)(2,1)S(1)}, bf16[96,1408]{1,0:T(8,128)(2,1)S(1)}, u32[]{:S(2)}, u32[]{:S(2)}) collective-permute-start(bf16[96,1408]{1,0:T(8,128)(2,1)S(1)} %collective-permute-done.13.up_ref.refs_8_), channel_id=1, source_target_pairs={{0,4},{4,8},{8,12},{12,16},{16,20},{20,24},{24,28},{28,0},{1,5},{5... | collective-permute-start | bytes 811016 | tf_op jit(solution)/shard_map/ppermute | solution.py:28
  129.8 15.0 %collective-permute-start.20 = (bf16[48,1408]{1,0:T(8,128)(2,1)S(1)}, bf16[48,1408]{1,0:T(8,128)(2,1)S(1)}, u32[]{:S(2)}, u32[]{:S(2)}) collective-permute-start(bf16[48,1408]{1,0:T(8,128)(2,1)S(1)} %get-tuple-element.59), channel_id=1, source_target_pairs={{0,8},{4,12},{8,16},{12,20},{16,24},{20,28},{24,0},{28,4},{1,9},{5... | collective-permute-start | bytes 405512 | tf_op jit(solution)/shard_map/ppermute | solution.py:28
  133.2 11.6 %collective-permute-start.21 = (bf16[48,1408]{1,0:T(8,128)(2,1)S(1)}, bf16[48,1408]{1,0:T(8,128)(2,1)S(1)}, u32[]{:S(2)}, u32[]{:S(2)}) collective-permute-start(bf16[48,1408]{1,0:T(8,128)(2,1)S(1)} %get-tuple-element.60), channel_id=1, source_target_pairs={{0,24},{4,28},{8,0},{12,4},{16,8},{20,12},{24,16},{28,20},{1,25},{... | collective-permute-start | bytes 405512 | tf_op jit(solution)/shard_map/ppermute | solution.py:28
  144.8 2.4 %collective-permute-start.26 = (bf16[96,1408]{1,0:T(8,128)(2,1)S(1)}, bf16[96,1408]{1,0:T(8,128)(2,1)S(1)}, u32[]{:S(2)}, u32[]{:S(2)}) collective-permute-start(bf16[96,1408]{1,0:T(8,128)(2,1)S(1)} %collective-permute-done.18.refs_0_), channel_id=1, source_target_pairs={{0,1},{1,0},{2,3},{3,2},{4,5},{5,4},{6,7},{7,6},{8,9},{9,8},{10,11... | collective-permute-start | bytes 811016 | tf_op jit(solution)/shard_map/ppermute | solution.py:23
  144.9 2.3 %collective-permute-start.27 = (bf16[96,1408]{1,0:T(8,128)(2,1)S(1)}, bf16[96,1408]{1,0:T(8,128)(2,1)S(1)}, u32[]{:S(2)}, u32[]{:S(2)}) collective-permute-start(bf16[96,1408]{1,0:T(8,128)(2,1)S(1)} %collective-permute-done.19.refs_2_), channel_id=1, source_target_pairs={{0,1},{1,0},{2,3},{3,2},{4,5},{5,4},{6,7},{7,6},{8,9},{9,8},{10,11... | collective-permute-start | bytes 811016 | tf_op jit(solution)/shard_map/ppermute | solution.py:23
  145.4 1.6 %collective-permute-start.28 = (bf16[48,1408]{1,0:T(8,128)(2,1)S(1)}, bf16[48,1408]{1,0:T(8,128)(2,1)S(1)}, u32[]{:S(2)}, u32[]{:S(2)}) collective-permute-start(bf16[48,1408]{1,0:T(8,128)(2,1)S(1)} %collective-permute-done.20.refs_4_), channel_id=1, source_target_pairs={{0,1},{1,0},{2,3},{3,2},{4,5},{5,4},{6,7},{7,6},{8,9},{9,8},{10,11... | collective-permute-start | bytes 405512 | tf_op jit(solution)/shard_map/ppermute | solution.py:23
  145.5 1.7 %collective-permute-start.29 = (bf16[48,1408]{1,0:T(8,128)(2,1)S(1)}, bf16[48,1408]{1,0:T(8,128)(2,1)S(1)}, u32[]{:S(2)}, u32[]{:S(2)}) collective-permute-start(bf16[48,1408]{1,0:T(8,128)(2,1)S(1)} %collective-permute-done.21.refs_5_), channel_id=1, source_target_pairs={{0,1},{1,0},{2,3},{3,2},{4,5},{5,4},{6,7},{7,6},{8,9},{9,8},{10,11... | collective-permute-start | bytes 405512 | tf_op jit(solution)/shard_map/ppermute | solution.py:23
  (2 other events, 9.0 us)

commit v8 on v7

v8 whole, which is shorter than its diff:
```python
import functools

import jax
import jax.numpy as jnp
from jax import lax
from jax.experimental import pallas as pl
from jax.experimental.pallas import tpu as pltpu
from jax.sharding import Mesh
from jax.sharding import PartitionSpec as P

F32 = jnp.float32
BF16 = jnp.bfloat16
SLABS = ("x", "yl")
VMEM = pl.BlockSpec(memory_space=pltpu.VMEM)
SMEM = pl.BlockSpec(memory_space=pltpu.SMEM)


def params(mib):
    return pltpu.CompilerParams(vmem_limit_bytes=mib * 1024 * 1024)


def swap(value, axis):
    return lax.ppermute(value, axis, [(0, 1), (1, 0)])


def shift(value, axis, step):
    size = lax.axis_size(axis)
    return lax.ppermute(value, axis, [(i, (i + step) % size) for i in range(size)])


def dot_nt(a, b):
    return lax.dot_general(a, b, (((1,), (1,)), ((), ())), preferred_element_type=F32)


def cost(flops, moved):
    return pl.CostEstimate(flops=flops, bytes_accessed=moved, transcendentals=0)


def fill(side, width, padded, pair_ref, orbital_ref, put):
    half = orbital_ref.shape[1] // 2
    gap = jnp.zeros((padded - width, orbital_ref.shape[2]), BF16)
    for p in range(pair_ref.shape[1]):
        left = orbital_ref[pair_ref[0, p]]
        right = orbital_ref[pair_ref[1, p]]
        for y in range(2):
            at = (2 * y + side) * width
            put(p, y, jnp.concatenate([left[at : at + width], gap], axis=0))
        put(p, 2, right[side * half : (side + 1) * half])


def select_kernel(width, padded, where_ref, pair_ref, orbital_ref, out_ref):
    def put(p, block, value):
        out_ref[p, block * padded : block * padded + value.shape[0]] = value

    for c in range(2):

        @pl.when(where_ref[1] == c)
        def _():
            fill(1 - c, width, padded, pair_ref, orbital_ref, put)


def own_kernel(width, padded, where_ref, pair_ref, orbital_ref, out_ref):
    groups, naux = pair_ref.shape[1], orbital_ref.shape[2]
    for c in range(2):
        lanes = slice(c * naux, (c + 1) * naux)

        def put(p, block, value, lanes=lanes):
            if block < 2:
                out_ref[block * groups + p, :padded, lanes] = value
            else:
                for y in range(2):
                    out_ref[y * groups + p, padded:, lanes] = value

        @pl.when(where_ref[1] == c)
        def _(c=c, put=put):
            fill(c, width, padded, pair_ref, orbital_ref, put)


def other_kernel(padded, where_ref, taken_ref, own_ref, out_ref):
    groups, naux = taken_ref.shape[0], taken_ref.shape[2]
    for c in range(2):
        lanes = slice((1 - c) * naux, (2 - c) * naux)

        @pl.when(where_ref[1] == c)
        def _(lanes=lanes):
            for p in range(groups):
                for y in range(2):
                    out_ref[y * groups + p, :padded, lanes] = taken_ref[p, y * padded : (y + 1) * padded]
                    out_ref[y * groups + p, padded:, lanes] = taken_ref[p, 2 * padded :]


def half_product(left, right_ref, padded):
    sources = right_ref.shape[0]
    half = sources // 2
    total = None
    for y in range(2):
        right = jnp.concatenate([right_ref[half * y + k, padded:, :] for k in range(half)], axis=0)
        term = dot_nt(left(y), right)
        total = term if total is None else total + term
    return total


def all_rows(near_ref, padded):
    half = near_ref.shape[0] // 2

    def left(y):
        return near_ref[half * y : half * (y + 1), :padded, :].reshape(half * padded, near_ref.shape[2])

    return left


def near_kernel(padded, near_ref, out_ref):
    out_ref[...] = half_product(all_rows(near_ref, padded), near_ref, padded).reshape(out_ref.shape)


def first_kernel(padded, where_ref, near_part_ref, near_ref, far_ref, *out_refs):
    nz = near_part_ref.shape[0]
    half = near_ref.shape[0] // 2
    cut = padded // 2
    places = [lax.rem(where_ref[0] + offset, nz) for offset in (nz // 2, nz // 2 - 1, nz // 2 + 1)]

    def left(y):
        return jnp.concatenate([near_ref[half * y + at, :padded, :] for at in places], axis=0)

    total = half_product(left, far_ref, padded)
    sums = [
        jnp.concatenate([near_part_ref[at], total[n * padded : (n + 1) * padded]], axis=1)
        for n, at in enumerate(places)
    ]
    for ref, value in zip(out_refs, (sums[0][:cut], sums[0][cut:], sums[1], sums[2])):
        ref[...] = value


def rest_kernel(padded, where_ref, pair_ref, occ_ref, vir_ref, near_part_ref, near_ref, far_ref, out_ref, denom_ref):
    total = half_product(all_rows(near_ref, padded), far_ref, padded).reshape(near_part_ref.shape)
    for k in range(near_part_ref.shape[0]):
        out_ref[k] = jnp.concatenate([near_part_ref[k], total[k]], axis=1)
    chunk, group, width = where_ref[2], where_ref[3], where_ref[5]
    columns = jnp.broadcast_to(vir_ref[...], denom_ref.shape)
    place = lax.broadcasted_iota(jnp.int32, denom_ref.shape, 1)
    row = lax.broadcasted_iota(jnp.int32, denom_ref.shape, 0)
    own = jnp.sum(jnp.where(place == chunk * width + row, columns, 0.0), axis=1, keepdims=True)
    denom_ref[...] = (own + columns) - occ_ref[pair_ref[0, group]] - occ_ref[pair_ref[1, group]]


def hop_kernel(step, where_ref, part_ref, *refs):
    nz, rows = part_ref.shape[:2]
    above = lax.rem(where_ref[0] + step, nz)
    below = lax.rem(where_ref[0] + nz - step, nz)
    up_in, down_in = refs[:2]
    up_ref, down_ref = refs[-2:]
    up_ref[...] = part_ref[above] + up_in[...]
    down_ref[...] = part_ref[below] + down_in[...]
    if len(refs) > 4:
        cut = rows // 2
        up_ref[:cut] += refs[2][...]
        down_ref[cut:] += refs[3][...]


def amplitude_kernel(where_ref, part_ref, up_in, down_in, denom_ref, out_ref, rounded_ref):
    sums = part_ref[where_ref[0]] + (up_in[...] + down_in[...])
    half = sums.shape[1] // 2
    near, far = sums[:, :half], sums[:, half:]
    halves = (jnp.where(where_ref[1] == 0, near, far), jnp.where(where_ref[1] == 0, far, near))
    step = half // part_ref.shape[0]
    parts = [h[:, k * step : (k + 1) * step] for k in range(part_ref.shape[0]) for h in halves]
    amps = jnp.concatenate(parts, axis=1) / denom_ref[...]
    out_ref[...] = amps
    rounded_ref[...] = amps.astype(BF16)


def blocks_kernel(rows_ref, blocks_ref):
    count, half, lanes = blocks_ref.shape
    width = rows_ref.shape[1] // count
    gap = jnp.zeros((half, lanes // 2 - width), F32)
    for k in range(count):
        block = rows_ref[:, k * width : (k + 1) * width]
        blocks_ref[k] = jnp.concatenate([block[:half], gap, block[half:], gap], axis=1)


def merge_kernel(width, first_ref, second_ref, out_ref):
    out_ref[...] = jnp.concatenate([first_ref[:width], second_ref[:width]], axis=0)


def halves_kernel(up_ref, down_ref, first_ref, second_ref):
    first_ref[...] = up_ref[: first_ref.shape[0]]
    second_ref[...] = down_ref[first_ref.shape[0] :]


def natural(c, yh, near, far):
    width = near.shape[1] // 2
    parts = []
    for y in range(2):
        for h in range(2):
            side = jnp.where(c == h, near, far)
            parts.append(jnp.where(yh == y, side[:, :width], side[:, width:]))
    return jnp.concatenate(parts, axis=1)


def relative(c, yh, block):
    width = block.shape[1] // 4
    sides = []
    for h in range(2):
        first, second = block[:, h * width : (h + 1) * width], block[:, (2 + h) * width : (3 + h) * width]
        sides.append(jnp.concatenate([jnp.where(yh == 0, first, second), jnp.where(yh == 0, second, first)], axis=1))
    return jnp.where(c == 0, sides[0], sides[1]), jnp.where(c == 0, sides[1], sides[0])


def density_pieces(steps, nz, where_ref, tilde, tilde_t_ref, pieces, total, blocks_ref):
    z, c, yh = where_ref[0], where_ref[1], where_ref[6]
    rows = tilde_t_ref.shape[3]
    pieces = list(pieces)
    for r in steps:
        at = lax.rem(z + r, nz)
        sides = []
        for slot in range(2):
            piece = pieces.pop(0)[...]
            if piece.shape[0] < rows:
                piece = jnp.concatenate([piece, pieces.pop(0)[...]], axis=0)
            term = jnp.dot(tilde_t_ref[at, slot], piece, preferred_element_type=F32)
            total = term if total is None else total + term
            sides.append(dot_nt(tilde, piece))
        blocks_ref[at] = natural(c, yh, sides[0], sides[1])
    return total


def early_kernel(steps, nz, where_ref, rows_ref, columns_ref, *refs):
    pieces = refs[:-4]
    total_ref, blocks_ref, tilde_ref, tilde_t_ref = refs[-4:]
    c, yh = where_ref[1], where_ref[6]
    rows = rows_ref[...]
    padded, nvir = rows.shape
    slab = nvir // nz
    width = slab // 4

    def turn(at):
        flipped = columns_ref[at].T
        return jnp.concatenate([flipped[:padded], flipped[padded:, : width - padded // 2]], axis=1)

    turned = []
    for k in range(nz):
        near, far = (
            jnp.concatenate([turn(4 * k + 2 * yh + h), turn(4 * k + 2 * (1 - yh) + h)], axis=1) for h in (c, 1 - c)
        )
        mine = relative(c, yh, rows[:, k * slab : (k + 1) * slab])
        tilde_t_ref[k, 0] = (2.0 * near - mine[0]).astype(BF16)
        tilde_t_ref[k, 1] = (2.0 * far - mine[1]).astype(BF16)
        turned.append(natural(c, yh, near, far))
    tilde = (2.0 * rows - jnp.concatenate(turned, axis=1)).astype(BF16)
    tilde_ref[...] = tilde
    total_ref[...] = density_pieces(steps, nz, where_ref, tilde, tilde_t_ref, pieces, None, blocks_ref)


def late_kernel(steps, nz, where_ref, total_ref, blocks_ref, tilde_ref, tilde_t_ref, *refs):
    pieces, out_ref = refs[:-1], refs[-1]
    slab = total_ref.shape[1] // nz
    for k in range(nz):
        out_ref[k] = blocks_ref[k]
    total = density_pieces(
        steps, nz, where_ref, tilde_ref[...], tilde_t_ref, pieces, total_ref[...], out_ref
    )
    for k in range(nz):
        out_ref[k] += total[:, k * slab : (k + 1) * slab]


def local(orbital_b, pair_list, eps_occ, eps_vir):
    slab, naux = orbital_b.shape[1:]
    nvir = eps_vir.shape[0]
    z, yh, c = (lax.axis_index(a) for a in ("z", "yh", "c"))
    nz = lax.axis_size("z")
    width = slab // 4
    padded = (width + 8) // 8 * 8
    where = jnp.stack([z, c, z * 4 + yh * 2 + c, lax.axis_index(SLABS), yh * 2 + c, jnp.int32(width), yh])

    pairs = pair_list.T

    sent = 2 * padded + slab // 2
    theirs = pl.pallas_call(
        functools.partial(select_kernel, width, padded),
        out_shape=jax.ShapeDtypeStruct((8, sent, naux), BF16),
        in_specs=[SMEM, SMEM, VMEM],
        out_specs=VMEM,
        compiler_params=params(8),
    )(where, pairs, orbital_b)
    taken = swap(theirs, "c")
    outgoing = jax.ShapeDtypeStruct((16, sent - padded, 2 * naux), BF16)
    ours = pl.pallas_call(
        functools.partial(own_kernel, width, padded),
        out_shape=outgoing,
        in_specs=[SMEM, SMEM, VMEM],
        out_specs=VMEM,
        compiler_params=params(8),
    )(where, pairs, orbital_b)
    ours = pl.pallas_call(
        functools.partial(other_kernel, padded),
        out_shape=outgoing,
        in_specs=[SMEM, VMEM, VMEM],
        out_specs=VMEM,
        input_output_aliases={2: 0},
        compiler_params=params(8),
    )(where, taken, ours)
    near = lax.all_to_all(ours, ("yh", "x", "yl"), split_axis=0, concat_axis=0, tiled=True)
    far = swap(near, "c")

    whole = jax.ShapeDtypeStruct((8, padded, nvir), F32)
    rows = jax.ShapeDtypeStruct((padded, nvir), F32)
    halves = jax.ShapeDtypeStruct((padded // 2, nvir), F32)
    flops = 16 * padded * 8 * slab * 2 * naux
    near_part = pl.pallas_call(
        functools.partial(near_kernel, padded),
        out_shape=jax.ShapeDtypeStruct((8, padded, nvir // 2), F32),
        in_specs=[VMEM],
        out_specs=VMEM,
        compiler_params=params(16),
        cost_estimate=cost(flops, 0),
    )(near)
    half_up, half_down, up, down = pl.pallas_call(
        functools.partial(first_kernel, padded),
        out_shape=(halves, halves, rows, rows),
        in_specs=[SMEM, VMEM, VMEM, VMEM],
        out_specs=(VMEM,) * 4,
        compiler_params=params(16),
        cost_estimate=cost(flops // 4, 0),
    )(where, near_part, near, far)
    sums = (shift(up, "z", 1), shift(down, "z", -1), shift(half_up, "z", 2), shift(half_down, "z", -2))
    part, denom = pl.pallas_call(
        functools.partial(rest_kernel, padded),
        out_shape=(whole, rows),
        in_specs=[SMEM, SMEM, SMEM, VMEM, VMEM, VMEM, VMEM],
        out_specs=(VMEM, VMEM),
        compiler_params=params(16),
        cost_estimate=cost(flops, 0),
    )(where, pairs, eps_occ, eps_vir[None], near_part, near, far)
    for step in range(nz // 2 - 2, 0, -1):
        up, down = pl.pallas_call(
            functools.partial(hop_kernel, step),
            out_shape=(rows, rows),
            in_specs=[SMEM] + [VMEM] * (1 + len(sums)),
            out_specs=(VMEM, VMEM),
            compiler_params=params(8),
        )(where, part, *sums)
        sums = (shift(up, "z", 1), shift(down, "z", -1))
    up, down = sums
    rows16 = jax.ShapeDtypeStruct((padded, nvir), BF16)
    amp_rows, mine = pl.pallas_call(
        amplitude_kernel,
        out_shape=(rows, rows16),
        in_specs=[SMEM, VMEM, VMEM, VMEM, VMEM],
        out_specs=(VMEM, VMEM),
        compiler_params=params(8),
    )(where, part, up, down, denom)

    other = swap(mine, "yh")
    columns = pl.pallas_call(
        blocks_kernel,
        out_shape=jax.ShapeDtypeStruct((4 * nz, padded // 2, 2 * padded), F32),
        in_specs=[VMEM],
        out_specs=VMEM,
        compiler_params=params(8),
    )(amp_rows)
    other, _ = lax.optimization_barrier((other, columns))
    columns = lax.all_to_all(columns, ("z", "yh", "c"), split_axis=0, concat_axis=0, tiled=True)
    both = pl.pallas_call(
        functools.partial(merge_kernel, width),
        out_shape=jax.ShapeDtypeStruct((2 * width, nvir), BF16),
        in_specs=[VMEM, VMEM],
        out_specs=VMEM,
        compiler_params=params(8),
    )(mine, other)
    ring = {0: both}
    up = down = both
    for step in range(1, nz // 2 - 1):
        up, down = shift(up, "z", 1), shift(down, "z", -1)
        ring[nz - step], ring[step] = up, down
        up, down = lax.optimization_barrier((up, down))
    far = {r: swap(ring[r], "c") for r in (0, 1, nz - 1)}
    up, down, far = lax.optimization_barrier((up, down, far))
    half_up, half_down = pl.pallas_call(
        halves_kernel,
        out_shape=(rows16, jax.ShapeDtypeStruct((2 * width - padded, nvir), BF16)),
        in_specs=[VMEM, VMEM],
        out_specs=(VMEM, VMEM),
        compiler_params=params(8),
    )(up, down)
    half_up, half_down, columns = lax.optimization_barrier((half_up, half_down, columns))
    last = (shift(down, "z", -1), shift(up, "z", 1), shift(half_up, "z", 2), shift(half_down, "z", -2))

    soon = (0, 1, nz - 1, 2, nz - 2)
    late = (3, nz - 3, nz // 2)
    far.update({r: swap(ring[r], "c") for r in (2, nz - 2)})
    ring[0] = both
    pieces = [v for r in soon for v in (ring[r], far[r])]
    state = pl.pallas_call(
        functools.partial(early_kernel, soon, nz),
        out_shape=(
            rows,
            jax.ShapeDtypeStruct((nz, padded, slab), F32),
            rows16,
            jax.ShapeDtypeStruct((nz, 2, padded, 2 * width), BF16),
        ),
        in_specs=[SMEM] + [VMEM] * (2 + 2 * len(soon)),
        out_specs=(VMEM,) * 4,
        compiler_params=params(16),
        cost_estimate=cost(len(soon) * 8 * padded * padded * nvir, len(soon) * 8 * padded * nvir),
    )(where, amp_rows, columns, *pieces)
    last, state = lax.optimization_barrier((last, state))
    added = pl.pallas_call(
        functools.partial(late_kernel, late, nz),
        out_shape=jax.ShapeDtypeStruct((nz, padded, slab), F32),
        in_specs=[SMEM] + [VMEM] * (6 + 2 * len(late)),
        out_specs=VMEM,
        compiler_params=params(16),
        cost_estimate=cost(len(late) * 8 * padded * padded * nvir, len(late) * 8 * padded * nvir),
    )(
        where,
        *state,
        last[0],
        swap(last[0], "c"),
        last[1],
        swap(last[1], "c"),
        last[2],
        last[3],
        swap(last[2], "c"),
        swap(last[3], "c"),
    )
    added = lax.all_to_all(added, SLABS, split_axis=0, concat_axis=0, tiled=True)
    return jnp.sum(added, axis=0)[:width]


def solution(mesh):
    fine = Mesh(mesh.devices.reshape(4, 2, 8, 2, 2), ("x", "yl", "z", "yh", "c"))
    pair, grid = SLABS, ("z", "yh", "c")
    in_specs = (P(None, pair, grid), P(), P(), P())
    return jax.shard_map(local, mesh=fine, in_specs=in_specs, out_specs=P(grid, pair), check_vma=False)
```

time: 161 us -> 161 us (level)
  starting transfers between devices: 31 us -> 36 us
  waiting for transfers between devices: 55.7 us -> 50.8 us
    all_to_all x1, waiting for transfers between devices: 9.96 us -> 0.01 us  [local(): lax.all_to_all(columns, ('z', 'yh', 'c'), split_axis=0, concat_axis=0, ti...]
    ppermute x16, starting transfers between devices: 20 us -> 24.5 us  [shift(): lax.ppermute(value, axis, [(i, (i + step) % size) for i in range(size)])]
    ppermute x16, waiting for transfers between devices: 35.5 us -> 39.7 us  [shift(): lax.ppermute(value, axis, [(i, (i + step) % size) for i in range(size)])]
    all_to_all x1, starting transfers between devices: 5.19 us -> 7.57 us  [local(): lax.all_to_all(columns, ('z', 'yh', 'c'), split_axis=0, concat_axis=0, ti...]
    ppermute x14 -> x12, starting transfers between devices: 5.89 us -> 3.99 us  [swap(): return lax.ppermute(value, axis, [(0, 1), (1, 0)])]
    ppermute x14 -> x12, waiting for transfers between devices: 10.3 us -> 11.1 us  [swap(): return lax.ppermute(value, axis, [(0, 1), (1, 0)])]
    pallas_call x6 -> x5, Pallas kernels: 7.73 us -> 7.23 us  [the longest x1 4.48 us: local(): pl.pallas_call(functools.partial(early_kernel, soon, nz), out_shape=(rows...]
  transfers between devices with their start and end apart: 31 -> 29, of which waited for: 17 -> 12; matrix products, arithmetic and copies ran while one was open for 0% -> 0% of each run, Pallas kernels for 6% -> 6%
where the time goes in v8:
time: 161 us; the launch traced here: 160 us
  blocking collectives  53.6 us (33%)
  waiting for transfers between devices  50.8 us (32%)
  starting transfers between devices  36 us (22%)
  Pallas kernels  16.1 us (10%)
  local copies, waits for them, and re-layouts  3.03 us (2%)
    all_to_all x1, blocking collectives, local(): lax.all_to_all(ours, ('yh', 'x', 'yl'), split_axis=0, concat_axis=0, tile...  42.1 us
    ppermute x16, waiting for transfers between devices, shift(): lax.ppermute(value, axis, [(i, (i + step) % size) for i in range(size)])  39.7 us
    ppermute x16, starting transfers between devices, shift(): lax.ppermute(value, axis, [(i, (i + step) % size) for i in range(size)])  24.5 us
    all_to_all x1, blocking collectives, local(): lax.all_to_all(added, SLABS, split_axis=0, concat_axis=0, tiled=True)  11.5 us
    ppermute x12, waiting for transfers between devices, swap(): return lax.ppermute(value, axis, [(0, 1), (1, 0)])  11.1 us
    all_to_all x1, starting transfers between devices, local(): lax.all_to_all(columns, ('z', 'yh', 'c'), split_axis=0, concat_axis=0, ti...  7.57 us
    pallas_call x1, Pallas kernels, local(): pl.pallas_call(functools.partial(early_kernel, soon, nz), out_shape=(rows...  4.48 us
    ppermute x12, starting transfers between devices, swap(): return lax.ppermute(value, axis, [(0, 1), (1, 0)])  3.99 us
  transfers between devices with their start and end apart: 29, of which 12 were waited for; matrix products, arithmetic and copies ran while one was open for 0% of the time, Pallas kernels for 6%

profile of v8, /device:TPU:32, one launch (start us, length us, event | category | flops | bytes accessed | tf_op | source)
XLA Modules:
  0.0 160.4 jit_solution(7782426802189985200)
XLA Ops:
  0.1 1.6 %copy-done = bf16[16,176,300]{2,1,0:T(8,128)(2,1)S(1)} copy-done((bf16[16,176,300]{2,1,0:T(8,128)(2,1)S(1)}, bf16[16,176,300]{2,1,0:T(8,128)(2,1)}, u32[]{:S(2)}) %copy-start) | copy-done | bytes 1689624
  3.9 2.0 %collective-permute-done.taken_ref = bf16[8,184,300]{2,1,0:T(8,128)(2,1)S(1)} collective-permute-done((bf16[8,184,300]{2,1,0:T(8,128)(2,1)S(1)}, bf16[8,184,300]{2,1,0:T(8,128)(2,1)S(1)}, u32[]{:S(2)}, u32[]{:S(2)}) %collective-permute-start) | collective-permute-done | bytes 883232 | tf_op jit(solution)/shard_map/ppermute | solution.py:23
  5.9 1.2 shard_map.48
  7.1 42.1 %all_to_all.15.near_ref = bf16[16,136,600]{2,1,0:T(8,128)(2,1)S(1)} all-to-all(bf16[16,136,600]{2,1,0:T(8,128)(2,1)S(1)} %shard_map.48), channel_id=1, replica_groups=mesh['x'=4,'yl'=2,'z'=8,'yh'=2,'c'=2] {'yh','x','yl'}, dimensions={0} | all-to-all | bytes 5222400 | tf_op jit(solution)/shard_map/all_to_all | solution.py:302
  49.3 1.1 shard_map.49.near_part_ref
  50.4 4.0 %collective-permute-done.1.far_ref = bf16[16,136,600]{2,1,0:T(8,128)(2,1)S(1)} collective-permute-done((bf16[16,136,600]{2,1,0:T(8,128)(2,1)S(1)}, bf16[16,136,600]{2,1,0:T(8,128)(2,1)S(1)}, u32[]{:S(2)}, u32[]{:S(2)}) %collective-permute-start.1) | collective-permute-done | bytes 2611232 | tf_op jit(solution)/shard_map/ppermute | solution.py:23
  54.4 1.3 shard_map.51
  55.7 2.0 %collective-permute-start.2 = (f32[48,1408]{1,0:T(8,128)S(1)}, f32[48,1408]{1,0:T(8,128)S(1)}, u32[]{:S(2)}, u32[]{:S(2)}) collective-permute-start(f32[48,1408]{1,0:T(8,128)S(1)} %get-tuple-element.45), channel_id=1, source_target_pairs={{0,4},{4,8},{8,12},{12,16},{16,20},{20,24},{24,28},{28,0},{1,5},{5... | collective-permute-start | bytes 811016 | tf_op jit(solution)/shard_map/ppermute | solution.py:28
  57.8 4.4 %collective-permute-start.4 = (f32[24,1408]{1,0:T(8,128)S(1)}, f32[24,1408]{1,0:T(8,128)S(1)}, u32[]{:S(2)}, u32[]{:S(2)}) collective-permute-start(f32[24,1408]{1,0:T(8,128)S(1)} %get-tuple-element.47), channel_id=1, source_target_pairs={{0,8},{4,12},{8,16},{12,20},{16,24},{20,28},{24,0},{28,4},{1,9},{5... | collective-permute-start | bytes 405512 | tf_op jit(solution)/shard_map/ppermute | solution.py:28
  62.2 1.0 collective-permute-start.5
  63.3 1.7 %shard_map.50 = (f32[8,48,1408]{2,1,0:T(8,128)S(1)}, f32[48,1408]{1,0:T(8,128)S(1)}) custom-call(s32[7]{0:T(128)S(1)} %stack.27.where_ref, s32[2,8]{1,0:T(2,128)S(1)} %bitcast.10, f32[16]{0:T(128)S(1)} %copy-done.3, f32[1,1408]{1,0:T(1,128)S(1)} %broadcast_in_dim.3.vir_ref, f32[8,48,704]{2,1,0:T(8,128)S(1)} %shard_map.49.near_part_ref, ...), custom_call_target="tpu_custom_call" | custom-call | flops 648806400 | tf_op jit(solution)/shard_map/pallas_call | solution.py:326
  65.0 8.8 %collective-permute-done.4.refs_2_ = f32[24,1408]{1,0:T(8,128)S(1)} collective-permute-done((f32[24,1408]{1,0:T(8,128)S(1)}, f32[24,1408]{1,0:T(8,128)S(1)}, u32[]{:S(2)}, u32[]{:S(2)}) %collective-permute-start.4) | collective-permute-done | bytes 135200 | tf_op jit(solution)/shard_map/ppermute | solution.py:28
  74.4 3.7 %collective-permute-start.6 = (f32[48,1408]{1,0:T(8,128)S(1)}, f32[48,1408]{1,0:T(8,128)S(1)}, u32[]{:S(2)}, u32[]{:S(2)}) collective-permute-start(f32[48,1408]{1,0:T(8,128)S(1)} %get-tuple-element.49), channel_id=1, source_target_pairs={{0,4},{4,8},{8,12},{12,16},{16,20},{20,24},{24,28},{28,0},{1,5},{5... | collective-permute-start | bytes 811016 | tf_op jit(solution)/shard_map/ppermute | solution.py:28
  78.2 4.9 %collective-permute-done.6.refs_0_ = f32[48,1408]{1,0:T(8,128)S(1)} collective-permute-done((f32[48,1408]{1,0:T(8,128)S(1)}, f32[48,1408]{1,0:T(8,128)S(1)}, u32[]{:S(2)}, u32[]{:S(2)}) %collective-permute-start.6) | collective-permute-done | bytes 270368 | tf_op jit(solution)/shard_map/ppermute | solution.py:28
  83.1 2.2 %collective-permute-done.7.refs_1_ = f32[48,1408]{1,0:T(8,128)S(1)} collective-permute-done((f32[48,1408]{1,0:T(8,128)S(1)}, f32[48,1408]{1,0:T(8,128)S(1)}, u32[]{:S(2)}, u32[]{:S(2)}) %collective-permute-start.7) | collective-permute-done | bytes 270368 | tf_op jit(solution)/shard_map/ppermute | solution.py:28
  86.3 1.6 %collective-permute-start.9 = (f32[48,1408]{1,0:T(8,128)S(1)}, f32[48,1408]{1,0:T(8,128)S(1)}, u32[]{:S(2)}, u32[]{:S(2)}) collective-permute-start(f32[48,1408]{1,0:T(8,128)S(1)} %get-tuple-element.52), channel_id=1, source_target_pairs={{0,28},{4,0},{8,4},{12,8},{16,12},{20,16},{24,20},{28,24},{1,29},{... | collective-permute-start | bytes 811016 | tf_op jit(solution)/shard_map/ppermute | solution.py:28
  88.0 4.4 %collective-permute-done.8.up_in = f32[48,1408]{1,0:T(8,128)S(1)} collective-permute-done((f32[48,1408]{1,0:T(8,128)S(1)}, f32[48,1408]{1,0:T(8,128)S(1)}, u32[]{:S(2)}, u32[]{:S(2)}) %collective-permute-start.8) | collective-permute-done | bytes 270368 | tf_op jit(solution)/shard_map/ppermute | solution.py:28
  93.7 1.9 %collective-permute-start.10 = (bf16[48,1408]{1,0:T(8,128)(2,1)S(1)}, bf16[48,1408]{1,0:T(8,128)(2,1)S(1)}, u32[]{:S(2)}, u32[]{:S(2)}) collective-permute-start(bf16[48,1408]{1,0:T(8,128)(2,1)S(1)} %get-tuple-element.54.first_ref), channel_id=1, source_target_pairs={{0,2},{2,0},{1,3},{3,1},{4,6},{6,4},{5,7},{7,5},{8,10},{10,8},{9,1... | collective-permute-start | bytes 405512 | tf_op jit(solution)/shard_map/ppermute | solution.py:23
  95.6 1.1 shard_map.55
  96.6 3.8 %collective-permute-done.10.second_ref = bf16[48,1408]{1,0:T(8,128)(2,1)S(1)} collective-permute-done((bf16[48,1408]{1,0:T(8,128)(2,1)S(1)}, bf16[48,1408]{1,0:T(8,128)(2,1)S(1)}, u32[]{:S(2)}, u32[]{:S(2)}) %collective-permute-start.10) | collective-permute-done | bytes 135200 | tf_op jit(solution)/shard_map/ppermute | solution.py:23
  100.5 1.8 %collective-permute-start.11 = (bf16[88,1408]{1,0:T(8,128)(2,1)S(1)}, bf16[88,1408]{1,0:T(8,128)(2,1)S(1)}, u32[]{:S(2)}, u32[]{:S(2)}) collective-permute-start(bf16[88,1408]{1,0:T(8,128)(2,1)S(1)} %shard_map.56.refs_0_), channel_id=1, source_target_pairs={{0,4},{4,8},{8,12},{12,16},{16,20},{20,24},{24,28},{28,0},{1,5},{5... | collective-permute-start | bytes 743432 | tf_op jit(solution)/shard_map/ppermute | solution.py:28
  102.6 7.6 %all-to-all-start.1 = ((f32[32,24,96]{2,1,0:T(8,128)}), f32[32,24,96]{2,1,0:T(8,128)S(1)}, u32[]{:S(2)}, u32[]{:S(2)}) async-start(f32[32,24,96]{2,1,0:T(8,128)} %shard_map.55), calls=%async_computation.1 | async-start | bytes 786432 | tf_op jit(solution)/shard_map/all_to_all | solution.py:362
  110.5 1.8 %collective-permute-start.13 = (bf16[88,1408]{1,0:T(8,128)(2,1)S(1)}, bf16[88,1408]{1,0:T(8,128)(2,1)S(1)}, u32[]{:S(2)}, u32[]{:S(2)}) collective-permute-start(bf16[88,1408]{1,0:T(8,128)(2,1)S(1)} %collective-permute-done.11.refs_4_), channel_id=1, source_target_pairs={{0,4},{4,8},{8,12},{12,16},{16,20},{20,24},{24,28},{28,0},{1,5},{5... | collective-permute-start | bytes 743432 | tf_op jit(solution)/shard_map/ppermute | solution.py:28
  112.8 13.7 %collective-permute-done.14.down_ref.refs_6_ = bf16[88,1408]{1,0:T(8,128)(2,1)S(1)} collective-permute-done((bf16[88,1408]{1,0:T(8,128)(2,1)S(1)}, bf16[88,1408]{1,0:T(8,128)(2,1)S(1)}, u32[]{:S(2)}, u32[]{:S(2)}) %collective-permute-start.14) | collective-permute-done | bytes 247840 | tf_op jit(solution)/shard_map/ppermute | solution.py:28
  127.0 1.4 collective-permute-start.18
  129.8 4.8 %collective-permute-start.20 = (bf16[48,1408]{1,0:T(8,128)(2,1)S(1)}, bf16[48,1408]{1,0:T(8,128)(2,1)S(1)}, u32[]{:S(2)}, u32[]{:S(2)}) collective-permute-start(bf16[48,1408]{1,0:T(8,128)(2,1)S(1)} %get-tuple-element.65), channel_id=1, source_target_pairs={{0,8},{4,12},{8,16},{12,20},{16,24},{20,28},{24,0},{28,4},{1,9},{5... | collective-permute-start | bytes 405512 | tf_op jit(solution)/shard_map/ppermute | solution.py:28
  134.6 4.5 %shard_map.58 = (f32[48,1408]{1,0:T(8,128)S(1)}, f32[8,48,176]{2,1,0:T(8,128)S(1)}, bf16[48,1408]{1,0:T(8,128)(2,1)S(1)}, bf16[8,2,48,88]{3,2,1,0:T(8,128)(2,1)S(1)}) custom-call(s32[7]{0:T(128)S(1)} %stack.27.where_ref, f32[48,1408]{1,0:T(8,128)S(1)} %get-tuple-element.55.rows_ref, f32[32,24,96]{2,1,0:T(8,128)S(1)} %all-to-all-done.1.columns_ref, ...), custom_call_target="tpu_custom_call" | custom-call | flops 129761280 | bytes 2703360 | tf_op jit(solution)/shard_map/pallas_call | solution.py:393
  139.1 1.5 collective-permute-done.21.refs_5_
  140.6 3.8 %collective-permute-done.20.refs_4_ = bf16[48,1408]{1,0:T(8,128)(2,1)S(1)} collective-permute-done((bf16[48,1408]{1,0:T(8,128)(2,1)S(1)}, bf16[48,1408]{1,0:T(8,128)(2,1)S(1)}, u32[]{:S(2)}, u32[]{:S(2)}) %collective-permute-start.20) | collective-permute-done | bytes 135200 | tf_op jit(solution)/shard_map/ppermute | solution.py:28
  145.5 1.2 collective-permute-done.27.refs_7_
  146.7 1.6 %shard_map.59 = f32[8,48,176]{2,1,0:T(8,128)S(1)} custom-call(s32[7]{0:T(128)S(1)} %stack.27.where_ref, f32[48,1408]{1,0:T(8,128)S(1)} %get-tuple-element.75.total_ref, f32[8,48,176]{2,1,0:T(8,128)S(1)} %get-tuple-element.76.blocks_ref, bf16[48,1408]{1,0:T(8,128)(2,1)S(1)} %get-tuple-element.77.tilde_ref, ...), custom_call_target="tpu_custom_call" | custom-call | flops 77856768 | bytes 1622016 | tf_op jit(solution)/shard_map/pallas_call | solution.py:407
  148.3 11.5 %all_to_all.16 = f32[8,48,176]{2,1,0:T(8,128)S(1)} all-to-all(f32[8,48,176]{2,1,0:T(8,128)S(1)} %shard_map.59), channel_id=1, replica_groups=mesh['x'=4,'yl'=2,'z'=8,'yh'=2,'c'=2] {'x','yl'}, dimensions={0} | all-to-all | bytes 540672 | tf_op jit(solution)/shard_map/all_to_all | solution.py:426
  (57 shorter events, 10.1 us)
Async XLA Ops:
  3.1 2.9 %collective-permute-start = (bf16[8,184,300]{2,1,0:T(8,128)(2,1)S(1)}, bf16[8,184,300]{2,1,0:T(8,128)(2,1)S(1)}, u32[]{:S(2)}, u32[]{:S(2)}) collective-permute-start(bf16[8,184,300]{2,1,0:T(8,128)(2,1)S(1)} %shard_map.46), channel_id=1, source_target_pairs={{0,1},{1,0},{2,3},{3,2},{4,5},{5,4},{6,7},{7,6},{8,9},{9,8},{10,11... | collective-permute-start | bytes 2649608 | tf_op jit(solution)/shard_map/ppermute | solution.py:23
  49.3 5.1 %collective-permute-start.1 = (bf16[16,136,600]{2,1,0:T(8,128)(2,1)S(1)}, bf16[16,136,600]{2,1,0:T(8,128)(2,1)S(1)}, u32[]{:S(2)}, u32[]{:S(2)}) collective-permute-start(bf16[16,136,600]{2,1,0:T(8,128)(2,1)S(1)} %all_to_all.15.near_ref), channel_id=1, source_target_pairs={{0,1},{1,0},{2,3},{3,2},{4,5},{5,4},{6,7},{7,6},{8,9},{9,8},{10,11... | collective-permute-start | bytes 7833608 | tf_op jit(solution)/shard_map/ppermute | solution.py:23
  50.4 12.9 %copy-start.5 = (f32[1408]{0:T(1024)S(1)}, f32[1408]{0:T(1024)}, u32[]{:S(2)}) copy-start(f32[1408]{0:T(1024)} %param.7) | copy-start | bytes 16900
  50.4 12.9 %copy-start.2 = (s32[8,2]{0,1:T(2,128)S(1)}, s32[8,2]{0,1:T(2,128)}, u32[]{:S(2)}) copy-start(s32[8,2]{0,1:T(2,128)} %param.5) | copy-start | bytes 196
  50.4 12.9 %copy-start.3 = (f32[16]{0:T(128)S(1)}, f32[16]{0:T(128)}, u32[]{:S(2)}) copy-start(f32[16]{0:T(128)} %occ_ref.1) | copy-start | bytes 196
  55.7 18.1 %collective-permute-start.2 = (f32[48,1408]{1,0:T(8,128)S(1)}, f32[48,1408]{1,0:T(8,128)S(1)}, u32[]{:S(2)}, u32[]{:S(2)}) collective-permute-start(f32[48,1408]{1,0:T(8,128)S(1)} %get-tuple-element.45), channel_id=1, source_target_pairs={{0,4},{4,8},{8,12},{12,16},{16,20},{20,24},{24,28},{28,0},{1,5},{5... | collective-permute-start | bytes 811016 | tf_op jit(solution)/shard_map/ppermute | solution.py:28
  57.7 16.1 %collective-permute-start.3 = (f32[48,1408]{1,0:T(8,128)S(1)}, f32[48,1408]{1,0:T(8,128)S(1)}, u32[]{:S(2)}, u32[]{:S(2)}) collective-permute-start(f32[48,1408]{1,0:T(8,128)S(1)} %get-tuple-element.46), channel_id=1, source_target_pairs={{0,28},{4,0},{8,4},{12,8},{16,12},{20,16},{24,20},{28,24},{1,29},{... | collective-permute-start | bytes 811016 | tf_op jit(solution)/shard_map/ppermute | solution.py:28
  57.8 15.9 %collective-permute-start.4 = (f32[24,1408]{1,0:T(8,128)S(1)}, f32[24,1408]{1,0:T(8,128)S(1)}, u32[]{:S(2)}, u32[]{:S(2)}) collective-permute-start(f32[24,1408]{1,0:T(8,128)S(1)} %get-tuple-element.47), channel_id=1, source_target_pairs={{0,8},{4,12},{8,16},{12,20},{16,24},{20,28},{24,0},{28,4},{1,9},{5... | collective-permute-start | bytes 405512 | tf_op jit(solution)/shard_map/ppermute | solution.py:28
  62.2 11.6 %collective-permute-start.5 = (f32[24,1408]{1,0:T(8,128)S(1)}, f32[24,1408]{1,0:T(8,128)S(1)}, u32[]{:S(2)}, u32[]{:S(2)}) collective-permute-start(f32[24,1408]{1,0:T(8,128)S(1)} %get-tuple-element.48), channel_id=1, source_target_pairs={{0,24},{4,28},{8,0},{12,4},{16,8},{20,12},{24,16},{28,20},{1,25},{... | collective-permute-start | bytes 405512 | tf_op jit(solution)/shard_map/ppermute | solution.py:28
  74.4 8.6 %collective-permute-start.6 = (f32[48,1408]{1,0:T(8,128)S(1)}, f32[48,1408]{1,0:T(8,128)S(1)}, u32[]{:S(2)}, u32[]{:S(2)}) collective-permute-start(f32[48,1408]{1,0:T(8,128)S(1)} %get-tuple-element.49), channel_id=1, source_target_pairs={{0,4},{4,8},{8,12},{12,16},{16,20},{20,24},{24,28},{28,0},{1,5},{5... | collective-permute-start | bytes 811016 | tf_op jit(solution)/shard_map/ppermute | solution.py:28
  78.2 7.1 %collective-permute-start.7 = (f32[48,1408]{1,0:T(8,128)S(1)}, f32[48,1408]{1,0:T(8,128)S(1)}, u32[]{:S(2)}, u32[]{:S(2)}) collective-permute-start(f32[48,1408]{1,0:T(8,128)S(1)} %get-tuple-element.50), channel_id=1, source_target_pairs={{0,28},{4,0},{8,4},{12,8},{16,12},{20,16},{24,20},{28,24},{1,29},{... | collective-permute-start | bytes 811016 | tf_op jit(solution)/shard_map/ppermute | solution.py:28
  85.9 6.5 %collective-permute-start.8 = (f32[48,1408]{1,0:T(8,128)S(1)}, f32[48,1408]{1,0:T(8,128)S(1)}, u32[]{:S(2)}, u32[]{:S(2)}) collective-permute-start(f32[48,1408]{1,0:T(8,128)S(1)} %get-tuple-element.51), channel_id=1, source_target_pairs={{0,4},{4,8},{8,12},{12,16},{16,20},{20,24},{24,28},{28,0},{1,5},{5... | collective-permute-start | bytes 811016 | tf_op jit(solution)/shard_map/ppermute | solution.py:28
  86.3 6.5 %collective-permute-start.9 = (f32[48,1408]{1,0:T(8,128)S(1)}, f32[48,1408]{1,0:T(8,128)S(1)}, u32[]{:S(2)}, u32[]{:S(2)}) collective-permute-start(f32[48,1408]{1,0:T(8,128)S(1)} %get-tuple-element.52), channel_id=1, source_target_pairs={{0,28},{4,0},{8,4},{12,8},{16,12},{20,16},{24,20},{28,24},{1,29},{... | collective-permute-start | bytes 811016 | tf_op jit(solution)/shard_map/ppermute | solution.py:28
  93.7 6.8 %collective-permute-start.10 = (bf16[48,1408]{1,0:T(8,128)(2,1)S(1)}, bf16[48,1408]{1,0:T(8,128)(2,1)S(1)}, u32[]{:S(2)}, u32[]{:S(2)}) collective-permute-start(bf16[48,1408]{1,0:T(8,128)(2,1)S(1)} %get-tuple-element.54.first_ref), channel_id=1, source_target_pairs={{0,2},{2,0},{1,3},{3,1},{4,6},{6,4},{5,7},{7,5},{8,10},{10,8},{9,1... | collective-permute-start | bytes 405512 | tf_op jit(solution)/shard_map/ppermute | solution.py:23
  100.5 9.7 %collective-permute-start.11 = (bf16[88,1408]{1,0:T(8,128)(2,1)S(1)}, bf16[88,1408]{1,0:T(8,128)(2,1)S(1)}, u32[]{:S(2)}, u32[]{:S(2)}) collective-permute-start(bf16[88,1408]{1,0:T(8,128)(2,1)S(1)} %shard_map.56.refs_0_), channel_id=1, source_target_pairs={{0,4},{4,8},{8,12},{12,16},{16,20},{20,24},{24,28},{28,0},{1,5},{5... | collective-permute-start | bytes 743432 | tf_op jit(solution)/shard_map/ppermute | solution.py:28
  102.3 7.9 %collective-permute-start.12 = (bf16[88,1408]{1,0:T(8,128)(2,1)S(1)}, bf16[88,1408]{1,0:T(8,128)(2,1)S(1)}, u32[]{:S(2)}, u32[]{:S(2)}) collective-permute-start(bf16[88,1408]{1,0:T(8,128)(2,1)S(1)} %shard_map.56.refs_0_), channel_id=1, source_target_pairs={{0,28},{4,0},{8,4},{12,8},{16,12},{20,16},{24,20},{28,24},{1,29},{... | collective-permute-start | bytes 743432 | tf_op jit(solution)/shard_map/ppermute | solution.py:28
  102.6 27.2 %all-to-all-start.1 = ((f32[32,24,96]{2,1,0:T(8,128)}), f32[32,24,96]{2,1,0:T(8,128)S(1)}, u32[]{:S(2)}, u32[]{:S(2)}) async-start(f32[32,24,96]{2,1,0:T(8,128)} %shard_map.55), calls=%async_computation.1 | async-start | bytes 786432 | tf_op jit(solution)/shard_map/all_to_all | solution.py:362
  110.2 16.3 %collective-permute-start.14 = (bf16[88,1408]{1,0:T(8,128)(2,1)S(1)}, bf16[88,1408]{1,0:T(8,128)(2,1)S(1)}, u32[]{:S(2)}, u32[]{:S(2)}) collective-permute-start(bf16[88,1408]{1,0:T(8,128)(2,1)S(1)} %collective-permute-done.12.refs_2_), channel_id=1, source_target_pairs={{0,28},{4,0},{8,4},{12,8},{16,12},{20,16},{24,20},{28,24},{1,29},{... | collective-permute-start | bytes 743432 | tf_op jit(solution)/shard_map/ppermute | solution.py:28
  110.5 16.0 %collective-permute-start.13 = (bf16[88,1408]{1,0:T(8,128)(2,1)S(1)}, bf16[88,1408]{1,0:T(8,128)(2,1)S(1)}, u32[]{:S(2)}, u32[]{:S(2)}) collective-permute-start(bf16[88,1408]{1,0:T(8,128)(2,1)S(1)} %collective-permute-done.11.refs_4_), channel_id=1, source_target_pairs={{0,4},{4,8},{8,12},{12,16},{16,20},{20,24},{24,28},{28,0},{1,5},{5... | collective-permute-start | bytes 743432 | tf_op jit(solution)/shard_map/ppermute | solution.py:28
  112.3 14.7 %collective-permute-start.15 = (bf16[88,1408]{1,0:T(8,128)(2,1)S(1)}, bf16[88,1408]{1,0:T(8,128)(2,1)S(1)}, u32[]{:S(2)}, u32[]{:S(2)}) collective-permute-start(bf16[88,1408]{1,0:T(8,128)(2,1)S(1)} %shard_map.56.refs_0_), channel_id=1, source_target_pairs={{0,1},{1,0},{2,3},{3,2},{4,5},{5,4},{6,7},{7,6},{8,9},{9,8},{10,11... | collective-permute-start | bytes 743432 | tf_op jit(solution)/shard_map/ppermute | solution.py:23
  112.3 14.7 %collective-permute-start.16 = (bf16[88,1408]{1,0:T(8,128)(2,1)S(1)}, bf16[88,1408]{1,0:T(8,128)(2,1)S(1)}, u32[]{:S(2)}, u32[]{:S(2)}) collective-permute-start(bf16[88,1408]{1,0:T(8,128)(2,1)S(1)} %collective-permute-done.12.refs_2_), channel_id=1, source_target_pairs={{0,1},{1,0},{2,3},{3,2},{4,5},{5,4},{6,7},{7,6},{8,9},{9,8},{10,11... | collective-permute-start | bytes 743432 | tf_op jit(solution)/shard_map/ppermute | solution.py:23
  112.8 14.2 %collective-permute-start.17 = (bf16[88,1408]{1,0:T(8,128)(2,1)S(1)}, bf16[88,1408]{1,0:T(8,128)(2,1)S(1)}, u32[]{:S(2)}, u32[]{:S(2)}) collective-permute-start(bf16[88,1408]{1,0:T(8,128)(2,1)S(1)} %collective-permute-done.11.refs_4_), channel_id=1, source_target_pairs={{0,1},{1,0},{2,3},{3,2},{4,5},{5,4},{6,7},{7,6},{8,9},{9,8},{10,11... | collective-permute-start | bytes 743432 | tf_op jit(solution)/shard_map/ppermute | solution.py:23
  126.5 8.1 %collective-permute-start.22 = (bf16[88,1408]{1,0:T(8,128)(2,1)S(1)}, bf16[88,1408]{1,0:T(8,128)(2,1)S(1)}, u32[]{:S(2)}, u32[]{:S(2)}) collective-permute-start(bf16[88,1408]{1,0:T(8,128)(2,1)S(1)} %collective-permute-done.14.down_ref.refs_6_), channel_id=1, source_target_pairs={{0,1},{1,0},{2,3},{3,2},{4,5},{5,4},{6,7},{7,6},{8,9},{9,8},{10,11... | collective-permute-start | bytes 743432 | tf_op jit(solution)/shard_map/ppermute | solution.py:23
  126.5 8.1 %collective-permute-start.23 = (bf16[88,1408]{1,0:T(8,128)(2,1)S(1)}, bf16[88,1408]{1,0:T(8,128)(2,1)}, u32[]{:S(2)}, u32[]{:S(2)}) collective-permute-start(bf16[88,1408]{1,0:T(8,128)(2,1)S(1)} %collective-permute-done.13.up_ref.refs_8_), channel_id=1, source_target_pairs={{0,1},{1,0},{2,3},{3,2},{4,5},{5,4},{6,7},{7,6},{8,9},{9,8},{10,11... | collective-permute-start | bytes 743432 | tf_op jit(solution)/shard_map/ppermute | solution.py:23
  127.0 17.4 %collective-permute-start.18 = (bf16[88,1408]{1,0:T(8,128)(2,1)S(1)}, bf16[88,1408]{1,0:T(8,128)(2,1)S(1)}, u32[]{:S(2)}, u32[]{:S(2)}) collective-permute-start(bf16[88,1408]{1,0:T(8,128)(2,1)S(1)} %collective-permute-done.14.down_ref.refs_6_), channel_id=1, source_target_pairs={{0,28},{4,0},{8,4},{12,8},{16,12},{20,16},{24,20},{28,24},{1,29},{... | collective-permute-start | bytes 743432 | tf_op jit(solution)/shard_map/ppermute | solution.py:28
  128.4 16.0 %collective-permute-start.19 = (bf16[88,1408]{1,0:T(8,128)(2,1)S(1)}, bf16[88,1408]{1,0:T(8,128)(2,1)S(1)}, u32[]{:S(2)}, u32[]{:S(2)}) collective-permute-start(bf16[88,1408]{1,0:T(8,128)(2,1)S(1)} %collective-permute-done.13.up_ref.refs_8_), channel_id=1, source_target_pairs={{0,4},{4,8},{8,12},{12,16},{16,20},{20,24},{24,28},{28,0},{1,5},{5... | collective-permute-start | bytes 743432 | tf_op jit(solution)/shard_map/ppermute | solution.py:28
  129.8 14.6 %collective-permute-start.20 = (bf16[48,1408]{1,0:T(8,128)(2,1)S(1)}, bf16[48,1408]{1,0:T(8,128)(2,1)S(1)}, u32[]{:S(2)}, u32[]{:S(2)}) collective-permute-start(bf16[48,1408]{1,0:T(8,128)(2,1)S(1)} %get-tuple-element.65), channel_id=1, source_target_pairs={{0,8},{4,12},{8,16},{12,20},{16,24},{20,28},{24,0},{28,4},{1,9},{5... | collective-permute-start | bytes 405512 | tf_op jit(solution)/shard_map/ppermute | solution.py:28
  134.6 6.0 %collective-permute-start.21 = (bf16[40,1408]{1,0:T(8,128)(2,1)}, bf16[40,1408]{1,0:T(8,128)(2,1)S(1)}, u32[]{:S(2)}, u32[]{:S(2)}) collective-permute-start(bf16[40,1408]{1,0:T(8,128)(2,1)} %copy-done.4), channel_id=1, source_target_pairs={{0,24},{4,28},{8,0},{12,4},{16,8},{20,12},{24,16},{28,20},{1,25},{... | collective-permute-start | bytes 337928 | tf_op jit(solution)/shard_map/ppermute | solution.py:28
  144.4 2.2 %collective-permute-start.24 = (bf16[88,1408]{1,0:T(8,128)(2,1)S(1)}, bf16[88,1408]{1,0:T(8,128)(2,1)S(1)}, u32[]{:S(2)}, u32[]{:S(2)}) collective-permute-start(bf16[88,1408]{1,0:T(8,128)(2,1)S(1)} %collective-permute-done.18.refs_0_), channel_id=1, source_target_pairs={{0,1},{1,0},{2,3},{3,2},{4,5},{5,4},{6,7},{7,6},{8,9},{9,8},{10,11... | collective-permute-start | bytes 743432 | tf_op jit(solution)/shard_map/ppermute | solution.py:23
  144.4 2.2 %collective-permute-start.25 = (bf16[88,1408]{1,0:T(8,128)(2,1)S(1)}, bf16[88,1408]{1,0:T(8,128)(2,1)S(1)}, u32[]{:S(2)}, u32[]{:S(2)}) collective-permute-start(bf16[88,1408]{1,0:T(8,128)(2,1)S(1)} %collective-permute-done.19.refs_2_), channel_id=1, source_target_pairs={{0,1},{1,0},{2,3},{3,2},{4,5},{5,4},{6,7},{7,6},{8,9},{9,8},{10,11... | collective-permute-start | bytes 743432 | tf_op jit(solution)/shard_map/ppermute | solution.py:23
  144.9 1.7 %collective-permute-start.26 = (bf16[48,1408]{1,0:T(8,128)(2,1)S(1)}, bf16[48,1408]{1,0:T(8,128)(2,1)S(1)}, u32[]{:S(2)}, u32[]{:S(2)}) collective-permute-start(bf16[48,1408]{1,0:T(8,128)(2,1)S(1)} %collective-permute-done.20.refs_4_), channel_id=1, source_target_pairs={{0,1},{1,0},{2,3},{3,2},{4,5},{5,4},{6,7},{7,6},{8,9},{9,8},{10,11... | collective-permute-start | bytes 405512 | tf_op jit(solution)/shard_map/ppermute | solution.py:23
  145.0 1.6 %collective-permute-start.27 = (bf16[40,1408]{1,0:T(8,128)(2,1)S(1)}, bf16[40,1408]{1,0:T(8,128)(2,1)S(1)}, u32[]{:S(2)}, u32[]{:S(2)}) collective-permute-start(bf16[40,1408]{1,0:T(8,128)(2,1)S(1)} %collective-permute-done.21.refs_5_), channel_id=1, source_target_pairs={{0,1},{1,0},{2,3},{3,2},{4,5},{5,4},{6,7},{7,6},{8,9},{9,8},{10,11... | collective-permute-start | bytes 337928 | tf_op jit(solution)/shard_map/ppermute | solution.py:23
  (3 other events, 2.9 us)

commit v9 on v8

--- a/solution.py
+++ b/solution.py
@@ -109,26 +109,20 @@
     return left
 
 
-def near_kernel(padded, near_ref, out_ref):
+def near_kernel(padded, where_ref, near_ref, out_ref, up_ref, down_ref):
     out_ref[...] = half_product(all_rows(near_ref, padded), near_ref, padded).reshape(out_ref.shape)
-
-
-def first_kernel(padded, where_ref, near_part_ref, near_ref, far_ref, *out_refs):
-    nz = near_part_ref.shape[0]
-    half = near_ref.shape[0] // 2
-    cut = padded // 2
-    places = [lax.rem(where_ref[0] + offset, nz) for offset in (nz // 2, nz // 2 - 1, nz // 2 + 1)]
-
-    def left(y):
-        return jnp.concatenate([near_ref[half * y + at, :padded, :] for at in places], axis=0)
-
-    total = half_product(left, far_ref, padded)
-    sums = [
-        jnp.concatenate([near_part_ref[at], total[n * padded : (n + 1) * padded]], axis=1)
-        for n, at in enumerate(places)
-    ]
-    for ref, value in zip(out_refs, (sums[0][:cut], sums[0][cut:], sums[1], sums[2])):
-        ref[...] = value
+    nz, cut = out_ref.shape[0], padded // 2
+    across = out_ref[lax.rem(where_ref[0] + nz // 2, nz)]
+    up_ref[...] = across[:cut]
+    down_ref[...] = across[cut:]
+
+
+def first_kernel(padded, nz, where_ref, near_ref, far_ref, up_ref, down_ref):
+    half, cut = near_ref.shape[0] // 2, padded // 2
+    at = lax.rem(where_ref[0] + nz // 2, nz)
+    across = half_product(lambda y: near_ref[half * y + at, :padded, :], far_ref, padded)
+    up_ref[...] = across[:cut]
+    down_ref[...] = across[cut:]
 
 
 def rest_kernel(padded, where_ref, pair_ref, occ_ref, vir_ref, near_part_ref, near_ref, far_ref, out_ref, denom_ref):
@@ -147,14 +141,16 @@
     nz, rows = part_ref.shape[:2]
     above = lax.rem(where_ref[0] + step, nz)
     below = lax.rem(where_ref[0] + nz - step, nz)
-    up_in, down_in = refs[:2]
     up_ref, down_ref = refs[-2:]
-    up_ref[...] = part_ref[above] + up_in[...]
-    down_ref[...] = part_ref[below] + down_in[...]
-    if len(refs) > 4:
+    if len(refs) == 4:
+        up_ref[...] = part_ref[above] + refs[0][...]
+        down_ref[...] = part_ref[below] + refs[1][...]
+    else:
         cut = rows // 2
-        up_ref[:cut] += refs[2][...]
-        down_ref[cut:] += refs[3][...]
+        up_ref[...] = part_ref[above]
+        down_ref[...] = part_ref[below]
+        up_ref[:cut] += jnp.concatenate([refs[0][...], refs[2][...]], axis=1)
+        down_ref[cut:] += jnp.concatenate([refs[1][...], refs[3][...]], axis=1)
 
 
 def amplitude_kernel(where_ref, part_ref, up_in, down_in, denom_ref, out_ref, rounded_ref):
@@ -178,8 +174,11 @@
         blocks_ref[k] = jnp.concatenate([block[:half], gap, block[half:], gap], axis=1)
 
 
-def merge_kernel(width, first_ref, second_ref, out_ref):
-    out_ref[...] = jnp.concatenate([first_ref[:width], second_ref[:width]], axis=0)
+def merge_kernel(width, *refs):
+    count = len(refs) // 3
+    for n in range(count):
+        first, second = refs[2 * n], refs[2 * n + 1]
+        refs[2 * count + n][...] = jnp.concatenate([first[:width], second[:width]], axis=0)
 
 
 def halves_kernel(up_ref, down_ref, first_ref, second_ref):
@@ -304,25 +303,26 @@
 
     whole = jax.ShapeDtypeStruct((8, padded, nvir), F32)
     rows = jax.ShapeDtypeStruct((padded, nvir), F32)
-    halves = jax.ShapeDtypeStruct((padded // 2, nvir), F32)
+    quarter = jax.ShapeDtypeStruct((padded // 2, nvir // 2), F32)
     flops = 16 * padded * 8 * slab * 2 * naux
-    near_part = pl.pallas_call(
+    near_part, up, down = pl.pallas_call(
         functools.partial(near_kernel, padded),
-        out_shape=jax.ShapeDtypeStruct((8, padded, nvir // 2), F32),
-        in_specs=[VMEM],
-        out_specs=VMEM,
+        out_shape=(jax.ShapeDtypeStruct((8, padded, nvir // 2), F32), quarter, quarter),
+        in_specs=[SMEM, VMEM],
+        out_specs=(VMEM,) * 3,
         compiler_params=params(16),
         cost_estimate=cost(flops, 0),
-    )(near)
-    half_up, half_down, up, down = pl.pallas_call(
-        functools.partial(first_kernel, padded),
-        out_shape=(halves, halves, rows, rows),
-        in_specs=[SMEM, VMEM, VMEM, VMEM],
-        out_specs=(VMEM,) * 4,
+    )(where, near)
+    sums = (shift(up, "z", 1), shift(down, "z", -1))
+    up, down = pl.pallas_call(
+        functools.partial(first_kernel, padded, nz),
+        out_shape=(quarter, quarter),
+        in_specs=[SMEM, VMEM, VMEM],
+        out_specs=(VMEM, VMEM),
         compiler_params=params(16),
-        cost_estimate=cost(flops // 4, 0),
-    )(where, near_part, near, far)
-    sums = (shift(up, "z", 1), shift(down, "z", -1), shift(half_up, "z", 2), shift(half_down, "z", -2))
+        cost_estimate=cost(flops // 8, 0),
+    )(where, near, far)
+    sums += (shift(up, "z", 1), shift(down, "z", -1))
     part, denom = pl.pallas_call(
         functools.partial(rest_kernel, padded),
         out_shape=(whole, rows),
@@ -331,7 +331,7 @@
         compiler_params=params(16),
         cost_estimate=cost(flops, 0),
     )(where, pairs, eps_occ, eps_vir[None], near_part, near, far)
-    for step in range(nz // 2 - 2, 0, -1):
+    for step in range(nz // 2 - 1, 0, -1):
         up, down = pl.pallas_call(
             functools.partial(hop_kernel, step),
             out_shape=(rows, rows),
@@ -360,19 +360,22 @@
     )(amp_rows)
     other, _ = lax.optimization_barrier((other, columns))
     columns = lax.all_to_all(columns, ("z", "yh", "c"), split_axis=0, concat_axis=0, tiled=True)
-    both = pl.pallas_call(
-        functools.partial(merge_kernel, width),
-        out_shape=jax.ShapeDtypeStruct((2 * width, nvir), BF16),
-        in_specs=[VMEM, VMEM],
-        out_specs=VMEM,
-        compiler_params=params(8),
-    )(mine, other)
-    ring = {0: both}
-    up = down = both
-    for step in range(1, nz // 2 - 1):
-        up, down = shift(up, "z", 1), shift(down, "z", -1)
-        ring[nz - step], ring[step] = up, down
-        up, down = lax.optimization_barrier((up, down))
+
+    def merge(*halves):
+        count = len(halves) // 2
+        return pl.pallas_call(
+            functools.partial(merge_kernel, width),
+            out_shape=(jax.ShapeDtypeStruct((2 * width, nvir), BF16),) * count,
+            in_specs=[VMEM] * (2 * count),
+            out_specs=(VMEM,) * count,
+            compiler_params=params(8),
+        )(*halves)
+
+    up, down = merge(shift(mine, "z", 1), shift(other, "z", 1), shift(mine, "z", -1), shift(other, "z", -1))
+    (both,) = merge(mine, other)
+    ring = {0: both, nz - 1: up, 1: down}
+    up, down = shift(up, "z", 1), shift(down, "z", -1)
+    ring[nz - 2], ring[2] = up, down
     far = {r: swap(ring[r], "c") for r in (0, 1, nz - 1)}
     up, down, far = lax.optimization_barrier((up, down, far))
     half_up, half_down = pl.pallas_call(

time: 161 us -> 159 us (0.988)
  waiting for transfers between devices: 50.8 us -> 47.5 us
    ppermute x12, waiting for transfers between devices: 11.1 us -> 6.5 us  [swap(): return lax.ppermute(value, axis, [(0, 1), (1, 0)])]
    ppermute x16 -> x20, waiting for transfers between devices: 39.7 us -> 41 us  [shift(): lax.ppermute(value, axis, [(i, (i + step) % size) for i in range(size)])]
    ppermute x16 -> x20, starting transfers between devices: 24.5 us -> 25.5 us  [shift(): lax.ppermute(value, axis, [(i, (i + step) % size) for i in range(size)])]
  transfers between devices with their start and end apart: 29 -> 33, of which waited for: 12 -> 15; matrix products, arithmetic and copies ran while one was open for 0% -> 0% of each run, Pallas kernels for 6% -> 7%
where the time goes in v9:
time: 159 us; the launch traced here: 158 us
  blocking collectives  53.6 us (34%)
  waiting for transfers between devices  47.5 us (30%)
  starting transfers between devices  36.2 us (23%)
  Pallas kernels  17.1 us (11%)
  local copies, waits for them, and re-layouts  3.02 us (2%)
    all_to_all x1, blocking collectives, local(): lax.all_to_all(ours, ('yh', 'x', 'yl'), split_axis=0, concat_axis=0, tile...  42.1 us
    ppermute x20, waiting for transfers between devices, shift(): lax.ppermute(value, axis, [(i, (i + step) % size) for i in range(size)])  41 us
    ppermute x20, starting transfers between devices, shift(): lax.ppermute(value, axis, [(i, (i + step) % size) for i in range(size)])  25.5 us
    all_to_all x1, blocking collectives, local(): lax.all_to_all(added, SLABS, split_axis=0, concat_axis=0, tiled=True)  11.5 us
    all_to_all x1, starting transfers between devices, local(): lax.all_to_all(columns, ('z', 'yh', 'c'), split_axis=0, concat_axis=0, ti...  6.76 us
    ppermute x12, waiting for transfers between devices, swap(): return lax.ppermute(value, axis, [(0, 1), (1, 0)])  6.5 us
    pallas_call x1, Pallas kernels, local(): pl.pallas_call(functools.partial(early_kernel, soon, nz), out_shape=(rows...  4.45 us
    ppermute x12, starting transfers between devices, swap(): return lax.ppermute(value, axis, [(0, 1), (1, 0)])  3.97 us
  transfers between devices with their start and end apart: 33, of which 15 were waited for; matrix products, arithmetic and copies ran while one was open for 0% of the time, Pallas kernels for 7%

profile of v9, /device:TPU:32, one launch (start us, length us, event | category | flops | bytes accessed | tf_op | source)
XLA Modules:
  0.0 158.4 jit_solution(14149032513121700493)
XLA Ops:
  0.1 1.6 %copy-done = bf16[16,176,300]{2,1,0:T(8,128)(2,1)S(1)} copy-done((bf16[16,176,300]{2,1,0:T(8,128)(2,1)S(1)}, bf16[16,176,300]{2,1,0:T(8,128)(2,1)}, u32[]{:S(2)}) %copy-start) | copy-done | bytes 1689624
  3.9 2.0 %collective-permute-done.taken_ref = bf16[8,184,300]{2,1,0:T(8,128)(2,1)S(1)} collective-permute-done((bf16[8,184,300]{2,1,0:T(8,128)(2,1)S(1)}, bf16[8,184,300]{2,1,0:T(8,128)(2,1)S(1)}, u32[]{:S(2)}, u32[]{:S(2)}) %collective-permute-start) | collective-permute-done | bytes 883232 | tf_op jit(solution)/shard_map/ppermute | solution.py:23
  7.1 42.1 %all_to_all.15.near_ref = bf16[16,136,600]{2,1,0:T(8,128)(2,1)S(1)} all-to-all(bf16[16,136,600]{2,1,0:T(8,128)(2,1)S(1)} %shard_map.48), channel_id=1, replica_groups=mesh['x'=4,'yl'=2,'z'=8,'yh'=2,'c'=2] {'yh','x','yl'}, dimensions={0} | all-to-all | bytes 5222400 | tf_op jit(solution)/shard_map/all_to_all | solution.py:301
  49.3 1.6 %shard_map.49 = (f32[8,48,704]{2,1,0:T(8,128)S(1)}, f32[24,704]{1,0:T(8,128)S(1)}, f32[24,704]{1,0:T(8,128)S(1)}) custom-call(s32[7]{0:T(128)S(1)} %stack.27.where_ref, bf16[16,136,600]{2,1,0:T(8,128)(2,1)S(1)} %all_to_all.15.near_ref), custom_call_target="tpu_custom_call" | custom-call | flops 648806400 | tf_op jit(solution)/shard_map/pallas_call | solution.py:308
  50.9 2.0 %collective-permute-start.2 = (f32[24,704]{1,0:T(8,128)S(1)}, f32[24,704]{1,0:T(8,128)S(1)}, u32[]{:S(2)}, u32[]{:S(2)}) collective-permute-start(f32[24,704]{1,0:T(8,128)S(1)} %get-tuple-element.47), channel_id=1, source_target_pairs={{0,4},{4,8},{8,12},{12,16},{16,20},{20,24},{24,28},{28,0},{1,5},{5... | collective-permute-start | bytes 202760 | tf_op jit(solution)/shard_map/ppermute | solution.py:28
  53.0 1.4 collective-permute-done.1.far_ref
  55.6 2.0 %collective-permute-start.4 = (f32[24,704]{1,0:T(8,128)S(1)}, f32[24,704]{1,0:T(8,128)S(1)}, u32[]{:S(2)}, u32[]{:S(2)}) collective-permute-start(f32[24,704]{1,0:T(8,128)S(1)} %get-tuple-element.49), channel_id=1, source_target_pairs={{0,4},{4,8},{8,12},{12,16},{16,20},{20,24},{24,28},{28,0},{1,5},{5... | collective-permute-start | bytes 202760 | tf_op jit(solution)/shard_map/ppermute | solution.py:28
  58.5 1.7 %shard_map.50 = (f32[8,48,1408]{2,1,0:T(8,128)S(1)}, f32[48,1408]{1,0:T(8,128)S(1)}) custom-call(s32[7]{0:T(128)S(1)} %stack.27.where_ref, s32[2,8]{1,0:T(2,128)S(1)} %bitcast.10, f32[16]{0:T(128)S(1)} %copy-done.3, f32[1,1408]{1,0:T(1,128)S(1)} %broadcast_in_dim.3.vir_ref, f32[8,48,704]{2,1,0:T(8,128)S(1)} %get-tuple-element.45.near_part_ref, ...), custom_call_target="tpu_custom_call" | custom-call | flops 648806400 | tf_op jit(solution)/shard_map/pallas_call | solution.py:326
  62.6 3.1 %collective-permute-start.6 = (f32[48,1408]{1,0:T(8,128)S(1)}, f32[48,1408]{1,0:T(8,128)S(1)}, u32[]{:S(2)}, u32[]{:S(2)}) collective-permute-start(f32[48,1408]{1,0:T(8,128)S(1)} %get-tuple-element.51), channel_id=1, source_target_pairs={{0,4},{4,8},{8,12},{12,16},{16,20},{20,24},{24,28},{28,0},{1,5},{5... | collective-permute-start | bytes 811016 | tf_op jit(solution)/shard_map/ppermute | solution.py:28
  65.7 5.5 %collective-permute-done.6.refs_0_ = f32[48,1408]{1,0:T(8,128)S(1)} collective-permute-done((f32[48,1408]{1,0:T(8,128)S(1)}, f32[48,1408]{1,0:T(8,128)S(1)}, u32[]{:S(2)}, u32[]{:S(2)}) %collective-permute-start.6) | collective-permute-done | bytes 270368 | tf_op jit(solution)/shard_map/ppermute | solution.py:28
  71.2 2.8 %collective-permute-done.7.refs_1_ = f32[48,1408]{1,0:T(8,128)S(1)} collective-permute-done((f32[48,1408]{1,0:T(8,128)S(1)}, f32[48,1408]{1,0:T(8,128)S(1)}, u32[]{:S(2)}, u32[]{:S(2)}) %collective-permute-start.7) | collective-permute-done | bytes 270368 | tf_op jit(solution)/shard_map/ppermute | solution.py:28
  74.6 1.8 %collective-permute-start.8 = (f32[48,1408]{1,0:T(8,128)S(1)}, f32[48,1408]{1,0:T(8,128)S(1)}, u32[]{:S(2)}, u32[]{:S(2)}) collective-permute-start(f32[48,1408]{1,0:T(8,128)S(1)} %get-tuple-element.53), channel_id=1, source_target_pairs={{0,4},{4,8},{8,12},{12,16},{16,20},{20,24},{24,28},{28,0},{1,5},{5... | collective-permute-start | bytes 811016 | tf_op jit(solution)/shard_map/ppermute | solution.py:28
  76.7 4.4 %collective-permute-done.8.refs_0_ = f32[48,1408]{1,0:T(8,128)S(1)} collective-permute-done((f32[48,1408]{1,0:T(8,128)S(1)}, f32[48,1408]{1,0:T(8,128)S(1)}, u32[]{:S(2)}, u32[]{:S(2)}) %collective-permute-start.8) | collective-permute-done | bytes 270368 | tf_op jit(solution)/shard_map/ppermute | solution.py:28
  81.1 1.7 %collective-permute-done.9.refs_1_ = f32[48,1408]{1,0:T(8,128)S(1)} collective-permute-done((f32[48,1408]{1,0:T(8,128)S(1)}, f32[48,1408]{1,0:T(8,128)S(1)}, u32[]{:S(2)}, u32[]{:S(2)}) %collective-permute-start.9) | collective-permute-done | bytes 270368 | tf_op jit(solution)/shard_map/ppermute | solution.py:28
  83.5 1.8 %collective-permute-start.10 = (f32[48,1408]{1,0:T(8,128)S(1)}, f32[48,1408]{1,0:T(8,128)S(1)}, u32[]{:S(2)}, u32[]{:S(2)}) collective-permute-start(f32[48,1408]{1,0:T(8,128)S(1)} %get-tuple-element.55), channel_id=1, source_target_pairs={{0,4},{4,8},{8,12},{12,16},{16,20},{20,24},{24,28},{28,0},{1,5},{5... | collective-permute-start | bytes 811016 | tf_op jit(solution)/shard_map/ppermute | solution.py:28
  85.8 4.4 %collective-permute-done.10.up_in = f32[48,1408]{1,0:T(8,128)S(1)} collective-permute-done((f32[48,1408]{1,0:T(8,128)S(1)}, f32[48,1408]{1,0:T(8,128)S(1)}, u32[]{:S(2)}, u32[]{:S(2)}) %collective-permute-start.10) | collective-permute-done | bytes 270368 | tf_op jit(solution)/shard_map/ppermute | solution.py:28
  90.2 1.6 %collective-permute-done.11.down_in = f32[48,1408]{1,0:T(8,128)S(1)} collective-permute-done((f32[48,1408]{1,0:T(8,128)S(1)}, f32[48,1408]{1,0:T(8,128)S(1)}, u32[]{:S(2)}, u32[]{:S(2)}) %collective-permute-start.11) | collective-permute-done | bytes 270368 | tf_op jit(solution)/shard_map/ppermute | solution.py:28
  92.7 1.7 %collective-permute-start.13 = (bf16[48,1408]{1,0:T(8,128)(2,1)S(1)}, bf16[48,1408]{1,0:T(8,128)(2,1)S(1)}, u32[]{:S(2)}, u32[]{:S(2)}) collective-permute-start(bf16[48,1408]{1,0:T(8,128)(2,1)S(1)} %get-tuple-element.58.refs_0_), channel_id=1, source_target_pairs={{0,2},{2,0},{1,3},{3,1},{4,6},{6,4},{5,7},{7,5},{8,10},{10,8},{9,1... | collective-permute-start | bytes 405512 | tf_op jit(solution)/shard_map/ppermute | solution.py:23
  94.3 1.5 collective-permute-start.12
  97.4 1.9 %collective-permute-done.13.refs_1_ = bf16[48,1408]{1,0:T(8,128)(2,1)S(1)} collective-permute-done((bf16[48,1408]{1,0:T(8,128)(2,1)S(1)}, bf16[48,1408]{1,0:T(8,128)(2,1)S(1)}, u32[]{:S(2)}, u32[]{:S(2)}) %collective-permute-start.13) | collective-permute-done | bytes 135200 | tf_op jit(solution)/shard_map/ppermute | solution.py:23
  99.3 1.5 collective-permute-start.14
  101.3 6.8 %all-to-all-start.1 = ((f32[32,24,96]{2,1,0:T(8,128)}), f32[32,24,96]{2,1,0:T(8,128)S(1)}, u32[]{:S(2)}, u32[]{:S(2)}) async-start(f32[32,24,96]{2,1,0:T(8,128)} %shard_map.56), calls=%async_computation.1 | async-start | bytes 786432 | tf_op jit(solution)/shard_map/all_to_all | solution.py:362
  108.5 1.8 %collective-permute-start.17 = (bf16[88,1408]{1,0:T(8,128)(2,1)S(1)}, bf16[88,1408]{1,0:T(8,128)(2,1)S(1)}, u32[]{:S(2)}, u32[]{:S(2)}) collective-permute-start(bf16[88,1408]{1,0:T(8,128)(2,1)S(1)} %get-tuple-element.61.refs_4_), channel_id=1, source_target_pairs={{0,4},{4,8},{8,12},{12,16},{16,20},{20,24},{24,28},{28,0},{1,5},{5... | collective-permute-start | bytes 743432 | tf_op jit(solution)/shard_map/ppermute | solution.py:28
  111.0 13.4 %collective-permute-done.18.down_ref.refs_6_ = bf16[88,1408]{1,0:T(8,128)(2,1)S(1)} collective-permute-done((bf16[88,1408]{1,0:T(8,128)(2,1)S(1)}, bf16[88,1408]{1,0:T(8,128)(2,1)S(1)}, u32[]{:S(2)}, u32[]{:S(2)}) %collective-permute-start.18) | collective-permute-done | bytes 247840 | tf_op jit(solution)/shard_map/ppermute | solution.py:28
  124.9 1.4 collective-permute-start.22
  127.7 4.8 %collective-permute-start.24 = (bf16[48,1408]{1,0:T(8,128)(2,1)S(1)}, bf16[48,1408]{1,0:T(8,128)(2,1)S(1)}, u32[]{:S(2)}, u32[]{:S(2)}) collective-permute-start(bf16[48,1408]{1,0:T(8,128)(2,1)S(1)} %get-tuple-element.67), channel_id=1, source_target_pairs={{0,8},{4,12},{8,16},{12,20},{16,24},{20,28},{24,0},{28,4},{1,9},{5... | collective-permute-start | bytes 405512 | tf_op jit(solution)/shard_map/ppermute | solution.py:28
  132.5 4.4 %shard_map.60 = (f32[48,1408]{1,0:T(8,128)S(1)}, f32[8,48,176]{2,1,0:T(8,128)S(1)}, bf16[48,1408]{1,0:T(8,128)(2,1)S(1)}, bf16[8,2,48,88]{3,2,1,0:T(8,128)(2,1)S(1)}) custom-call(s32[7]{0:T(128)S(1)} %stack.27.where_ref, f32[48,1408]{1,0:T(8,128)S(1)} %get-tuple-element.59.rows_ref, f32[32,24,96]{2,1,0:T(8,128)S(1)} %all-to-all-done.1.columns_ref, ...), custom_call_target="tpu_custom_call" | custom-call | flops 129761280 | bytes 2703360 | tf_op jit(solution)/shard_map/pallas_call | solution.py:396
  136.9 1.5 collective-permute-done.25.refs_5_
  138.5 3.8 %collective-permute-done.24.refs_4_ = bf16[48,1408]{1,0:T(8,128)(2,1)S(1)} collective-permute-done((bf16[48,1408]{1,0:T(8,128)(2,1)S(1)}, bf16[48,1408]{1,0:T(8,128)(2,1)S(1)}, u32[]{:S(2)}, u32[]{:S(2)}) %collective-permute-start.24) | collective-permute-done | bytes 135200 | tf_op jit(solution)/shard_map/ppermute | solution.py:28
  143.4 1.2 collective-permute-done.31.refs_7_
  144.6 1.6 %shard_map.61 = f32[8,48,176]{2,1,0:T(8,128)S(1)} custom-call(s32[7]{0:T(128)S(1)} %stack.27.where_ref, f32[48,1408]{1,0:T(8,128)S(1)} %get-tuple-element.77.total_ref, f32[8,48,176]{2,1,0:T(8,128)S(1)} %get-tuple-element.78.blocks_ref, bf16[48,1408]{1,0:T(8,128)(2,1)S(1)} %get-tuple-element.79.tilde_ref, ...), custom_call_target="tpu_custom_call" | custom-call | flops 77856768 | bytes 1622016 | tf_op jit(solution)/shard_map/pallas_call | solution.py:410
  146.2 11.5 %all_to_all.16 = f32[8,48,176]{2,1,0:T(8,128)S(1)} all-to-all(f32[8,48,176]{2,1,0:T(8,128)S(1)} %shard_map.61), channel_id=1, replica_groups=mesh['x'=4,'yl'=2,'z'=8,'yh'=2,'c'=2] {'x','yl'}, dimensions={0} | all-to-all | bytes 540672 | tf_op jit(solution)/shard_map/all_to_all | solution.py:429
  (67 shorter events, 17.6 us)
Async XLA Ops:
  3.1 2.9 %collective-permute-start = (bf16[8,184,300]{2,1,0:T(8,128)(2,1)S(1)}, bf16[8,184,300]{2,1,0:T(8,128)(2,1)S(1)}, u32[]{:S(2)}, u32[]{:S(2)}) collective-permute-start(bf16[8,184,300]{2,1,0:T(8,128)(2,1)S(1)} %shard_map.46), channel_id=1, source_target_pairs={{0,1},{1,0},{2,3},{3,2},{4,5},{5,4},{6,7},{7,6},{8,9},{9,8},{10,11... | collective-permute-start | bytes 2649608 | tf_op jit(solution)/shard_map/ppermute | solution.py:23
  49.3 5.1 %collective-permute-start.1 = (bf16[16,136,600]{2,1,0:T(8,128)(2,1)S(1)}, bf16[16,136,600]{2,1,0:T(8,128)(2,1)S(1)}, u32[]{:S(2)}, u32[]{:S(2)}) collective-permute-start(bf16[16,136,600]{2,1,0:T(8,128)(2,1)S(1)} %all_to_all.15.near_ref), channel_id=1, source_target_pairs={{0,1},{1,0},{2,3},{3,2},{4,5},{5,4},{6,7},{7,6},{8,9},{9,8},{10,11... | collective-permute-start | bytes 7833608 | tf_op jit(solution)/shard_map/ppermute | solution.py:23
  50.9 9.3 %collective-permute-start.2 = (f32[24,704]{1,0:T(8,128)S(1)}, f32[24,704]{1,0:T(8,128)S(1)}, u32[]{:S(2)}, u32[]{:S(2)}) collective-permute-start(f32[24,704]{1,0:T(8,128)S(1)} %get-tuple-element.47), channel_id=1, source_target_pairs={{0,4},{4,8},{8,12},{12,16},{16,20},{20,24},{24,28},{28,0},{1,5},{5... | collective-permute-start | bytes 202760 | tf_op jit(solution)/shard_map/ppermute | solution.py:28
  52.9 7.3 %collective-permute-start.3 = (f32[24,704]{1,0:T(8,128)S(1)}, f32[24,704]{1,0:T(8,128)S(1)}, u32[]{:S(2)}, u32[]{:S(2)}) collective-permute-start(f32[24,704]{1,0:T(8,128)S(1)} %get-tuple-element.48), channel_id=1, source_target_pairs={{0,28},{4,0},{8,4},{12,8},{16,12},{20,16},{24,20},{28,24},{1,29},{... | collective-permute-start | bytes 202760 | tf_op jit(solution)/shard_map/ppermute | solution.py:28
  55.6 5.4 %collective-permute-start.4 = (f32[24,704]{1,0:T(8,128)S(1)}, f32[24,704]{1,0:T(8,128)S(1)}, u32[]{:S(2)}, u32[]{:S(2)}) collective-permute-start(f32[24,704]{1,0:T(8,128)S(1)} %get-tuple-element.49), channel_id=1, source_target_pairs={{0,4},{4,8},{8,12},{12,16},{16,20},{20,24},{24,28},{28,0},{1,5},{5... | collective-permute-start | bytes 202760 | tf_op jit(solution)/shard_map/ppermute | solution.py:28
  57.6 4.4 %collective-permute-start.5 = (f32[24,704]{1,0:T(8,128)S(1)}, f32[24,704]{1,0:T(8,128)S(1)}, u32[]{:S(2)}, u32[]{:S(2)}) collective-permute-start(f32[24,704]{1,0:T(8,128)S(1)} %get-tuple-element.50), channel_id=1, source_target_pairs={{0,28},{4,0},{8,4},{12,8},{16,12},{20,16},{24,20},{28,24},{1,29},{... | collective-permute-start | bytes 202760 | tf_op jit(solution)/shard_map/ppermute | solution.py:28
  62.6 8.6 %collective-permute-start.6 = (f32[48,1408]{1,0:T(8,128)S(1)}, f32[48,1408]{1,0:T(8,128)S(1)}, u32[]{:S(2)}, u32[]{:S(2)}) collective-permute-start(f32[48,1408]{1,0:T(8,128)S(1)} %get-tuple-element.51), channel_id=1, source_target_pairs={{0,4},{4,8},{8,12},{12,16},{16,20},{20,24},{24,28},{28,0},{1,5},{5... | collective-permute-start | bytes 811016 | tf_op jit(solution)/shard_map/ppermute | solution.py:28
  65.7 8.3 %collective-permute-start.7 = (f32[48,1408]{1,0:T(8,128)S(1)}, f32[48,1408]{1,0:T(8,128)S(1)}, u32[]{:S(2)}, u32[]{:S(2)}) collective-permute-start(f32[48,1408]{1,0:T(8,128)S(1)} %get-tuple-element.52), channel_id=1, source_target_pairs={{0,28},{4,0},{8,4},{12,8},{16,12},{20,16},{24,20},{28,24},{1,29},{... | collective-permute-start | bytes 811016 | tf_op jit(solution)/shard_map/ppermute | solution.py:28
  74.6 6.5 %collective-permute-start.8 = (f32[48,1408]{1,0:T(8,128)S(1)}, f32[48,1408]{1,0:T(8,128)S(1)}, u32[]{:S(2)}, u32[]{:S(2)}) collective-permute-start(f32[48,1408]{1,0:T(8,128)S(1)} %get-tuple-element.53), channel_id=1, source_target_pairs={{0,4},{4,8},{8,12},{12,16},{16,20},{20,24},{24,28},{28,0},{1,5},{5... | collective-permute-start | bytes 811016 | tf_op jit(solution)/shard_map/ppermute | solution.py:28
  76.4 6.5 %collective-permute-start.9 = (f32[48,1408]{1,0:T(8,128)S(1)}, f32[48,1408]{1,0:T(8,128)S(1)}, u32[]{:S(2)}, u32[]{:S(2)}) collective-permute-start(f32[48,1408]{1,0:T(8,128)S(1)} %get-tuple-element.54), channel_id=1, source_target_pairs={{0,28},{4,0},{8,4},{12,8},{16,12},{20,16},{24,20},{28,24},{1,29},{... | collective-permute-start | bytes 811016 | tf_op jit(solution)/shard_map/ppermute | solution.py:28
  83.5 6.7 %collective-permute-start.10 = (f32[48,1408]{1,0:T(8,128)S(1)}, f32[48,1408]{1,0:T(8,128)S(1)}, u32[]{:S(2)}, u32[]{:S(2)}) collective-permute-start(f32[48,1408]{1,0:T(8,128)S(1)} %get-tuple-element.55), channel_id=1, source_target_pairs={{0,4},{4,8},{8,12},{12,16},{16,20},{20,24},{24,28},{28,0},{1,5},{5... | collective-permute-start | bytes 811016 | tf_op jit(solution)/shard_map/ppermute | solution.py:28
  85.3 6.5 %collective-permute-start.11 = (f32[48,1408]{1,0:T(8,128)S(1)}, f32[48,1408]{1,0:T(8,128)S(1)}, u32[]{:S(2)}, u32[]{:S(2)}) collective-permute-start(f32[48,1408]{1,0:T(8,128)S(1)} %get-tuple-element.56), channel_id=1, source_target_pairs={{0,28},{4,0},{8,4},{12,8},{16,12},{20,16},{24,20},{28,24},{1,29},{... | collective-permute-start | bytes 811016 | tf_op jit(solution)/shard_map/ppermute | solution.py:28
  92.7 6.6 %collective-permute-start.13 = (bf16[48,1408]{1,0:T(8,128)(2,1)S(1)}, bf16[48,1408]{1,0:T(8,128)(2,1)S(1)}, u32[]{:S(2)}, u32[]{:S(2)}) collective-permute-start(bf16[48,1408]{1,0:T(8,128)(2,1)S(1)} %get-tuple-element.58.refs_0_), channel_id=1, source_target_pairs={{0,2},{2,0},{1,3},{3,1},{4,6},{6,4},{5,7},{7,5},{8,10},{10,8},{9,1... | collective-permute-start | bytes 405512 | tf_op jit(solution)/shard_map/ppermute | solution.py:23
  94.3 13.7 %collective-permute-start.12 = (bf16[48,1408]{1,0:T(8,128)(2,1)S(1)}, bf16[48,1408]{1,0:T(8,128)(2,1)S(1)}, u32[]{:S(2)}, u32[]{:S(2)}) collective-permute-start(bf16[48,1408]{1,0:T(8,128)(2,1)S(1)} %get-tuple-element.58.refs_0_), channel_id=1, source_target_pairs={{0,4},{4,8},{8,12},{12,16},{16,20},{20,24},{24,28},{28,0},{1,5},{5... | collective-permute-start | bytes 405512 | tf_op jit(solution)/shard_map/ppermute | solution.py:28
  95.8 12.3 %collective-permute-start.15 = (bf16[48,1408]{1,0:T(8,128)(2,1)S(1)}, bf16[48,1408]{1,0:T(8,128)(2,1)S(1)}, u32[]{:S(2)}, u32[]{:S(2)}) collective-permute-start(bf16[48,1408]{1,0:T(8,128)(2,1)S(1)} %get-tuple-element.58.refs_0_), channel_id=1, source_target_pairs={{0,28},{4,0},{8,4},{12,8},{16,12},{20,16},{24,20},{28,24},{1,29},{... | collective-permute-start | bytes 405512 | tf_op jit(solution)/shard_map/ppermute | solution.py:28
  99.3 8.8 %collective-permute-start.14 = (bf16[48,1408]{1,0:T(8,128)(2,1)S(1)}, bf16[48,1408]{1,0:T(8,128)(2,1)S(1)}, u32[]{:S(2)}, u32[]{:S(2)}) collective-permute-start(bf16[48,1408]{1,0:T(8,128)(2,1)S(1)} %collective-permute-done.13.refs_1_), channel_id=1, source_target_pairs={{0,4},{4,8},{8,12},{12,16},{16,20},{20,24},{24,28},{28,0},{1,5},{5... | collective-permute-start | bytes 405512 | tf_op jit(solution)/shard_map/ppermute | solution.py:28
  100.8 7.4 %collective-permute-start.16 = (bf16[48,1408]{1,0:T(8,128)(2,1)S(1)}, bf16[48,1408]{1,0:T(8,128)(2,1)S(1)}, u32[]{:S(2)}, u32[]{:S(2)}) collective-permute-start(bf16[48,1408]{1,0:T(8,128)(2,1)S(1)} %collective-permute-done.13.refs_1_), channel_id=1, source_target_pairs={{0,28},{4,0},{8,4},{12,8},{16,12},{20,16},{24,20},{28,24},{1,29},{... | collective-permute-start | bytes 405512 | tf_op jit(solution)/shard_map/ppermute | solution.py:28
  101.3 26.4 %all-to-all-start.1 = ((f32[32,24,96]{2,1,0:T(8,128)}), f32[32,24,96]{2,1,0:T(8,128)S(1)}, u32[]{:S(2)}, u32[]{:S(2)}) async-start(f32[32,24,96]{2,1,0:T(8,128)} %shard_map.56), calls=%async_computation.1 | async-start | bytes 786432 | tf_op jit(solution)/shard_map/all_to_all | solution.py:362
  108.2 16.2 %collective-permute-start.18 = (bf16[88,1408]{1,0:T(8,128)(2,1)S(1)}, bf16[88,1408]{1,0:T(8,128)(2,1)S(1)}, u32[]{:S(2)}, u32[]{:S(2)}) collective-permute-start(bf16[88,1408]{1,0:T(8,128)(2,1)S(1)} %get-tuple-element.62.refs_2_), channel_id=1, source_target_pairs={{0,28},{4,0},{8,4},{12,8},{16,12},{20,16},{24,20},{28,24},{1,29},{... | collective-permute-start | bytes 743432 | tf_op jit(solution)/shard_map/ppermute | solution.py:28
  108.5 15.9 %collective-permute-start.17 = (bf16[88,1408]{1,0:T(8,128)(2,1)S(1)}, bf16[88,1408]{1,0:T(8,128)(2,1)S(1)}, u32[]{:S(2)}, u32[]{:S(2)}) collective-permute-start(bf16[88,1408]{1,0:T(8,128)(2,1)S(1)} %get-tuple-element.61.refs_4_), channel_id=1, source_target_pairs={{0,4},{4,8},{8,12},{12,16},{16,20},{20,24},{24,28},{28,0},{1,5},{5... | collective-permute-start | bytes 743432 | tf_op jit(solution)/shard_map/ppermute | solution.py:28
  110.3 14.6 %collective-permute-start.19 = (bf16[88,1408]{1,0:T(8,128)(2,1)S(1)}, bf16[88,1408]{1,0:T(8,128)(2,1)S(1)}, u32[]{:S(2)}, u32[]{:S(2)}) collective-permute-start(bf16[88,1408]{1,0:T(8,128)(2,1)S(1)} %shard_map.58.refs_0_), channel_id=1, source_target_pairs={{0,1},{1,0},{2,3},{3,2},{4,5},{5,4},{6,7},{7,6},{8,9},{9,8},{10,11... | collective-permute-start | bytes 743432 | tf_op jit(solution)/shard_map/ppermute | solution.py:23
  110.4 14.5 %collective-permute-start.20 = (bf16[88,1408]{1,0:T(8,128)(2,1)S(1)}, bf16[88,1408]{1,0:T(8,128)(2,1)S(1)}, u32[]{:S(2)}, u32[]{:S(2)}) collective-permute-start(bf16[88,1408]{1,0:T(8,128)(2,1)S(1)} %get-tuple-element.62.refs_2_), channel_id=1, source_target_pairs={{0,1},{1,0},{2,3},{3,2},{4,5},{5,4},{6,7},{7,6},{8,9},{9,8},{10,11... | collective-permute-start | bytes 743432 | tf_op jit(solution)/shard_map/ppermute | solution.py:23
  110.9 14.0 %collective-permute-start.21 = (bf16[88,1408]{1,0:T(8,128)(2,1)S(1)}, bf16[88,1408]{1,0:T(8,128)(2,1)S(1)}, u32[]{:S(2)}, u32[]{:S(2)}) collective-permute-start(bf16[88,1408]{1,0:T(8,128)(2,1)S(1)} %get-tuple-element.61.refs_4_), channel_id=1, source_target_pairs={{0,1},{1,0},{2,3},{3,2},{4,5},{5,4},{6,7},{7,6},{8,9},{9,8},{10,11... | collective-permute-start | bytes 743432 | tf_op jit(solution)/shard_map/ppermute | solution.py:23
  124.4 8.1 %collective-permute-start.26 = (bf16[88,1408]{1,0:T(8,128)(2,1)S(1)}, bf16[88,1408]{1,0:T(8,128)(2,1)S(1)}, u32[]{:S(2)}, u32[]{:S(2)}) collective-permute-start(bf16[88,1408]{1,0:T(8,128)(2,1)S(1)} %collective-permute-done.18.down_ref.refs_6_), channel_id=1, source_target_pairs={{0,1},{1,0},{2,3},{3,2},{4,5},{5,4},{6,7},{7,6},{8,9},{9,8},{10,11... | collective-permute-start | bytes 743432 | tf_op jit(solution)/shard_map/ppermute | solution.py:23
  124.4 8.1 %collective-permute-start.27 = (bf16[88,1408]{1,0:T(8,128)(2,1)S(1)}, bf16[88,1408]{1,0:T(8,128)(2,1)}, u32[]{:S(2)}, u32[]{:S(2)}) collective-permute-start(bf16[88,1408]{1,0:T(8,128)(2,1)S(1)} %collective-permute-done.17.up_ref.refs_8_), channel_id=1, source_target_pairs={{0,1},{1,0},{2,3},{3,2},{4,5},{5,4},{6,7},{7,6},{8,9},{9,8},{10,11... | collective-permute-start | bytes 743432 | tf_op jit(solution)/shard_map/ppermute | solution.py:23
  124.9 17.4 %collective-permute-start.22 = (bf16[88,1408]{1,0:T(8,128)(2,1)S(1)}, bf16[88,1408]{1,0:T(8,128)(2,1)S(1)}, u32[]{:S(2)}, u32[]{:S(2)}) collective-permute-start(bf16[88,1408]{1,0:T(8,128)(2,1)S(1)} %collective-permute-done.18.down_ref.refs_6_), channel_id=1, source_target_pairs={{0,28},{4,0},{8,4},{12,8},{16,12},{20,16},{24,20},{28,24},{1,29},{... | collective-permute-start | bytes 743432 | tf_op jit(solution)/shard_map/ppermute | solution.py:28
  126.3 16.0 %collective-permute-start.23 = (bf16[88,1408]{1,0:T(8,128)(2,1)S(1)}, bf16[88,1408]{1,0:T(8,128)(2,1)S(1)}, u32[]{:S(2)}, u32[]{:S(2)}) collective-permute-start(bf16[88,1408]{1,0:T(8,128)(2,1)S(1)} %collective-permute-done.17.up_ref.refs_8_), channel_id=1, source_target_pairs={{0,4},{4,8},{8,12},{12,16},{16,20},{20,24},{24,28},{28,0},{1,5},{5... | collective-permute-start | bytes 743432 | tf_op jit(solution)/shard_map/ppermute | solution.py:28
  127.7 14.6 %collective-permute-start.24 = (bf16[48,1408]{1,0:T(8,128)(2,1)S(1)}, bf16[48,1408]{1,0:T(8,128)(2,1)S(1)}, u32[]{:S(2)}, u32[]{:S(2)}) collective-permute-start(bf16[48,1408]{1,0:T(8,128)(2,1)S(1)} %get-tuple-element.67), channel_id=1, source_target_pairs={{0,8},{4,12},{8,16},{12,20},{16,24},{20,28},{24,0},{28,4},{1,9},{5... | collective-permute-start | bytes 405512 | tf_op jit(solution)/shard_map/ppermute | solution.py:28
  132.5 6.0 %collective-permute-start.25 = (bf16[40,1408]{1,0:T(8,128)(2,1)}, bf16[40,1408]{1,0:T(8,128)(2,1)S(1)}, u32[]{:S(2)}, u32[]{:S(2)}) collective-permute-start(bf16[40,1408]{1,0:T(8,128)(2,1)} %copy-done.4), channel_id=1, source_target_pairs={{0,24},{4,28},{8,0},{12,4},{16,8},{20,12},{24,16},{28,20},{1,25},{... | collective-permute-start | bytes 337928 | tf_op jit(solution)/shard_map/ppermute | solution.py:28
  142.3 2.2 %collective-permute-start.28 = (bf16[88,1408]{1,0:T(8,128)(2,1)S(1)}, bf16[88,1408]{1,0:T(8,128)(2,1)S(1)}, u32[]{:S(2)}, u32[]{:S(2)}) collective-permute-start(bf16[88,1408]{1,0:T(8,128)(2,1)S(1)} %collective-permute-done.22.refs_0_), channel_id=1, source_target_pairs={{0,1},{1,0},{2,3},{3,2},{4,5},{5,4},{6,7},{7,6},{8,9},{9,8},{10,11... | collective-permute-start | bytes 743432 | tf_op jit(solution)/shard_map/ppermute | solution.py:23
  142.3 2.2 %collective-permute-start.29 = (bf16[88,1408]{1,0:T(8,128)(2,1)S(1)}, bf16[88,1408]{1,0:T(8,128)(2,1)S(1)}, u32[]{:S(2)}, u32[]{:S(2)}) collective-permute-start(bf16[88,1408]{1,0:T(8,128)(2,1)S(1)} %collective-permute-done.23.refs_2_), channel_id=1, source_target_pairs={{0,1},{1,0},{2,3},{3,2},{4,5},{5,4},{6,7},{7,6},{8,9},{9,8},{10,11... | collective-permute-start | bytes 743432 | tf_op jit(solution)/shard_map/ppermute | solution.py:23
  142.8 1.7 %collective-permute-start.30 = (bf16[48,1408]{1,0:T(8,128)(2,1)S(1)}, bf16[48,1408]{1,0:T(8,128)(2,1)S(1)}, u32[]{:S(2)}, u32[]{:S(2)}) collective-permute-start(bf16[48,1408]{1,0:T(8,128)(2,1)S(1)} %collective-permute-done.24.refs_4_), channel_id=1, source_target_pairs={{0,1},{1,0},{2,3},{3,2},{4,5},{5,4},{6,7},{7,6},{8,9},{9,8},{10,11... | collective-permute-start | bytes 405512 | tf_op jit(solution)/shard_map/ppermute | solution.py:23
  (7 other events, 21.1 us)

commit v10 on v9

--- a/solution.py
+++ b/solution.py
@@ -166,12 +166,18 @@
 
 
 def blocks_kernel(rows_ref, blocks_ref):
-    count, half, lanes = blocks_ref.shape
+    count, rows, lanes = blocks_ref.shape
     width = rows_ref.shape[1] // count
-    gap = jnp.zeros((half, lanes // 2 - width), F32)
+    rest, room = width - 2 * rows, lanes - 2 * width
+    left = width - room
+    tails = [rows_ref[2 * rows : 3 * rows, (k + 1) * width - left : (k + 1) * width] for k in range(count)]
+    tails = jnp.concatenate(tails, axis=1).T
+    gap = jnp.zeros((left, room - rows), F32)
     for k in range(count):
         block = rows_ref[:, k * width : (k + 1) * width]
-        blocks_ref[k] = jnp.concatenate([block[:half], gap, block[half:], gap], axis=1)
+        tail = jnp.concatenate([tails[k * left : (k + 1) * left], gap], axis=1)
+        third = jnp.concatenate([block[2 * rows : width, :room], tail], axis=0)
+        blocks_ref[k] = jnp.concatenate([block[:rows], block[rows : 2 * rows], third], axis=1)
 
 
 def merge_kernel(width, *refs):
@@ -233,8 +239,13 @@
     width = slab // 4
 
     def turn(at):
-        flipped = columns_ref[at].T
-        return jnp.concatenate([flipped[:padded], flipped[padded:, : width - padded // 2]], axis=1)
+        block = columns_ref[at]
+        flipped = block.T
+        lanes, rows = flipped.shape
+        rest = width - 2 * rows
+        third = jnp.concatenate([flipped[2 * width :, :rest], block[rest:, 2 * width : 2 * width + rest]], axis=0)
+        found = jnp.concatenate([flipped[:width], flipped[width : 2 * width], third], axis=1)
+        return jnp.concatenate([found, jnp.zeros((padded - width, width), F32)], axis=0)
 
     turned = []
     for k in range(nz):
@@ -353,7 +364,7 @@
     other = swap(mine, "yh")
     columns = pl.pallas_call(
         blocks_kernel,
-        out_shape=jax.ShapeDtypeStruct((4 * nz, padded // 2, 2 * padded), F32),
+        out_shape=jax.ShapeDtypeStruct((4 * nz, 16, 128), F32),
         in_specs=[VMEM],
         out_specs=VMEM,
         compiler_params=params(8),

time: 159 us -> 156 us (0.981)
  waiting for transfers between devices: 47.5 us -> 42.3 us
  Pallas kernels: 17.1 us -> 18.8 us
    ppermute x20, waiting for transfers between devices: 41 us -> 36.5 us  [shift(): lax.ppermute(value, axis, [(i, (i + step) % size) for i in range(size)])]
    unnamed x12 -> x14, local copies, waits for them, and re-layouts: 2.94 us -> 3.6 us
  transfers between devices with their start and end apart: 33 -> 33, of which waited for: 15 -> 15; matrix products, arithmetic and copies ran while one was open for 0% -> 0% of each run, Pallas kernels for 7% -> 8%
where the time goes in v10:
time: 156 us
  blocking collectives  53.6 us (34%)
  waiting for transfers between devices  42.3 us (27%)
  starting transfers between devices  36.6 us (23%)
  Pallas kernels  18.8 us (12%)
  local copies, waits for them, and re-layouts  3.69 us (2%)
    all_to_all x1, blocking collectives, local(): lax.all_to_all(ours, ('yh', 'x', 'yl'), split_axis=0, concat_axis=0, tile...  42.1 us
    ppermute x20, waiting for transfers between devices, shift(): lax.ppermute(value, axis, [(i, (i + step) % size) for i in range(size)])  36.5 us
    ppermute x20, starting transfers between devices, shift(): lax.ppermute(value, axis, [(i, (i + step) % size) for i in range(size)])  25.5 us
    all_to_all x1, blocking collectives, local(): lax.all_to_all(added, SLABS, split_axis=0, concat_axis=0, tiled=True)  11.5 us
    all_to_all x1, starting transfers between devices, local(): lax.all_to_all(columns, ('z', 'yh', 'c'), split_axis=0, concat_axis=0, ti...  7.19 us
    ppermute x12, waiting for transfers between devices, swap(): return lax.ppermute(value, axis, [(0, 1), (1, 0)])  5.82 us
    pallas_call x1, Pallas kernels, local(): pl.pallas_call(functools.partial(early_kernel, soon, nz), out_shape=(rows...  5.44 us
    ppermute x12, starting transfers between devices, swap(): return lax.ppermute(value, axis, [(0, 1), (1, 0)])  3.97 us
  transfers between devices with their start and end apart: 33, of which 15 were waited for; matrix products, arithmetic and copies ran while one was open for 0% of the time, Pallas kernels for 8%

profile of v10, /device:TPU:32, one launch (start us, length us, event | category | flops | bytes accessed | tf_op | source)
XLA Modules:
  0.0 156.0 jit_solution(11466741402039953074)
XLA Ops:
  0.1 1.6 %copy-done = bf16[16,176,300]{2,1,0:T(8,128)(2,1)S(1)} copy-done((bf16[16,176,300]{2,1,0:T(8,128)(2,1)S(1)}, bf16[16,176,300]{2,1,0:T(8,128)(2,1)}, u32[]{:S(2)}) %copy-start) | copy-done | bytes 1689624
  3.9 2.0 %collective-permute-done.taken_ref = bf16[8,184,300]{2,1,0:T(8,128)(2,1)S(1)} collective-permute-done((bf16[8,184,300]{2,1,0:T(8,128)(2,1)S(1)}, bf16[8,184,300]{2,1,0:T(8,128)(2,1)S(1)}, u32[]{:S(2)}, u32[]{:S(2)}) %collective-permute-start) | collective-permute-done | bytes 883232 | tf_op jit(solution)/shard_map/ppermute | solution.py:23
  7.1 42.1 %all_to_all.15.near_ref = bf16[16,136,600]{2,1,0:T(8,128)(2,1)S(1)} all-to-all(bf16[16,136,600]{2,1,0:T(8,128)(2,1)S(1)} %shard_map.48), channel_id=1, replica_groups=mesh['x'=4,'yl'=2,'z'=8,'yh'=2,'c'=2] {'yh','x','yl'}, dimensions={0} | all-to-all | bytes 5222400 | tf_op jit(solution)/shard_map/all_to_all | solution.py:312
  49.3 1.6 %shard_map.49 = (f32[8,48,704]{2,1,0:T(8,128)S(1)}, f32[24,704]{1,0:T(8,128)S(1)}, f32[24,704]{1,0:T(8,128)S(1)}) custom-call(s32[7]{0:T(128)S(1)} %stack.27.where_ref, bf16[16,136,600]{2,1,0:T(8,128)(2,1)S(1)} %all_to_all.15.near_ref), custom_call_target="tpu_custom_call" | custom-call | flops 648806400 | tf_op jit(solution)/shard_map/pallas_call | solution.py:319
  50.9 2.0 %collective-permute-start.2 = (f32[24,704]{1,0:T(8,128)S(1)}, f32[24,704]{1,0:T(8,128)S(1)}, u32[]{:S(2)}, u32[]{:S(2)}) collective-permute-start(f32[24,704]{1,0:T(8,128)S(1)} %get-tuple-element.47), channel_id=1, source_target_pairs={{0,4},{4,8},{8,12},{12,16},{16,20},{20,24},{24,28},{28,0},{1,5},{5... | collective-permute-start | bytes 202760 | tf_op jit(solution)/shard_map/ppermute | solution.py:28
  53.0 1.4 collective-permute-done.1.far_ref
  55.6 2.0 %collective-permute-start.4 = (f32[24,704]{1,0:T(8,128)S(1)}, f32[24,704]{1,0:T(8,128)S(1)}, u32[]{:S(2)}, u32[]{:S(2)}) collective-permute-start(f32[24,704]{1,0:T(8,128)S(1)} %get-tuple-element.49), channel_id=1, source_target_pairs={{0,4},{4,8},{8,12},{12,16},{16,20},{20,24},{24,28},{28,0},{1,5},{5... | collective-permute-start | bytes 202760 | tf_op jit(solution)/shard_map/ppermute | solution.py:28
  58.5 1.7 %shard_map.50 = (f32[8,48,1408]{2,1,0:T(8,128)S(1)}, f32[48,1408]{1,0:T(8,128)S(1)}) custom-call(s32[7]{0:T(128)S(1)} %stack.27.where_ref, s32[2,8]{1,0:T(2,128)S(1)} %bitcast.10, f32[16]{0:T(128)S(1)} %copy-done.3, f32[1,1408]{1,0:T(1,128)S(1)} %broadcast_in_dim.3.vir_ref, f32[8,48,704]{2,1,0:T(8,128)S(1)} %get-tuple-element.45.near_part_ref, ...), custom_call_target="tpu_custom_call" | custom-call | flops 648806400 | tf_op jit(solution)/shard_map/pallas_call | solution.py:337
  62.6 3.1 %collective-permute-start.6 = (f32[48,1408]{1,0:T(8,128)S(1)}, f32[48,1408]{1,0:T(8,128)S(1)}, u32[]{:S(2)}, u32[]{:S(2)}) collective-permute-start(f32[48,1408]{1,0:T(8,128)S(1)} %get-tuple-element.51), channel_id=1, source_target_pairs={{0,4},{4,8},{8,12},{12,16},{16,20},{20,24},{24,28},{28,0},{1,5},{5... | collective-permute-start | bytes 811016 | tf_op jit(solution)/shard_map/ppermute | solution.py:28
  65.7 5.5 %collective-permute-done.6.refs_0_ = f32[48,1408]{1,0:T(8,128)S(1)} collective-permute-done((f32[48,1408]{1,0:T(8,128)S(1)}, f32[48,1408]{1,0:T(8,128)S(1)}, u32[]{:S(2)}, u32[]{:S(2)}) %collective-permute-start.6) | collective-permute-done | bytes 270368 | tf_op jit(solution)/shard_map/ppermute | solution.py:28
  71.2 2.8 %collective-permute-done.7.refs_1_ = f32[48,1408]{1,0:T(8,128)S(1)} collective-permute-done((f32[48,1408]{1,0:T(8,128)S(1)}, f32[48,1408]{1,0:T(8,128)S(1)}, u32[]{:S(2)}, u32[]{:S(2)}) %collective-permute-start.7) | collective-permute-done | bytes 270368 | tf_op jit(solution)/shard_map/ppermute | solution.py:28
  74.6 1.8 %collective-permute-start.8 = (f32[48,1408]{1,0:T(8,128)S(1)}, f32[48,1408]{1,0:T(8,128)S(1)}, u32[]{:S(2)}, u32[]{:S(2)}) collective-permute-start(f32[48,1408]{1,0:T(8,128)S(1)} %get-tuple-element.53), channel_id=1, source_target_pairs={{0,4},{4,8},{8,12},{12,16},{16,20},{20,24},{24,28},{28,0},{1,5},{5... | collective-permute-start | bytes 811016 | tf_op jit(solution)/shard_map/ppermute | solution.py:28
  76.7 4.4 %collective-permute-done.8.refs_0_ = f32[48,1408]{1,0:T(8,128)S(1)} collective-permute-done((f32[48,1408]{1,0:T(8,128)S(1)}, f32[48,1408]{1,0:T(8,128)S(1)}, u32[]{:S(2)}, u32[]{:S(2)}) %collective-permute-start.8) | collective-permute-done | bytes 270368 | tf_op jit(solution)/shard_map/ppermute | solution.py:28
  81.1 1.7 %collective-permute-done.9.refs_1_ = f32[48,1408]{1,0:T(8,128)S(1)} collective-permute-done((f32[48,1408]{1,0:T(8,128)S(1)}, f32[48,1408]{1,0:T(8,128)S(1)}, u32[]{:S(2)}, u32[]{:S(2)}) %collective-permute-start.9) | collective-permute-done | bytes 270368 | tf_op jit(solution)/shard_map/ppermute | solution.py:28
  83.5 1.8 %collective-permute-start.10 = (f32[48,1408]{1,0:T(8,128)S(1)}, f32[48,1408]{1,0:T(8,128)S(1)}, u32[]{:S(2)}, u32[]{:S(2)}) collective-permute-start(f32[48,1408]{1,0:T(8,128)S(1)} %get-tuple-element.55), channel_id=1, source_target_pairs={{0,4},{4,8},{8,12},{12,16},{16,20},{20,24},{24,28},{28,0},{1,5},{5... | collective-permute-start | bytes 811016 | tf_op jit(solution)/shard_map/ppermute | solution.py:28
  85.8 4.4 %collective-permute-done.10.up_in = f32[48,1408]{1,0:T(8,128)S(1)} collective-permute-done((f32[48,1408]{1,0:T(8,128)S(1)}, f32[48,1408]{1,0:T(8,128)S(1)}, u32[]{:S(2)}, u32[]{:S(2)}) %collective-permute-start.10) | collective-permute-done | bytes 270368 | tf_op jit(solution)/shard_map/ppermute | solution.py:28
  90.2 1.6 %collective-permute-done.11.down_in = f32[48,1408]{1,0:T(8,128)S(1)} collective-permute-done((f32[48,1408]{1,0:T(8,128)S(1)}, f32[48,1408]{1,0:T(8,128)S(1)}, u32[]{:S(2)}, u32[]{:S(2)}) %collective-permute-start.11) | collective-permute-done | bytes 270368 | tf_op jit(solution)/shard_map/ppermute | solution.py:28
  92.7 1.7 %collective-permute-start.13 = (bf16[48,1408]{1,0:T(8,128)(2,1)S(1)}, bf16[48,1408]{1,0:T(8,128)(2,1)S(1)}, u32[]{:S(2)}, u32[]{:S(2)}) collective-permute-start(bf16[48,1408]{1,0:T(8,128)(2,1)S(1)} %get-tuple-element.58.refs_0_), channel_id=1, source_target_pairs={{0,2},{2,0},{1,3},{3,1},{4,6},{6,4},{5,7},{7,5},{8,10},{10,8},{9,1... | collective-permute-start | bytes 405512 | tf_op jit(solution)/shard_map/ppermute | solution.py:23
  94.3 1.5 collective-permute-start.12
  96.4 1.7 %shard_map.56 = f32[32,16,128]{2,1,0:T(8,128)} custom-call(f32[48,1408]{1,0:T(8,128)S(1)} %get-tuple-element.59.rows_ref), custom_call_target="tpu_custom_call" | custom-call | tf_op jit(solution)/shard_map/pallas_call | solution.py:365
  99.3 1.5 collective-permute-start.14
  101.3 7.2 %all-to-all-start.1 = ((f32[32,16,128]{2,1,0:T(8,128)}), f32[32,16,128]{2,1,0:T(8,128)S(1)}, u32[]{:S(2)}, u32[]{:S(2)}) async-start(f32[32,16,128]{2,1,0:T(8,128)} %shard_map.56), calls=%async_computation.1 | async-start | bytes 524288 | tf_op jit(solution)/shard_map/all_to_all | solution.py:373
  108.9 1.8 %collective-permute-start.17 = (bf16[88,1408]{1,0:T(8,128)(2,1)S(1)}, bf16[88,1408]{1,0:T(8,128)(2,1)S(1)}, u32[]{:S(2)}, u32[]{:S(2)}) collective-permute-start(bf16[88,1408]{1,0:T(8,128)(2,1)S(1)} %get-tuple-element.61.refs_4_), channel_id=1, source_target_pairs={{0,4},{4,8},{8,12},{12,16},{16,20},{20,24},{24,28},{28,0},{1,5},{5... | collective-permute-start | bytes 743432 | tf_op jit(solution)/shard_map/ppermute | solution.py:28
  111.5 10.5 %collective-permute-done.18.down_ref.refs_6_ = bf16[88,1408]{1,0:T(8,128)(2,1)S(1)} collective-permute-done((bf16[88,1408]{1,0:T(8,128)(2,1)S(1)}, bf16[88,1408]{1,0:T(8,128)(2,1)S(1)}, u32[]{:S(2)}, u32[]{:S(2)}) %collective-permute-start.18) | collective-permute-done | bytes 247840 | tf_op jit(solution)/shard_map/ppermute | solution.py:28
  122.5 1.4 collective-permute-start.22
  126.0 4.8 %collective-permute-start.24 = (bf16[48,1408]{1,0:T(8,128)(2,1)}, bf16[48,1408]{1,0:T(8,128)(2,1)S(1)}, u32[]{:S(2)}, u32[]{:S(2)}) collective-permute-start(bf16[48,1408]{1,0:T(8,128)(2,1)} %copy-done.4), channel_id=1, source_target_pairs={{0,8},{4,12},{8,16},{12,20},{16,24},{20,28},{24,0},{28,4},{1,9},{5... | collective-permute-start | bytes 405512 | tf_op jit(solution)/shard_map/ppermute | solution.py:28
  130.8 5.4 %shard_map.60 = (f32[48,1408]{1,0:T(8,128)S(1)}, f32[8,48,176]{2,1,0:T(8,128)S(1)}, bf16[48,1408]{1,0:T(8,128)(2,1)S(1)}, bf16[8,2,48,88]{3,2,1,0:T(8,128)(2,1)S(1)}) custom-call(s32[7]{0:T(128)S(1)} %stack.27.where_ref, f32[48,1408]{1,0:T(8,128)S(1)} %get-tuple-element.59.rows_ref, f32[32,16,128]{2,1,0:T(8,128)S(1)} %all-to-all-done.1.columns_ref, ...), custom_call_target="tpu_custom_call" | custom-call | flops 129761280 | bytes 2703360 | tf_op jit(solution)/shard_map/pallas_call | solution.py:407
  136.2 2.5 %collective-permute-done.25.refs_5_ = bf16[40,1408]{1,0:T(8,128)(2,1)S(1)} collective-permute-done((bf16[40,1408]{1,0:T(8,128)(2,1)}, bf16[40,1408]{1,0:T(8,128)(2,1)S(1)}, u32[]{:S(2)}, u32[]{:S(2)}) %collective-permute-start.25) | collective-permute-done | bytes 112672 | tf_op jit(solution)/shard_map/ppermute | solution.py:28
  138.7 1.3 collective-permute-done.24.refs_4_
  141.0 1.2 collective-permute-done.31.refs_7_
  142.2 1.6 %shard_map.61 = f32[8,48,176]{2,1,0:T(8,128)S(1)} custom-call(s32[7]{0:T(128)S(1)} %stack.27.where_ref, f32[48,1408]{1,0:T(8,128)S(1)} %get-tuple-element.77.total_ref, f32[8,48,176]{2,1,0:T(8,128)S(1)} %get-tuple-element.78.blocks_ref, bf16[48,1408]{1,0:T(8,128)(2,1)S(1)} %get-tuple-element.79.tilde_ref, ...), custom_call_target="tpu_custom_call" | custom-call | flops 77856768 | bytes 1622016 | tf_op jit(solution)/shard_map/pallas_call | solution.py:421
  143.8 11.5 %all_to_all.16 = f32[8,48,176]{2,1,0:T(8,128)S(1)} all-to-all(f32[8,48,176]{2,1,0:T(8,128)S(1)} %shard_map.61), channel_id=1, replica_groups=mesh['x'=4,'yl'=2,'z'=8,'yh'=2,'c'=2] {'x','yl'}, dimensions={0} | all-to-all | bytes 540672 | tf_op jit(solution)/shard_map/all_to_all | solution.py:440
  (69 shorter events, 18.4 us)
Async XLA Ops:
  3.1 2.9 %collective-permute-start = (bf16[8,184,300]{2,1,0:T(8,128)(2,1)S(1)}, bf16[8,184,300]{2,1,0:T(8,128)(2,1)S(1)}, u32[]{:S(2)}, u32[]{:S(2)}) collective-permute-start(bf16[8,184,300]{2,1,0:T(8,128)(2,1)S(1)} %shard_map.46), channel_id=1, source_target_pairs={{0,1},{1,0},{2,3},{3,2},{4,5},{5,4},{6,7},{7,6},{8,9},{9,8},{10,11... | collective-permute-start | bytes 2649608 | tf_op jit(solution)/shard_map/ppermute | solution.py:23
  49.3 5.1 %collective-permute-start.1 = (bf16[16,136,600]{2,1,0:T(8,128)(2,1)S(1)}, bf16[16,136,600]{2,1,0:T(8,128)(2,1)S(1)}, u32[]{:S(2)}, u32[]{:S(2)}) collective-permute-start(bf16[16,136,600]{2,1,0:T(8,128)(2,1)S(1)} %all_to_all.15.near_ref), channel_id=1, source_target_pairs={{0,1},{1,0},{2,3},{3,2},{4,5},{5,4},{6,7},{7,6},{8,9},{9,8},{10,11... | collective-permute-start | bytes 7833608 | tf_op jit(solution)/shard_map/ppermute | solution.py:23
  50.9 9.3 %collective-permute-start.2 = (f32[24,704]{1,0:T(8,128)S(1)}, f32[24,704]{1,0:T(8,128)S(1)}, u32[]{:S(2)}, u32[]{:S(2)}) collective-permute-start(f32[24,704]{1,0:T(8,128)S(1)} %get-tuple-element.47), channel_id=1, source_target_pairs={{0,4},{4,8},{8,12},{12,16},{16,20},{20,24},{24,28},{28,0},{1,5},{5... | collective-permute-start | bytes 202760 | tf_op jit(solution)/shard_map/ppermute | solution.py:28
  52.9 7.3 %collective-permute-start.3 = (f32[24,704]{1,0:T(8,128)S(1)}, f32[24,704]{1,0:T(8,128)S(1)}, u32[]{:S(2)}, u32[]{:S(2)}) collective-permute-start(f32[24,704]{1,0:T(8,128)S(1)} %get-tuple-element.48), channel_id=1, source_target_pairs={{0,28},{4,0},{8,4},{12,8},{16,12},{20,16},{24,20},{28,24},{1,29},{... | collective-permute-start | bytes 202760 | tf_op jit(solution)/shard_map/ppermute | solution.py:28
  55.6 5.4 %collective-permute-start.4 = (f32[24,704]{1,0:T(8,128)S(1)}, f32[24,704]{1,0:T(8,128)S(1)}, u32[]{:S(2)}, u32[]{:S(2)}) collective-permute-start(f32[24,704]{1,0:T(8,128)S(1)} %get-tuple-element.49), channel_id=1, source_target_pairs={{0,4},{4,8},{8,12},{12,16},{16,20},{20,24},{24,28},{28,0},{1,5},{5... | collective-permute-start | bytes 202760 | tf_op jit(solution)/shard_map/ppermute | solution.py:28
  57.6 4.4 %collective-permute-start.5 = (f32[24,704]{1,0:T(8,128)S(1)}, f32[24,704]{1,0:T(8,128)S(1)}, u32[]{:S(2)}, u32[]{:S(2)}) collective-permute-start(f32[24,704]{1,0:T(8,128)S(1)} %get-tuple-element.50), channel_id=1, source_target_pairs={{0,28},{4,0},{8,4},{12,8},{16,12},{20,16},{24,20},{28,24},{1,29},{... | collective-permute-start | bytes 202760 | tf_op jit(solution)/shard_map/ppermute | solution.py:28
  62.6 8.6 %collective-permute-start.6 = (f32[48,1408]{1,0:T(8,128)S(1)}, f32[48,1408]{1,0:T(8,128)S(1)}, u32[]{:S(2)}, u32[]{:S(2)}) collective-permute-start(f32[48,1408]{1,0:T(8,128)S(1)} %get-tuple-element.51), channel_id=1, source_target_pairs={{0,4},{4,8},{8,12},{12,16},{16,20},{20,24},{24,28},{28,0},{1,5},{5... | collective-permute-start | bytes 811016 | tf_op jit(solution)/shard_map/ppermute | solution.py:28
  65.7 8.3 %collective-permute-start.7 = (f32[48,1408]{1,0:T(8,128)S(1)}, f32[48,1408]{1,0:T(8,128)S(1)}, u32[]{:S(2)}, u32[]{:S(2)}) collective-permute-start(f32[48,1408]{1,0:T(8,128)S(1)} %get-tuple-element.52), channel_id=1, source_target_pairs={{0,28},{4,0},{8,4},{12,8},{16,12},{20,16},{24,20},{28,24},{1,29},{... | collective-permute-start | bytes 811016 | tf_op jit(solution)/shard_map/ppermute | solution.py:28
  74.6 6.5 %collective-permute-start.8 = (f32[48,1408]{1,0:T(8,128)S(1)}, f32[48,1408]{1,0:T(8,128)S(1)}, u32[]{:S(2)}, u32[]{:S(2)}) collective-permute-start(f32[48,1408]{1,0:T(8,128)S(1)} %get-tuple-element.53), channel_id=1, source_target_pairs={{0,4},{4,8},{8,12},{12,16},{16,20},{20,24},{24,28},{28,0},{1,5},{5... | collective-permute-start | bytes 811016 | tf_op jit(solution)/shard_map/ppermute | solution.py:28
  76.4 6.5 %collective-permute-start.9 = (f32[48,1408]{1,0:T(8,128)S(1)}, f32[48,1408]{1,0:T(8,128)S(1)}, u32[]{:S(2)}, u32[]{:S(2)}) collective-permute-start(f32[48,1408]{1,0:T(8,128)S(1)} %get-tuple-element.54), channel_id=1, source_target_pairs={{0,28},{4,0},{8,4},{12,8},{16,12},{20,16},{24,20},{28,24},{1,29},{... | collective-permute-start | bytes 811016 | tf_op jit(solution)/shard_map/ppermute | solution.py:28
  83.5 6.7 %collective-permute-start.10 = (f32[48,1408]{1,0:T(8,128)S(1)}, f32[48,1408]{1,0:T(8,128)S(1)}, u32[]{:S(2)}, u32[]{:S(2)}) collective-permute-start(f32[48,1408]{1,0:T(8,128)S(1)} %get-tuple-element.55), channel_id=1, source_target_pairs={{0,4},{4,8},{8,12},{12,16},{16,20},{20,24},{24,28},{28,0},{1,5},{5... | collective-permute-start | bytes 811016 | tf_op jit(solution)/shard_map/ppermute | solution.py:28
  85.3 6.5 %collective-permute-start.11 = (f32[48,1408]{1,0:T(8,128)S(1)}, f32[48,1408]{1,0:T(8,128)S(1)}, u32[]{:S(2)}, u32[]{:S(2)}) collective-permute-start(f32[48,1408]{1,0:T(8,128)S(1)} %get-tuple-element.56), channel_id=1, source_target_pairs={{0,28},{4,0},{8,4},{12,8},{16,12},{20,16},{24,20},{28,24},{1,29},{... | collective-permute-start | bytes 811016 | tf_op jit(solution)/shard_map/ppermute | solution.py:28
  92.7 6.6 %collective-permute-start.13 = (bf16[48,1408]{1,0:T(8,128)(2,1)S(1)}, bf16[48,1408]{1,0:T(8,128)(2,1)S(1)}, u32[]{:S(2)}, u32[]{:S(2)}) collective-permute-start(bf16[48,1408]{1,0:T(8,128)(2,1)S(1)} %get-tuple-element.58.refs_0_), channel_id=1, source_target_pairs={{0,2},{2,0},{1,3},{3,1},{4,6},{6,4},{5,7},{7,5},{8,10},{10,8},{9,1... | collective-permute-start | bytes 405512 | tf_op jit(solution)/shard_map/ppermute | solution.py:23
  94.3 14.2 %collective-permute-start.12 = (bf16[48,1408]{1,0:T(8,128)(2,1)S(1)}, bf16[48,1408]{1,0:T(8,128)(2,1)S(1)}, u32[]{:S(2)}, u32[]{:S(2)}) collective-permute-start(bf16[48,1408]{1,0:T(8,128)(2,1)S(1)} %get-tuple-element.58.refs_0_), channel_id=1, source_target_pairs={{0,4},{4,8},{8,12},{12,16},{16,20},{20,24},{24,28},{28,0},{1,5},{5... | collective-permute-start | bytes 405512 | tf_op jit(solution)/shard_map/ppermute | solution.py:28
  95.8 12.7 %collective-permute-start.15 = (bf16[48,1408]{1,0:T(8,128)(2,1)S(1)}, bf16[48,1408]{1,0:T(8,128)(2,1)S(1)}, u32[]{:S(2)}, u32[]{:S(2)}) collective-permute-start(bf16[48,1408]{1,0:T(8,128)(2,1)S(1)} %get-tuple-element.58.refs_0_), channel_id=1, source_target_pairs={{0,28},{4,0},{8,4},{12,8},{16,12},{20,16},{24,20},{28,24},{1,29},{... | collective-permute-start | bytes 405512 | tf_op jit(solution)/shard_map/ppermute | solution.py:28
  99.3 9.3 %collective-permute-start.14 = (bf16[48,1408]{1,0:T(8,128)(2,1)S(1)}, bf16[48,1408]{1,0:T(8,128)(2,1)S(1)}, u32[]{:S(2)}, u32[]{:S(2)}) collective-permute-start(bf16[48,1408]{1,0:T(8,128)(2,1)S(1)} %collective-permute-done.13.refs_1_), channel_id=1, source_target_pairs={{0,4},{4,8},{8,12},{12,16},{16,20},{20,24},{24,28},{28,0},{1,5},{5... | collective-permute-start | bytes 405512 | tf_op jit(solution)/shard_map/ppermute | solution.py:28
  100.8 7.8 %collective-permute-start.16 = (bf16[48,1408]{1,0:T(8,128)(2,1)S(1)}, bf16[48,1408]{1,0:T(8,128)(2,1)S(1)}, u32[]{:S(2)}, u32[]{:S(2)}) collective-permute-start(bf16[48,1408]{1,0:T(8,128)(2,1)S(1)} %collective-permute-done.13.refs_1_), channel_id=1, source_target_pairs={{0,28},{4,0},{8,4},{12,8},{16,12},{20,16},{24,20},{28,24},{1,29},{... | collective-permute-start | bytes 405512 | tf_op jit(solution)/shard_map/ppermute | solution.py:28
  101.3 24.6 %all-to-all-start.1 = ((f32[32,16,128]{2,1,0:T(8,128)}), f32[32,16,128]{2,1,0:T(8,128)S(1)}, u32[]{:S(2)}, u32[]{:S(2)}) async-start(f32[32,16,128]{2,1,0:T(8,128)} %shard_map.56), calls=%async_computation.1 | async-start | bytes 524288 | tf_op jit(solution)/shard_map/all_to_all | solution.py:373
  108.6 13.4 %collective-permute-start.18 = (bf16[88,1408]{1,0:T(8,128)(2,1)S(1)}, bf16[88,1408]{1,0:T(8,128)(2,1)S(1)}, u32[]{:S(2)}, u32[]{:S(2)}) collective-permute-start(bf16[88,1408]{1,0:T(8,128)(2,1)S(1)} %get-tuple-element.62.refs_2_), channel_id=1, source_target_pairs={{0,28},{4,0},{8,4},{12,8},{16,12},{20,16},{24,20},{28,24},{1,29},{... | collective-permute-start | bytes 743432 | tf_op jit(solution)/shard_map/ppermute | solution.py:28
  108.9 13.1 %collective-permute-start.17 = (bf16[88,1408]{1,0:T(8,128)(2,1)S(1)}, bf16[88,1408]{1,0:T(8,128)(2,1)S(1)}, u32[]{:S(2)}, u32[]{:S(2)}) collective-permute-start(bf16[88,1408]{1,0:T(8,128)(2,1)S(1)} %get-tuple-element.61.refs_4_), channel_id=1, source_target_pairs={{0,4},{4,8},{8,12},{12,16},{16,20},{20,24},{24,28},{28,0},{1,5},{5... | collective-permute-start | bytes 743432 | tf_op jit(solution)/shard_map/ppermute | solution.py:28
  110.8 11.8 %collective-permute-start.19 = (bf16[88,1408]{1,0:T(8,128)(2,1)S(1)}, bf16[88,1408]{1,0:T(8,128)(2,1)S(1)}, u32[]{:S(2)}, u32[]{:S(2)}) collective-permute-start(bf16[88,1408]{1,0:T(8,128)(2,1)S(1)} %shard_map.58.refs_0_), channel_id=1, source_target_pairs={{0,1},{1,0},{2,3},{3,2},{4,5},{5,4},{6,7},{7,6},{8,9},{9,8},{10,11... | collective-permute-start | bytes 743432 | tf_op jit(solution)/shard_map/ppermute | solution.py:23
  110.9 11.7 %collective-permute-start.20 = (bf16[88,1408]{1,0:T(8,128)(2,1)S(1)}, bf16[88,1408]{1,0:T(8,128)(2,1)S(1)}, u32[]{:S(2)}, u32[]{:S(2)}) collective-permute-start(bf16[88,1408]{1,0:T(8,128)(2,1)S(1)} %get-tuple-element.62.refs_2_), channel_id=1, source_target_pairs={{0,1},{1,0},{2,3},{3,2},{4,5},{5,4},{6,7},{7,6},{8,9},{9,8},{10,11... | collective-permute-start | bytes 743432 | tf_op jit(solution)/shard_map/ppermute | solution.py:23
  111.4 11.2 %collective-permute-start.21 = (bf16[88,1408]{1,0:T(8,128)(2,1)S(1)}, bf16[88,1408]{1,0:T(8,128)(2,1)S(1)}, u32[]{:S(2)}, u32[]{:S(2)}) collective-permute-start(bf16[88,1408]{1,0:T(8,128)(2,1)S(1)} %get-tuple-element.61.refs_4_), channel_id=1, source_target_pairs={{0,1},{1,0},{2,3},{3,2},{4,5},{5,4},{6,7},{7,6},{8,9},{9,8},{10,11... | collective-permute-start | bytes 743432 | tf_op jit(solution)/shard_map/ppermute | solution.py:23
  122.0 8.8 %collective-permute-start.26 = (bf16[88,1408]{1,0:T(8,128)(2,1)S(1)}, bf16[88,1408]{1,0:T(8,128)(2,1)S(1)}, u32[]{:S(2)}, u32[]{:S(2)}) collective-permute-start(bf16[88,1408]{1,0:T(8,128)(2,1)S(1)} %collective-permute-done.18.down_ref.refs_6_), channel_id=1, source_target_pairs={{0,1},{1,0},{2,3},{3,2},{4,5},{5,4},{6,7},{7,6},{8,9},{9,8},{10,11... | collective-permute-start | bytes 743432 | tf_op jit(solution)/shard_map/ppermute | solution.py:23
  122.0 8.8 %collective-permute-start.27 = (bf16[88,1408]{1,0:T(8,128)(2,1)S(1)}, bf16[88,1408]{1,0:T(8,128)(2,1)S(1)}, u32[]{:S(2)}, u32[]{:S(2)}) collective-permute-start(bf16[88,1408]{1,0:T(8,128)(2,1)S(1)} %collective-permute-done.17.up_ref.refs_8_), channel_id=1, source_target_pairs={{0,1},{1,0},{2,3},{3,2},{4,5},{5,4},{6,7},{7,6},{8,9},{9,8},{10,11... | collective-permute-start | bytes 743432 | tf_op jit(solution)/shard_map/ppermute | solution.py:23
  122.5 17.4 %collective-permute-start.22 = (bf16[88,1408]{1,0:T(8,128)(2,1)S(1)}, bf16[88,1408]{1,0:T(8,128)(2,1)S(1)}, u32[]{:S(2)}, u32[]{:S(2)}) collective-permute-start(bf16[88,1408]{1,0:T(8,128)(2,1)S(1)} %collective-permute-done.18.down_ref.refs_6_), channel_id=1, source_target_pairs={{0,28},{4,0},{8,4},{12,8},{16,12},{20,16},{24,20},{28,24},{1,29},{... | collective-permute-start | bytes 743432 | tf_op jit(solution)/shard_map/ppermute | solution.py:28
  124.0 16.0 %collective-permute-start.23 = (bf16[88,1408]{1,0:T(8,128)(2,1)S(1)}, bf16[88,1408]{1,0:T(8,128)(2,1)S(1)}, u32[]{:S(2)}, u32[]{:S(2)}) collective-permute-start(bf16[88,1408]{1,0:T(8,128)(2,1)S(1)} %collective-permute-done.17.up_ref.refs_8_), channel_id=1, source_target_pairs={{0,4},{4,8},{8,12},{12,16},{16,20},{20,24},{24,28},{28,0},{1,5},{5... | collective-permute-start | bytes 743432 | tf_op jit(solution)/shard_map/ppermute | solution.py:28
  126.0 14.0 %collective-permute-start.24 = (bf16[48,1408]{1,0:T(8,128)(2,1)}, bf16[48,1408]{1,0:T(8,128)(2,1)S(1)}, u32[]{:S(2)}, u32[]{:S(2)}) collective-permute-start(bf16[48,1408]{1,0:T(8,128)(2,1)} %copy-done.4), channel_id=1, source_target_pairs={{0,8},{4,12},{8,16},{12,20},{16,24},{20,28},{24,0},{28,4},{1,9},{5... | collective-permute-start | bytes 405512 | tf_op jit(solution)/shard_map/ppermute | solution.py:28
  130.8 7.9 %collective-permute-start.25 = (bf16[40,1408]{1,0:T(8,128)(2,1)}, bf16[40,1408]{1,0:T(8,128)(2,1)S(1)}, u32[]{:S(2)}, u32[]{:S(2)}) collective-permute-start(bf16[40,1408]{1,0:T(8,128)(2,1)} %copy-done.5), channel_id=1, source_target_pairs={{0,24},{4,28},{8,0},{12,4},{16,8},{20,12},{24,16},{28,20},{1,25},{... | collective-permute-start | bytes 337928 | tf_op jit(solution)/shard_map/ppermute | solution.py:28
  140.0 2.2 %collective-permute-start.28 = (bf16[88,1408]{1,0:T(8,128)(2,1)S(1)}, bf16[88,1408]{1,0:T(8,128)(2,1)S(1)}, u32[]{:S(2)}, u32[]{:S(2)}) collective-permute-start(bf16[88,1408]{1,0:T(8,128)(2,1)S(1)} %collective-permute-done.22.refs_0_), channel_id=1, source_target_pairs={{0,1},{1,0},{2,3},{3,2},{4,5},{5,4},{6,7},{7,6},{8,9},{9,8},{10,11... | collective-permute-start | bytes 743432 | tf_op jit(solution)/shard_map/ppermute | solution.py:23
  140.0 2.2 %collective-permute-start.29 = (bf16[88,1408]{1,0:T(8,128)(2,1)S(1)}, bf16[88,1408]{1,0:T(8,128)(2,1)S(1)}, u32[]{:S(2)}, u32[]{:S(2)}) collective-permute-start(bf16[88,1408]{1,0:T(8,128)(2,1)S(1)} %collective-permute-done.23.refs_2_), channel_id=1, source_target_pairs={{0,1},{1,0},{2,3},{3,2},{4,5},{5,4},{6,7},{7,6},{8,9},{9,8},{10,11... | collective-permute-start | bytes 743432 | tf_op jit(solution)/shard_map/ppermute | solution.py:23
  140.5 1.7 %collective-permute-start.30 = (bf16[48,1408]{1,0:T(8,128)(2,1)S(1)}, bf16[48,1408]{1,0:T(8,128)(2,1)S(1)}, u32[]{:S(2)}, u32[]{:S(2)}) collective-permute-start(bf16[48,1408]{1,0:T(8,128)(2,1)S(1)} %collective-permute-done.24.refs_4_), channel_id=1, source_target_pairs={{0,1},{1,0},{2,3},{3,2},{4,5},{5,4},{6,7},{7,6},{8,9},{9,8},{10,11... | collective-permute-start | bytes 405512 | tf_op jit(solution)/shard_map/ppermute | solution.py:23
  (8 other events, 21.8 us)

commit v11 on v10

--- a/solution.py
+++ b/solution.py
@@ -187,9 +187,9 @@
         refs[2 * count + n][...] = jnp.concatenate([first[:width], second[:width]], axis=0)
 
 
-def halves_kernel(up_ref, down_ref, first_ref, second_ref):
+def halves_kernel(up_ref, down_ref, after_ref, first_ref, second_ref):
     first_ref[...] = up_ref[: first_ref.shape[0]]
-    second_ref[...] = down_ref[first_ref.shape[0] :]
+    second_ref[...] = down_ref[down_ref.shape[0] - second_ref.shape[0] :]
 
 
 def natural(c, yh, near, far):
@@ -221,7 +221,7 @@
         for slot in range(2):
             piece = pieces.pop(0)[...]
             if piece.shape[0] < rows:
-                piece = jnp.concatenate([piece, pieces.pop(0)[...]], axis=0)
+                piece = jnp.concatenate([piece, pieces.pop(0)[2 * piece.shape[0] - rows :]], axis=0)
             term = jnp.dot(tilde_t_ref[at, slot], piece, preferred_element_type=F32)
             total = term if total is None else total + term
             sides.append(dot_nt(tilde, piece))
@@ -262,15 +262,33 @@
 
 
 def late_kernel(steps, nz, where_ref, total_ref, blocks_ref, tilde_ref, tilde_t_ref, *refs):
-    pieces, out_ref = refs[:-1], refs[-1]
-    slab = total_ref.shape[1] // nz
+    pieces, out_ref, sums_ref = refs[:-2], refs[-2], refs[-1]
+    padded, nvir = total_ref.shape
+    slab = nvir // nz
+    lanes = out_ref.shape[2]
+    gap = jnp.zeros((padded // 2, 3 * lanes - 2 * slab), F32)
     for k in range(nz):
-        out_ref[k] = blocks_ref[k]
+        sums_ref[k] = blocks_ref[k]
     total = density_pieces(
-        steps, nz, where_ref, tilde_ref[...], tilde_t_ref, pieces, total_ref[...], out_ref
+        steps, nz, where_ref, tilde_ref[...], tilde_t_ref, pieces, total_ref[...], sums_ref
     )
     for k in range(nz):
-        out_ref[k] += total[:, k * slab : (k + 1) * slab]
+        block = sums_ref[k] + total[:, k * slab : (k + 1) * slab]
+        out_ref[k, :padded] = block[:, :lanes]
+        rest = block[:, lanes:]
+        out_ref[k, padded:] = jnp.concatenate([rest[: padded // 2], rest[padded // 2 :], gap], axis=1)
+
+
+def sum_kernel(parts_ref, out_ref):
+    width, slab = out_ref.shape
+    total = parts_ref[0]
+    for k in range(1, parts_ref.shape[0]):
+        total = total + parts_ref[k]
+    rows, lanes = total.shape[0] * 2 // 3, total.shape[1]
+    rest = total[rows:]
+    extra = slab - lanes
+    rest = jnp.concatenate([rest[:, :extra], rest[:, extra : 2 * extra]], axis=0)
+    out_ref[...] = jnp.concatenate([total[:rows], rest], axis=1)[:width]
 
 
 def local(orbital_b, pair_list, eps_occ, eps_vir):
@@ -391,12 +409,11 @@
     up, down, far = lax.optimization_barrier((up, down, far))
     half_up, half_down = pl.pallas_call(
         halves_kernel,
-        out_shape=(rows16, jax.ShapeDtypeStruct((2 * width - padded, nvir), BF16)),
-        in_specs=[VMEM, VMEM],
+        out_shape=(rows16, rows16),
+        in_specs=[VMEM, VMEM, pl.BlockSpec(memory_space=pl.ANY)],
         out_specs=(VMEM, VMEM),
         compiler_params=params(8),
-    )(up, down)
-    half_up, half_down, columns = lax.optimization_barrier((half_up, half_down, columns))
+    )(up, down, columns)
     last = (shift(down, "z", -1), shift(up, "z", 1), shift(half_up, "z", 2), shift(half_down, "z", -2))
 
     soon = (0, 1, nz - 1, 2, nz - 2)
@@ -420,9 +437,10 @@
     last, state = lax.optimization_barrier((last, state))
     added = pl.pallas_call(
         functools.partial(late_kernel, late, nz),
-        out_shape=jax.ShapeDtypeStruct((nz, padded, slab), F32),
+        out_shape=jax.ShapeDtypeStruct((nz, padded * 3 // 2, 128), F32),
         in_specs=[SMEM] + [VMEM] * (6 + 2 * len(late)),
         out_specs=VMEM,
+        scratch_shapes=[pltpu.VMEM((nz, padded, slab), F32)],
         compiler_params=params(16),
         cost_estimate=cost(len(late) * 8 * padded * padded * nvir, len(late) * 8 * padded * nvir),
     )(
@@ -438,7 +456,13 @@
         swap(last[3], "c"),
     )
     added = lax.all_to_all(added, SLABS, split_axis=0, concat_axis=0, tiled=True)
-    return jnp.sum(added, axis=0)[:width]
+    return pl.pallas_call(
+        sum_kernel,
+        out_shape=jax.ShapeDtypeStruct((width, slab), F32),
+        in_specs=[VMEM],
+        out_specs=VMEM,
+        compiler_params=params(8),
+    )(added)
 
 
 def solution(mesh):

time: 156 us -> 156 us (level)
    unnamed x14 -> x10, local copies, waits for them, and re-layouts: 3.6 us -> 2.3 us
where the time goes in v11:
time: 156 us; the launch traced here: 155 us
  blocking collectives  52.9 us (34%)
  waiting for transfers between devices  43.6 us (28%)
  starting transfers between devices  36.8 us (24%)
  Pallas kernels  19.5 us (12%)
  local copies, waits for them, and re-layouts  2.39 us (2%)
    all_to_all x1, blocking collectives, local(): lax.all_to_all(ours, ('yh', 'x', 'yl'), split_axis=0, concat_axis=0, tile...  42.1 us
    ppermute x20, waiting for transfers between devices, shift(): lax.ppermute(value, axis, [(i, (i + step) % size) for i in range(size)])  37.7 us
    ppermute x20, starting transfers between devices, shift(): lax.ppermute(value, axis, [(i, (i + step) % size) for i in range(size)])  25.6 us
    all_to_all x1, blocking collectives, local(): lax.all_to_all(added, SLABS, split_axis=0, concat_axis=0, tiled=True)  10.8 us
    all_to_all x1, starting transfers between devices, local(): lax.all_to_all(columns, ('z', 'yh', 'c'), split_axis=0, concat_axis=0, ti...  7.21 us
    ppermute x12, waiting for transfers between devices, swap(): return lax.ppermute(value, axis, [(0, 1), (1, 0)])  5.86 us
    pallas_call x1, Pallas kernels, local(): pl.pallas_call(functools.partial(early_kernel, soon, nz), out_shape=(rows...  5.44 us
    ppermute x12, starting transfers between devices, swap(): return lax.ppermute(value, axis, [(0, 1), (1, 0)])  4.05 us
  transfers between devices with their start and end apart: 33, of which 15 were waited for; matrix products, arithmetic and copies ran while one was open for 0% of the time, Pallas kernels for 8%

profile of v11, /device:TPU:32, one launch (start us, length us, event | category | flops | bytes accessed | tf_op | source)
XLA Modules:
  0.0 155.4 jit_solution(5227342181603392366)
XLA Ops:
  0.1 1.6 %copy-done = bf16[16,176,300]{2,1,0:T(8,128)(2,1)S(1)} copy-done((bf16[16,176,300]{2,1,0:T(8,128)(2,1)S(1)}, bf16[16,176,300]{2,1,0:T(8,128)(2,1)}, u32[]{:S(2)}) %copy-start) | copy-done | bytes 1689624
  3.9 2.0 %collective-permute-done.taken_ref = bf16[8,184,300]{2,1,0:T(8,128)(2,1)S(1)} collective-permute-done((bf16[8,184,300]{2,1,0:T(8,128)(2,1)S(1)}, bf16[8,184,300]{2,1,0:T(8,128)(2,1)S(1)}, u32[]{:S(2)}, u32[]{:S(2)}) %collective-permute-start) | collective-permute-done | bytes 883232 | tf_op jit(solution)/shard_map/ppermute | solution.py:23
  5.9 1.2 shard_map.48
  7.1 42.1 %all_to_all.15.near_ref = bf16[16,136,600]{2,1,0:T(8,128)(2,1)S(1)} all-to-all(bf16[16,136,600]{2,1,0:T(8,128)(2,1)S(1)} %shard_map.48), channel_id=1, replica_groups=mesh['x'=4,'yl'=2,'z'=8,'yh'=2,'c'=2] {'yh','x','yl'}, dimensions={0} | all-to-all | bytes 5222400 | tf_op jit(solution)/shard_map/all_to_all | solution.py:330
  49.3 1.6 %shard_map.49 = (f32[8,48,704]{2,1,0:T(8,128)S(1)}, f32[24,704]{1,0:T(8,128)S(1)}, f32[24,704]{1,0:T(8,128)S(1)}) custom-call(s32[7]{0:T(128)S(1)} %stack.27.where_ref, bf16[16,136,600]{2,1,0:T(8,128)(2,1)S(1)} %all_to_all.15.near_ref), custom_call_target="tpu_custom_call" | custom-call | flops 648806400 | tf_op jit(solution)/shard_map/pallas_call | solution.py:337
  50.9 2.0 %collective-permute-start.2 = (f32[24,704]{1,0:T(8,128)S(1)}, f32[24,704]{1,0:T(8,128)S(1)}, u32[]{:S(2)}, u32[]{:S(2)}) collective-permute-start(f32[24,704]{1,0:T(8,128)S(1)} %get-tuple-element.44), channel_id=1, source_target_pairs={{0,4},{4,8},{8,12},{12,16},{16,20},{20,24},{24,28},{28,0},{1,5},{5... | collective-permute-start | bytes 202760 | tf_op jit(solution)/shard_map/ppermute | solution.py:28
  53.0 1.4 collective-permute-done.1.far_ref
  55.6 2.0 %collective-permute-start.4 = (f32[24,704]{1,0:T(8,128)S(1)}, f32[24,704]{1,0:T(8,128)S(1)}, u32[]{:S(2)}, u32[]{:S(2)}) collective-permute-start(f32[24,704]{1,0:T(8,128)S(1)} %get-tuple-element.46), channel_id=1, source_target_pairs={{0,4},{4,8},{8,12},{12,16},{16,20},{20,24},{24,28},{28,0},{1,5},{5... | collective-permute-start | bytes 202760 | tf_op jit(solution)/shard_map/ppermute | solution.py:28
  58.5 1.7 %shard_map.50 = (f32[8,48,1408]{2,1,0:T(8,128)S(1)}, f32[48,1408]{1,0:T(8,128)S(1)}) custom-call(s32[7]{0:T(128)S(1)} %stack.27.where_ref, s32[2,8]{1,0:T(2,128)S(1)} %bitcast.9, f32[16]{0:T(128)S(1)} %copy-done.3, f32[1,1408]{1,0:T(1,128)S(1)} %broadcast_in_dim.3.vir_ref, f32[8,48,704]{2,1,0:T(8,128)S(1)} %get-tuple-element.42.near_part_ref, ...), custom_call_target="tpu_custom_call" | custom-call | flops 648806400 | tf_op jit(solution)/shard_map/pallas_call | solution.py:355
  62.6 3.1 %collective-permute-start.6 = (f32[48,1408]{1,0:T(8,128)S(1)}, f32[48,1408]{1,0:T(8,128)S(1)}, u32[]{:S(2)}, u32[]{:S(2)}) collective-permute-start(f32[48,1408]{1,0:T(8,128)S(1)} %get-tuple-element.48), channel_id=1, source_target_pairs={{0,4},{4,8},{8,12},{12,16},{16,20},{20,24},{24,28},{28,0},{1,5},{5... | collective-permute-start | bytes 811016 | tf_op jit(solution)/shard_map/ppermute | solution.py:28
  65.7 5.5 %collective-permute-done.6.refs_0_ = f32[48,1408]{1,0:T(8,128)S(1)} collective-permute-done((f32[48,1408]{1,0:T(8,128)S(1)}, f32[48,1408]{1,0:T(8,128)S(1)}, u32[]{:S(2)}, u32[]{:S(2)}) %collective-permute-start.6) | collective-permute-done | bytes 270368 | tf_op jit(solution)/shard_map/ppermute | solution.py:28
  71.2 2.8 %collective-permute-done.7.refs_1_ = f32[48,1408]{1,0:T(8,128)S(1)} collective-permute-done((f32[48,1408]{1,0:T(8,128)S(1)}, f32[48,1408]{1,0:T(8,128)S(1)}, u32[]{:S(2)}, u32[]{:S(2)}) %collective-permute-start.7) | collective-permute-done | bytes 270368 | tf_op jit(solution)/shard_map/ppermute | solution.py:28
  74.6 1.8 %collective-permute-start.8 = (f32[48,1408]{1,0:T(8,128)S(1)}, f32[48,1408]{1,0:T(8,128)S(1)}, u32[]{:S(2)}, u32[]{:S(2)}) collective-permute-start(f32[48,1408]{1,0:T(8,128)S(1)} %get-tuple-element.50), channel_id=1, source_target_pairs={{0,4},{4,8},{8,12},{12,16},{16,20},{20,24},{24,28},{28,0},{1,5},{5... | collective-permute-start | bytes 811016 | tf_op jit(solution)/shard_map/ppermute | solution.py:28
  76.7 4.4 %collective-permute-done.8.refs_0_ = f32[48,1408]{1,0:T(8,128)S(1)} collective-permute-done((f32[48,1408]{1,0:T(8,128)S(1)}, f32[48,1408]{1,0:T(8,128)S(1)}, u32[]{:S(2)}, u32[]{:S(2)}) %collective-permute-start.8) | collective-permute-done | bytes 270368 | tf_op jit(solution)/shard_map/ppermute | solution.py:28
  81.1 1.7 %collective-permute-done.9.refs_1_ = f32[48,1408]{1,0:T(8,128)S(1)} collective-permute-done((f32[48,1408]{1,0:T(8,128)S(1)}, f32[48,1408]{1,0:T(8,128)S(1)}, u32[]{:S(2)}, u32[]{:S(2)}) %collective-permute-start.9) | collective-permute-done | bytes 270368 | tf_op jit(solution)/shard_map/ppermute | solution.py:28
  83.5 1.8 %collective-permute-start.10 = (f32[48,1408]{1,0:T(8,128)S(1)}, f32[48,1408]{1,0:T(8,128)S(1)}, u32[]{:S(2)}, u32[]{:S(2)}) collective-permute-start(f32[48,1408]{1,0:T(8,128)S(1)} %get-tuple-element.52), channel_id=1, source_target_pairs={{0,4},{4,8},{8,12},{12,16},{16,20},{20,24},{24,28},{28,0},{1,5},{5... | collective-permute-start | bytes 811016 | tf_op jit(solution)/shard_map/ppermute | solution.py:28
  85.8 4.4 %collective-permute-done.10.up_in = f32[48,1408]{1,0:T(8,128)S(1)} collective-permute-done((f32[48,1408]{1,0:T(8,128)S(1)}, f32[48,1408]{1,0:T(8,128)S(1)}, u32[]{:S(2)}, u32[]{:S(2)}) %collective-permute-start.10) | collective-permute-done | bytes 270368 | tf_op jit(solution)/shard_map/ppermute | solution.py:28
  90.2 1.6 %collective-permute-done.11.down_in = f32[48,1408]{1,0:T(8,128)S(1)} collective-permute-done((f32[48,1408]{1,0:T(8,128)S(1)}, f32[48,1408]{1,0:T(8,128)S(1)}, u32[]{:S(2)}, u32[]{:S(2)}) %collective-permute-start.11) | collective-permute-done | bytes 270368 | tf_op jit(solution)/shard_map/ppermute | solution.py:28
  92.7 1.7 %collective-permute-start.13 = (bf16[48,1408]{1,0:T(8,128)(2,1)S(1)}, bf16[48,1408]{1,0:T(8,128)(2,1)S(1)}, u32[]{:S(2)}, u32[]{:S(2)}) collective-permute-start(bf16[48,1408]{1,0:T(8,128)(2,1)S(1)} %get-tuple-element.55.refs_0_), channel_id=1, source_target_pairs={{0,2},{2,0},{1,3},{3,1},{4,6},{6,4},{5,7},{7,5},{8,10},{10,8},{9,1... | collective-permute-start | bytes 405512 | tf_op jit(solution)/shard_map/ppermute | solution.py:23
  94.3 1.5 collective-permute-start.12
  96.4 1.7 %shard_map.56 = f32[32,16,128]{2,1,0:T(8,128)} custom-call(f32[48,1408]{1,0:T(8,128)S(1)} %get-tuple-element.56.rows_ref), custom_call_target="tpu_custom_call" | custom-call | tf_op jit(solution)/shard_map/pallas_call | solution.py:383
  98.1 1.2 collective-permute-done.13.refs_1_
  99.3 1.5 collective-permute-start.14
  101.3 7.2 %all-to-all-start.1 = ((f32[32,16,128]{2,1,0:T(8,128)}), f32[32,16,128]{2,1,0:T(8,128)S(1)}, u32[]{:S(2)}, u32[]{:S(2)}) async-start(f32[32,16,128]{2,1,0:T(8,128)} %shard_map.56), calls=%async_computation.1 | async-start | bytes 524288 | tf_op jit(solution)/shard_map/all_to_all | solution.py:391
  108.9 1.8 %collective-permute-start.17 = (bf16[88,1408]{1,0:T(8,128)(2,1)S(1)}, bf16[88,1408]{1,0:T(8,128)(2,1)S(1)}, u32[]{:S(2)}, u32[]{:S(2)}) collective-permute-start(bf16[88,1408]{1,0:T(8,128)(2,1)S(1)} %get-tuple-element.58.refs_4_), channel_id=1, source_target_pairs={{0,4},{4,8},{8,12},{12,16},{16,20},{20,24},{24,28},{28,0},{1,5},{5... | collective-permute-start | bytes 743432 | tf_op jit(solution)/shard_map/ppermute | solution.py:28
  111.5 10.5 %collective-permute-done.18.down_ref.refs_6_ = bf16[88,1408]{1,0:T(8,128)(2,1)S(1)} collective-permute-done((bf16[88,1408]{1,0:T(8,128)(2,1)S(1)}, bf16[88,1408]{1,0:T(8,128)(2,1)S(1)}, u32[]{:S(2)}, u32[]{:S(2)}) %collective-permute-start.18) | collective-permute-done | bytes 247840 | tf_op jit(solution)/shard_map/ppermute | solution.py:28
  122.5 1.4 collective-permute-start.22
  124.7 4.9 %collective-permute-start.24 = (bf16[48,1408]{1,0:T(8,128)(2,1)S(1)}, bf16[48,1408]{1,0:T(8,128)(2,1)S(1)}, u32[]{:S(2)}, u32[]{:S(2)}) collective-permute-start(bf16[48,1408]{1,0:T(8,128)(2,1)S(1)} %get-tuple-element.62), channel_id=1, source_target_pairs={{0,8},{4,12},{8,16},{12,20},{16,24},{20,28},{24,0},{28,4},{1,9},{5... | collective-permute-start | bytes 405512 | tf_op jit(solution)/shard_map/ppermute | solution.py:28
  129.5 5.4 %shard_map.60 = (f32[48,1408]{1,0:T(8,128)S(1)}, f32[8,48,176]{2,1,0:T(8,128)S(1)}, bf16[48,1408]{1,0:T(8,128)(2,1)S(1)}, bf16[8,2,48,88]{3,2,1,0:T(8,128)(2,1)S(1)}) custom-call(s32[7]{0:T(128)S(1)} %stack.27.where_ref, f32[48,1408]{1,0:T(8,128)S(1)} %get-tuple-element.56.rows_ref, f32[32,16,128]{2,1,0:T(8,128)S(1)} %all-to-all-done.1.after_ref.columns_ref, ...), custom_call_target="tpu_custom_call" | custom-call | flops 129761280 | bytes 2703360 | tf_op jit(solution)/shard_map/pallas_call | solution.py:424
  135.0 5.0 %collective-permute-done.24.refs_4_ = bf16[48,1408]{1,0:T(8,128)(2,1)S(1)} collective-permute-done((bf16[48,1408]{1,0:T(8,128)(2,1)S(1)}, bf16[48,1408]{1,0:T(8,128)(2,1)S(1)}, u32[]{:S(2)}, u32[]{:S(2)}) %collective-permute-start.24) | collective-permute-done | bytes 135200 | tf_op jit(solution)/shard_map/ppermute | solution.py:28
  142.3 1.7 %shard_map.61 = f32[8,72,128]{2,1,0:T(8,128)S(1)} custom-call(s32[7]{0:T(128)S(1)} %stack.27.where_ref, f32[48,1408]{1,0:T(8,128)S(1)} %get-tuple-element.71.total_ref, f32[8,48,176]{2,1,0:T(8,128)S(1)} %get-tuple-element.72.blocks_ref, bf16[48,1408]{1,0:T(8,128)(2,1)S(1)} %get-tuple-element.73.tilde_ref, ...), custom_call_target="tpu_custom_call" | custom-call | flops 77856768 | bytes 1622016 | tf_op jit(solution)/shard_map/pallas_call | solution.py:438
  144.0 10.8 %all_to_all.16.parts_ref = f32[8,72,128]{2,1,0:T(8,128)S(1)} all-to-all(f32[8,72,128]{2,1,0:T(8,128)S(1)} %shard_map.61), channel_id=1, replica_groups=mesh['x'=4,'yl'=2,'z'=8,'yh'=2,'c'=2] {'x','yl'}, dimensions={0} | all-to-all | bytes 589824 | tf_op jit(solution)/shard_map/all_to_all | solution.py:458
  (65 shorter events, 16.0 us)
Async XLA Ops:
  3.1 2.9 %collective-permute-start = (bf16[8,184,300]{2,1,0:T(8,128)(2,1)S(1)}, bf16[8,184,300]{2,1,0:T(8,128)(2,1)S(1)}, u32[]{:S(2)}, u32[]{:S(2)}) collective-permute-start(bf16[8,184,300]{2,1,0:T(8,128)(2,1)S(1)} %shard_map.46), channel_id=1, source_target_pairs={{0,1},{1,0},{2,3},{3,2},{4,5},{5,4},{6,7},{7,6},{8,9},{9,8},{10,11... | collective-permute-start | bytes 2649608 | tf_op jit(solution)/shard_map/ppermute | solution.py:23
  49.3 5.1 %collective-permute-start.1 = (bf16[16,136,600]{2,1,0:T(8,128)(2,1)S(1)}, bf16[16,136,600]{2,1,0:T(8,128)(2,1)S(1)}, u32[]{:S(2)}, u32[]{:S(2)}) collective-permute-start(bf16[16,136,600]{2,1,0:T(8,128)(2,1)S(1)} %all_to_all.15.near_ref), channel_id=1, source_target_pairs={{0,1},{1,0},{2,3},{3,2},{4,5},{5,4},{6,7},{7,6},{8,9},{9,8},{10,11... | collective-permute-start | bytes 7833608 | tf_op jit(solution)/shard_map/ppermute | solution.py:23
  50.9 9.3 %collective-permute-start.2 = (f32[24,704]{1,0:T(8,128)S(1)}, f32[24,704]{1,0:T(8,128)S(1)}, u32[]{:S(2)}, u32[]{:S(2)}) collective-permute-start(f32[24,704]{1,0:T(8,128)S(1)} %get-tuple-element.44), channel_id=1, source_target_pairs={{0,4},{4,8},{8,12},{12,16},{16,20},{20,24},{24,28},{28,0},{1,5},{5... | collective-permute-start | bytes 202760 | tf_op jit(solution)/shard_map/ppermute | solution.py:28
  52.9 7.3 %collective-permute-start.3 = (f32[24,704]{1,0:T(8,128)S(1)}, f32[24,704]{1,0:T(8,128)S(1)}, u32[]{:S(2)}, u32[]{:S(2)}) collective-permute-start(f32[24,704]{1,0:T(8,128)S(1)} %get-tuple-element.45), channel_id=1, source_target_pairs={{0,28},{4,0},{8,4},{12,8},{16,12},{20,16},{24,20},{28,24},{1,29},{... | collective-permute-start | bytes 202760 | tf_op jit(solution)/shard_map/ppermute | solution.py:28
  55.6 5.4 %collective-permute-start.4 = (f32[24,704]{1,0:T(8,128)S(1)}, f32[24,704]{1,0:T(8,128)S(1)}, u32[]{:S(2)}, u32[]{:S(2)}) collective-permute-start(f32[24,704]{1,0:T(8,128)S(1)} %get-tuple-element.46), channel_id=1, source_target_pairs={{0,4},{4,8},{8,12},{12,16},{16,20},{20,24},{24,28},{28,0},{1,5},{5... | collective-permute-start | bytes 202760 | tf_op jit(solution)/shard_map/ppermute | solution.py:28
  57.6 4.4 %collective-permute-start.5 = (f32[24,704]{1,0:T(8,128)S(1)}, f32[24,704]{1,0:T(8,128)S(1)}, u32[]{:S(2)}, u32[]{:S(2)}) collective-permute-start(f32[24,704]{1,0:T(8,128)S(1)} %get-tuple-element.47), channel_id=1, source_target_pairs={{0,28},{4,0},{8,4},{12,8},{16,12},{20,16},{24,20},{28,24},{1,29},{... | collective-permute-start | bytes 202760 | tf_op jit(solution)/shard_map/ppermute | solution.py:28
  62.6 8.6 %collective-permute-start.6 = (f32[48,1408]{1,0:T(8,128)S(1)}, f32[48,1408]{1,0:T(8,128)S(1)}, u32[]{:S(2)}, u32[]{:S(2)}) collective-permute-start(f32[48,1408]{1,0:T(8,128)S(1)} %get-tuple-element.48), channel_id=1, source_target_pairs={{0,4},{4,8},{8,12},{12,16},{16,20},{20,24},{24,28},{28,0},{1,5},{5... | collective-permute-start | bytes 811016 | tf_op jit(solution)/shard_map/ppermute | solution.py:28
  65.7 8.3 %collective-permute-start.7 = (f32[48,1408]{1,0:T(8,128)S(1)}, f32[48,1408]{1,0:T(8,128)S(1)}, u32[]{:S(2)}, u32[]{:S(2)}) collective-permute-start(f32[48,1408]{1,0:T(8,128)S(1)} %get-tuple-element.49), channel_id=1, source_target_pairs={{0,28},{4,0},{8,4},{12,8},{16,12},{20,16},{24,20},{28,24},{1,29},{... | collective-permute-start | bytes 811016 | tf_op jit(solution)/shard_map/ppermute | solution.py:28
  74.6 6.5 %collective-permute-start.8 = (f32[48,1408]{1,0:T(8,128)S(1)}, f32[48,1408]{1,0:T(8,128)S(1)}, u32[]{:S(2)}, u32[]{:S(2)}) collective-permute-start(f32[48,1408]{1,0:T(8,128)S(1)} %get-tuple-element.50), channel_id=1, source_target_pairs={{0,4},{4,8},{8,12},{12,16},{16,20},{20,24},{24,28},{28,0},{1,5},{5... | collective-permute-start | bytes 811016 | tf_op jit(solution)/shard_map/ppermute | solution.py:28
  76.4 6.5 %collective-permute-start.9 = (f32[48,1408]{1,0:T(8,128)S(1)}, f32[48,1408]{1,0:T(8,128)S(1)}, u32[]{:S(2)}, u32[]{:S(2)}) collective-permute-start(f32[48,1408]{1,0:T(8,128)S(1)} %get-tuple-element.51), channel_id=1, source_target_pairs={{0,28},{4,0},{8,4},{12,8},{16,12},{20,16},{24,20},{28,24},{1,29},{... | collective-permute-start | bytes 811016 | tf_op jit(solution)/shard_map/ppermute | solution.py:28
  83.5 6.7 %collective-permute-start.10 = (f32[48,1408]{1,0:T(8,128)S(1)}, f32[48,1408]{1,0:T(8,128)S(1)}, u32[]{:S(2)}, u32[]{:S(2)}) collective-permute-start(f32[48,1408]{1,0:T(8,128)S(1)} %get-tuple-element.52), channel_id=1, source_target_pairs={{0,4},{4,8},{8,12},{12,16},{16,20},{20,24},{24,28},{28,0},{1,5},{5... | collective-permute-start | bytes 811016 | tf_op jit(solution)/shard_map/ppermute | solution.py:28
  85.3 6.5 %collective-permute-start.11 = (f32[48,1408]{1,0:T(8,128)S(1)}, f32[48,1408]{1,0:T(8,128)S(1)}, u32[]{:S(2)}, u32[]{:S(2)}) collective-permute-start(f32[48,1408]{1,0:T(8,128)S(1)} %get-tuple-element.53), channel_id=1, source_target_pairs={{0,28},{4,0},{8,4},{12,8},{16,12},{20,16},{24,20},{28,24},{1,29},{... | collective-permute-start | bytes 811016 | tf_op jit(solution)/shard_map/ppermute | solution.py:28
  92.7 6.6 %collective-permute-start.13 = (bf16[48,1408]{1,0:T(8,128)(2,1)S(1)}, bf16[48,1408]{1,0:T(8,128)(2,1)S(1)}, u32[]{:S(2)}, u32[]{:S(2)}) collective-permute-start(bf16[48,1408]{1,0:T(8,128)(2,1)S(1)} %get-tuple-element.55.refs_0_), channel_id=1, source_target_pairs={{0,2},{2,0},{1,3},{3,1},{4,6},{6,4},{5,7},{7,5},{8,10},{10,8},{9,1... | collective-permute-start | bytes 405512 | tf_op jit(solution)/shard_map/ppermute | solution.py:23
  94.3 14.2 %collective-permute-start.12 = (bf16[48,1408]{1,0:T(8,128)(2,1)S(1)}, bf16[48,1408]{1,0:T(8,128)(2,1)S(1)}, u32[]{:S(2)}, u32[]{:S(2)}) collective-permute-start(bf16[48,1408]{1,0:T(8,128)(2,1)S(1)} %get-tuple-element.55.refs_0_), channel_id=1, source_target_pairs={{0,4},{4,8},{8,12},{12,16},{16,20},{20,24},{24,28},{28,0},{1,5},{5... | collective-permute-start | bytes 405512 | tf_op jit(solution)/shard_map/ppermute | solution.py:28
  95.8 12.7 %collective-permute-start.15 = (bf16[48,1408]{1,0:T(8,128)(2,1)S(1)}, bf16[48,1408]{1,0:T(8,128)(2,1)S(1)}, u32[]{:S(2)}, u32[]{:S(2)}) collective-permute-start(bf16[48,1408]{1,0:T(8,128)(2,1)S(1)} %get-tuple-element.55.refs_0_), channel_id=1, source_target_pairs={{0,28},{4,0},{8,4},{12,8},{16,12},{20,16},{24,20},{28,24},{1,29},{... | collective-permute-start | bytes 405512 | tf_op jit(solution)/shard_map/ppermute | solution.py:28
  99.3 9.3 %collective-permute-start.14 = (bf16[48,1408]{1,0:T(8,128)(2,1)S(1)}, bf16[48,1408]{1,0:T(8,128)(2,1)S(1)}, u32[]{:S(2)}, u32[]{:S(2)}) collective-permute-start(bf16[48,1408]{1,0:T(8,128)(2,1)S(1)} %collective-permute-done.13.refs_1_), channel_id=1, source_target_pairs={{0,4},{4,8},{8,12},{12,16},{16,20},{20,24},{24,28},{28,0},{1,5},{5... | collective-permute-start | bytes 405512 | tf_op jit(solution)/shard_map/ppermute | solution.py:28
  100.8 7.8 %collective-permute-start.16 = (bf16[48,1408]{1,0:T(8,128)(2,1)S(1)}, bf16[48,1408]{1,0:T(8,128)(2,1)S(1)}, u32[]{:S(2)}, u32[]{:S(2)}) collective-permute-start(bf16[48,1408]{1,0:T(8,128)(2,1)S(1)} %collective-permute-done.13.refs_1_), channel_id=1, source_target_pairs={{0,28},{4,0},{8,4},{12,8},{16,12},{20,16},{24,20},{28,24},{1,29},{... | collective-permute-start | bytes 405512 | tf_op jit(solution)/shard_map/ppermute | solution.py:28
  101.3 23.3 %all-to-all-start.1 = ((f32[32,16,128]{2,1,0:T(8,128)}), f32[32,16,128]{2,1,0:T(8,128)S(1)}, u32[]{:S(2)}, u32[]{:S(2)}) async-start(f32[32,16,128]{2,1,0:T(8,128)} %shard_map.56), calls=%async_computation.1 | async-start | bytes 524288 | tf_op jit(solution)/shard_map/all_to_all | solution.py:391
  108.6 13.4 %collective-permute-start.18 = (bf16[88,1408]{1,0:T(8,128)(2,1)S(1)}, bf16[88,1408]{1,0:T(8,128)(2,1)S(1)}, u32[]{:S(2)}, u32[]{:S(2)}) collective-permute-start(bf16[88,1408]{1,0:T(8,128)(2,1)S(1)} %get-tuple-element.59.refs_2_), channel_id=1, source_target_pairs={{0,28},{4,0},{8,4},{12,8},{16,12},{20,16},{24,20},{28,24},{1,29},{... | collective-permute-start | bytes 743432 | tf_op jit(solution)/shard_map/ppermute | solution.py:28
  108.9 13.1 %collective-permute-start.17 = (bf16[88,1408]{1,0:T(8,128)(2,1)S(1)}, bf16[88,1408]{1,0:T(8,128)(2,1)S(1)}, u32[]{:S(2)}, u32[]{:S(2)}) collective-permute-start(bf16[88,1408]{1,0:T(8,128)(2,1)S(1)} %get-tuple-element.58.refs_4_), channel_id=1, source_target_pairs={{0,4},{4,8},{8,12},{12,16},{16,20},{20,24},{24,28},{28,0},{1,5},{5... | collective-permute-start | bytes 743432 | tf_op jit(solution)/shard_map/ppermute | solution.py:28
  110.8 11.8 %collective-permute-start.19 = (bf16[88,1408]{1,0:T(8,128)(2,1)S(1)}, bf16[88,1408]{1,0:T(8,128)(2,1)S(1)}, u32[]{:S(2)}, u32[]{:S(2)}) collective-permute-start(bf16[88,1408]{1,0:T(8,128)(2,1)S(1)} %shard_map.58.refs_0_), channel_id=1, source_target_pairs={{0,1},{1,0},{2,3},{3,2},{4,5},{5,4},{6,7},{7,6},{8,9},{9,8},{10,11... | collective-permute-start | bytes 743432 | tf_op jit(solution)/shard_map/ppermute | solution.py:23
  110.9 11.7 %collective-permute-start.20 = (bf16[88,1408]{1,0:T(8,128)(2,1)S(1)}, bf16[88,1408]{1,0:T(8,128)(2,1)S(1)}, u32[]{:S(2)}, u32[]{:S(2)}) collective-permute-start(bf16[88,1408]{1,0:T(8,128)(2,1)S(1)} %get-tuple-element.59.refs_2_), channel_id=1, source_target_pairs={{0,1},{1,0},{2,3},{3,2},{4,5},{5,4},{6,7},{7,6},{8,9},{9,8},{10,11... | collective-permute-start | bytes 743432 | tf_op jit(solution)/shard_map/ppermute | solution.py:23
  111.4 11.2 %collective-permute-start.21 = (bf16[88,1408]{1,0:T(8,128)(2,1)S(1)}, bf16[88,1408]{1,0:T(8,128)(2,1)S(1)}, u32[]{:S(2)}, u32[]{:S(2)}) collective-permute-start(bf16[88,1408]{1,0:T(8,128)(2,1)S(1)} %get-tuple-element.58.refs_4_), channel_id=1, source_target_pairs={{0,1},{1,0},{2,3},{3,2},{4,5},{5,4},{6,7},{7,6},{8,9},{9,8},{10,11... | collective-permute-start | bytes 743432 | tf_op jit(solution)/shard_map/ppermute | solution.py:23
  122.0 7.5 %collective-permute-start.26 = (bf16[88,1408]{1,0:T(8,128)(2,1)S(1)}, bf16[88,1408]{1,0:T(8,128)(2,1)S(1)}, u32[]{:S(2)}, u32[]{:S(2)}) collective-permute-start(bf16[88,1408]{1,0:T(8,128)(2,1)S(1)} %collective-permute-done.18.down_ref.refs_6_), channel_id=1, source_target_pairs={{0,1},{1,0},{2,3},{3,2},{4,5},{5,4},{6,7},{7,6},{8,9},{9,8},{10,11... | collective-permute-start | bytes 743432 | tf_op jit(solution)/shard_map/ppermute | solution.py:23
  122.0 7.5 %collective-permute-start.27 = (bf16[88,1408]{1,0:T(8,128)(2,1)S(1)}, bf16[88,1408]{1,0:T(8,128)(2,1)S(1)}, u32[]{:S(2)}, u32[]{:S(2)}) collective-permute-start(bf16[88,1408]{1,0:T(8,128)(2,1)S(1)} %collective-permute-done.17.up_ref.refs_8_), channel_id=1, source_target_pairs={{0,1},{1,0},{2,3},{3,2},{4,5},{5,4},{6,7},{7,6},{8,9},{9,8},{10,11... | collective-permute-start | bytes 743432 | tf_op jit(solution)/shard_map/ppermute | solution.py:23
  122.5 17.4 %collective-permute-start.22 = (bf16[88,1408]{1,0:T(8,128)(2,1)S(1)}, bf16[88,1408]{1,0:T(8,128)(2,1)S(1)}, u32[]{:S(2)}, u32[]{:S(2)}) collective-permute-start(bf16[88,1408]{1,0:T(8,128)(2,1)S(1)} %collective-permute-done.18.down_ref.refs_6_), channel_id=1, source_target_pairs={{0,28},{4,0},{8,4},{12,8},{16,12},{20,16},{24,20},{28,24},{1,29},{... | collective-permute-start | bytes 743432 | tf_op jit(solution)/shard_map/ppermute | solution.py:28
  124.0 16.0 %collective-permute-start.23 = (bf16[88,1408]{1,0:T(8,128)(2,1)S(1)}, bf16[88,1408]{1,0:T(8,128)(2,1)S(1)}, u32[]{:S(2)}, u32[]{:S(2)}) collective-permute-start(bf16[88,1408]{1,0:T(8,128)(2,1)S(1)} %collective-permute-done.17.up_ref.refs_8_), channel_id=1, source_target_pairs={{0,4},{4,8},{8,12},{12,16},{16,20},{20,24},{24,28},{28,0},{1,5},{5... | collective-permute-start | bytes 743432 | tf_op jit(solution)/shard_map/ppermute | solution.py:28
  124.7 15.3 %collective-permute-start.24 = (bf16[48,1408]{1,0:T(8,128)(2,1)S(1)}, bf16[48,1408]{1,0:T(8,128)(2,1)S(1)}, u32[]{:S(2)}, u32[]{:S(2)}) collective-permute-start(bf16[48,1408]{1,0:T(8,128)(2,1)S(1)} %get-tuple-element.62), channel_id=1, source_target_pairs={{0,8},{4,12},{8,16},{12,20},{16,24},{20,28},{24,0},{28,4},{1,9},{5... | collective-permute-start | bytes 405512 | tf_op jit(solution)/shard_map/ppermute | solution.py:28
  129.5 10.4 %collective-permute-start.25 = (bf16[48,1408]{1,0:T(8,128)(2,1)S(1)}, bf16[48,1408]{1,0:T(8,128)(2,1)S(1)}, u32[]{:S(2)}, u32[]{:S(2)}) collective-permute-start(bf16[48,1408]{1,0:T(8,128)(2,1)S(1)} %get-tuple-element.63), channel_id=1, source_target_pairs={{0,24},{4,28},{8,0},{12,4},{16,8},{20,12},{24,16},{28,20},{1,25},{... | collective-permute-start | bytes 405512 | tf_op jit(solution)/shard_map/ppermute | solution.py:28
  140.0 2.3 %collective-permute-start.28 = (bf16[88,1408]{1,0:T(8,128)(2,1)S(1)}, bf16[88,1408]{1,0:T(8,128)(2,1)S(1)}, u32[]{:S(2)}, u32[]{:S(2)}) collective-permute-start(bf16[88,1408]{1,0:T(8,128)(2,1)S(1)} %collective-permute-done.22.refs_0_), channel_id=1, source_target_pairs={{0,1},{1,0},{2,3},{3,2},{4,5},{5,4},{6,7},{7,6},{8,9},{9,8},{10,11... | collective-permute-start | bytes 743432 | tf_op jit(solution)/shard_map/ppermute | solution.py:23
  140.1 2.2 %collective-permute-start.29 = (bf16[88,1408]{1,0:T(8,128)(2,1)S(1)}, bf16[88,1408]{1,0:T(8,128)(2,1)S(1)}, u32[]{:S(2)}, u32[]{:S(2)}) collective-permute-start(bf16[88,1408]{1,0:T(8,128)(2,1)S(1)} %collective-permute-done.23.refs_2_), channel_id=1, source_target_pairs={{0,1},{1,0},{2,3},{3,2},{4,5},{5,4},{6,7},{7,6},{8,9},{9,8},{10,11... | collective-permute-start | bytes 743432 | tf_op jit(solution)/shard_map/ppermute | solution.py:23
  140.7 1.6 %collective-permute-start.31 = (bf16[48,1408]{1,0:T(8,128)(2,1)S(1)}, bf16[48,1408]{1,0:T(8,128)(2,1)S(1)}, u32[]{:S(2)}, u32[]{:S(2)}) collective-permute-start(bf16[48,1408]{1,0:T(8,128)(2,1)S(1)} %collective-permute-done.25.refs_5_), channel_id=1, source_target_pairs={{0,1},{1,0},{2,3},{3,2},{4,5},{5,4},{6,7},{7,6},{8,9},{9,8},{10,11... | collective-permute-start | bytes 405512 | tf_op jit(solution)/shard_map/ppermute | solution.py:23
  (6 other events, 20.4 us)

commit v12 on v11

--- a/solution.py
+++ b/solution.py
@@ -89,12 +89,12 @@
                     out_ref[y * groups + p, padded:, lanes] = taken_ref[p, 2 * padded :]
 
 
-def half_product(left, right_ref, padded):
+def half_product(left, right_ref, start):
     sources = right_ref.shape[0]
     half = sources // 2
     total = None
     for y in range(2):
-        right = jnp.concatenate([right_ref[half * y + k, padded:, :] for k in range(half)], axis=0)
+        right = jnp.concatenate([right_ref[half * y + k, start:, :] for k in range(half)], axis=0)
         term = dot_nt(left(y), right)
         total = term if total is None else total + term
     return total
@@ -120,13 +120,13 @@
 def first_kernel(padded, nz, where_ref, near_ref, far_ref, up_ref, down_ref):
     half, cut = near_ref.shape[0] // 2, padded // 2
     at = lax.rem(where_ref[0] + nz // 2, nz)
-    across = half_product(lambda y: near_ref[half * y + at, :padded, :], far_ref, padded)
+    across = half_product(lambda y: near_ref[half * y + at, :padded, :], far_ref, 0)
     up_ref[...] = across[:cut]
     down_ref[...] = across[cut:]
 
 
 def rest_kernel(padded, where_ref, pair_ref, occ_ref, vir_ref, near_part_ref, near_ref, far_ref, out_ref, denom_ref):
-    total = half_product(all_rows(near_ref, padded), far_ref, padded).reshape(near_part_ref.shape)
+    total = half_product(all_rows(near_ref, padded), far_ref, 0).reshape(near_part_ref.shape)
     for k in range(near_part_ref.shape[0]):
         out_ref[k] = jnp.concatenate([near_part_ref[k], total[k]], axis=1)
     chunk, group, width = where_ref[2], where_ref[3], where_ref[5]
@@ -328,7 +328,7 @@
         compiler_params=params(8),
     )(where, taken, ours)
     near = lax.all_to_all(ours, ("yh", "x", "yl"), split_axis=0, concat_axis=0, tiled=True)
-    far = swap(near, "c")
+    far = swap(near[:, padded:], "c")
 
     whole = jax.ShapeDtypeStruct((8, padded, nvir), F32)
     rows = jax.ShapeDtypeStruct((padded, nvir), F32)

time: 156 us -> 156 us (level)
  waiting for transfers between devices: 43.6 us -> 41.6 us
  starting transfers between devices: 36.8 us -> 38.5 us
  transfers between devices with their start and end apart: 33 -> 33, of which waited for: 15 -> 14; matrix products, arithmetic and copies ran while one was open for 0% -> 0% of each run, Pallas kernels for 8% -> 8%
where the time goes in v12:
time: 156 us; the launch traced here: 155 us
  blocking collectives  52.9 us (34%)
  waiting for transfers between devices  41.6 us (27%)
  starting transfers between devices  38.5 us (25%)
  Pallas kernels  19.5 us (12%)
  local copies, waits for them, and re-layouts  2.54 us (2%)
    all_to_all x1, blocking collectives, local(): lax.all_to_all(ours, ('yh', 'x', 'yl'), split_axis=0, concat_axis=0, tile...  42.1 us
    ppermute x20, waiting for transfers between devices, shift(): lax.ppermute(value, axis, [(i, (i + step) % size) for i in range(size)])  37.2 us
    ppermute x20, starting transfers between devices, shift(): lax.ppermute(value, axis, [(i, (i + step) % size) for i in range(size)])  27.1 us
    all_to_all x1, blocking collectives, local(): lax.all_to_all(added, SLABS, split_axis=0, concat_axis=0, tiled=True)  10.8 us
    all_to_all x1, starting transfers between devices, local(): lax.all_to_all(columns, ('z', 'yh', 'c'), split_axis=0, concat_axis=0, ti...  7.21 us
    pallas_call x1, Pallas kernels, local(): pl.pallas_call(functools.partial(early_kernel, soon, nz), out_shape=(rows...  5.44 us
    ppermute x12, waiting for transfers between devices, swap(): return lax.ppermute(value, axis, [(0, 1), (1, 0)])  4.47 us
    ppermute x12, starting transfers between devices, swap(): return lax.ppermute(value, axis, [(0, 1), (1, 0)])  4.14 us
  transfers between devices with their start and end apart: 33, of which 14 were waited for; matrix products, arithmetic and copies ran while one was open for 0% of the time, Pallas kernels for 8%

profile of v12, /device:TPU:32, one launch (start us, length us, event | category | flops | bytes accessed | tf_op | source)
XLA Modules:
  0.0 155.4 jit_solution(3965839565820511033)
XLA Ops:
  0.1 1.6 %copy-done = bf16[16,176,300]{2,1,0:T(8,128)(2,1)S(1)} copy-done((bf16[16,176,300]{2,1,0:T(8,128)(2,1)S(1)}, bf16[16,176,300]{2,1,0:T(8,128)(2,1)}, u32[]{:S(2)}) %copy-start) | copy-done | bytes 1689624
  3.9 2.0 %collective-permute-done.taken_ref = bf16[8,184,300]{2,1,0:T(8,128)(2,1)S(1)} collective-permute-done((bf16[8,184,300]{2,1,0:T(8,128)(2,1)S(1)}, bf16[8,184,300]{2,1,0:T(8,128)(2,1)S(1)}, u32[]{:S(2)}, u32[]{:S(2)}) %collective-permute-start) | collective-permute-done | bytes 883232 | tf_op jit(solution)/shard_map/ppermute | solution.py:23
  5.9 1.2 shard_map.48
  7.1 42.1 %all_to_all.15.near_ref = bf16[16,136,600]{2,1,0:T(8,128)(2,1)S(1)} all-to-all(bf16[16,136,600]{2,1,0:T(8,128)(2,1)S(1)} %shard_map.48), channel_id=1, replica_groups=mesh['x'=4,'yl'=2,'z'=8,'yh'=2,'c'=2] {'yh','x','yl'}, dimensions={0} | all-to-all | bytes 5222400 | tf_op jit(solution)/shard_map/all_to_all | solution.py:330
  49.5 1.6 %shard_map.49 = (f32[8,48,704]{2,1,0:T(8,128)S(1)}, f32[24,704]{1,0:T(8,128)S(1)}, f32[24,704]{1,0:T(8,128)S(1)}) custom-call(s32[7]{0:T(128)S(1)} %stack.27.where_ref, bf16[16,136,600]{2,1,0:T(8,128)(2,1)S(1)} %all_to_all.15.near_ref), custom_call_target="tpu_custom_call" | custom-call | flops 648806400 | tf_op jit(solution)/shard_map/pallas_call | solution.py:337
  51.2 2.0 %collective-permute-start.2 = (f32[24,704]{1,0:T(8,128)S(1)}, f32[24,704]{1,0:T(8,128)S(1)}, u32[]{:S(2)}, u32[]{:S(2)}) collective-permute-start(f32[24,704]{1,0:T(8,128)S(1)} %get-tuple-element.44), channel_id=1, source_target_pairs={{0,4},{4,8},{8,12},{12,16},{16,20},{20,24},{24,28},{28,0},{1,5},{5... | collective-permute-start | bytes 202760 | tf_op jit(solution)/shard_map/ppermute | solution.py:28
  54.5 2.0 %collective-permute-start.4 = (f32[24,704]{1,0:T(8,128)S(1)}, f32[24,704]{1,0:T(8,128)S(1)}, u32[]{:S(2)}, u32[]{:S(2)}) collective-permute-start(f32[24,704]{1,0:T(8,128)S(1)} %get-tuple-element.46), channel_id=1, source_target_pairs={{0,4},{4,8},{8,12},{12,16},{16,20},{20,24},{24,28},{28,0},{1,5},{5... | collective-permute-start | bytes 202760 | tf_op jit(solution)/shard_map/ppermute | solution.py:28
  56.5 2.2 %collective-permute-start.5 = (f32[24,704]{1,0:T(8,128)S(1)}, f32[24,704]{1,0:T(8,128)S(1)}, u32[]{:S(2)}, u32[]{:S(2)}) collective-permute-start(f32[24,704]{1,0:T(8,128)S(1)} %get-tuple-element.47), channel_id=1, source_target_pairs={{0,28},{4,0},{8,4},{12,8},{16,12},{20,16},{24,20},{28,24},{1,29},{... | collective-permute-start | bytes 202760 | tf_op jit(solution)/shard_map/ppermute | solution.py:28
  58.7 1.8 %shard_map.50 = (f32[8,48,1408]{2,1,0:T(8,128)S(1)}, f32[48,1408]{1,0:T(8,128)S(1)}) custom-call(s32[7]{0:T(128)S(1)} %stack.27.where_ref, s32[2,8]{1,0:T(2,128)S(1)} %bitcast.9, f32[16]{0:T(128)S(1)} %copy-done.3, f32[1,1408]{1,0:T(1,128)S(1)} %broadcast_in_dim.3.vir_ref, f32[8,48,704]{2,1,0:T(8,128)S(1)} %get-tuple-element.42.near_part_ref, ...), custom_call_target="tpu_custom_call" | custom-call | flops 648806400 | tf_op jit(solution)/shard_map/pallas_call | solution.py:355
  62.5 3.3 %collective-permute-start.6 = (f32[48,1408]{1,0:T(8,128)S(1)}, f32[48,1408]{1,0:T(8,128)S(1)}, u32[]{:S(2)}, u32[]{:S(2)}) collective-permute-start(f32[48,1408]{1,0:T(8,128)S(1)} %get-tuple-element.48), channel_id=1, source_target_pairs={{0,4},{4,8},{8,12},{12,16},{16,20},{20,24},{24,28},{28,0},{1,5},{5... | collective-permute-start | bytes 811016 | tf_op jit(solution)/shard_map/ppermute | solution.py:28
  65.8 5.2 %collective-permute-done.6.refs_0_ = f32[48,1408]{1,0:T(8,128)S(1)} collective-permute-done((f32[48,1408]{1,0:T(8,128)S(1)}, f32[48,1408]{1,0:T(8,128)S(1)}, u32[]{:S(2)}, u32[]{:S(2)}) %collective-permute-start.6) | collective-permute-done | bytes 270368 | tf_op jit(solution)/shard_map/ppermute | solution.py:28
  71.0 2.9 %collective-permute-done.7.refs_1_ = f32[48,1408]{1,0:T(8,128)S(1)} collective-permute-done((f32[48,1408]{1,0:T(8,128)S(1)}, f32[48,1408]{1,0:T(8,128)S(1)}, u32[]{:S(2)}, u32[]{:S(2)}) %collective-permute-start.7) | collective-permute-done | bytes 270368 | tf_op jit(solution)/shard_map/ppermute | solution.py:28
  74.5 1.8 %collective-permute-start.8 = (f32[48,1408]{1,0:T(8,128)S(1)}, f32[48,1408]{1,0:T(8,128)S(1)}, u32[]{:S(2)}, u32[]{:S(2)}) collective-permute-start(f32[48,1408]{1,0:T(8,128)S(1)} %get-tuple-element.50), channel_id=1, source_target_pairs={{0,4},{4,8},{8,12},{12,16},{16,20},{20,24},{24,28},{28,0},{1,5},{5... | collective-permute-start | bytes 811016 | tf_op jit(solution)/shard_map/ppermute | solution.py:28
  76.6 4.4 %collective-permute-done.8.refs_0_ = f32[48,1408]{1,0:T(8,128)S(1)} collective-permute-done((f32[48,1408]{1,0:T(8,128)S(1)}, f32[48,1408]{1,0:T(8,128)S(1)}, u32[]{:S(2)}, u32[]{:S(2)}) %collective-permute-start.8) | collective-permute-done | bytes 270368 | tf_op jit(solution)/shard_map/ppermute | solution.py:28
  81.0 1.7 %collective-permute-done.9.refs_1_ = f32[48,1408]{1,0:T(8,128)S(1)} collective-permute-done((f32[48,1408]{1,0:T(8,128)S(1)}, f32[48,1408]{1,0:T(8,128)S(1)}, u32[]{:S(2)}, u32[]{:S(2)}) %collective-permute-start.9) | collective-permute-done | bytes 270368 | tf_op jit(solution)/shard_map/ppermute | solution.py:28
  83.4 1.8 %collective-permute-start.10 = (f32[48,1408]{1,0:T(8,128)S(1)}, f32[48,1408]{1,0:T(8,128)S(1)}, u32[]{:S(2)}, u32[]{:S(2)}) collective-permute-start(f32[48,1408]{1,0:T(8,128)S(1)} %get-tuple-element.52), channel_id=1, source_target_pairs={{0,4},{4,8},{8,12},{12,16},{16,20},{20,24},{24,28},{28,0},{1,5},{5... | collective-permute-start | bytes 811016 | tf_op jit(solution)/shard_map/ppermute | solution.py:28
  85.7 4.4 %collective-permute-done.10.up_in = f32[48,1408]{1,0:T(8,128)S(1)} collective-permute-done((f32[48,1408]{1,0:T(8,128)S(1)}, f32[48,1408]{1,0:T(8,128)S(1)}, u32[]{:S(2)}, u32[]{:S(2)}) %collective-permute-start.10) | collective-permute-done | bytes 270368 | tf_op jit(solution)/shard_map/ppermute | solution.py:28
  90.1 1.6 %collective-permute-done.11.down_in = f32[48,1408]{1,0:T(8,128)S(1)} collective-permute-done((f32[48,1408]{1,0:T(8,128)S(1)}, f32[48,1408]{1,0:T(8,128)S(1)}, u32[]{:S(2)}, u32[]{:S(2)}) %collective-permute-start.11) | collective-permute-done | bytes 270368 | tf_op jit(solution)/shard_map/ppermute | solution.py:28
  92.6 1.7 %collective-permute-start.13 = (bf16[48,1408]{1,0:T(8,128)(2,1)S(1)}, bf16[48,1408]{1,0:T(8,128)(2,1)S(1)}, u32[]{:S(2)}, u32[]{:S(2)}) collective-permute-start(bf16[48,1408]{1,0:T(8,128)(2,1)S(1)} %get-tuple-element.55.refs_0_), channel_id=1, source_target_pairs={{0,2},{2,0},{1,3},{3,1},{4,6},{6,4},{5,7},{7,5},{8,10},{10,8},{9,1... | collective-permute-start | bytes 405512 | tf_op jit(solution)/shard_map/ppermute | solution.py:23
  94.2 1.5 collective-permute-start.12
  96.3 1.7 %shard_map.56 = f32[32,16,128]{2,1,0:T(8,128)} custom-call(f32[48,1408]{1,0:T(8,128)S(1)} %get-tuple-element.56.rows_ref), custom_call_target="tpu_custom_call" | custom-call | tf_op jit(solution)/shard_map/pallas_call | solution.py:383
  98.0 1.2 collective-permute-done.13.refs_1_
  99.2 1.5 collective-permute-start.14
  101.2 7.2 %all-to-all-start.1 = ((f32[32,16,128]{2,1,0:T(8,128)}), f32[32,16,128]{2,1,0:T(8,128)S(1)}, u32[]{:S(2)}, u32[]{:S(2)}) async-start(f32[32,16,128]{2,1,0:T(8,128)} %shard_map.56), calls=%async_computation.1 | async-start | bytes 524288 | tf_op jit(solution)/shard_map/all_to_all | solution.py:391
  108.8 1.8 %collective-permute-start.17 = (bf16[88,1408]{1,0:T(8,128)(2,1)S(1)}, bf16[88,1408]{1,0:T(8,128)(2,1)S(1)}, u32[]{:S(2)}, u32[]{:S(2)}) collective-permute-start(bf16[88,1408]{1,0:T(8,128)(2,1)S(1)} %get-tuple-element.58.refs_4_), channel_id=1, source_target_pairs={{0,4},{4,8},{8,12},{12,16},{16,20},{20,24},{24,28},{28,0},{1,5},{5... | collective-permute-start | bytes 743432 | tf_op jit(solution)/shard_map/ppermute | solution.py:28
  111.4 10.5 %collective-permute-done.18.down_ref.refs_6_ = bf16[88,1408]{1,0:T(8,128)(2,1)S(1)} collective-permute-done((bf16[88,1408]{1,0:T(8,128)(2,1)S(1)}, bf16[88,1408]{1,0:T(8,128)(2,1)S(1)}, u32[]{:S(2)}, u32[]{:S(2)}) %collective-permute-start.18) | collective-permute-done | bytes 247840 | tf_op jit(solution)/shard_map/ppermute | solution.py:28
  122.4 1.4 collective-permute-start.22
  124.6 4.9 %collective-permute-start.24 = (bf16[48,1408]{1,0:T(8,128)(2,1)S(1)}, bf16[48,1408]{1,0:T(8,128)(2,1)S(1)}, u32[]{:S(2)}, u32[]{:S(2)}) collective-permute-start(bf16[48,1408]{1,0:T(8,128)(2,1)S(1)} %get-tuple-element.62), channel_id=1, source_target_pairs={{0,8},{4,12},{8,16},{12,20},{16,24},{20,28},{24,0},{28,4},{1,9},{5... | collective-permute-start | bytes 405512 | tf_op jit(solution)/shard_map/ppermute | solution.py:28
  129.4 5.4 %shard_map.60 = (f32[48,1408]{1,0:T(8,128)S(1)}, f32[8,48,176]{2,1,0:T(8,128)S(1)}, bf16[48,1408]{1,0:T(8,128)(2,1)S(1)}, bf16[8,2,48,88]{3,2,1,0:T(8,128)(2,1)S(1)}) custom-call(s32[7]{0:T(128)S(1)} %stack.27.where_ref, f32[48,1408]{1,0:T(8,128)S(1)} %get-tuple-element.56.rows_ref, f32[32,16,128]{2,1,0:T(8,128)S(1)} %all-to-all-done.1.after_ref.columns_ref, ...), custom_call_target="tpu_custom_call" | custom-call | flops 129761280 | bytes 2703360 | tf_op jit(solution)/shard_map/pallas_call | solution.py:424
  134.9 5.0 %collective-permute-done.24.refs_4_ = bf16[48,1408]{1,0:T(8,128)(2,1)S(1)} collective-permute-done((bf16[48,1408]{1,0:T(8,128)(2,1)S(1)}, bf16[48,1408]{1,0:T(8,128)(2,1)S(1)}, u32[]{:S(2)}, u32[]{:S(2)}) %collective-permute-start.24) | collective-permute-done | bytes 135200 | tf_op jit(solution)/shard_map/ppermute | solution.py:28
  142.2 1.7 %shard_map.61 = f32[8,72,128]{2,1,0:T(8,128)S(1)} custom-call(s32[7]{0:T(128)S(1)} %stack.27.where_ref, f32[48,1408]{1,0:T(8,128)S(1)} %get-tuple-element.71.total_ref, f32[8,48,176]{2,1,0:T(8,128)S(1)} %get-tuple-element.72.blocks_ref, bf16[48,1408]{1,0:T(8,128)(2,1)S(1)} %get-tuple-element.73.tilde_ref, ...), custom_call_target="tpu_custom_call" | custom-call | flops 77856768 | bytes 1622016 | tf_op jit(solution)/shard_map/pallas_call | solution.py:438
  143.9 10.8 %all_to_all.16.parts_ref = f32[8,72,128]{2,1,0:T(8,128)S(1)} all-to-all(f32[8,72,128]{2,1,0:T(8,128)S(1)} %shard_map.61), channel_id=1, replica_groups=mesh['x'=4,'yl'=2,'z'=8,'yh'=2,'c'=2] {'x','yl'}, dimensions={0} | all-to-all | bytes 589824 | tf_op jit(solution)/shard_map/all_to_all | solution.py:458
  (66 shorter events, 15.1 us)
Async XLA Ops:
  3.1 2.9 %collective-permute-start = (bf16[8,184,300]{2,1,0:T(8,128)(2,1)S(1)}, bf16[8,184,300]{2,1,0:T(8,128)(2,1)S(1)}, u32[]{:S(2)}, u32[]{:S(2)}) collective-permute-start(bf16[8,184,300]{2,1,0:T(8,128)(2,1)S(1)} %shard_map.46), channel_id=1, source_target_pairs={{0,1},{1,0},{2,3},{3,2},{4,5},{5,4},{6,7},{7,6},{8,9},{9,8},{10,11... | collective-permute-start | bytes 2649608 | tf_op jit(solution)/shard_map/ppermute | solution.py:23
  49.4 3.9 %collective-permute-start.1 = (bf16[16,88,600]{2,1,0:T(8,128)(2,1)S(1)}, bf16[16,88,600]{2,1,0:T(8,128)(2,1)S(1)}, u32[]{:S(2)}, u32[]{:S(2)}) collective-permute-start(bf16[16,88,600]{2,1,0:T(8,128)(2,1)S(1)} %slice.4), channel_id=1, source_target_pairs={{0,1},{1,0},{2,3},{3,2},{4,5},{5,4},{6,7},{7,6},{8,9},{9,8},{10,11... | collective-permute-start | bytes 5068808 | tf_op jit(solution)/shard_map/ppermute | solution.py:23
  51.2 9.3 %collective-permute-start.2 = (f32[24,704]{1,0:T(8,128)S(1)}, f32[24,704]{1,0:T(8,128)S(1)}, u32[]{:S(2)}, u32[]{:S(2)}) collective-permute-start(f32[24,704]{1,0:T(8,128)S(1)} %get-tuple-element.44), channel_id=1, source_target_pairs={{0,4},{4,8},{8,12},{12,16},{16,20},{20,24},{24,28},{28,0},{1,5},{5... | collective-permute-start | bytes 202760 | tf_op jit(solution)/shard_map/ppermute | solution.py:28
  53.2 7.3 %collective-permute-start.3 = (f32[24,704]{1,0:T(8,128)S(1)}, f32[24,704]{1,0:T(8,128)S(1)}, u32[]{:S(2)}, u32[]{:S(2)}) collective-permute-start(f32[24,704]{1,0:T(8,128)S(1)} %get-tuple-element.45), channel_id=1, source_target_pairs={{0,28},{4,0},{8,4},{12,8},{16,12},{20,16},{24,20},{28,24},{1,29},{... | collective-permute-start | bytes 202760 | tf_op jit(solution)/shard_map/ppermute | solution.py:28
  54.5 6.8 %collective-permute-start.4 = (f32[24,704]{1,0:T(8,128)S(1)}, f32[24,704]{1,0:T(8,128)S(1)}, u32[]{:S(2)}, u32[]{:S(2)}) collective-permute-start(f32[24,704]{1,0:T(8,128)S(1)} %get-tuple-element.46), channel_id=1, source_target_pairs={{0,4},{4,8},{8,12},{12,16},{16,20},{20,24},{24,28},{28,0},{1,5},{5... | collective-permute-start | bytes 202760 | tf_op jit(solution)/shard_map/ppermute | solution.py:28
  56.5 5.4 %collective-permute-start.5 = (f32[24,704]{1,0:T(8,128)S(1)}, f32[24,704]{1,0:T(8,128)S(1)}, u32[]{:S(2)}, u32[]{:S(2)}) collective-permute-start(f32[24,704]{1,0:T(8,128)S(1)} %get-tuple-element.47), channel_id=1, source_target_pairs={{0,28},{4,0},{8,4},{12,8},{16,12},{20,16},{24,20},{28,24},{1,29},{... | collective-permute-start | bytes 202760 | tf_op jit(solution)/shard_map/ppermute | solution.py:28
  62.5 8.5 %collective-permute-start.6 = (f32[48,1408]{1,0:T(8,128)S(1)}, f32[48,1408]{1,0:T(8,128)S(1)}, u32[]{:S(2)}, u32[]{:S(2)}) collective-permute-start(f32[48,1408]{1,0:T(8,128)S(1)} %get-tuple-element.48), channel_id=1, source_target_pairs={{0,4},{4,8},{8,12},{12,16},{16,20},{20,24},{24,28},{28,0},{1,5},{5... | collective-permute-start | bytes 811016 | tf_op jit(solution)/shard_map/ppermute | solution.py:28
  65.8 8.1 %collective-permute-start.7 = (f32[48,1408]{1,0:T(8,128)S(1)}, f32[48,1408]{1,0:T(8,128)S(1)}, u32[]{:S(2)}, u32[]{:S(2)}) collective-permute-start(f32[48,1408]{1,0:T(8,128)S(1)} %get-tuple-element.49), channel_id=1, source_target_pairs={{0,28},{4,0},{8,4},{12,8},{16,12},{20,16},{24,20},{28,24},{1,29},{... | collective-permute-start | bytes 811016 | tf_op jit(solution)/shard_map/ppermute | solution.py:28
  74.5 6.5 %collective-permute-start.8 = (f32[48,1408]{1,0:T(8,128)S(1)}, f32[48,1408]{1,0:T(8,128)S(1)}, u32[]{:S(2)}, u32[]{:S(2)}) collective-permute-start(f32[48,1408]{1,0:T(8,128)S(1)} %get-tuple-element.50), channel_id=1, source_target_pairs={{0,4},{4,8},{8,12},{12,16},{16,20},{20,24},{24,28},{28,0},{1,5},{5... | collective-permute-start | bytes 811016 | tf_op jit(solution)/shard_map/ppermute | solution.py:28
  76.3 6.5 %collective-permute-start.9 = (f32[48,1408]{1,0:T(8,128)S(1)}, f32[48,1408]{1,0:T(8,128)S(1)}, u32[]{:S(2)}, u32[]{:S(2)}) collective-permute-start(f32[48,1408]{1,0:T(8,128)S(1)} %get-tuple-element.51), channel_id=1, source_target_pairs={{0,28},{4,0},{8,4},{12,8},{16,12},{20,16},{24,20},{28,24},{1,29},{... | collective-permute-start | bytes 811016 | tf_op jit(solution)/shard_map/ppermute | solution.py:28
  83.4 6.7 %collective-permute-start.10 = (f32[48,1408]{1,0:T(8,128)S(1)}, f32[48,1408]{1,0:T(8,128)S(1)}, u32[]{:S(2)}, u32[]{:S(2)}) collective-permute-start(f32[48,1408]{1,0:T(8,128)S(1)} %get-tuple-element.52), channel_id=1, source_target_pairs={{0,4},{4,8},{8,12},{12,16},{16,20},{20,24},{24,28},{28,0},{1,5},{5... | collective-permute-start | bytes 811016 | tf_op jit(solution)/shard_map/ppermute | solution.py:28
  85.2 6.5 %collective-permute-start.11 = (f32[48,1408]{1,0:T(8,128)S(1)}, f32[48,1408]{1,0:T(8,128)S(1)}, u32[]{:S(2)}, u32[]{:S(2)}) collective-permute-start(f32[48,1408]{1,0:T(8,128)S(1)} %get-tuple-element.53), channel_id=1, source_target_pairs={{0,28},{4,0},{8,4},{12,8},{16,12},{20,16},{24,20},{28,24},{1,29},{... | collective-permute-start | bytes 811016 | tf_op jit(solution)/shard_map/ppermute | solution.py:28
  92.6 6.6 %collective-permute-start.13 = (bf16[48,1408]{1,0:T(8,128)(2,1)S(1)}, bf16[48,1408]{1,0:T(8,128)(2,1)S(1)}, u32[]{:S(2)}, u32[]{:S(2)}) collective-permute-start(bf16[48,1408]{1,0:T(8,128)(2,1)S(1)} %get-tuple-element.55.refs_0_), channel_id=1, source_target_pairs={{0,2},{2,0},{1,3},{3,1},{4,6},{6,4},{5,7},{7,5},{8,10},{10,8},{9,1... | collective-permute-start | bytes 405512 | tf_op jit(solution)/shard_map/ppermute | solution.py:23
  94.2 14.2 %collective-permute-start.12 = (bf16[48,1408]{1,0:T(8,128)(2,1)S(1)}, bf16[48,1408]{1,0:T(8,128)(2,1)S(1)}, u32[]{:S(2)}, u32[]{:S(2)}) collective-permute-start(bf16[48,1408]{1,0:T(8,128)(2,1)S(1)} %get-tuple-element.55.refs_0_), channel_id=1, source_target_pairs={{0,4},{4,8},{8,12},{12,16},{16,20},{20,24},{24,28},{28,0},{1,5},{5... | collective-permute-start | bytes 405512 | tf_op jit(solution)/shard_map/ppermute | solution.py:28
  95.7 12.7 %collective-permute-start.15 = (bf16[48,1408]{1,0:T(8,128)(2,1)S(1)}, bf16[48,1408]{1,0:T(8,128)(2,1)S(1)}, u32[]{:S(2)}, u32[]{:S(2)}) collective-permute-start(bf16[48,1408]{1,0:T(8,128)(2,1)S(1)} %get-tuple-element.55.refs_0_), channel_id=1, source_target_pairs={{0,28},{4,0},{8,4},{12,8},{16,12},{20,16},{24,20},{28,24},{1,29},{... | collective-permute-start | bytes 405512 | tf_op jit(solution)/shard_map/ppermute | solution.py:28
  99.2 9.3 %collective-permute-start.14 = (bf16[48,1408]{1,0:T(8,128)(2,1)S(1)}, bf16[48,1408]{1,0:T(8,128)(2,1)S(1)}, u32[]{:S(2)}, u32[]{:S(2)}) collective-permute-start(bf16[48,1408]{1,0:T(8,128)(2,1)S(1)} %collective-permute-done.13.refs_1_), channel_id=1, source_target_pairs={{0,4},{4,8},{8,12},{12,16},{16,20},{20,24},{24,28},{28,0},{1,5},{5... | collective-permute-start | bytes 405512 | tf_op jit(solution)/shard_map/ppermute | solution.py:28
  100.7 7.8 %collective-permute-start.16 = (bf16[48,1408]{1,0:T(8,128)(2,1)S(1)}, bf16[48,1408]{1,0:T(8,128)(2,1)S(1)}, u32[]{:S(2)}, u32[]{:S(2)}) collective-permute-start(bf16[48,1408]{1,0:T(8,128)(2,1)S(1)} %collective-permute-done.13.refs_1_), channel_id=1, source_target_pairs={{0,28},{4,0},{8,4},{12,8},{16,12},{20,16},{24,20},{28,24},{1,29},{... | collective-permute-start | bytes 405512 | tf_op jit(solution)/shard_map/ppermute | solution.py:28
  101.2 23.3 %all-to-all-start.1 = ((f32[32,16,128]{2,1,0:T(8,128)}), f32[32,16,128]{2,1,0:T(8,128)S(1)}, u32[]{:S(2)}, u32[]{:S(2)}) async-start(f32[32,16,128]{2,1,0:T(8,128)} %shard_map.56), calls=%async_computation.1 | async-start | bytes 524288 | tf_op jit(solution)/shard_map/all_to_all | solution.py:391
  108.5 13.4 %collective-permute-start.18 = (bf16[88,1408]{1,0:T(8,128)(2,1)S(1)}, bf16[88,1408]{1,0:T(8,128)(2,1)S(1)}, u32[]{:S(2)}, u32[]{:S(2)}) collective-permute-start(bf16[88,1408]{1,0:T(8,128)(2,1)S(1)} %get-tuple-element.59.refs_2_), channel_id=1, source_target_pairs={{0,28},{4,0},{8,4},{12,8},{16,12},{20,16},{24,20},{28,24},{1,29},{... | collective-permute-start | bytes 743432 | tf_op jit(solution)/shard_map/ppermute | solution.py:28
  108.8 13.1 %collective-permute-start.17 = (bf16[88,1408]{1,0:T(8,128)(2,1)S(1)}, bf16[88,1408]{1,0:T(8,128)(2,1)S(1)}, u32[]{:S(2)}, u32[]{:S(2)}) collective-permute-start(bf16[88,1408]{1,0:T(8,128)(2,1)S(1)} %get-tuple-element.58.refs_4_), channel_id=1, source_target_pairs={{0,4},{4,8},{8,12},{12,16},{16,20},{20,24},{24,28},{28,0},{1,5},{5... | collective-permute-start | bytes 743432 | tf_op jit(solution)/shard_map/ppermute | solution.py:28
  110.7 11.8 %collective-permute-start.19 = (bf16[88,1408]{1,0:T(8,128)(2,1)S(1)}, bf16[88,1408]{1,0:T(8,128)(2,1)S(1)}, u32[]{:S(2)}, u32[]{:S(2)}) collective-permute-start(bf16[88,1408]{1,0:T(8,128)(2,1)S(1)} %shard_map.58.refs_0_), channel_id=1, source_target_pairs={{0,1},{1,0},{2,3},{3,2},{4,5},{5,4},{6,7},{7,6},{8,9},{9,8},{10,11... | collective-permute-start | bytes 743432 | tf_op jit(solution)/shard_map/ppermute | solution.py:23
  110.8 11.7 %collective-permute-start.20 = (bf16[88,1408]{1,0:T(8,128)(2,1)S(1)}, bf16[88,1408]{1,0:T(8,128)(2,1)S(1)}, u32[]{:S(2)}, u32[]{:S(2)}) collective-permute-start(bf16[88,1408]{1,0:T(8,128)(2,1)S(1)} %get-tuple-element.59.refs_2_), channel_id=1, source_target_pairs={{0,1},{1,0},{2,3},{3,2},{4,5},{5,4},{6,7},{7,6},{8,9},{9,8},{10,11... | collective-permute-start | bytes 743432 | tf_op jit(solution)/shard_map/ppermute | solution.py:23
  111.3 11.2 %collective-permute-start.21 = (bf16[88,1408]{1,0:T(8,128)(2,1)S(1)}, bf16[88,1408]{1,0:T(8,128)(2,1)S(1)}, u32[]{:S(2)}, u32[]{:S(2)}) collective-permute-start(bf16[88,1408]{1,0:T(8,128)(2,1)S(1)} %get-tuple-element.58.refs_4_), channel_id=1, source_target_pairs={{0,1},{1,0},{2,3},{3,2},{4,5},{5,4},{6,7},{7,6},{8,9},{9,8},{10,11... | collective-permute-start | bytes 743432 | tf_op jit(solution)/shard_map/ppermute | solution.py:23
  121.9 7.5 %collective-permute-start.26 = (bf16[88,1408]{1,0:T(8,128)(2,1)S(1)}, bf16[88,1408]{1,0:T(8,128)(2,1)S(1)}, u32[]{:S(2)}, u32[]{:S(2)}) collective-permute-start(bf16[88,1408]{1,0:T(8,128)(2,1)S(1)} %collective-permute-done.18.down_ref.refs_6_), channel_id=1, source_target_pairs={{0,1},{1,0},{2,3},{3,2},{4,5},{5,4},{6,7},{7,6},{8,9},{9,8},{10,11... | collective-permute-start | bytes 743432 | tf_op jit(solution)/shard_map/ppermute | solution.py:23
  121.9 7.5 %collective-permute-start.27 = (bf16[88,1408]{1,0:T(8,128)(2,1)S(1)}, bf16[88,1408]{1,0:T(8,128)(2,1)S(1)}, u32[]{:S(2)}, u32[]{:S(2)}) collective-permute-start(bf16[88,1408]{1,0:T(8,128)(2,1)S(1)} %collective-permute-done.17.up_ref.refs_8_), channel_id=1, source_target_pairs={{0,1},{1,0},{2,3},{3,2},{4,5},{5,4},{6,7},{7,6},{8,9},{9,8},{10,11... | collective-permute-start | bytes 743432 | tf_op jit(solution)/shard_map/ppermute | solution.py:23
  122.4 17.4 %collective-permute-start.22 = (bf16[88,1408]{1,0:T(8,128)(2,1)S(1)}, bf16[88,1408]{1,0:T(8,128)(2,1)S(1)}, u32[]{:S(2)}, u32[]{:S(2)}) collective-permute-start(bf16[88,1408]{1,0:T(8,128)(2,1)S(1)} %collective-permute-done.18.down_ref.refs_6_), channel_id=1, source_target_pairs={{0,28},{4,0},{8,4},{12,8},{16,12},{20,16},{24,20},{28,24},{1,29},{... | collective-permute-start | bytes 743432 | tf_op jit(solution)/shard_map/ppermute | solution.py:28
  123.9 16.0 %collective-permute-start.23 = (bf16[88,1408]{1,0:T(8,128)(2,1)S(1)}, bf16[88,1408]{1,0:T(8,128)(2,1)S(1)}, u32[]{:S(2)}, u32[]{:S(2)}) collective-permute-start(bf16[88,1408]{1,0:T(8,128)(2,1)S(1)} %collective-permute-done.17.up_ref.refs_8_), channel_id=1, source_target_pairs={{0,4},{4,8},{8,12},{12,16},{16,20},{20,24},{24,28},{28,0},{1,5},{5... | collective-permute-start | bytes 743432 | tf_op jit(solution)/shard_map/ppermute | solution.py:28
  124.6 15.3 %collective-permute-start.24 = (bf16[48,1408]{1,0:T(8,128)(2,1)S(1)}, bf16[48,1408]{1,0:T(8,128)(2,1)S(1)}, u32[]{:S(2)}, u32[]{:S(2)}) collective-permute-start(bf16[48,1408]{1,0:T(8,128)(2,1)S(1)} %get-tuple-element.62), channel_id=1, source_target_pairs={{0,8},{4,12},{8,16},{12,20},{16,24},{20,28},{24,0},{28,4},{1,9},{5... | collective-permute-start | bytes 405512 | tf_op jit(solution)/shard_map/ppermute | solution.py:28
  129.4 10.4 %collective-permute-start.25 = (bf16[48,1408]{1,0:T(8,128)(2,1)S(1)}, bf16[48,1408]{1,0:T(8,128)(2,1)S(1)}, u32[]{:S(2)}, u32[]{:S(2)}) collective-permute-start(bf16[48,1408]{1,0:T(8,128)(2,1)S(1)} %get-tuple-element.63), channel_id=1, source_target_pairs={{0,24},{4,28},{8,0},{12,4},{16,8},{20,12},{24,16},{28,20},{1,25},{... | collective-permute-start | bytes 405512 | tf_op jit(solution)/shard_map/ppermute | solution.py:28
  139.9 2.3 %collective-permute-start.28 = (bf16[88,1408]{1,0:T(8,128)(2,1)S(1)}, bf16[88,1408]{1,0:T(8,128)(2,1)S(1)}, u32[]{:S(2)}, u32[]{:S(2)}) collective-permute-start(bf16[88,1408]{1,0:T(8,128)(2,1)S(1)} %collective-permute-done.22.refs_0_), channel_id=1, source_target_pairs={{0,1},{1,0},{2,3},{3,2},{4,5},{5,4},{6,7},{7,6},{8,9},{9,8},{10,11... | collective-permute-start | bytes 743432 | tf_op jit(solution)/shard_map/ppermute | solution.py:23
  140.0 2.2 %collective-permute-start.29 = (bf16[88,1408]{1,0:T(8,128)(2,1)S(1)}, bf16[88,1408]{1,0:T(8,128)(2,1)S(1)}, u32[]{:S(2)}, u32[]{:S(2)}) collective-permute-start(bf16[88,1408]{1,0:T(8,128)(2,1)S(1)} %collective-permute-done.23.refs_2_), channel_id=1, source_target_pairs={{0,1},{1,0},{2,3},{3,2},{4,5},{5,4},{6,7},{7,6},{8,9},{9,8},{10,11... | collective-permute-start | bytes 743432 | tf_op jit(solution)/shard_map/ppermute | solution.py:23
  140.6 1.6 %collective-permute-start.31 = (bf16[48,1408]{1,0:T(8,128)(2,1)S(1)}, bf16[48,1408]{1,0:T(8,128)(2,1)S(1)}, u32[]{:S(2)}, u32[]{:S(2)}) collective-permute-start(bf16[48,1408]{1,0:T(8,128)(2,1)S(1)} %collective-permute-done.25.refs_5_), channel_id=1, source_target_pairs={{0,1},{1,0},{2,3},{3,2},{4,5},{5,4},{6,7},{7,6},{8,9},{9,8},{10,11... | collective-permute-start | bytes 405512 | tf_op jit(solution)/shard_map/ppermute | solution.py:23
  (6 other events, 20.4 us)
